TPU v7x, 128 devices: a whole 4x4x4 slice. The times are simulated.
128 devices in a mesh: dp: 2 (over core), ctx: 16 (over y, z), tp: 4 (over x).
Axes of the slice: x: 4, y: 4, z: 4, core: 2. Of those that a mesh axis runs over, the one named last changes fastest.
Arguments:
- queries: bfloat16 [2, 32768, 1024], P('dp', 'ctx', 'tp'), may hold values from -16 to 16
- key_vectors: bfloat16 [2, 32768, 1024], P('dp', 'ctx', 'tp'), may hold values from -16 to 16
- value_vectors: bfloat16 [2, 32768, 1024], P('dp', 'ctx', 'tp'), may hold values from -6 to 6
- grad_output: bfloat16 [2, 32768, 1024], P('dp', 'ctx', 'tp'), may hold values from -6 to 6
- out_weight: bfloat16 [1024, 1024], P('tp'), may hold values from -0.1875 to 0.1875
- random_ids: int32 [2, 512, 3], P('dp'), may hold values from 0 to 511, as said below
- random_valid: int32 [2, 512, 3], P('dp'), may hold values 0 or 1
- global_ids: int32 [2, 2], P('dp'), may hold values from 0 to 511, as said below
Outputs:
- projected: bfloat16 [2, 32768, 1024], P('dp', 'ctx', 'tp')
- grad_queries: bfloat16 [2, 32768, 1024], P('dp', 'ctx', 'tp')
- grad_keys: bfloat16 [2, 32768, 1024], P('dp', 'ctx', 'tp')
- grad_values: bfloat16 [2, 32768, 1024], P('dp', 'ctx', 'tp')
- grad_weight: float32 [1024, 1024], P('tp')
Inputs may be any that keep to these rules, and one draw needn't show every extreme that they name: `random_ids`: entries name blocks of the same document. For each document and each ctx index i (query blocks 32 * i to 32 * i + 31), the random entries of those rows name blocks of exactly 12 ctx indices, 8 entries for each of them, padding entries included. `global_ids`: the 2 numbers of a document differ; one of them is the document's last block, 511.
All inputs are finite; a program needn't handle non-finite values. No bound on the sum of `random_valid` on one device may be relied on, other than what follows from the above.
Results may differ from a plain program's by a relative error of at most 0.02.
Values may be sent and summed in bfloat16 or wider, within the bound.
No kernel may reach another device: no remote copies, remote signals or barrier semaphores. Data moves between devices by JAX's collectives and lax.ppermute only.
A program may use at most 192 MiB of HBM per device.

v0:
```python
import math

import jax
import jax.numpy as jnp
from jax import lax
from jax.sharding import PartitionSpec as P

HD = 64
BLK = 64
R = 3
G = 2


NEG_FILL = -1e30


def padded_2(array, sides, width):
    for axis, dim in sides:
        size, length = (lax.axis_size(axis), array.shape[dim])
        up = [(i, (i + 1) % size) for i in range(size - 1)]
        down = [(j, i) for i, j in up]
        last = lax.slice_in_dim(array, length - width, length, axis=dim)
        initial = lax.slice_in_dim(array, 0, width, axis=dim)
        before = lax.ppermute(last, axis, up)
        after = lax.ppermute(initial, axis, down)
        array = jnp.concatenate([before, array, after], axis=dim)
    return array


def passed_along(array, axis, by):
    size = lax.axis_size(axis)
    pairs = [(i, i + by) for i in range(size) if 0 <= i + by < size]
    return lax.ppermute(array, axis, pairs)


def attend_block(query_now, key_set, value_set, present, grad_now):
    scaling = 1.0 / math.sqrt(query_now.shape[-1])
    scores = (
        jnp.einsum("gqhd,gkhd->ghqk", query_now, key_set, preferred_element_type=jnp.float32)
        * scaling
    )
    keep_mask = present[:, None, None, :]
    scores = jnp.where(keep_mask, scores, NEG_FILL)
    row_peak = jnp.max(scores, axis=-1, keepdims=True)
    exp_terms = jnp.where(keep_mask, jnp.exp(scores - row_peak), 0.0)
    prob_full = exp_terms / jnp.sum(exp_terms, axis=-1, keepdims=True)
    prob_low = prob_full.astype(jnp.bfloat16)
    context = jnp.einsum(
        "ghqk,gkhd->gqhd", prob_low, value_set, preferred_element_type=jnp.float32
    ).astype(jnp.bfloat16)
    grad_prob = jnp.einsum(
        "gqhd,gkhd->ghqk", grad_now, value_set, preferred_element_type=jnp.float32
    )
    row_delta = jnp.sum(prob_full * grad_prob, axis=-1, keepdims=True)
    grad_score = (prob_full * (grad_prob - row_delta) * scaling).astype(jnp.bfloat16)
    grad_query = jnp.einsum(
        "ghqk,gkhd->gqhd", grad_score, key_set, preferred_element_type=jnp.float32
    ).astype(jnp.bfloat16)
    grad_key = jnp.einsum(
        "ghqk,gqhd->gkhd", grad_score, query_now, preferred_element_type=jnp.float32
    )
    grad_value = jnp.einsum(
        "ghqk,gqhd->gkhd", prob_low, grad_now, preferred_element_type=jnp.float32
    )
    return (context, grad_query, grad_key, grad_value)


def per_device(
    queries,
    key_vectors,
    value_vectors,
    grad_output,
    out_weight,
    random_ids,
    random_valid,
    global_ids,
):
    ctx_count = lax.axis_size("ctx")
    my_pos = lax.axis_index("ctx")
    token_count = queries.shape[1]
    width_local = queries.shape[2]
    heads_local = width_local // HD
    block_count = token_count // BLK
    total_blocks = block_count * ctx_count
    used_count = ctx_count * 3 // 4
    capacity = block_count * R // used_count
    request_count = block_count * R
    entry_count = 3 + R + G
    group_size = math.gcd(block_count, 8)
    group_count = block_count // group_size
    grad_full = lax.all_gather(grad_output, "tp", axis=2, tiled=True)[0]
    grad_context = jnp.einsum(
        "td,hd->th", grad_full, out_weight, preferred_element_type=jnp.float32
    ).astype(jnp.bfloat16)
    key_value = jnp.stack([key_vectors[0], value_vectors[0]])
    blocks_kv = key_value.reshape(2, block_count, BLK, width_local)
    padded = padded_2(key_value, (("ctx", 1),), BLK)
    padded_blocks = padded.reshape(2, block_count + 2, BLK, width_local)
    glob_list = global_ids[0]
    glob_owner = glob_list // block_count
    glob_local = glob_list % block_count
    owned_here = glob_owner == my_pos
    picked = blocks_kv[:, glob_local]
    picked = jnp.where(owned_here[None, :, None, None], picked.astype(jnp.float32), 0.0)
    global_kv = lax.psum(picked.astype(jnp.bfloat16), "ctx")
    flat_ids = random_ids[0].reshape(ctx_count, request_count)
    owner_all = flat_ids // block_count
    local_all = flat_ids % block_count
    onehot = (
        owner_all[:, :, None] == jnp.arange(ctx_count, dtype=jnp.int32)[None, None, :]
    ).astype(jnp.int32)
    rank_all = jnp.sum((jnp.cumsum(onehot, axis=1) - 1) * onehot, axis=2)
    to_me = owner_all == my_pos
    slot_col = jnp.where(to_me, rank_all, capacity)
    requester = jnp.broadcast_to(jnp.arange(ctx_count, dtype=jnp.int32)[:, None], owner_all.shape)
    send_idx = (
        jnp.zeros((ctx_count, capacity), jnp.int32)
        .at[requester, slot_col]
        .set(local_all, mode="drop")
    )
    send_kv = blocks_kv[:, send_idx]
    fetched = lax.all_to_all(send_kv, "ctx", split_axis=1, concat_axis=1, tiled=True)
    my_owner = lax.dynamic_index_in_dim(owner_all, my_pos, 0, keepdims=False)
    my_rank = lax.dynamic_index_in_dim(rank_all, my_pos, 0, keepdims=False)
    random_kv = fetched[:, my_owner, my_rank].reshape(2, block_count, R, BLK, width_local)
    global_block = my_pos * block_count + jnp.arange(block_count, dtype=jnp.int32)
    window_ok = jnp.stack(
        [global_block > 0, global_block >= 0, global_block < total_blocks - 1], axis=1
    )
    random_ok = lax.dynamic_slice_in_dim(random_valid[0], my_pos * block_count, block_count, 0) == 1
    entry_ok = jnp.concatenate(
        [window_ok, random_ok, jnp.ones((block_count, G), dtype=bool)], axis=1
    )
    query_blocks = queries[0].reshape(block_count, BLK, heads_local, HD)
    grad_blocks = grad_context.reshape(block_count, BLK, heads_local, HD)

    def group_step(carry, group_index):
        win_acc, glob_acc, rand_acc = carry
        row_start = group_index * group_size
        window_src = lax.dynamic_slice_in_dim(padded_blocks, row_start, group_size + 2, 1)
        window = jnp.stack(
            [
                window_src[:, 0:group_size],
                window_src[:, 1 : group_size + 1],
                window_src[:, 2 : group_size + 2],
            ],
            axis=2,
        )
        rand_now = lax.dynamic_slice_in_dim(random_kv, row_start, group_size, 1)
        glob_now = jnp.broadcast_to(global_kv[:, None], (2, group_size) + global_kv.shape[1:])
        entries = jnp.concatenate([window, rand_now, glob_now], axis=2)
        key_set = entries[0].reshape(group_size, entry_count * BLK, heads_local, HD)
        value_set = entries[1].reshape(group_size, entry_count * BLK, heads_local, HD)
        present = jnp.repeat(
            lax.dynamic_slice_in_dim(entry_ok, row_start, group_size, 0), BLK, axis=1
        )
        query_now = lax.dynamic_slice_in_dim(query_blocks, row_start, group_size, 0)
        grad_now = lax.dynamic_slice_in_dim(grad_blocks, row_start, group_size, 0)
        context, grad_query, grad_key, grad_value = attend_block(
            query_now, key_set, value_set, present, grad_now
        )
        grads = jnp.stack([grad_key, grad_value]).reshape(
            2, group_size, entry_count, BLK, width_local
        )
        for offset in range(3):
            current = lax.dynamic_slice_in_dim(win_acc, row_start + offset, group_size, 1)
            win_acc = lax.dynamic_update_slice_in_dim(
                win_acc, current + grads[:, :, offset], row_start + offset, 1
            )
        glob_acc = glob_acc + jnp.sum(grads[:, :, 3 + R :], axis=1)
        rand_terms = grads[:, :, 3 : 3 + R].astype(jnp.bfloat16)
        rand_acc = lax.dynamic_update_slice_in_dim(rand_acc, rand_terms, row_start, 1)
        return ((win_acc, glob_acc, rand_acc), (context, grad_query))

    win_init = jnp.zeros((2, block_count + 2, BLK, width_local), jnp.float32)
    glob_init = jnp.zeros((2, G, BLK, width_local), jnp.float32)
    rand_init = jnp.zeros((2, block_count, R, BLK, width_local), jnp.bfloat16)
    (win_acc, glob_acc, rand_acc), (contexts, grad_queries) = lax.scan(
        group_step, (win_init, glob_init, rand_init), jnp.arange(group_count, dtype=jnp.int32)
    )
    context_loc = contexts.reshape(token_count, width_local)
    from_next = passed_along(win_acc[:, 0].astype(jnp.bfloat16), "ctx", -1).astype(jnp.float32)
    from_prev = passed_along(win_acc[:, block_count + 1].astype(jnp.bfloat16), "ctx", 1).astype(
        jnp.float32
    )
    block_grads = win_acc[:, 1 : block_count + 1]
    block_grads = block_grads.at[:, block_count - 1].add(from_next)
    block_grads = block_grads.at[:, 0].add(from_prev)
    return_slots = jnp.zeros((2, ctx_count, capacity, BLK, width_local), jnp.bfloat16)
    return_slots = return_slots.at[:, my_owner, my_rank].set(
        rand_acc.reshape(2, request_count, BLK, width_local)
    )
    returned = lax.all_to_all(return_slots, "ctx", split_axis=1, concat_axis=1, tiled=True)
    block_grads = block_grads.at[:, send_idx.reshape(-1)].add(
        returned.reshape(2, ctx_count * capacity, BLK, width_local).astype(jnp.float32)
    )
    weight_term = jnp.einsum(
        "th,td->hd", context_loc, grad_full, preferred_element_type=jnp.float32
    )
    global_sum = lax.psum(glob_acc.astype(jnp.bfloat16), "ctx").astype(jnp.float32)
    grad_weight = lax.psum(weight_term.astype(jnp.bfloat16), ("dp", "ctx")).astype(jnp.float32)
    block_grads = block_grads.at[:, glob_local].add(
        jnp.where(owned_here[None, :, None, None], global_sum, 0.0)
    )
    partial_out = jnp.dot(context_loc, out_weight, preferred_element_type=jnp.float32)
    projected = lax.psum_scatter(partial_out, "tp", scatter_dimension=1, tiled=True).astype(
        jnp.bfloat16
    )
    grad_keys = block_grads[0].reshape(1, token_count, width_local).astype(jnp.bfloat16)
    grad_values = block_grads[1].reshape(1, token_count, width_local).astype(jnp.bfloat16)
    return (
        projected[None],
        grad_queries.reshape(1, token_count, width_local),
        grad_keys,
        grad_values,
        grad_weight,
    )


def solution(mesh):
    in_specs = (
        P("dp", "ctx", "tp"),
        P("dp", "ctx", "tp"),
        P("dp", "ctx", "tp"),
        P("dp", "ctx", "tp"),
        P("tp", None),
        P("dp", None, None),
        P("dp", None, None),
        P("dp", None),
    )
    out_specs = (
        P("dp", "ctx", "tp"),
        P("dp", "ctx", "tp"),
        P("dp", "ctx", "tp"),
        P("dp", "ctx", "tp"),
        P("tp", None),
    )
    return jax.shard_map(
        per_device, mesh=mesh, in_specs=in_specs, out_specs=out_specs, check_vma=False
    )
```

profile of v0, /device:TPU:0, one launch (start us, length us, event | category | flops | bytes accessed | tf_op | source)
XLA Modules:
  0.0 1524.7 jit_solution(17656433606468202984)
XLA Ops:
  30.0 8.3 copy.315
  38.2 8.3 all-to-all-start
  60.6 59.7 %collective-permute-done = bf16[2,64,256]{2,1,0:T(8,128)(2,1)S(1)} collective-permute-done((bf16[2,64,256]{2,1,0:T(8,128)(2,1)S(1)}, bf16[2,64,256]{2,1,0:T(8,128)(2,1)S(1)}, u32[]{:S(2)}, u32[]{:S(2)}) %collective-permute-start) | collective-permute-done | bytes 65568 | tf_op jit(solution)/shard_map/ppermute | solution.py:24
  125.4 102.7 %all-reduce.4.cloned.1.call-done = bf16[2,2,64,256]{3,2,0,1:T(8,128)(2,1)} async-done(((bf16[2,2,64,256]{3,2,0,1:T(8,128)(2,1)}), bf16[2,2,64,256]{3,2,0,1:T(8,128)(2,1)}) %all-reduce.4.cloned.1.call-update) | async-done | bytes 131088 | tf_op jit(solution)/shard_map/psum | solution.py:105
  234.5 8.3 copy.261
  242.8 10.0 gather_fusion.1
  260.9 896.1 %while.23 = (s32[]{:T(128)}, f32[2,34,64,256]{2,3,1,0:T(8,128)}, f32[2,2,64,256]{2,1,3,0:T(2,128)}, bf16[2,32,3,64,256]{4,3,0,2,1:T(8,128)(2,1)}, bf16[4,8,64,4,...) while((s32[]{:T(128)}, f32[2,34,64,256]{2,3,1,0:T(8,128)}, ...), condition=%wide.region_9.10_spmd.clone, body=%wide.region_4.9_spmd.clone.sunk | while | flops 833164800 | bytes 245032976 | solution.py:178
  307.7 38.9 %concatenate.37 = bf16[2,8,8,64,256]{3,2,4,1,0:T(8,128)(2,1)} concatenate(bf16[2,8,1,64,256]{3,2,4,1,0:T(2,128)(2,1)S(1)} %copy.334, bf16[2,8,1,64,256]{3,2,4,1,0:T(2,128)(2,1)} %copy.335, bf16[2,8,1,64,256]{3,2,4,1,0:T(2,128)(2,1)} %copy.336, bf16[2,8,3,64,256]{3,2,4,1,0:T(4,128)(2,1)} %copy.337, bf16[2,8,2,64,256]{3,2,4,1,0:T(2,128)(2,1)} %broadcast_in_dim.165), dimensions={2} | concatenate | bytes 8388608 | tf_op jit(solution)/shard_map/while/body/eval_jaxpr/concatenate | solution.py:151
  378.1 18.9 %fusion.128 = bf16[1,8,64,4,64]{2,4,3,1,0:T(8,128)(2,1)} fusion(bf16[8,512,4,64]{1,3,2,0:T(8,128)(2,1)} %copy-done.2, f32[8,4,64,512]{3,2,1,0:T(8,128)} %fusion.122, f32[8,4,64,512]{3,2,1,0:T(8,128)} %get-tuple-element.498, f32[8,4,64]{2,1,0:T(4,128)S(1)} %get-tuple-element.499), kind=kOutput, calls=%fused_computation.33.clone.1 | convolution fusion | flops 141691392 | bytes 10756096 | tf_op jit(solution)/shard_map/while/body/eval_jaxpr/ghqk,gkhd->gqhd/dot_general | solution.py:56
  404.6 7.1 stack.43
  411.7 18.9 %fusion.125 = f32[8,512,4,64]{1,3,2,0:T(8,128)} fusion(f32[8,4,64,512]{3,2,1,0:T(8,128)} %fusion.122, bf16[8,64,4,64]{3,2,1,0:T(4,128)(2,1)S(1)} %copy-done.4, f32[8,4,64,512]{3,2,1,0:T(8,128)} %get-tuple-element.498, f32[8,4,64]{2,1,0:T(4,128)S(1)} %get-tuple-element.499), kind=kOutput, calls=%fused_computation.19.clone.1 | convolution fusion | flops 141560320 | bytes 12853248 | tf_op jit(solution)/shard_map/while/body/eval_jaxpr/ghqk,gqhd->gkhd/dot_general | solution.py:59
  430.6 7.0 stack.42
  470.3 10.1 slice.219
  487.1 8.9 slice_reduce_fusion.2
  527.4 38.9 %concatenate.37 = bf16[2,8,8,64,256]{3,2,4,1,0:T(8,128)(2,1)} concatenate(bf16[2,8,1,64,256]{3,2,4,1,0:T(2,128)(2,1)S(1)} %copy.334, bf16[2,8,1,64,256]{3,2,4,1,0:T(2,128)(2,1)} %copy.335, bf16[2,8,1,64,256]{3,2,4,1,0:T(2,128)(2,1)} %copy.336, bf16[2,8,3,64,256]{3,2,4,1,0:T(4,128)(2,1)} %copy.337, bf16[2,8,2,64,256]{3,2,4,1,0:T(2,128)(2,1)} %broadcast_in_dim.165), dimensions={2} | concatenate | bytes 8388608 | tf_op jit(solution)/shard_map/while/body/eval_jaxpr/concatenate | solution.py:151
  582.7 7.0 fusion.124
  597.8 18.9 %fusion.128 = bf16[1,8,64,4,64]{2,4,3,1,0:T(8,128)(2,1)} fusion(bf16[8,512,4,64]{1,3,2,0:T(8,128)(2,1)} %copy-done.2, f32[8,4,64,512]{3,2,1,0:T(8,128)} %fusion.122, f32[8,4,64,512]{3,2,1,0:T(8,128)} %get-tuple-element.498, f32[8,4,64]{2,1,0:T(4,128)S(1)} %get-tuple-element.499), kind=kOutput, calls=%fused_computation.33.clone.1 | convolution fusion | flops 141691392 | bytes 10756096 | tf_op jit(solution)/shard_map/while/body/eval_jaxpr/ghqk,gkhd->gqhd/dot_general | solution.py:56
  624.2 7.1 stack.43
  631.3 18.9 %fusion.125 = f32[8,512,4,64]{1,3,2,0:T(8,128)} fusion(f32[8,4,64,512]{3,2,1,0:T(8,128)} %fusion.122, bf16[8,64,4,64]{3,2,1,0:T(4,128)(2,1)S(1)} %copy-done.4, f32[8,4,64,512]{3,2,1,0:T(8,128)} %get-tuple-element.498, f32[8,4,64]{2,1,0:T(4,128)S(1)} %get-tuple-element.499), kind=kOutput, calls=%fused_computation.19.clone.1 | convolution fusion | flops 141560320 | bytes 12853248 | tf_op jit(solution)/shard_map/while/body/eval_jaxpr/ghqk,gqhd->gkhd/dot_general | solution.py:59
  650.2 7.0 stack.42
  689.9 10.1 slice.219
  706.7 8.9 slice_reduce_fusion.2
  747.0 38.9 %concatenate.37 = bf16[2,8,8,64,256]{3,2,4,1,0:T(8,128)(2,1)} concatenate(bf16[2,8,1,64,256]{3,2,4,1,0:T(2,128)(2,1)S(1)} %copy.334, bf16[2,8,1,64,256]{3,2,4,1,0:T(2,128)(2,1)} %copy.335, bf16[2,8,1,64,256]{3,2,4,1,0:T(2,128)(2,1)} %copy.336, bf16[2,8,3,64,256]{3,2,4,1,0:T(4,128)(2,1)} %copy.337, bf16[2,8,2,64,256]{3,2,4,1,0:T(2,128)(2,1)} %broadcast_in_dim.165), dimensions={2} | concatenate | bytes 8388608 | tf_op jit(solution)/shard_map/while/body/eval_jaxpr/concatenate | solution.py:151
  802.4 7.0 fusion.124
  817.4 18.9 %fusion.128 = bf16[1,8,64,4,64]{2,4,3,1,0:T(8,128)(2,1)} fusion(bf16[8,512,4,64]{1,3,2,0:T(8,128)(2,1)} %copy-done.2, f32[8,4,64,512]{3,2,1,0:T(8,128)} %fusion.122, f32[8,4,64,512]{3,2,1,0:T(8,128)} %get-tuple-element.498, f32[8,4,64]{2,1,0:T(4,128)S(1)} %get-tuple-element.499), kind=kOutput, calls=%fused_computation.33.clone.1 | convolution fusion | flops 141691392 | bytes 10756096 | tf_op jit(solution)/shard_map/while/body/eval_jaxpr/ghqk,gkhd->gqhd/dot_general | solution.py:56
  843.8 7.1 stack.43
  850.9 18.9 %fusion.125 = f32[8,512,4,64]{1,3,2,0:T(8,128)} fusion(f32[8,4,64,512]{3,2,1,0:T(8,128)} %fusion.122, bf16[8,64,4,64]{3,2,1,0:T(4,128)(2,1)S(1)} %copy-done.4, f32[8,4,64,512]{3,2,1,0:T(8,128)} %get-tuple-element.498, f32[8,4,64]{2,1,0:T(4,128)S(1)} %get-tuple-element.499), kind=kOutput, calls=%fused_computation.19.clone.1 | convolution fusion | flops 141560320 | bytes 12853248 | tf_op jit(solution)/shard_map/while/body/eval_jaxpr/ghqk,gqhd->gkhd/dot_general | solution.py:59
  869.8 7.0 stack.42
  909.5 10.1 slice.219
  926.3 8.9 slice_reduce_fusion.2
  966.6 38.9 %concatenate.37 = bf16[2,8,8,64,256]{3,2,4,1,0:T(8,128)(2,1)} concatenate(bf16[2,8,1,64,256]{3,2,4,1,0:T(2,128)(2,1)S(1)} %copy.334, bf16[2,8,1,64,256]{3,2,4,1,0:T(2,128)(2,1)} %copy.335, bf16[2,8,1,64,256]{3,2,4,1,0:T(2,128)(2,1)} %copy.336, bf16[2,8,3,64,256]{3,2,4,1,0:T(4,128)(2,1)} %copy.337, bf16[2,8,2,64,256]{3,2,4,1,0:T(2,128)(2,1)} %broadcast_in_dim.165), dimensions={2} | concatenate | bytes 8388608 | tf_op jit(solution)/shard_map/while/body/eval_jaxpr/concatenate | solution.py:151
  1037.0 18.9 %fusion.128 = bf16[1,8,64,4,64]{2,4,3,1,0:T(8,128)(2,1)} fusion(bf16[8,512,4,64]{1,3,2,0:T(8,128)(2,1)} %copy-done.2, f32[8,4,64,512]{3,2,1,0:T(8,128)} %fusion.122, f32[8,4,64,512]{3,2,1,0:T(8,128)} %get-tuple-element.498, f32[8,4,64]{2,1,0:T(4,128)S(1)} %get-tuple-element.499), kind=kOutput, calls=%fused_computation.33.clone.1 | convolution fusion | flops 141691392 | bytes 10756096 | tf_op jit(solution)/shard_map/while/body/eval_jaxpr/ghqk,gkhd->gqhd/dot_general | solution.py:56
  1063.4 7.1 stack.43
  1070.5 18.9 %fusion.125 = f32[8,512,4,64]{1,3,2,0:T(8,128)} fusion(f32[8,4,64,512]{3,2,1,0:T(8,128)} %fusion.122, bf16[8,64,4,64]{3,2,1,0:T(4,128)(2,1)S(1)} %copy-done.4, f32[8,4,64,512]{3,2,1,0:T(8,128)} %get-tuple-element.498, f32[8,4,64]{2,1,0:T(4,128)S(1)} %get-tuple-element.499), kind=kOutput, calls=%fused_computation.19.clone.1 | convolution fusion | flops 141560320 | bytes 12853248 | tf_op jit(solution)/shard_map/while/body/eval_jaxpr/ghqk,gqhd->gkhd/dot_general | solution.py:59
  1089.4 7.0 stack.42
  1129.3 10.1 slice.219
  1146.2 8.9 slice_reduce_fusion.2
  1175.3 19.2 %scatter_fusion = bf16[2,16,8,64,256]{4,3,2,1,0:T(8,128)(2,1)} fusion(bf16[2,16,8,64,256]{4,3,2,1,0:T(8,128)(2,1)} %broadcast_in_dim.130, s32[96]{0:T(128)S(1)} %copy-done.8, bf16[96,2,64,256]{3,2,1,0:T(8,128)(2,1)} %bitcast.186), kind=kCustom, calls=%fused_computation.3 | custom fusion | bytes 18875136 | tf_op jit(solution)/shard_map/scatter | solution.py:190
  1194.5 8.3 copy.277
  1207.9 8.6 copy.271
  1220.8 8.3 copy.270
  1240.8 38.7 %collective-permute-done.2 = bf16[2,64,256]{2,1,0:T(8,128)(2,1)S(1)} collective-permute-done((bf16[2,64,256]{2,1,0:T(8,128)(2,1)S(1)}, bf16[2,64,256]{2,1,0:T(8,128)(2,1)S(1)}, u32[]{:S(2)}, u32[]{:S(2)}) %collective-permute-start.2) | collective-permute-done | bytes 65568 | tf_op jit(solution)/shard_map/ppermute | solution.py:33
  1282.7 13.2 all-reduce.6.cloned.1.call-done
  1297.0 140.1 %all-reduce.8.cloned.1.call-done = bf16[256,1024]{1,0:T(8,128)(2,1)} async-done(((bf16[256,1024]{1,0:T(8,128)(2,1)}), bf16[256,1024]{1,0:T(8,128)(2,1)}) %all-reduce.8.cloned.1.call-update) | async-done | bytes 524304 | tf_op jit(solution)/shard_map/psum | solution.py:201
  1439.2 8.3 copy.278
  1447.5 11.3 convert_bitcast_fusion
  1458.8 11.6 copy.279
  1470.4 38.1 %scatter_fusion.1 = f32[2,32,64,256]{3,2,1,0:T(8,128)} fusion(f32[2,32,64,256]{3,2,1,0:T(8,128)} %fusion.55, s32[128]{0:T(128)S(1)} %fusion.66, f32[128,2,64,256]{3,2,1,0:T(8,128)} %copy.279), kind=kCustom, calls=%fused_computation.4 | custom fusion | flops 4194304 | bytes 50332160 | tf_op jit(solution)/shard_map/scatter-add | solution.py:194
  (308 shorter events, 532.1 us)
Async XLA Ops:
  8.0 221.2 %copy-start = (bf16[256,1024]{1,0:T(8,128)(2,1)S(1)}, bf16[256,1024]{1,0:T(8,128)(2,1)}, u32[]{:S(2)}) copy-start(bf16[256,1024]{1,0:T(8,128)(2,1)} %param.18) | copy-start | bytes 1572868
  20.0 0.8 copy-start.10
  20.8 9.1 copy-start.14
  38.2 8.9 copy-start.16
  38.2 196.3 %all-to-all-start = ((bf16[2,16,8,64,256]{4,3,2,0,1:T(8,128)(2,1)}), bf16[2,16,8,64,256]{4,3,2,0,1:T(8,128)(2,1)}, u32[]{:S(2)}, u32[]{:S(2)}) async-start(bf16[2,16,8,64,256]{4,3,2,0,1:T(8,128)(2,1)} %bitcast.183), calls=%async_computation | async-start | bytes 16777216 | tf_op jit(solution)/shard_map/all_to_all | solution.py:122
  46.5 181.6 %all-reduce.4.cloned.1.call-start = ((), (), s32[]{:S(2)}) async-start(), calls=%async_computation.3 | async-start | bytes 262144 | tf_op jit(solution)/shard_map/psum | solution.py:105
  48.4 180.8 %all-gather.2.cloned.1.call-start = ((), (), s32[]{:S(2)}) async-start(), calls=%async_computation.4 | async-start | bytes 5242880 | tf_op jit(solution)/shard_map/all_gather | solution.py:91
  49.0 1246.9 %all-reduce.6.cloned.1.call-start = ((), (), s32[]{:S(2)}) async-start(), calls=%async_computation.6 | async-start | bytes 262144 | tf_op jit(solution)/shard_map/psum | solution.py:200
  49.1 71.2 %collective-permute-start = (bf16[2,64,256]{2,1,0:T(8,128)(2,1)S(1)}, bf16[2,64,256]{2,1,0:T(8,128)(2,1)S(1)}, u32[]{:S(2)}, u32[]{:S(2)}) collective-permute-start(bf16[2,64,256]{2,1,0:T(8,128)(2,1)S(1)} %get-tuple-element.388), channel_id=1, source_target_pairs={{0,4},{4,8},{8,12},{12,16},{16,20},{20,24},{24,28},{28,32},{32,36}... | collective-permute-start | bytes 196616 | tf_op jit(solution)/shard_map/ppermute | solution.py:24
  52.9 70.9 %collective-permute-start.1 = (bf16[2,64,256]{2,1,0:T(8,128)(2,1)S(1)}, bf16[2,64,256]{2,1,0:T(8,128)(2,1)S(1)}, u32[]{:S(2)}, u32[]{:S(2)}) collective-permute-start(bf16[2,64,256]{2,1,0:T(8,128)(2,1)S(1)} %get-tuple-element.389), channel_id=1, source_target_pairs={{4,0},{8,4},{12,8},{16,12},{20,16},{24,20},{28,24},{32,28},{36,32}... | collective-permute-start | bytes 196616 | tf_op jit(solution)/shard_map/ppermute | solution.py:25
  357.8 5.0 copy-start.2
  360.1 2.7 copy-start.3
  360.1 15.4 %copy-start.5 = (bf16[8,64,4,64]{3,2,1,0:T(4,128)(2,1)}, bf16[8,64,4,64]{3,2,1,0:T(4,128)(2,1)S(1)}, u32[]{:S(2)}) copy-start(bf16[8,64,4,64]{3,2,1,0:T(4,128)(2,1)S(1)} %get-tuple-element.495) | copy-start | bytes 786436 | tf_op jit(solution)/shard_map/while
  404.6 7.1 copy-start.4
  445.6 5.7 copy-start.1
  464.2 4.0 copy-start.17
  485.8 10.2 copy-start.6
  577.4 5.0 copy-start.2
  579.7 2.7 copy-start.3
  579.7 15.4 %copy-start.5 = (bf16[8,64,4,64]{3,2,1,0:T(4,128)(2,1)}, bf16[8,64,4,64]{3,2,1,0:T(4,128)(2,1)S(1)}, u32[]{:S(2)}) copy-start(bf16[8,64,4,64]{3,2,1,0:T(4,128)(2,1)S(1)} %get-tuple-element.495) | copy-start | bytes 786436 | tf_op jit(solution)/shard_map/while
  624.2 7.1 copy-start.4
  665.2 5.7 copy-start.1
  683.9 3.9 copy-start.17
  705.4 10.2 copy-start.6
  797.0 5.0 copy-start.2
  799.4 2.7 copy-start.3
  799.4 15.4 %copy-start.5 = (bf16[8,64,4,64]{3,2,1,0:T(4,128)(2,1)}, bf16[8,64,4,64]{3,2,1,0:T(4,128)(2,1)S(1)}, u32[]{:S(2)}) copy-start(bf16[8,64,4,64]{3,2,1,0:T(4,128)(2,1)S(1)} %get-tuple-element.495) | copy-start | bytes 786436 | tf_op jit(solution)/shard_map/while
  843.8 7.1 copy-start.4
  884.9 5.7 copy-start.1
  903.5 3.9 copy-start.17
  925.0 10.2 copy-start.6
  1016.6 5.0 copy-start.2
  1019.0 2.7 copy-start.3
  1019.0 15.4 %copy-start.5 = (bf16[8,64,4,64]{3,2,1,0:T(4,128)(2,1)}, bf16[8,64,4,64]{3,2,1,0:T(4,128)(2,1)S(1)}, u32[]{:S(2)}) copy-start(bf16[8,64,4,64]{3,2,1,0:T(4,128)(2,1)S(1)} %get-tuple-element.495) | copy-start | bytes 786436 | tf_op jit(solution)/shard_map/while
  1063.4 7.1 copy-start.4
  1104.5 5.7 copy-start.1
  1123.2 4.0 copy-start.17
  1144.9 10.2 copy-start.6
  1158.8 278.3 %all-reduce.8.cloned.1.call-start = ((), (), s32[]{:S(2)}) async-start(), calls=%async_computation.7 | async-start | bytes 1048576 | tf_op jit(solution)/shard_map/psum | solution.py:201
  1166.5 348.3 %reduce-scatter.2.cloned.1.call-start = ((), (), s32[]{:S(2)}) async-start(), calls=%async_computation.5 | async-start | bytes 10485760 | tf_op jit(solution)/shard_map/reduce_scatter | solution.py:206
  1171.0 4.3 copy-start.8
  1202.9 4.9 copy-start.11
  1202.9 236.4 %all-to-all-start.1 = ((bf16[2,16,8,64,256]{4,3,2,0,1:T(8,128)(2,1)}), bf16[2,16,8,64,256]{4,3,2,0,1:T(8,128)(2,1)}, u32[]{:S(2)}, u32[]{:S(2)}) async-start(bf16[2,16,8,64,256]{4,3,2,0,1:T(8,128)(2,1)} %copy.277), calls=%async_computation.2 | async-start | bytes 16777216 | tf_op jit(solution)/shard_map/all_to_all | solution.py:193
  1219.5 60.1 %collective-permute-start.2 = (bf16[2,64,256]{2,1,0:T(8,128)(2,1)S(1)}, bf16[2,64,256]{2,1,0:T(8,128)(2,1)S(1)}, u32[]{:S(2)}, u32[]{:S(2)}) collective-permute-start(bf16[2,64,256]{2,1,0:T(8,128)(2,1)S(1)} %get-tuple-element.385), channel_id=1, source_target_pairs={{4,0},{8,4},{12,8},{16,12},{20,16},{24,20},{28,24},{32,28},{36,32}... | collective-permute-start | bytes 196616 | tf_op jit(solution)/shard_map/ppermute | solution.py:33
  1229.0 9.5 copy-start.9
  1229.0 66.9 %copy-start.13 = (pred[2]{0:T(512)(128)(4,1)S(1)}, pred[2]{0:T(512)(128)(4,1)}, u32[]{:S(2)}) copy-start(pred[2]{0:T(512)(128)(4,1)} %copy-done.12) | copy-start | bytes 10
  1233.8 47.3 %collective-permute-start.3 = (bf16[2,64,256]{2,1,0:T(8,128)(2,1)S(1)}, bf16[2,64,256]{2,1,0:T(8,128)(2,1)S(1)}, u32[]{:S(2)}, u32[]{:S(2)}) collective-permute-start(bf16[2,64,256]{2,1,0:T(8,128)(2,1)S(1)} %get-tuple-element.384), channel_id=1, source_target_pairs={{0,4},{4,8},{8,12},{12,16},{16,20},{20,24},{24,28},{28,32},{32,36}... | collective-permute-start | bytes 196616 | tf_op jit(solution)/shard_map/ppermute | solution.py:33
  1470.4 38.1 %copy-start.15 = (s32[2]{0:T(128)S(1)}, s32[2]{0:T(128)}, u32[]{:S(2)}) copy-start(s32[2]{0:T(128)} %copy-done.14) | copy-start | bytes 28
  (5 other events, 3.7 us)
Sparse Core Ops, SparseCore 0:
  51.1 176.9 all-reduce.3
  1158.9 137.0 all-reduce.5
  1299.7 137.3 all-reduce.7
Sparse Core Ops, SparseCore 1:
  50.6 53.0 all-gather.1
  1171.1 79.6 reduce-scatter.1
where the time goes:
time: 1550 us; the launch traced here: 1520 us
  local copies, waits for them, and re-layouts  712 us (46%)
  waiting for transfers between devices  359 us (23%)
  matrix products  209 us (13%)
  other arithmetic  184 us (12%)
  starting transfers between devices  24.8 us (2%)
  loops' own time  20.6 us (1%)
  between operations  15.7 us (1%)
    concatenate x4, local copies, waits for them, and re-layouts, group_step(): entries = jnp.concatenate([window, rand_now, glob_now], axis=2)  156 us
    psum x1, waiting for transfers between devices, per_device(): lax.psum(weight_term.astype(jnp.bfloat16), ('dp', 'ctx'))  140 us
    psum x1, waiting for transfers between devices, per_device(): global_kv = lax.psum(picked.astype(jnp.bfloat16), 'ctx')  103 us
    dot_general x4, matrix products, attend_block(): jnp.einsum('ghqk,gqhd->gkhd', grad_score, query_now, preferred_element_ty...  75.7 us
    dot_general x4, matrix products, attend_block(): jnp.einsum('ghqk,gkhd->gqhd', grad_score, key_set, preferred_element_type...  75.6 us
    another operation x12, local copies, waits for them, and re-layouts, group_step(): jnp.stack([grad_key, grad_value])  72.5 us
    another operation x16, local copies, waits for them, and re-layouts, group_step(): jnp.stack([window_src[:, 0:group_size], window_src[:, 1:group_size + 1],...  64.5 us
    ppermute x1, waiting for transfers between devices, padded_2(): before = lax.ppermute(last, axis, up)  59.7 us
  transfers between devices with their start and end apart: 11, of which 6 were waited for; matrix products, arithmetic and copies ran while one was open for 11% of the time, Pallas kernels for 0%

commit v1 on v0

v1 whole, which is shorter than its diff:
```python
import functools

import jax
import jax.numpy as jnp
from jax import lax
from jax.experimental import pallas as pl
from jax.experimental.pallas import tpu as pltpu
from jax.sharding import PartitionSpec as P

HD = 64
BLK = 64
R = 3
G = 2
LANES = 128
NEG_FILL = -1e30
VMEM_LIMIT = 56 * 1024 * 1024

NT = (((1,), (1,)), ((), ()))
NN = (((1,), (0,)), ((), ()))
TN = (((0,), (0,)), ((), ()))


def dot(a, b, dims):
    return lax.dot_general(a, b, dims, preferred_element_type=jnp.float32)


def smem():
    return pl.BlockSpec(memory_space=pltpu.SMEM)


def whole(shape, column=None):
    if column is None:
        return pl.BlockSpec(shape, lambda i: (0,) * len(shape))
    return pl.BlockSpec(shape, lambda i: (0,) * (len(shape) - 1) + (column,))


def params(**more):
    return pltpu.CompilerParams(vmem_limit_bytes=VMEM_LIMIT, **more)


def pick_kernel(slots, idx_ref, k_ref, v_ref, out_ref):
    def body(s, _):
        src = pl.multiple_of(idx_ref[s] * BLK, BLK)
        dst = pl.multiple_of(s * 2 * BLK, 2 * BLK)
        out_ref[pl.ds(dst, BLK), :] = k_ref[pl.ds(src, BLK), :]
        out_ref[pl.ds(dst + BLK, BLK), :] = v_ref[pl.ds(src, BLK), :]
        return 0

    lax.fori_loop(0, slots, body, 0, unroll=4)


def pick_blocks(idx, keys, values, column, slots):
    rows = keys.shape[0]
    return pl.pallas_call(
        functools.partial(pick_kernel, slots),
        grid=(1,),
        in_specs=[smem(), whole((rows, LANES), column), whole((rows, LANES), column)],
        out_specs=whole((slots * 2 * BLK, LANES)),
        out_shape=jax.ShapeDtypeStruct((slots * 2 * BLK, LANES), jnp.bfloat16),
        compiler_params=params(),
        cost_estimate=pl.CostEstimate(flops=0, bytes_accessed=10 << 20, transcendentals=0),
    )(idx, keys, values)


def grad_context_kernel(g0, g1, g2, g3, w_ref, out_ref):
    width = g0.shape[1]
    total = None
    for i, g in enumerate((g0, g1, g2, g3)):
        term = dot(g[...], w_ref[:, i * width : (i + 1) * width], NT)
        total = term if total is None else total + term
    out_ref[...] = total.astype(jnp.bfloat16)


def grad_context_of(pieces, weight):
    rows, width = pieces[0].shape
    heads = weight.shape[0]
    tile = 512
    return pl.pallas_call(
        grad_context_kernel,
        grid=(rows // tile,),
        in_specs=[pl.BlockSpec((tile, width), lambda i: (i, 0))] * 4
        + [pl.BlockSpec(weight.shape, lambda i: (0, 0))],
        out_specs=pl.BlockSpec((tile, heads), lambda i: (i, 0)),
        out_shape=jax.ShapeDtypeStruct((rows, heads), jnp.bfloat16),
        compiler_params=params(),
        cost_estimate=pl.CostEstimate(flops=2 * rows * 1024 * heads, bytes_accessed=6 << 20, transcendentals=0),
    )(*pieces, weight)


def attend_kernel(
    blocks, slot_ref, bias_ref, q_ref, k_ref, v_ref, g_ref, edge_ref, glob_ref, fetched_ref, dq_in_ref,
    ctx_ref, dq_ref, ret_ref, win_ref, gsum_ref, kpad, vpad,
):
    del dq_in_ref
    rows = blocks * BLK
    kpad[0:BLK, :] = edge_ref[0]
    vpad[0:BLK, :] = edge_ref[1]
    kpad[rows + BLK : rows + 2 * BLK, :] = edge_ref[2]
    vpad[rows + BLK : rows + 2 * BLK, :] = edge_ref[3]
    kpad[BLK : rows + BLK, :] = k_ref[...]
    vpad[BLK : rows + BLK, :] = v_ref[...]
    win_ref[...] = jnp.zeros_like(win_ref)
    gsum_ref[...] = jnp.zeros_like(gsum_ref)
    low = lax.broadcasted_iota(jnp.int32, (BLK, LANES), 1) < HD

    def body(i, _):
        row = pl.multiple_of(i * BLK, BLK)
        q = q_ref[pl.ds(row, BLK), :] * jnp.bfloat16(0.125)
        g = g_ref[pl.ds(row, BLK), :]
        zero = jnp.zeros_like(q)
        qbd = jnp.concatenate([jnp.where(low, q, zero), jnp.where(low, zero, q)], axis=0)
        gbd = jnp.concatenate([jnp.where(low, g, zero), jnp.where(low, zero, g)], axis=0)
        starts = [pl.multiple_of(slot_ref[i * R + r] * 2 * BLK, 2 * BLK) for r in range(R)]
        kcat = jnp.concatenate(
            [kpad[pl.ds(row, 3 * BLK), :]]
            + [fetched_ref[pl.ds(s, BLK), :] for s in starts]
            + [glob_ref[0, 0], glob_ref[1, 0]],
            axis=0,
        )
        vcat = jnp.concatenate(
            [vpad[pl.ds(row, 3 * BLK), :]]
            + [fetched_ref[pl.ds(s + BLK, BLK), :] for s in starts]
            + [glob_ref[0, 1], glob_ref[1, 1]],
            axis=0,
        )
        scores = dot(kcat, qbd, NT)
        scores = jnp.concatenate(
            [
                scores[e * BLK : (e + 1) * BLK] + (bias_ref[i * 8 + e] if e in (0, 2, 3, 4, 5) else 0.0)
                for e in range(8)
            ],
            axis=0,
        )
        peak = jnp.max(scores, axis=0, keepdims=True)
        terms = jnp.exp(scores - peak)
        probs = terms * (1.0 / jnp.sum(terms, axis=0, keepdims=True))
        probs_low = probs.astype(jnp.bfloat16)
        grad_probs = dot(vcat, gbd, NT)
        delta = jnp.sum(probs * grad_probs, axis=0, keepdims=True)
        grad_scores = (probs * (grad_probs - delta)).astype(jnp.bfloat16)
        context = dot(probs_low, vcat, TN)
        grad_q = dot(grad_scores, kcat, TN)
        grad_k = dot(grad_scores, qbd, NN)
        grad_v = dot(probs_low, gbd, NN)
        ctx_ref[pl.ds(row, BLK), :] = jnp.where(low, context[:BLK], context[BLK:]).astype(jnp.bfloat16)
        dq_ref[pl.ds(row, BLK), :] = (
            jnp.where(low, grad_q[:BLK], grad_q[BLK:]) * 0.125
        ).astype(jnp.bfloat16)
        win_ref[0, pl.ds(row, 3 * BLK), :] += grad_k[: 3 * BLK]
        win_ref[1, pl.ds(row, 3 * BLK), :] += grad_v[: 3 * BLK]
        for r, s in enumerate(starts):
            part = slice((3 + r) * BLK, (4 + r) * BLK)
            ret_ref[pl.ds(s, BLK), :] = grad_k[part].astype(jnp.bfloat16)
            ret_ref[pl.ds(s + BLK, BLK), :] = grad_v[part].astype(jnp.bfloat16)
        for e in range(G):
            part = slice((3 + R + e) * BLK, (4 + R + e) * BLK)
            gsum_ref[e, 0] += grad_k[part]
            gsum_ref[e, 1] += grad_v[part]
        return 0

    lax.fori_loop(0, blocks, body, 0, unroll=2)


def attend(slot, bias, q, k, v, g, edges, glob, fetched, dq_in, column):
    rows, width = q.shape
    blocks = rows // BLK
    half = whole((rows, LANES), column)
    out_shape = (
        jax.ShapeDtypeStruct((rows, LANES), jnp.bfloat16),
        jax.ShapeDtypeStruct((rows, width), jnp.bfloat16),
        jax.ShapeDtypeStruct(fetched.shape, jnp.bfloat16),
        jax.ShapeDtypeStruct((2, rows + 2 * BLK, LANES), jnp.float32),
        jax.ShapeDtypeStruct((G, 2, BLK, LANES), jnp.float32),
    )
    first = dq_in is None
    if first:
        dq_in = jnp.zeros((8, 128), jnp.bfloat16)
    return pl.pallas_call(
        functools.partial(attend_kernel, blocks),
        grid=(1,),
        in_specs=[
            smem(), smem(), half, half, half, half,
            whole((4, BLK, LANES), column),
            whole((G, 2, BLK, LANES), column),
            whole(fetched.shape),
            pl.BlockSpec(memory_space=pl.ANY),
        ],
        out_specs=(
            whole((rows, LANES)), half, whole(fetched.shape),
            whole(out_shape[3].shape), whole(out_shape[4].shape),
        ),
        out_shape=out_shape,
        scratch_shapes=[
            pltpu.VMEM((rows + 2 * BLK, LANES), jnp.bfloat16),
            pltpu.VMEM((rows + 2 * BLK, LANES), jnp.bfloat16),
        ],
        input_output_aliases={} if first else {9: 1},
        compiler_params=params(),
        cost_estimate=pl.CostEstimate(
            flops=12 * blocks * 512 * 128 * 128 * 2, bytes_accessed=16 << 20, transcendentals=blocks * 512 * 128
        ),
    )(slot, bias, q, k, v, g, edges, glob, fetched, dq_in)


def collect_kernel(
    requesters, capacity, blocks, idx_ref, used_ref, glob_ref, win_ref, back_ref, edge_ref, gsum_ref,
    dk_in_ref, dv_in_ref, dk_ref, dv_ref, acc,
):
    del dk_in_ref, dv_in_ref
    rows = blocks * BLK
    acc[...] = win_ref[:, BLK : rows + BLK, :]
    acc[:, rows - BLK : rows, :] += edge_ref[0].astype(jnp.float32)
    acc[:, 0:BLK, :] += edge_ref[1].astype(jnp.float32)
    for e in range(G):

        @pl.when(glob_ref[G + e] == 1)
        def _():
            at = pl.multiple_of(glob_ref[e] * BLK, BLK)
            acc[:, pl.ds(at, BLK), :] += gsum_ref[e].astype(jnp.float32)

    def body(a, _):
        @pl.when(used_ref[a] > 0)
        def _():
            for c in range(capacity):
                s = a * capacity + c
                at = pl.multiple_of(idx_ref[s] * BLK, BLK)
                src = pl.multiple_of(s * 2 * BLK, 2 * BLK)
                acc[0, pl.ds(at, BLK), :] += back_ref[pl.ds(src, BLK), :].astype(jnp.float32)
                acc[1, pl.ds(at, BLK), :] += back_ref[pl.ds(src + BLK, BLK), :].astype(jnp.float32)

        return 0

    lax.fori_loop(0, requesters, body, 0)
    dk_ref[...] = acc[0].astype(jnp.bfloat16)
    dv_ref[...] = acc[1].astype(jnp.bfloat16)


def collect(idx, used, glob, win, back, edges, gsum, before, width, column, requesters, capacity):
    rows = win.shape[1] - 2 * BLK
    first = before is None
    if first:
        before = (jnp.zeros((8, 128), jnp.bfloat16),) * 2
    half = whole((rows, LANES), column)
    out = jax.ShapeDtypeStruct((rows, width), jnp.bfloat16)
    return pl.pallas_call(
        functools.partial(collect_kernel, requesters, capacity, rows // BLK),
        grid=(1,),
        in_specs=[
            smem(), smem(), smem(), whole(win.shape), whole(back.shape), whole(edges.shape),
            whole(gsum.shape), pl.BlockSpec(memory_space=pl.ANY), pl.BlockSpec(memory_space=pl.ANY),
        ],
        out_specs=(half, half),
        out_shape=(out, out),
        scratch_shapes=[pltpu.VMEM((2, rows, LANES), jnp.float32)],
        input_output_aliases={} if first else {7: 0, 8: 1},
        compiler_params=params(),
        cost_estimate=pl.CostEstimate(flops=4 << 20, bytes_accessed=8 << 20, transcendentals=0),
    )(idx, used, glob, win, back, edges, gsum, *before)


def weight_kernel(c0, c1, g0, g1, g2, g3, out_ref, acc):
    @pl.when(pl.program_id(0) == 0)
    def _():
        acc[...] = jnp.zeros_like(acc)

    width = g0.shape[1]
    for r, c in enumerate((c0, c1)):
        for i, g in enumerate((g0, g1, g2, g3)):
            acc[r * LANES : (r + 1) * LANES, i * width : (i + 1) * width] += dot(c[...], g[...], TN)

    @pl.when(pl.program_id(0) == pl.num_programs(0) - 1)
    def _():
        out_ref[...] = acc[...].astype(jnp.bfloat16)


def weight_terms(contexts, pieces):
    rows, width = pieces[0].shape
    tile = 512
    shape = (2 * LANES, 4 * width)
    return pl.pallas_call(
        weight_kernel,
        grid=(rows // tile,),
        in_specs=[pl.BlockSpec((tile, LANES), lambda i: (i, 0))] * 2
        + [pl.BlockSpec((tile, width), lambda i: (i, 0))] * 4,
        out_specs=pl.BlockSpec(shape, lambda i: (0, 0)),
        out_shape=jax.ShapeDtypeStruct(shape, jnp.bfloat16),
        scratch_shapes=[pltpu.VMEM(shape, jnp.float32)],
        compiler_params=params(),
        cost_estimate=pl.CostEstimate(flops=2 * rows * 1024 * 256, bytes_accessed=6 << 20, transcendentals=0),
    )(*contexts, *pieces)


def project_kernel(*refs):
    contexts, w_ref, out_ref = refs[:8], refs[8], refs[9]
    total = None
    for i, c in enumerate(contexts):
        term = dot(c[...], w_ref[i * LANES : (i + 1) * LANES, :], NN)
        total = term if total is None else total + term
    out_ref[...] = total.astype(jnp.bfloat16)


def project(contexts, weight):
    rows = contexts[0].shape[0]
    width = weight.shape[1]
    tile = 512
    return pl.pallas_call(
        project_kernel,
        grid=(rows // tile,),
        in_specs=[pl.BlockSpec((tile, LANES), lambda i: (i, 0))] * 8
        + [pl.BlockSpec(weight.shape, lambda i: (0, 0))],
        out_specs=pl.BlockSpec((tile, width), lambda i: (i, 0)),
        out_shape=jax.ShapeDtypeStruct((rows, width), jnp.bfloat16),
        compiler_params=params(),
        cost_estimate=pl.CostEstimate(flops=2 * rows * 1024 * width, bytes_accessed=6 << 20, transcendentals=0),
    )(*contexts, weight)


def from_others(array, axis):
    size = lax.axis_size(axis)
    found = [array]
    for by in range(1, size):
        found.append(lax.ppermute(array, axis, [((i + by) % size, i) for i in range(size)]))
    return found


def passed_along(array, axis, by):
    size = lax.axis_size(axis)
    pairs = [(i, i + by) for i in range(size) if 0 <= i + by < size]
    return lax.ppermute(array, axis, pairs)


def per_device(
    queries, key_vectors, value_vectors, grad_output, out_weight, random_ids, random_valid, global_ids
):
    ctx_count = lax.axis_size("ctx")
    tp_count = lax.axis_size("tp")
    me = lax.axis_index("ctx")
    tp_me = lax.axis_index("tp")
    q, k, v, g_out = queries[0], key_vectors[0], value_vectors[0], grad_output[0]
    rows, width = q.shape
    blocks = rows // BLK
    requests = blocks * R
    capacity = requests // (ctx_count * 3 // 4)
    slots = ctx_count * capacity

    ids = random_ids[0].reshape(ctx_count, requests)
    owner = ids // blocks
    local = ids % blocks
    order = jnp.arange(requests, dtype=jnp.int32)
    earlier = order[None, :] < order[:, None]
    mine = owner == me
    rank = jnp.sum((mine[:, None, :] & earlier[None]).astype(jnp.int32), axis=2)
    hit = mine[:, None, :] & (rank[:, None, :] == jnp.arange(capacity, dtype=jnp.int32)[None, :, None])
    send_idx = jnp.sum(jnp.where(hit, local[:, None, :], 0), axis=2).reshape(slots)
    used = jnp.sum(mine.astype(jnp.int32), axis=1)
    my_owner = lax.dynamic_index_in_dim(owner, me, 0, keepdims=False)
    my_rank = jnp.sum(((my_owner[:, None] == my_owner[None, :]) & earlier).astype(jnp.int32), axis=1)
    my_slot = my_owner * capacity + my_rank

    def exchange(array):
        parts = array.reshape(ctx_count, capacity * 2 * BLK, LANES)
        return lax.all_to_all(parts, "ctx", split_axis=0, concat_axis=0, tiled=True).reshape(array.shape)

    send_a = pick_blocks(send_idx, k, v, 0, slots)
    fetched_a = exchange(send_a)
    send_b = pick_blocks(send_idx, k, v, 1, slots)

    glob_owner = global_ids[0] // blocks
    glob_local = global_ids[0] % blocks
    owned = glob_owner == me
    picked = jnp.stack(
        [
            jnp.stack([lax.dynamic_slice_in_dim(x, glob_local[e] * BLK, BLK, 0) for x in (k, v)])
            * owned[e].astype(jnp.bfloat16)
            for e in range(G)
        ]
    ).reshape(ctx_count, -1, width)
    picked = lax.all_to_all(picked, "ctx", split_axis=0, concat_axis=0, tiled=True)
    picked = jnp.sum(picked.astype(jnp.float32), axis=0).astype(jnp.bfloat16)
    glob = lax.all_gather(picked, "ctx", axis=0, tiled=True).reshape(G, 2, BLK, width)

    last = jnp.stack([k[rows - BLK :], v[rows - BLK :]])
    initial = jnp.stack([k[:BLK], v[:BLK]])
    edges = jnp.concatenate([passed_along(last, "ctx", 1), passed_along(initial, "ctx", -1)])

    pieces = from_others(g_out, "tp")
    turned = jnp.roll(out_weight, -tp_me * width, axis=1)
    grad_context = grad_context_of(pieces, turned)
    wparts = out_weight.reshape(width, tp_count, width).transpose(1, 0, 2)
    wcols = lax.all_to_all(wparts, "tp", split_axis=0, concat_axis=0, tiled=True).reshape(tp_count * width, width)
    wcols = jnp.roll(wcols, -tp_me * width, axis=0)

    block_no = me * blocks + jnp.arange(blocks, dtype=jnp.int32)
    valid = lax.dynamic_slice_in_dim(random_valid[0], me * blocks, blocks, 0)
    present = jnp.concatenate(
        [
            (block_no > 0)[:, None],
            jnp.ones((blocks, 1), bool),
            (block_no < blocks * ctx_count - 1)[:, None],
            valid == 1,
            jnp.ones((blocks, G), bool),
        ],
        axis=1,
    )
    bias = jnp.where(present, 0.0, NEG_FILL).astype(jnp.float32).reshape(-1)

    send_b, fetched_a = lax.optimization_barrier((send_b, fetched_a))
    fetched_b = exchange(send_b)
    ctx_a, dq_a, ret_a, win_a, gsum_a = attend(
        my_slot, bias, q, k, v, grad_context, edges, glob, fetched_a, None, 0
    )
    ret_a, fetched_b = lax.optimization_barrier((ret_a, fetched_b))
    back_a = exchange(ret_a)
    ctx_pieces_a = from_others(ctx_a, "tp")
    ctx_b, grad_q, ret_b, win_b, gsum_b = attend(
        my_slot, bias, q, k, v, grad_context, edges, glob, fetched_b, dq_a, 1
    )
    ret_b, back_a = lax.optimization_barrier((ret_b, back_a))
    back_b = exchange(ret_b)
    ctx_pieces_b = from_others(ctx_b, "tp")

    terms = weight_terms((ctx_a, ctx_b), pieces)
    gsum = jnp.concatenate([gsum_a, gsum_b], axis=-1).astype(jnp.bfloat16)
    share = jnp.concatenate(
        [terms.reshape(ctx_count, -1, 4 * width), gsum.reshape(ctx_count, -1, 4 * width)], axis=1
    )
    share = lax.all_to_all(share, "ctx", split_axis=0, concat_axis=0, tiled=True)
    share = jnp.sum(share.astype(jnp.float32), axis=0)
    wrows = 2 * LANES // ctx_count
    other = lax.ppermute(share[:wrows], "dp", [(0, 1), (1, 0)])
    share = jnp.concatenate([share[:wrows] + other, share[wrows:]]).astype(jnp.bfloat16)
    share = lax.all_gather(share, "ctx", axis=0)
    grad_weight = share[:, :wrows].reshape(2 * LANES, 4 * width).astype(jnp.float32)
    grad_weight = jnp.roll(grad_weight, tp_me * width, axis=1)
    gsum = share[:, wrows:].reshape(G, 2, BLK, width)

    def outer(win):
        first = passed_along(win[:, :BLK].astype(jnp.bfloat16), "ctx", -1)
        final = passed_along(win[:, rows + BLK :].astype(jnp.bfloat16), "ctx", 1)
        return jnp.stack([first, final])

    glob_at = jnp.concatenate([glob_local, owned.astype(jnp.int32)])
    half = functools.partial(collect, send_idx, used, glob_at)
    grads = half(win_a, back_a, outer(win_a), gsum[..., :LANES], None, width, 0, ctx_count, capacity)
    grads = half(win_b, back_b, outer(win_b), gsum[..., LANES:], grads, width, 1, ctx_count, capacity)
    ordered = [c for pair in zip(ctx_pieces_a, ctx_pieces_b) for c in pair]
    projected = project(ordered, wcols)
    return projected[None], grad_q[None], grads[0][None], grads[1][None], grad_weight


def solution(mesh):
    tokens = P("dp", "ctx", "tp")
    in_specs = (
        tokens, tokens, tokens, tokens, P("tp", None), P("dp", None, None), P("dp", None, None), P("dp", None),
    )
    out_specs = (tokens, tokens, tokens, tokens, P("tp", None))
    return jax.shard_map(per_device, mesh=mesh, in_specs=in_specs, out_specs=out_specs, check_vma=False)
```

time: 1550 us -> 426 us (0.27); the launches traced: 1520 us -> 424 us
  local copies, waits for them, and re-layouts: 712 us -> 11.3 us
  matrix products: 209 us -> 0 us
  waiting for transfers between devices: 359 us -> 151 us
  other arithmetic: 184 us -> 15.3 us
  Pallas kernels: 0 us -> 87.2 us
  blocking collectives: 0 us -> 73.8 us
  starting transfers between devices: 24.8 us -> 81.4 us
  loops' own time: 20.6 us -> 0 us
    psum x3 -> x0, waiting for transfers between devices: 256 us -> none  [the longest x1 140 us: per_device(): lax.psum(weight_term.astype(jnp.bfloat16), ('dp', 'ctx'))]
    dot_general x27 -> x0, matrix products: 209 us -> none  [the longest x4 75.7 us: attend_block(): jnp.einsum('ghqk,gqhd->gkhd', grad_score, query_now, preferred_element_ty...]
    concatenate x5 -> x3, local copies, waits for them, and re-layouts: 156 us -> 1.5 us  [the longest x1 1.46 us: per_device(): jnp.concatenate([passed_along(last, 'ctx', 1), passed_along(initial, 'ctx...]
    another operation x34 -> x3, local copies, waits for them, and re-layouts: 143 us -> 1.61 us  [the longest x1 0.9 us: per_device(): jnp.stack([lax.dynamic_slice_in_dim(x, glob_local[e] * BLK, BLK, 0) for x...]
    slice x15 -> x8, local copies, waits for them, and re-layouts: 93.2 us -> 1.94 us  [the longest x1 0.68 us: per_device(): gsum[..., :LANES]]
    pallas_call x0 -> x9, Pallas kernels: none -> 87.2 us  [the longest x2 53.4 us: attend(): pl.pallas_call(functools.partial(attend_kernel, blocks), grid=(1,), in_sp...]
    all_to_all x2 -> x7, waiting for transfers between devices: 0.01 us -> 87.1 us  [the longest x4 70.5 us: exchange(): lax.all_to_all(parts, 'ctx', split_axis=0, concat_axis=0, tiled=True)]
    all_gather x0 -> x2, blocking collectives: none -> 73.8 us  [the longest x1 42.9 us: per_device(): share = lax.all_gather(share, 'ctx', axis=0)]
  transfers between devices with their start and end apart: 11 -> 23, of which waited for: 6 -> 12; matrix products, arithmetic and copies ran while one was open for 11% -> 5% of each run, Pallas kernels for 0% -> 18%
where the time goes in v1:
time: 426 us; the launch traced here: 424 us
  waiting for transfers between devices  151 us (35%)
  Pallas kernels  87.2 us (20%)
  starting transfers between devices  81.4 us (19%)
  blocking collectives  73.8 us (17%)
  other arithmetic  15.3 us (4%)
  local copies, waits for them, and re-layouts  11.3 us (3%)
    all_to_all x4, waiting for transfers between devices, exchange(): lax.all_to_all(parts, 'ctx', split_axis=0, concat_axis=0, tiled=True)  70.5 us
    pallas_call x2, Pallas kernels, attend(): pl.pallas_call(functools.partial(attend_kernel, blocks), grid=(1,), in_sp...  53.4 us
    ppermute x6, waiting for transfers between devices, passed_along(): return lax.ppermute(array, axis, pairs)  49.7 us
    all_gather x1, blocking collectives, per_device(): share = lax.all_gather(share, 'ctx', axis=0)  42.9 us
    all_gather x1, blocking collectives, per_device(): lax.all_gather(picked, 'ctx', axis=0, tiled=True).reshape(G, 2, BLK, width)  31 us
    all_to_all x4, starting transfers between devices, exchange(): lax.all_to_all(parts, 'ctx', split_axis=0, concat_axis=0, tiled=True)  26.5 us
    ppermute x6, starting transfers between devices, passed_along(): return lax.ppermute(array, axis, pairs)  16 us
    ppermute x9, starting transfers between devices, from_others(): lax.ppermute(array, axis, [((i + by) % size, i) for i in range(size)])  15.6 us
  transfers between devices with their start and end apart: 23, of which 12 were waited for; matrix products, arithmetic and copies ran while one was open for 5% of the time, Pallas kernels for 18%

profile of v1, /device:TPU:0, one launch (start us, length us, event | category | flops | bytes accessed | tf_op | source)
XLA Modules:
  0.0 424.1 jit_solution(12528333885449499088)
XLA Ops:
  3.0 3.9 shard_map.121
  7.0 8.3 %all-to-all-start.1 = ((bf16[16,1024,128]{2,1,0:T(8,128)(2,1)}), bf16[16,1024,128]{2,1,0:T(8,128)(2,1)}, u32[]{:S(2)}, u32[]{:S(2)}) async-start(bf16[16,1024,128]{2,1,0:T(8,128)(2,1)} %bitcast.76), calls=%async_computation.1 | async-start | bytes 8388608 | tf_op jit(solution)/shard_map/all_to_all | solution.py:362
  20.7 57.5 %all-to-all-done.1 = bf16[16,1024,128]{2,1,0:T(8,128)(2,1)} async-done(((bf16[16,1024,128]{2,1,0:T(8,128)(2,1)}), bf16[16,1024,128]{2,1,0:T(8,128)(2,1)}, u32[]{:S(2)}, u32[]{:S(2)}) %all-to-all-start.1) | async-done | bytes 4194336 | tf_op jit(solution)/shard_map/all_to_all | solution.py:362
  78.2 10.2 %all-to-all-start = ((bf16[16,16,256]{2,1,0:T(8,128)(2,1)}), bf16[16,16,256]{2,1,0:T(8,128)(2,1)S(1)}, u32[]{:S(2)}, u32[]{:S(2)}) async-start(bf16[16,16,256]{2,1,0:T(8,128)(2,1)} %bitcast.14), calls=%async_computation | async-start | bytes 262144 | tf_op jit(solution)/shard_map/all_to_all | solution.py:378
  88.4 3.9 shard_map.120
  92.3 3.9 all-to-all-done
  96.2 4.7 %all-to-all-start.2 = ((bf16[16,1024,128]{2,1,0:T(8,128)(2,1)}), bf16[16,1024,128]{2,1,0:T(8,128)(2,1)}, u32[]{:S(2)}, u32[]{:S(2)}) async-start(bf16[16,1024,128]{2,1,0:T(8,128)(2,1)} %bitcast.75), calls=%async_computation.2 | async-start | bytes 8388608 | tf_op jit(solution)/shard_map/all_to_all | solution.py:362
  100.9 2.8 collective-permute-start
  105.5 3.6 collective-permute-start.3
  109.1 1.3 collective-permute-start.4
  112.0 1.9 copy.30
  114.7 2.0 fusion.3.w_ref
  116.7 29.1 %collective-permute-done.3 = bf16[2,64,256]{2,1,0:T(8,128)(2,1)S(1)} collective-permute-done((bf16[2,64,256]{2,1,0:T(8,128)(2,1)S(1)}, bf16[2,64,256]{2,1,0:T(8,128)(2,1)S(1)}, u32[]{:S(2)}, u32[]{:S(2)}) %collective-permute-start.3) | collective-permute-done | bytes 65568 | tf_op jit(solution)/shard_map/ppermute | solution.py:329
  146.4 1.4 collective-permute-done.4
  147.8 1.5 constant_dynamic-update-slice_fusion.edge_ref
  149.3 31.0 %all_gather.7 = bf16[256,256]{1,0:T(8,128)(2,1)} all-gather(bf16[16,256]{1,0:T(8,128)(2,1)S(1)} %reduce_sum.65), channel_id=1, replica_groups=mesh['dp'=2,'ctx'=16,'tp'=4] {'ctx'}, dimensions={0}, use_global_device_ids=true | all-gather | bytes 139264 | tf_op jit(solution)/shard_map/all_gather | solution.py:380
  180.3 0.9 copy-done.3
  181.6 5.1 %shard_map.119.g_ref = bf16[2048,256]{1,0:T(8,128)(2,1)} custom-call(bf16[2048,256]{1,0:T(8,128)(2,1)} %bitcast.87, bf16[2048,256]{1,0:T(8,128)(2,1)} %copy-done.3, bf16[2048,256]{1,0:T(8,128)(2,1)} %copy-done.4, bf16[2048,256]{1,0:T(8,128)(2,1)} %collective-permute-done.2.g3, bf16[256,1024]{1,0:T(8,128)(2,1)} %fusion.3.w_ref), custom_call_target="tpu_custom_call" | custom-call | flops 1073741824 | bytes 6291456 | tf_op jit(solution)/shard_map/pallas_call | solution.py:78
  186.7 4.3 %all-to-all-start.3 = ((bf16[4,256,256]{2,1,0:T(8,128)(2,1)}), bf16[4,256,256]{2,1,0:T(8,128)(2,1)S(1)}, u32[]{:S(2)}, u32[]{:S(2)}) async-start(bf16[4,256,256]{2,1,0:T(8,128)(2,1)} %bitcast.94), calls=%async_computation.3 | async-start | bytes 1048576 | tf_op jit(solution)/shard_map/all_to_all | solution.py:390
  191.6 26.7 %shard_map.122 = (bf16[2048,128]{1,0:T(8,128)(2,1)}, bf16[2048,256]{1,0:T(8,128)(2,1)}, bf16[16384,128]{1,0:T(8,128)(2,1)}, f32[2,2176,128]{2,1,0:T(8,128)}, f32[2,2,64,128]{3,2,1,0:T(8,128)}) custom-call(s32[96]{0:T(128)} %multiply_add_fusion.slot_ref, f32[256]{0:T(256)} %select_n.93.bias_ref, bf16[2048,256]{1,0:T(8,128)(2,1)} %bitcast.106, ...), custom_call_target="tpu_custom_call" | custom-call | flops 6442450944 | bytes 16777216 | tf_op jit(solution)/shard_map/pallas_call | solution.py:178
  218.3 4.7 %all-to-all-start.4 = ((bf16[16,1024,128]{2,1,0:T(8,128)(2,1)}), bf16[16,1024,128]{2,1,0:T(8,128)(2,1)}, u32[]{:S(2)}, u32[]{:S(2)}) async-start(bf16[16,1024,128]{2,1,0:T(8,128)(2,1)} %bitcast.86), calls=%async_computation.4 | async-start | bytes 8388608 | tf_op jit(solution)/shard_map/all_to_all | solution.py:362
  223.0 26.7 %shard_map.123 = (bf16[2048,128]{1,0:T(8,128)(2,1)}, bf16[2048,256]{1,0:T(8,128)(2,1)}, bf16[16384,128]{1,0:T(8,128)(2,1)}, f32[2,2176,128]{2,1,0:T(8,128)}, f32[2,2,64,128]{3,2,1,0:T(8,128)}) custom-call(s32[96]{0:T(128)} %multiply_add_fusion.slot_ref, f32[256]{0:T(256)} %select_n.93.bias_ref, ...), custom_call_target="tpu_custom_call", output_to_operand_aliasing={{1}: (9, {})} | custom-call | flops 6442450944 | bytes 16777216 | tf_op jit(solution)/shard_map/pallas_call | solution.py:178
  250.8 5.1 %shard_map.125 = bf16[256,1024]{1,0:T(8,128)(2,1)} custom-call(bf16[2048,128]{1,0:T(8,128)(2,1)} %get-tuple-element.26.refs_0_.c0, bf16[2048,128]{1,0:T(8,128)(2,1)} %get-tuple-element.31.refs_1_.c1, bf16[2048,256]{1,0:T(8,128)(2,1)} %bitcast.88, bf16[2048,256]{1,0:T(8,128)(2,1)} %copy-done.3, bf16[2048,256]{1,0:T(8,128)(2,1)} %copy-done.4, ...), custom_call_target="tpu_custom_call" | custom-call | flops 1073741824 | bytes 6291456 | tf_op jit(solution)/shard_map/pallas_call | solution.py:280
  255.9 2.0 pad_maximum_fusion
  257.9 13.0 %all-to-all-done.4 = bf16[16,1024,128]{2,1,0:T(8,128)(2,1)} async-done(((bf16[16,1024,128]{2,1,0:T(8,128)(2,1)}), bf16[16,1024,128]{2,1,0:T(8,128)(2,1)}, u32[]{:S(2)}, u32[]{:S(2)}) %all-to-all-start.4) | async-done | bytes 4194336 | tf_op jit(solution)/shard_map/all_to_all | solution.py:362
  270.9 8.8 %all-to-all-start.6 = ((bf16[16,20,1024]{2,1,0:T(8,128)(2,1)}), bf16[16,20,1024]{2,1,0:T(8,128)(2,1)S(1)}, u32[]{:S(2)}, u32[]{:S(2)}) async-start(bf16[16,20,1024]{2,1,0:T(8,128)(2,1)} %pad_maximum_fusion), calls=%async_computation.6 | async-start | bytes 1572864 | tf_op jit(solution)/shard_map/all_to_all | solution.py:427
  279.7 12.7 %all-to-all-done.6 = bf16[16,20,1024]{2,1,0:T(8,128)(2,1)S(1)} async-done(((bf16[16,20,1024]{2,1,0:T(8,128)(2,1)}), bf16[16,20,1024]{2,1,0:T(8,128)(2,1)S(1)}, u32[]{:S(2)}, u32[]{:S(2)}) %all-to-all-start.6) | async-done | bytes 655392 | tf_op jit(solution)/shard_map/all_to_all | solution.py:427
  292.4 8.8 %all-to-all-start.5 = ((bf16[16,1024,128]{2,1,0:T(8,128)(2,1)}), bf16[16,1024,128]{2,1,0:T(8,128)(2,1)}, u32[]{:S(2)}, u32[]{:S(2)}) async-start(bf16[16,1024,128]{2,1,0:T(8,128)(2,1)} %bitcast.85), calls=%async_computation.5 | async-start | bytes 8388608 | tf_op jit(solution)/shard_map/all_to_all | solution.py:362
  301.5 3.9 collective-permute-start.15
  305.4 1.3 collective-permute-start.14
  306.9 4.5 %collective-permute-start.12 = (bf16[2,64,128]{2,1,0:T(8,128)(2,1)S(1)}, bf16[2,64,128]{2,1,0:T(8,128)(2,1)S(1)}, u32[]{:S(2)}, u32[]{:S(2)}) collective-permute-start(bf16[2,64,128]{2,1,0:T(8,128)(2,1)S(1)} %get-tuple-element.52), channel_id=1, source_target_pairs={{0,4},{4,8},{8,12},{12,16},{16,20},{20,24},{24,28},{28,32},{32,36}... | collective-permute-start | bytes 98312 | tf_op jit(solution)/shard_map/ppermute | solution.py:329
  311.5 1.3 collective-permute-start.11
  312.8 19.2 %collective-permute-done.15 = bf16[2,64,128]{2,1,0:T(8,128)(2,1)S(1)} collective-permute-done((bf16[2,64,128]{2,1,0:T(8,128)(2,1)S(1)}, bf16[2,64,128]{2,1,0:T(8,128)(2,1)S(1)}, u32[]{:S(2)}, u32[]{:S(2)}) %collective-permute-start.15) | collective-permute-done | bytes 32800 | tf_op jit(solution)/shard_map/ppermute | solution.py:329
  332.0 5.8 %collective-permute-start.7 = (bf16[2048,128]{1,0:T(8,128)(2,1)S(1)}, bf16[2048,128]{1,0:T(8,128)(2,1)S(1)}, u32[]{:S(2)}, u32[]{:S(2)}) collective-permute-start(bf16[2048,128]{1,0:T(8,128)(2,1)S(1)} %copy-done.5), channel_id=1, source_target_pairs={{2,0},{3,1},{0,2},{1,3},{6,4},{7,5},{4,6},{5,7},{10,8},{11,9},{8,1... | collective-permute-start | bytes 1572872 | tf_op jit(solution)/shard_map/ppermute | solution.py:322
  337.8 1.1 collective-permute-start.9
  338.8 2.2 collective-permute-start.6
  341.1 1.4 collective-permute-start.8
  344.5 2.1 fusion.2.refs_8_
  347.3 1.4 pad_maximum_fusion.5.edge_ref
  348.6 1.9 collective-permute-done.9.refs_6_
  351.3 5.2 %collective-permute-done.8.refs_5_ = bf16[2048,128]{1,0:T(8,128)(2,1)} collective-permute-done((bf16[2048,128]{1,0:T(8,128)(2,1)S(1)}, bf16[2048,128]{1,0:T(8,128)(2,1)}, u32[]{:S(2)}, u32[]{:S(2)}) %collective-permute-start.8) | collective-permute-done | bytes 524320 | tf_op jit(solution)/shard_map/ppermute | solution.py:322
  356.4 5.5 %collective-permute-done.10.refs_7_ = bf16[2048,128]{1,0:T(8,128)(2,1)} collective-permute-done((bf16[2048,128]{1,0:T(8,128)(2,1)S(1)}, bf16[2048,128]{1,0:T(8,128)(2,1)}, u32[]{:S(2)}, u32[]{:S(2)}) %collective-permute-start.10) | collective-permute-done | bytes 524320 | tf_op jit(solution)/shard_map/ppermute | solution.py:322
  361.9 5.8 %shard_map.124 = bf16[2048,256]{1,0:T(8,128)(2,1)} custom-call(bf16[2048,128]{1,0:T(8,128)(2,1)} %get-tuple-element.26.refs_0_.c0, bf16[2048,128]{1,0:T(8,128)(2,1)} %get-tuple-element.31.refs_1_.c1, bf16[2048,128]{1,0:T(8,128)(2,1)} %copy-done.7, bf16[2048,128]{1,0:T(8,128)(2,1)} %collective-permute-done.6.refs_3_, bf16[2048,128]{1,0:T(8,128)(2,1)} %copy-done.8, ...), custom_call_target="tpu_custom_call" | custom-call | flops 1073741824 | bytes 6291456 | tf_op jit(solution)/shard_map/pallas_call | solution.py:306
  368.0 1.2 collective-permute-done.13
  369.3 42.9 %all_gather.8 = bf16[16,20,1024]{2,1,0:T(8,128)(2,1)S(1)} all-gather(bf16[1,20,1024]{2,1,0:T(8,128)(2,1)S(1)} %pad_maximum_fusion.7), channel_id=1, replica_groups=mesh['dp'=2,'ctx'=16,'tp'=4] {'ctx'}, dimensions={0}, use_global_device_ids=true | all-gather | bytes 696320 | tf_op jit(solution)/shard_map/all_gather | solution.py:432
  412.3 1.3 fusion.1
  414.3 4.9 %shard_map.126 = (bf16[2048,256]{1,0:T(8,128)(2,1)}, bf16[2048,256]{1,0:T(8,128)(2,1)}) custom-call(s32[128]{0:T(128)} %reshape.264.idx_ref, s32[16]{0:T(128)} %reduce_sum.70.used_ref, s32[4]{0:T(128)} %pad_add_fusion.glob_ref, f32[2,2176,128]{2,1,0:T(8,128)} %get-tuple-element.39.win_ref, bf16[16384,128]{1,0:T(8,128)(2,1)} %bitcast.25.back_ref, ...), custom_call_target="tpu_custom_call" | custom-call | flops 4194304 | bytes 8388608 | tf_op jit(solution)/shard_map/pallas_call | solution.py:245
  419.2 4.9 %shard_map.127 = (bf16[2048,256]{1,0:T(8,128)(2,1)}, bf16[2048,256]{1,0:T(8,128)(2,1)}) custom-call(s32[128]{0:T(128)} %reshape.264.idx_ref, s32[16]{0:T(128)} %reduce_sum.70.used_ref, s32[4]{0:T(128)} %pad_add_fusion.glob_ref, f32[2,2176,128]{2,1,0:T(8,128)} %get-tuple-element.33.win_ref, ...), custom_call_target="tpu_custom_call", output_to_operand_aliasing={{0}: (7, {}), {1}: (8, {})} | custom-call | flops 4194304 | bytes 8388608 | tf_op jit(solution)/shard_map/pallas_call | solution.py:245
  (97 shorter events, 16.6 us)
Async XLA Ops:
  7.0 8.3 %copy-start.12 = (s32[1,2]{1,0:T(1,128)S(1)}, s32[1,2]{1,0:T(1,128)}, u32[]{:S(2)}) copy-start(s32[1,2]{1,0:T(1,128)} %param.15) | copy-start | bytes 28
  7.0 71.3 %all-to-all-start.1 = ((bf16[16,1024,128]{2,1,0:T(8,128)(2,1)}), bf16[16,1024,128]{2,1,0:T(8,128)(2,1)}, u32[]{:S(2)}, u32[]{:S(2)}) async-start(bf16[16,1024,128]{2,1,0:T(8,128)(2,1)} %bitcast.76), calls=%async_computation.1 | async-start | bytes 8388608 | tf_op jit(solution)/shard_map/all_to_all | solution.py:362
  78.2 18.0 %all-to-all-start = ((bf16[16,16,256]{2,1,0:T(8,128)(2,1)}), bf16[16,16,256]{2,1,0:T(8,128)(2,1)S(1)}, u32[]{:S(2)}, u32[]{:S(2)}) async-start(bf16[16,16,256]{2,1,0:T(8,128)(2,1)} %bitcast.14), calls=%async_computation | async-start | bytes 262144 | tf_op jit(solution)/shard_map/all_to_all | solution.py:378
  96.2 4.7 %copy-start.2 = (bf16[1,2048,256]{2,1,0:T(8,128)(2,1)S(1)}, bf16[1,2048,256]{2,1,0:T(8,128)(2,1)}, u32[]{:S(2)}) copy-start(bf16[1,2048,256]{2,1,0:T(8,128)(2,1)} %param.11) | copy-start | bytes 3145732
  96.2 90.5 %all-to-all-start.2 = ((bf16[16,1024,128]{2,1,0:T(8,128)(2,1)}), bf16[16,1024,128]{2,1,0:T(8,128)(2,1)}, u32[]{:S(2)}, u32[]{:S(2)}) async-start(bf16[16,1024,128]{2,1,0:T(8,128)(2,1)} %bitcast.75), calls=%async_computation.2 | async-start | bytes 8388608 | tf_op jit(solution)/shard_map/all_to_all | solution.py:362
  100.9 79.3 %collective-permute-start = (bf16[2048,256]{1,0:T(8,128)(2,1)S(1)}, bf16[2048,256]{1,0:T(8,128)(2,1)S(1)}, u32[]{:S(2)}, u32[]{:S(2)}) collective-permute-start(bf16[2048,256]{1,0:T(8,128)(2,1)S(1)} %bitcast.89), channel_id=1, source_target_pairs={{1,0},{2,1},{3,2},{0,3},{5,4},{6,5},{7,6},{4,7},{9,8},{10,9},{11,1... | collective-permute-start | bytes 3145736 | tf_op jit(solution)/shard_map/ppermute | solution.py:322
  103.8 76.5 %collective-permute-start.1 = (bf16[2048,256]{1,0:T(8,128)(2,1)S(1)}, bf16[2048,256]{1,0:T(8,128)(2,1)S(1)}, u32[]{:S(2)}, u32[]{:S(2)}) collective-permute-start(bf16[2048,256]{1,0:T(8,128)(2,1)S(1)} %bitcast.90), channel_id=1, source_target_pairs={{2,0},{3,1},{0,2},{1,3},{6,4},{7,5},{4,6},{5,7},{10,8},{11,9},{8,1... | collective-permute-start | bytes 3145736 | tf_op jit(solution)/shard_map/ppermute | solution.py:322
  104.6 75.7 %collective-permute-start.2 = (bf16[2048,256]{1,0:T(8,128)(2,1)S(1)}, bf16[2048,256]{1,0:T(8,128)(2,1)}, u32[]{:S(2)}, u32[]{:S(2)}) collective-permute-start(bf16[2048,256]{1,0:T(8,128)(2,1)S(1)} %bitcast.91), channel_id=1, source_target_pairs={{3,0},{0,1},{1,2},{2,3},{7,4},{4,5},{5,6},{6,7},{11,8},{8,9},{9,10... | collective-permute-start | bytes 3145736 | tf_op jit(solution)/shard_map/ppermute | solution.py:322
  105.5 40.3 %collective-permute-start.3 = (bf16[2,64,256]{2,1,0:T(8,128)(2,1)S(1)}, bf16[2,64,256]{2,1,0:T(8,128)(2,1)S(1)}, u32[]{:S(2)}, u32[]{:S(2)}) collective-permute-start(bf16[2,64,256]{2,1,0:T(8,128)(2,1)S(1)} %pad_maximum_fusion.3), channel_id=1, source_target_pairs={{0,4},{4,8},{8,12},{12,16},{16,20},{20,24},{24,28},{28,32},{32,36}... | collective-permute-start | bytes 196616 | tf_op jit(solution)/shard_map/ppermute | solution.py:329
  109.1 38.7 %collective-permute-start.4 = (bf16[2,64,256]{2,1,0:T(8,128)(2,1)S(1)}, bf16[2,64,256]{2,1,0:T(8,128)(2,1)}, u32[]{:S(2)}, u32[]{:S(2)}) collective-permute-start(bf16[2,64,256]{2,1,0:T(8,128)(2,1)S(1)} %pad_maximum_fusion.4), channel_id=1, source_target_pairs={{4,0},{8,4},{12,8},{16,12},{20,16},{24,20},{28,24},{32,28},{36,32}... | collective-permute-start | bytes 196616 | tf_op jit(solution)/shard_map/ppermute | solution.py:329
  180.3 1.0 copy-start.3
  180.3 1.3 copy-start.4
  186.7 31.6 %all-to-all-start.3 = ((bf16[4,256,256]{2,1,0:T(8,128)(2,1)}), bf16[4,256,256]{2,1,0:T(8,128)(2,1)S(1)}, u32[]{:S(2)}, u32[]{:S(2)}) async-start(bf16[4,256,256]{2,1,0:T(8,128)(2,1)} %bitcast.94), calls=%async_computation.3 | async-start | bytes 1048576 | tf_op jit(solution)/shard_map/all_to_all | solution.py:390
  218.3 4.7 %copy-start.10 = (f32[2,2,64,128]{3,2,1,0:T(8,128)S(1)}, f32[2,2,64,128]{3,2,1,0:T(8,128)}, u32[]{:S(2)}) copy-start(f32[2,2,64,128]{3,2,1,0:T(8,128)} %get-tuple-element.37) | copy-start | bytes 393220
  218.3 52.6 %all-to-all-start.4 = ((bf16[16,1024,128]{2,1,0:T(8,128)(2,1)}), bf16[16,1024,128]{2,1,0:T(8,128)(2,1)}, u32[]{:S(2)}, u32[]{:S(2)}) async-start(bf16[16,1024,128]{2,1,0:T(8,128)(2,1)} %bitcast.86), calls=%async_computation.4 | async-start | bytes 8388608 | tf_op jit(solution)/shard_map/all_to_all | solution.py:362
  270.9 21.5 %all-to-all-start.6 = ((bf16[16,20,1024]{2,1,0:T(8,128)(2,1)}), bf16[16,20,1024]{2,1,0:T(8,128)(2,1)S(1)}, u32[]{:S(2)}, u32[]{:S(2)}) async-start(bf16[16,20,1024]{2,1,0:T(8,128)(2,1)} %pad_maximum_fusion), calls=%async_computation.6 | async-start | bytes 1572864 | tf_op jit(solution)/shard_map/all_to_all | solution.py:427
  292.4 8.9 %copy-start = (f32[2,2176,128]{2,1,0:T(8,128)S(1)}, f32[2,2176,128]{2,1,0:T(8,128)}, u32[]{:S(2)}) copy-start(f32[2,2176,128]{2,1,0:T(8,128)} %get-tuple-element.39.win_ref) | copy-start | bytes 6684676
  292.4 126.7 %all-to-all-start.5 = ((bf16[16,1024,128]{2,1,0:T(8,128)(2,1)}), bf16[16,1024,128]{2,1,0:T(8,128)(2,1)}, u32[]{:S(2)}, u32[]{:S(2)}) async-start(bf16[16,1024,128]{2,1,0:T(8,128)(2,1)} %bitcast.85), calls=%async_computation.5 | async-start | bytes 8388608 | tf_op jit(solution)/shard_map/all_to_all | solution.py:362
  301.2 5.5 %copy-start.1 = (f32[2,2176,128]{2,1,0:T(8,128)S(1)}, f32[2,2176,128]{2,1,0:T(8,128)}, u32[]{:S(2)}) copy-start(f32[2,2176,128]{2,1,0:T(8,128)} %get-tuple-element.33.win_ref) | copy-start | bytes 6684676
  301.2 37.6 %collective-permute-start.5 = (bf16[2048,128]{1,0:T(8,128)(2,1)}, bf16[2048,128]{1,0:T(8,128)(2,1)S(1)}, u32[]{:S(2)}, u32[]{:S(2)}) collective-permute-start(bf16[2048,128]{1,0:T(8,128)(2,1)} %get-tuple-element.26.refs_0_.c0), channel_id=1, source_target_pairs={{1,0},{2,1},{3,2},{0,3},{5,4},{6,5},{7,6},{4,7},{9,8},{10,9},{11,1... | collective-permute-start | bytes 1572872 | tf_op jit(solution)/shard_map/ppermute | solution.py:322
  301.5 30.5 %copy-start.5 = (bf16[2048,128]{1,0:T(8,128)(2,1)S(1)}, bf16[2048,128]{1,0:T(8,128)(2,1)}, u32[]{:S(2)}) copy-start(bf16[2048,128]{1,0:T(8,128)(2,1)} %get-tuple-element.26.refs_0_.c0) | copy-start | bytes 1572868
  301.5 37.4 %copy-start.6 = (bf16[2048,128]{1,0:T(8,128)(2,1)S(1)}, bf16[2048,128]{1,0:T(8,128)(2,1)}, u32[]{:S(2)}) copy-start(bf16[2048,128]{1,0:T(8,128)(2,1)} %get-tuple-element.31.refs_1_.c1) | copy-start | bytes 1572868
  301.5 41.5 %copy-start.11 = (s32[1,512,3]{1,0,2:T(1,128)S(1)}, s32[1,512,3]{1,0,2:T(1,128)}, u32[]{:S(2)}) copy-start(s32[1,512,3]{1,0,2:T(1,128)} %param.13) | copy-start | bytes 18436
  301.5 30.5 %collective-permute-start.15 = (bf16[2,64,128]{2,1,0:T(8,128)(2,1)S(1)}, bf16[2,64,128]{2,1,0:T(8,128)(2,1)S(1)}, u32[]{:S(2)}, u32[]{:S(2)}) collective-permute-start(bf16[2,64,128]{2,1,0:T(8,128)(2,1)S(1)} %get-tuple-element.50), channel_id=1, source_target_pairs={{0,4},{4,8},{8,12},{12,16},{16,20},{20,24},{24,28},{28,32},{32,36}... | collective-permute-start | bytes 98312 | tf_op jit(solution)/shard_map/ppermute | solution.py:329
  305.4 32.4 %collective-permute-start.14 = (bf16[2,64,128]{2,1,0:T(8,128)(2,1)S(1)}, bf16[2,64,128]{2,1,0:T(8,128)(2,1)S(1)}, u32[]{:S(2)}, u32[]{:S(2)}) collective-permute-start(bf16[2,64,128]{2,1,0:T(8,128)(2,1)S(1)} %get-tuple-element.49), channel_id=1, source_target_pairs={{4,0},{8,4},{12,8},{16,12},{20,16},{24,20},{28,24},{32,28},{36,32}... | collective-permute-start | bytes 98312 | tf_op jit(solution)/shard_map/ppermute | solution.py:329
  306.9 34.2 %collective-permute-start.12 = (bf16[2,64,128]{2,1,0:T(8,128)(2,1)S(1)}, bf16[2,64,128]{2,1,0:T(8,128)(2,1)S(1)}, u32[]{:S(2)}, u32[]{:S(2)}) collective-permute-start(bf16[2,64,128]{2,1,0:T(8,128)(2,1)S(1)} %get-tuple-element.52), channel_id=1, source_target_pairs={{0,4},{4,8},{8,12},{12,16},{16,20},{20,24},{24,28},{28,32},{32,36}... | collective-permute-start | bytes 98312 | tf_op jit(solution)/shard_map/ppermute | solution.py:329
  311.5 31.0 %collective-permute-start.11 = (bf16[2,64,128]{2,1,0:T(8,128)(2,1)S(1)}, bf16[2,64,128]{2,1,0:T(8,128)(2,1)}, u32[]{:S(2)}, u32[]{:S(2)}) collective-permute-start(bf16[2,64,128]{2,1,0:T(8,128)(2,1)S(1)} %get-tuple-element.51), channel_id=1, source_target_pairs={{4,0},{8,4},{12,8},{16,12},{20,16},{24,20},{28,24},{32,28},{36,32}... | collective-permute-start | bytes 98312 | tf_op jit(solution)/shard_map/ppermute | solution.py:329
  332.0 16.6 %collective-permute-start.7 = (bf16[2048,128]{1,0:T(8,128)(2,1)S(1)}, bf16[2048,128]{1,0:T(8,128)(2,1)S(1)}, u32[]{:S(2)}, u32[]{:S(2)}) collective-permute-start(bf16[2048,128]{1,0:T(8,128)(2,1)S(1)} %copy-done.5), channel_id=1, source_target_pairs={{2,0},{3,1},{0,2},{1,3},{6,4},{7,5},{4,6},{5,7},{10,8},{11,9},{8,1... | collective-permute-start | bytes 1572872 | tf_op jit(solution)/shard_map/ppermute | solution.py:322
  337.8 12.8 %collective-permute-start.9 = (bf16[2048,128]{1,0:T(8,128)(2,1)S(1)}, bf16[2048,128]{1,0:T(8,128)(2,1)S(1)}, u32[]{:S(2)}, u32[]{:S(2)}) collective-permute-start(bf16[2048,128]{1,0:T(8,128)(2,1)S(1)} %copy-done.5), channel_id=1, source_target_pairs={{3,0},{0,1},{1,2},{2,3},{7,4},{4,5},{5,6},{6,7},{11,8},{8,9},{9,10... | collective-permute-start | bytes 1572872 | tf_op jit(solution)/shard_map/ppermute | solution.py:322
  338.8 4.2 copy-start.7
  338.8 12.4 %collective-permute-start.6 = (bf16[2048,128]{1,0:T(8,128)(2,1)S(1)}, bf16[2048,128]{1,0:T(8,128)(2,1)}, u32[]{:S(2)}, u32[]{:S(2)}) collective-permute-start(bf16[2048,128]{1,0:T(8,128)(2,1)S(1)} %copy-done.6), channel_id=1, source_target_pairs={{1,0},{2,1},{3,2},{0,3},{5,4},{6,5},{7,6},{4,7},{9,8},{10,9},{11,1... | collective-permute-start | bytes 1572872 | tf_op jit(solution)/shard_map/ppermute | solution.py:322
  341.1 15.3 %collective-permute-start.8 = (bf16[2048,128]{1,0:T(8,128)(2,1)S(1)}, bf16[2048,128]{1,0:T(8,128)(2,1)}, u32[]{:S(2)}, u32[]{:S(2)}) collective-permute-start(bf16[2048,128]{1,0:T(8,128)(2,1)S(1)} %copy-done.6), channel_id=1, source_target_pairs={{2,0},{3,1},{0,2},{1,3},{6,4},{7,5},{4,6},{5,7},{10,8},{11,9},{8,1... | collective-permute-start | bytes 1572872 | tf_op jit(solution)/shard_map/ppermute | solution.py:322
  342.5 19.4 %collective-permute-start.10 = (bf16[2048,128]{1,0:T(8,128)(2,1)S(1)}, bf16[2048,128]{1,0:T(8,128)(2,1)}, u32[]{:S(2)}, u32[]{:S(2)}) collective-permute-start(bf16[2048,128]{1,0:T(8,128)(2,1)S(1)} %copy-done.6), channel_id=1, source_target_pairs={{3,0},{0,1},{1,2},{2,3},{7,4},{4,5},{5,6},{6,7},{11,8},{8,9},{9,10... | collective-permute-start | bytes 1572872 | tf_op jit(solution)/shard_map/ppermute | solution.py:322
  348.6 13.3 %copy-start.8 = (bf16[2048,128]{1,0:T(8,128)(2,1)}, bf16[2048,128]{1,0:T(8,128)(2,1)S(1)}, u32[]{:S(2)}) copy-start(bf16[2048,128]{1,0:T(8,128)(2,1)S(1)} %collective-permute-done.7.refs_4_) | copy-start | bytes 1572868
  350.6 11.3 %copy-start.9 = (bf16[2048,128]{1,0:T(8,128)(2,1)}, bf16[2048,128]{1,0:T(8,128)(2,1)S(1)}, u32[]{:S(2)}) copy-start(bf16[2048,128]{1,0:T(8,128)(2,1)S(1)} %collective-permute-done.9.refs_6_) | copy-start | bytes 1572868
  367.9 1.3 collective-permute-start.13

commit v2 on v1

v2 whole, which is shorter than its diff:
```python
import functools

import jax
import jax.numpy as jnp
from jax import lax
from jax.experimental import pallas as pl
from jax.experimental.pallas import tpu as pltpu
from jax.sharding import PartitionSpec as P

HD = 64
BLK = 64
R = 3
G = 2
LANES = 128
NEG_FILL = -1e30
VMEM_LIMIT = 56 * 1024 * 1024

NT = (((1,), (1,)), ((), ()))
NN = (((1,), (0,)), ((), ()))
TN = (((0,), (0,)), ((), ()))


def dot(a, b, dims):
    return lax.dot_general(a, b, dims, preferred_element_type=jnp.float32)


def smem():
    return pl.BlockSpec(memory_space=pltpu.SMEM)


def whole(shape, column=None):
    if column is None:
        return pl.BlockSpec(shape, lambda i: (0,) * len(shape))
    return pl.BlockSpec(shape, lambda i: (0,) * (len(shape) - 1) + (column,))


def params(**more):
    return pltpu.CompilerParams(vmem_limit_bytes=VMEM_LIMIT, **more)


def pick_kernel(slots, idx_ref, k_ref, v_ref, out_ref):
    def body(s, _):
        src = pl.multiple_of(idx_ref[s] * BLK, BLK)
        dst = pl.multiple_of(s * 2 * BLK, 2 * BLK)
        out_ref[pl.ds(dst, BLK), :] = k_ref[pl.ds(src, BLK), :]
        out_ref[pl.ds(dst + BLK, BLK), :] = v_ref[pl.ds(src, BLK), :]
        return 0

    lax.fori_loop(0, slots, body, 0, unroll=4)


def pick_blocks(idx, keys, values, column, slots):
    rows = keys.shape[0]
    return pl.pallas_call(
        functools.partial(pick_kernel, slots),
        grid=(1,),
        in_specs=[smem(), whole((rows, LANES), column), whole((rows, LANES), column)],
        out_specs=whole((slots * 2 * BLK, LANES)),
        out_shape=jax.ShapeDtypeStruct((slots * 2 * BLK, LANES), jnp.bfloat16),
        compiler_params=params(),
        cost_estimate=pl.CostEstimate(flops=0, bytes_accessed=10 << 20, transcendentals=0),
    )(idx, keys, values)


def grad_context_kernel(at_ref, *refs):
    del at_ref
    total = None
    for g, w in zip(refs[:4], refs[4:8]):
        term = dot(g[...], w[...], NT)
        total = term if total is None else total + term
    refs[8][...] = total.astype(jnp.bfloat16)


def grad_context_of(at, pieces, weight):
    rows, width = pieces[0].shape
    heads = weight.shape[0]
    tile = 512
    turned = [
        pl.BlockSpec((heads, width), functools.partial(lambda j, i, at: (0, (at[0] + j) % 4), j))
        for j in range(4)
    ]
    return pl.pallas_call(
        grad_context_kernel,
        grid_spec=pltpu.PrefetchScalarGridSpec(
            num_scalar_prefetch=1,
            grid=(rows // tile,),
            in_specs=[pl.BlockSpec((tile, width), lambda i, at: (i, 0))] * 4 + turned,
            out_specs=pl.BlockSpec((tile, heads), lambda i, at: (i, 0)),
        ),
        out_shape=jax.ShapeDtypeStruct((rows, heads), jnp.bfloat16),
        compiler_params=params(),
        cost_estimate=pl.CostEstimate(flops=2 * rows * 1024 * heads, bytes_accessed=6 << 20, transcendentals=0),
    )(at, *pieces, weight, weight, weight, weight)


def attend_kernel(
    blocks, last_block, me_ref, slot_ref, valid_ref, q_ref, k_ref, v_ref, g_ref, before_ref, after_ref, glob_ref,
    fetched_ref, dq_in_ref, ctx_ref, dq_ref, ret_ref, win_out_ref, outer_ref, gsum_out_ref,
    kpad, vpad, win_ref, gsum_ref,
):
    del dq_in_ref
    rows = blocks * BLK
    kpad[0:BLK, :] = before_ref[0]
    vpad[0:BLK, :] = before_ref[1]
    kpad[rows + BLK : rows + 2 * BLK, :] = after_ref[0]
    vpad[rows + BLK : rows + 2 * BLK, :] = after_ref[1]
    kpad[BLK : rows + BLK, :] = k_ref[...]
    vpad[BLK : rows + BLK, :] = v_ref[...]
    win_ref[...] = jnp.zeros_like(win_ref)
    gsum_ref[...] = jnp.zeros_like(gsum_ref)
    low = lax.broadcasted_iota(jnp.int32, (BLK, LANES), 1) < HD

    def body(i, _):
        row = pl.multiple_of(i * BLK, BLK)
        q = q_ref[pl.ds(row, BLK), :] * jnp.bfloat16(0.125)
        g = g_ref[pl.ds(row, BLK), :]
        zero = jnp.zeros_like(q)
        qbd = jnp.concatenate([jnp.where(low, q, zero), jnp.where(low, zero, q)], axis=0)
        gbd = jnp.concatenate([jnp.where(low, g, zero), jnp.where(low, zero, g)], axis=0)
        starts = [pl.multiple_of(slot_ref[i * R + r] * 2 * BLK, 2 * BLK) for r in range(R)]
        kcat = jnp.concatenate(
            [kpad[pl.ds(row, 3 * BLK), :]]
            + [fetched_ref[pl.ds(s, BLK), :] for s in starts]
            + [glob_ref[0, 0], glob_ref[1, 0]],
            axis=0,
        )
        vcat = jnp.concatenate(
            [vpad[pl.ds(row, 3 * BLK), :]]
            + [fetched_ref[pl.ds(s + BLK, BLK), :] for s in starts]
            + [glob_ref[0, 1], glob_ref[1, 1]],
            axis=0,
        )
        scores = dot(kcat, qbd, NT)
        block = me_ref[0] * blocks + i
        present = [block > 0, None, block < last_block]
        present += [valid_ref[i * R + r] == 1 for r in range(R)] + [None] * G
        parts = []
        for e, there in enumerate(present):
            part = scores[e * BLK : (e + 1) * BLK]
            parts.append(part if there is None else part + jnp.where(there, 0.0, NEG_FILL))
        scores = jnp.concatenate(parts, axis=0)
        peak = jnp.max(scores, axis=0, keepdims=True)
        terms = jnp.exp(scores - peak)
        probs = terms * (1.0 / jnp.sum(terms, axis=0, keepdims=True))
        probs_low = probs.astype(jnp.bfloat16)
        grad_probs = dot(vcat, gbd, NT)
        delta = jnp.sum(probs * grad_probs, axis=0, keepdims=True)
        grad_scores = (probs * (grad_probs - delta)).astype(jnp.bfloat16)
        context = dot(probs_low, vcat, TN)
        grad_q = dot(grad_scores, kcat, TN)
        grad_k = dot(grad_scores, qbd, NN)
        grad_v = dot(probs_low, gbd, NN)
        ctx_ref[pl.ds(row, BLK), :] = jnp.where(low, context[:BLK], context[BLK:]).astype(jnp.bfloat16)
        dq_ref[pl.ds(row, BLK), :] = (
            jnp.where(low, grad_q[:BLK], grad_q[BLK:]) * 0.125
        ).astype(jnp.bfloat16)
        win_ref[0, pl.ds(row, 3 * BLK), :] += grad_k[: 3 * BLK]
        win_ref[1, pl.ds(row, 3 * BLK), :] += grad_v[: 3 * BLK]
        for r, s in enumerate(starts):
            part = slice((3 + r) * BLK, (4 + r) * BLK)
            ret_ref[pl.ds(s, BLK), :] = grad_k[part].astype(jnp.bfloat16)
            ret_ref[pl.ds(s + BLK, BLK), :] = grad_v[part].astype(jnp.bfloat16)
        for e in range(G):
            part = slice((3 + R + e) * BLK, (4 + R + e) * BLK)
            gsum_ref[e, 0] += grad_k[part]
            gsum_ref[e, 1] += grad_v[part]
        return 0

    lax.fori_loop(0, blocks, body, 0, unroll=2)
    win_out_ref[...] = win_ref[:, BLK : rows + BLK, :]
    outer_ref[0] = win_ref[:, 0:BLK, :].astype(jnp.bfloat16)
    outer_ref[1] = win_ref[:, rows + BLK : rows + 2 * BLK, :].astype(jnp.bfloat16)
    gsum_out_ref[...] = gsum_ref[...].reshape(G * 2 * BLK, LANES).astype(jnp.bfloat16)


def attend(last_block, me, slot, valid, q, k, v, g, before, after, glob, fetched, dq_in, column):
    rows, width = q.shape
    blocks = rows // BLK
    half = whole((rows, LANES), column)
    out_shape = (
        jax.ShapeDtypeStruct((rows, LANES), jnp.bfloat16),
        jax.ShapeDtypeStruct((rows, width), jnp.bfloat16),
        jax.ShapeDtypeStruct(fetched.shape, jnp.bfloat16),
        jax.ShapeDtypeStruct((2, rows, LANES), jnp.float32),
        jax.ShapeDtypeStruct((2, 2, BLK, LANES), jnp.bfloat16),
        jax.ShapeDtypeStruct((G * 2 * BLK, LANES), jnp.bfloat16),
    )
    first = dq_in is None
    if first:
        dq_in = jnp.zeros((8, 128), jnp.bfloat16)
    return pl.pallas_call(
        functools.partial(attend_kernel, blocks, last_block),
        grid=(1,),
        in_specs=[
            smem(), smem(), smem(), half, half, half, half,
            whole((2, BLK, LANES), column),
            whole((2, BLK, LANES), column),
            whole((G, 2, BLK, LANES), column),
            whole(fetched.shape),
            pl.BlockSpec(memory_space=pl.ANY),
        ],
        out_specs=(
            whole((rows, LANES)), half, whole(fetched.shape),
            whole(out_shape[3].shape), whole(out_shape[4].shape), whole(out_shape[5].shape),
        ),
        out_shape=out_shape,
        scratch_shapes=[
            pltpu.VMEM((rows + 2 * BLK, LANES), jnp.bfloat16),
            pltpu.VMEM((rows + 2 * BLK, LANES), jnp.bfloat16),
            pltpu.VMEM((2, rows + 2 * BLK, LANES), jnp.float32),
            pltpu.VMEM((G, 2, BLK, LANES), jnp.float32),
        ],
        input_output_aliases={} if first else {11: 1},
        compiler_params=params(),
        cost_estimate=pl.CostEstimate(
            flops=12 * blocks * 512 * 128 * 128 * 2, bytes_accessed=16 << 20, transcendentals=blocks * 512 * 128
        ),
    )(me, slot, valid, q, k, v, g, before, after, glob, fetched, dq_in)


def land(requesters, capacity, idx_ref, used_ref, win_ref, back_ref, up_ref, down_ref, acc):
    rows = acc.shape[1]
    acc[...] = win_ref[...]
    acc[:, rows - BLK : rows, :] += up_ref[...].astype(jnp.float32)
    acc[:, 0:BLK, :] += down_ref[...].astype(jnp.float32)

    def body(a, _):
        @pl.when(used_ref[a] > 0)
        def _():
            for c in range(capacity):
                s = a * capacity + c
                at = pl.multiple_of(idx_ref[s] * BLK, BLK)
                src = pl.multiple_of(s * 2 * BLK, 2 * BLK)
                acc[0, pl.ds(at, BLK), :] += back_ref[pl.ds(src, BLK), :].astype(jnp.float32)
                acc[1, pl.ds(at, BLK), :] += back_ref[pl.ds(src + BLK, BLK), :].astype(jnp.float32)

        return 0

    lax.fori_loop(0, requesters, body, 0)


def first_kernel(
    requesters, capacity, idx_ref, used_ref, glob_ref, win_ref, back_ref, up_ref, down_ref,
    dk_ref, dv_ref, kept_ref, acc,
):
    land(requesters, capacity, idx_ref, used_ref, win_ref, back_ref, up_ref, down_ref, acc)
    dk_ref[...] = acc[0].astype(jnp.bfloat16)
    dv_ref[...] = acc[1].astype(jnp.bfloat16)
    for e in range(G):
        at = pl.multiple_of(glob_ref[e] * BLK, BLK)
        kept_ref[e] = acc[:, pl.ds(at, BLK), :]


def second_kernel(
    requesters, capacity, idx_ref, used_ref, glob_ref, win_ref, back_ref, up_ref, down_ref, gsum_a_ref, gsum_b_ref,
    kept_ref, dk_in_ref, dv_in_ref, dk_ref, dv_ref, acc,
):
    land(requesters, capacity, idx_ref, used_ref, win_ref, back_ref, up_ref, down_ref, acc)
    for e in range(G):

        @pl.when(glob_ref[G + e] == 1)
        def _():
            at = pl.multiple_of(glob_ref[e] * BLK, BLK)
            acc[:, pl.ds(at, BLK), :] += gsum_b_ref[e].astype(jnp.float32)

    dk_ref[:, LANES:] = acc[0].astype(jnp.bfloat16)
    dv_ref[:, LANES:] = acc[1].astype(jnp.bfloat16)
    dk_ref[:, :LANES] = dk_in_ref[...]
    dv_ref[:, :LANES] = dv_in_ref[...]
    for e in range(G):

        @pl.when(glob_ref[G + e] == 1)
        def _():
            at = pl.multiple_of(glob_ref[e] * BLK, BLK)
            total = (kept_ref[e] + gsum_a_ref[e].astype(jnp.float32)).astype(jnp.bfloat16)
            dk_ref[pl.ds(at, BLK), :LANES] = total[0]
            dv_ref[pl.ds(at, BLK), :LANES] = total[1]


def collect_first(idx, used, glob, win, back, up, down, requesters, capacity):
    rows = win.shape[1]
    out = jax.ShapeDtypeStruct((rows, LANES), jnp.bfloat16)
    kept = jax.ShapeDtypeStruct((G, 2, BLK, LANES), jnp.float32)
    return pl.pallas_call(
        functools.partial(first_kernel, requesters, capacity),
        grid=(1,),
        in_specs=[smem()] * 3 + [whole(x.shape) for x in (win, back, up, down)],
        out_specs=(whole(out.shape), whole(out.shape), whole(kept.shape)),
        out_shape=(out, out, kept),
        scratch_shapes=[pltpu.VMEM((2, rows, LANES), jnp.float32)],
        compiler_params=params(),
        cost_estimate=pl.CostEstimate(flops=4 << 20, bytes_accessed=8 << 20, transcendentals=0),
    )(idx, used, glob, win, back, up, down)


def collect_second(idx, used, glob, win, back, up, down, gsum_a, gsum_b, before, requesters, capacity):
    rows = win.shape[1]
    out = jax.ShapeDtypeStruct((rows, 2 * LANES), jnp.bfloat16)
    dk, dv, kept = before
    arrays = (win, back, up, down, gsum_a, gsum_b, kept, dk, dv)
    return pl.pallas_call(
        functools.partial(second_kernel, requesters, capacity),
        grid=(1,),
        in_specs=[smem()] * 3 + [whole(x.shape) for x in arrays],
        out_specs=(whole(out.shape), whole(out.shape)),
        out_shape=(out, out),
        scratch_shapes=[pltpu.VMEM((2, rows, LANES), jnp.float32)],
        compiler_params=params(),
        cost_estimate=pl.CostEstimate(flops=4 << 20, bytes_accessed=8 << 20, transcendentals=0),
    )(idx, used, glob, *arrays)


def share_kernel(at_ref, c0, c1, g0, g1, g2, g3, s0, s1, out_ref, acc):
    @pl.when(pl.program_id(0) == 0)
    def _():
        acc[...] = jnp.zeros_like(acc)

    width = g0.shape[1]
    for r, c in enumerate((c0, c1)):
        for i, g in enumerate((g0, g1, g2, g3)):
            acc[r * LANES : (r + 1) * LANES, i * width : (i + 1) * width] += dot(c[...], g[...], TN)

    @pl.when(pl.program_id(0) == pl.num_programs(0) - 1)
    def _():
        for i in range(4):
            to = pl.multiple_of(((at_ref[0] + i) % 4) * width, width)
            out_ref[:, pl.ds(to, width)] = acc[:, i * width : (i + 1) * width].astype(jnp.bfloat16)
        out_ref[:, 4 * width : 4 * width + LANES] = s0[...]
        out_ref[:, 4 * width + LANES :] = s1[...]


def share_terms(at, contexts, pieces, sums):
    rows, width = pieces[0].shape
    tile = 512
    shape = (2 * LANES, 4 * width + 2 * LANES)
    return pl.pallas_call(
        share_kernel,
        grid=(rows // tile,),
        in_specs=[smem()]
        + [pl.BlockSpec((tile, LANES), lambda i: (i, 0))] * 2
        + [pl.BlockSpec((tile, width), lambda i: (i, 0))] * 4
        + [whole(x.shape) for x in sums],
        out_specs=pl.BlockSpec(shape, lambda i: (0, 0)),
        out_shape=jax.ShapeDtypeStruct(shape, jnp.bfloat16),
        scratch_shapes=[pltpu.VMEM((2 * LANES, 4 * width), jnp.float32)],
        compiler_params=params(),
        cost_estimate=pl.CostEstimate(flops=2 * rows * 1024 * 256, bytes_accessed=6 << 20, transcendentals=0),
    )(at, *contexts, *pieces, *sums)


def project_kernel(*refs):
    contexts, weights, out_ref = refs[:8], refs[8:12], refs[12]
    total = None
    for i, c in enumerate(contexts):
        w = weights[i // 2]
        term = dot(c[...], w[(i % 2) * LANES : (i % 2 + 1) * LANES, :], NN)
        total = term if total is None else total + term
    out_ref[...] = total.astype(jnp.bfloat16)


def project(contexts, weights):
    rows = contexts[0].shape[0]
    width = weights[0].shape[1]
    tile = 512
    return pl.pallas_call(
        project_kernel,
        grid=(rows // tile,),
        in_specs=[pl.BlockSpec((tile, LANES), lambda i: (i, 0))] * 8
        + [pl.BlockSpec(w.shape, lambda i: (0, 0)) for w in weights],
        out_specs=pl.BlockSpec((tile, width), lambda i: (i, 0)),
        out_shape=jax.ShapeDtypeStruct((rows, width), jnp.bfloat16),
        compiler_params=params(),
        cost_estimate=pl.CostEstimate(flops=2 * rows * 1024 * width, bytes_accessed=6 << 20, transcendentals=0),
    )(*contexts, *weights)


def from_others(array, axis):
    size = lax.axis_size(axis)
    found = [array]
    for by in range(1, size):
        found.append(lax.ppermute(array, axis, [((i + by) % size, i) for i in range(size)]))
    return found


def passed_along(array, axis, by):
    size = lax.axis_size(axis)
    pairs = [(i, i + by) for i in range(size) if 0 <= i + by < size]
    return lax.ppermute(array, axis, pairs)


def one_of_four(array, stride):
    span = 4 * stride
    total = array
    for by in (1, 3, 2):
        pairs = [(i, i // span * span + (i + by * stride) % span) for i in range(16)]
        total = total + lax.ppermute(array, "ctx", pairs)
    return total


def per_device(
    queries, key_vectors, value_vectors, grad_output, out_weight, random_ids, random_valid, global_ids
):
    ctx_count = lax.axis_size("ctx")
    tp_count = lax.axis_size("tp")
    me = lax.axis_index("ctx")
    tp_me = lax.axis_index("tp")
    q, k, v, g_out = queries[0], key_vectors[0], value_vectors[0], grad_output[0]
    rows, width = q.shape
    blocks = rows // BLK
    requests = blocks * R
    capacity = requests // (ctx_count * 3 // 4)
    slots = ctx_count * capacity
    barrier = lax.optimization_barrier

    pieces = from_others(g_out, "tp")

    glob_owner = global_ids[0] // blocks
    glob_local = global_ids[0] % blocks
    owned = glob_owner == me
    picked = jnp.concatenate(
        [
            lax.dynamic_slice_in_dim(x, glob_local[e] * BLK, BLK, 0) * owned[e].astype(jnp.bfloat16)
            for e in range(G)
            for x in (k, v)
        ]
    )
    glob = one_of_four(picked, 1)
    before = passed_along(jnp.stack([k[rows - BLK :], v[rows - BLK :]]), "ctx", 1)
    after = passed_along(jnp.stack([k[:BLK], v[:BLK]]), "ctx", -1)

    ids = random_ids[0].reshape(ctx_count, requests)
    owner = ids // blocks
    local = ids % blocks
    order = jnp.arange(requests, dtype=jnp.int32)
    earlier = order[None, :] < order[:, None]
    mine = owner == me
    rank = jnp.sum((mine[:, None, :] & earlier[None]).astype(jnp.int32), axis=2)
    hit = mine[:, None, :] & (rank[:, None, :] == jnp.arange(capacity, dtype=jnp.int32)[None, :, None])
    send_idx = jnp.sum(jnp.where(hit, local[:, None, :], 0), axis=2).reshape(slots)
    send_a = pick_blocks(send_idx, k, v, 0, slots)

    def exchange(array):
        parts = array.reshape(ctx_count, -1, array.shape[-1])
        return lax.all_to_all(parts, "ctx", split_axis=0, concat_axis=0, tiled=True).reshape(array.shape)

    send_a, glob, before, after = barrier((send_a, glob, before, after))
    fetched_a = exchange(send_a)
    glob = one_of_four(glob, 4).reshape(G, 2, BLK, width)
    send_b = pick_blocks(send_idx, k, v, 1, slots)
    used = jnp.sum(mine.astype(jnp.int32), axis=1)
    my_owner = lax.dynamic_index_in_dim(owner, me, 0, keepdims=False)
    my_rank = jnp.sum(((my_owner[:, None] == my_owner[None, :]) & earlier).astype(jnp.int32), axis=1)
    my_slot = my_owner * capacity + my_rank
    valid = lax.dynamic_slice_in_dim(random_valid[0], me * blocks, blocks, 0).reshape(-1)
    tp_at = tp_me.reshape(1)
    wcols = [None] * tp_count
    for by in range(tp_count):
        part = lax.dynamic_slice_in_dim(out_weight, (tp_me + by) % tp_count * width, width, 1)
        if by:
            part = lax.ppermute(part, "tp", [(i, (i + by) % tp_count) for i in range(tp_count)])
        wcols[-by % tp_count] = part
    grad_context = grad_context_of(tp_at, pieces, out_weight)

    ready = barrier((send_b, fetched_a, grad_context, glob, used, my_slot, valid, *wcols))
    send_b, fetched_a, grad_context, glob, used, my_slot, valid, *wcols = ready
    fetched_b = exchange(send_b)
    half = functools.partial(
        attend, blocks * ctx_count - 1, me.reshape(1), my_slot, valid, q, k, v, grad_context, before, after, glob
    )
    ctx_a, dq_a, ret_a, win_a, outer_a, gsum_a = half(fetched_a, None, 0)
    ret_a, fetched_b = barrier((ret_a, fetched_b))
    back_a = exchange(ret_a)
    up_a, down_a = passed_along(outer_a[0], "ctx", -1), passed_along(outer_a[1], "ctx", 1)
    ctx_pieces_a = from_others(ctx_a, "tp")
    ctx_b, grad_q, ret_b, win_b, outer_b, gsum_b = half(fetched_b, dq_a, 1)
    ctx_pieces_b = from_others(ctx_b, "tp")
    up_b, down_b = passed_along(outer_b[0], "ctx", -1), passed_along(outer_b[1], "ctx", 1)

    share = share_terms(tp_at, (ctx_a, ctx_b), pieces, (gsum_a, gsum_b))
    share, back_a = barrier((share, back_a))
    share = exchange(share)
    glob_at = jnp.concatenate([glob_local, owned.astype(jnp.int32)])
    first = collect_first(send_idx, used, glob_at, win_a, back_a, up_a, down_a, ctx_count, capacity)
    ordered = [c for pair in zip(ctx_pieces_a, ctx_pieces_b) for c in pair]
    projected = project(ordered, wcols)
    ready = barrier((ret_b, share, projected, up_b, down_b, *first))
    ret_b, share, projected, up_b, down_b, *first = ready
    back_b = exchange(ret_b)
    share = jnp.sum(share.reshape(ctx_count, -1, share.shape[-1]).astype(jnp.float32), axis=0)
    other = lax.ppermute(share[:, : 4 * width], "dp", [(0, 1), (1, 0)])
    share = jnp.concatenate([share[:, : 4 * width] + other, share[:, 4 * width :]], axis=1).astype(jnp.bfloat16)
    share = lax.all_gather(share, "ctx", axis=0, tiled=True)
    grad_weight = share[:, : 4 * width].astype(jnp.float32)
    gsums = [
        share[:, 4 * width + c * LANES : 4 * width + (c + 1) * LANES].reshape(G, 2, BLK, LANES) for c in range(2)
    ]
    grads = collect_second(
        send_idx, used, glob_at, win_b, back_b, up_b, down_b, *gsums, first, ctx_count, capacity
    )
    return projected[None], grad_q[None], grads[0][None], grads[1][None], grad_weight


def solution(mesh):
    tokens = P("dp", "ctx", "tp")
    in_specs = (
        tokens, tokens, tokens, tokens, P("tp", None), P("dp", None, None), P("dp", None, None), P("dp", None),
    )
    out_specs = (tokens, tokens, tokens, tokens, P("tp", None))
    return jax.shard_map(per_device, mesh=mesh, in_specs=in_specs, out_specs=out_specs, check_vma=False)
```

time: 426 us -> 340 us (0.80)
  waiting for transfers between devices: 151 us -> 75.6 us
  blocking collectives: 73.8 us -> 64.3 us
  other arithmetic: 15.3 us -> 6.92 us
  starting transfers between devices: 81.4 us -> 88.3 us
    ppermute x6, waiting for transfers between devices: 49.7 us -> 0.02 us  [passed_along(): return lax.ppermute(array, axis, pairs)]
    ppermute x1 -> x10, waiting for transfers between devices: 1.23 us -> 45.1 us  [the longest x6 43.4 us: one_of_four(): total = total + lax.ppermute(array, 'ctx', pairs)]
    all_to_all x4 -> x5, waiting for transfers between devices: 70.5 us -> 30.5 us  [exchange(): lax.all_to_all(parts, 'ctx', split_axis=0, concat_axis=0, tiled=True)]
    all_to_all x3 -> x0, starting transfers between devices: 23.2 us -> none  [the longest x1 10.2 us: per_device(): lax.all_to_all(picked, 'ctx', split_axis=0, concat_axis=0, tiled=True)]
    all_to_all x4 -> x5, starting transfers between devices: 26.5 us -> 44.8 us  [exchange(): lax.all_to_all(parts, 'ctx', split_axis=0, concat_axis=0, tiled=True)]
    all_to_all x3 -> x0, waiting for transfers between devices: 16.6 us -> none  [the longest x1 12.7 us: per_device(): lax.all_to_all(share, 'ctx', split_axis=0, concat_axis=0, tiled=True)]
    ppermute x1 -> x10, starting transfers between devices: 0.09 us -> 16.6 us  [the longest x6 12.1 us: one_of_four(): total = total + lax.ppermute(array, 'ctx', pairs)]
    ppermute x9, waiting for transfers between devices: 13.3 us -> 0.02 us  [from_others(): lax.ppermute(array, axis, [((i + by) % size, i) for i in range(size)])]
  transfers between devices with their start and end apart: 23 -> 30, of which waited for: 12 -> 5; matrix products, arithmetic and copies ran while one was open for 5% -> 3% of each run, Pallas kernels for 18% -> 25%
where the time goes in v2:
time: 340 us; the launch traced here: 337 us
  Pallas kernels  89.2 us (26%)
  starting transfers between devices  88.3 us (26%)
  waiting for transfers between devices  75.6 us (22%)
  blocking collectives  64.3 us (19%)
  local copies, waits for them, and re-layouts  8.92 us (3%)
  other arithmetic  6.92 us (2%)
  between operations  3.82 us (1%)
    all_gather x1, blocking collectives, per_device(): share = lax.all_gather(share, 'ctx', axis=0, tiled=True)  64.3 us
    pallas_call x2, Pallas kernels, attend(): pl.pallas_call(functools.partial(attend_kernel, blocks, last_block), grid...  53.9 us
    all_to_all x5, starting transfers between devices, exchange(): lax.all_to_all(parts, 'ctx', split_axis=0, concat_axis=0, tiled=True)  44.8 us
    ppermute x6, waiting for transfers between devices, one_of_four(): total = total + lax.ppermute(array, 'ctx', pairs)  43.4 us
    all_to_all x5, waiting for transfers between devices, exchange(): lax.all_to_all(parts, 'ctx', split_axis=0, concat_axis=0, tiled=True)  30.5 us
    ppermute x6, starting transfers between devices, passed_along(): return lax.ppermute(array, axis, pairs)  15.9 us
    ppermute x6, starting transfers between devices, one_of_four(): total = total + lax.ppermute(array, 'ctx', pairs)  12.1 us
    ppermute x9, starting transfers between devices, from_others(): lax.ppermute(array, axis, [((i + by) % size, i) for i in range(size)])  11 us
  transfers between devices with their start and end apart: 30, of which 5 were waited for; matrix products, arithmetic and copies ran while one was open for 3% of the time, Pallas kernels for 25%

profile of v2, /device:TPU:0, one launch (start us, length us, event | category | flops | bytes accessed | tf_op | source)
XLA Modules:
  0.0 337.1 jit_solution(16398270126384592595)
XLA Ops:
  0.6 0.7 and_select_fusion.2
  3.2 0.7 fusion.6
  5.8 0.9 fusion.8
  6.7 2.1 collective-permute-start
  8.8 2.2 collective-permute-start.1
  11.0 1.8 collective-permute-start.2
  12.8 2.9 collective-permute-start.3
  15.7 1.3 collective-permute-start.4
  17.1 0.8 copy.17
  19.4 4.0 %shard_map.120 = bf16[16384,128]{1,0:T(8,128)(2,1)} custom-call(s32[128]{0:T(128)} %reshape.161.idx_ref, bf16[2048,256]{1,0:T(8,128)(2,1)} %bitcast.69, bf16[2048,256]{1,0:T(8,128)(2,1)} %bitcast.73), custom_call_target="tpu_custom_call" | custom-call | bytes 10485760 | tf_op jit(solution)/shard_map/pallas_call | solution.py:54
  24.1 8.4 %all-to-all-start = ((bf16[16,1024,128]{2,1,0:T(8,128)(2,1)}), bf16[16,1024,128]{2,1,0:T(8,128)(2,1)}, u32[]{:S(2)}, u32[]{:S(2)}) async-start(bf16[16,1024,128]{2,1,0:T(8,128)(2,1)} %bitcast.67), calls=%async_computation | async-start | bytes 8388608 | tf_op jit(solution)/shard_map/all_to_all | solution.py:444
  32.5 2.8 collective-permute-start.5
  35.3 0.8 collective-permute-start.6
  36.1 0.9 collective-permute-start.7
  37.2 3.5 %collective-permute-start.10 = (bf16[256,256]{1,0:T(8,128)(2,1)S(1)}, bf16[256,256]{1,0:T(8,128)(2,1)S(1)}, u32[]{:S(2)}, u32[]{:S(2)}) collective-permute-start(bf16[256,256]{1,0:T(8,128)(2,1)S(1)} %add_add_fusion.1), channel_id=1, source_target_pairs={{0,32},{4,36},{8,40},{12,44},{16,48},{20,52},{24,56},{28,60},{32,0... | collective-permute-start | bytes 393224 | tf_op jit(solution)/shard_map/ppermute | solution.py:396
  41.9 43.4 %collective-permute-done.10 = bf16[256,256]{1,0:T(8,128)(2,1)S(1)} collective-permute-done((bf16[256,256]{1,0:T(8,128)(2,1)S(1)}, bf16[256,256]{1,0:T(8,128)(2,1)S(1)}, u32[]{:S(2)}, u32[]{:S(2)}) %collective-permute-start.10) | collective-permute-done | bytes 131104 | tf_op jit(solution)/shard_map/ppermute | solution.py:396
  85.3 2.0 collective-permute-start.9
  87.4 3.9 %shard_map.119 = bf16[16384,128]{1,0:T(8,128)(2,1)} custom-call(s32[128]{0:T(128)} %reshape.161.idx_ref, bf16[2048,256]{1,0:T(8,128)(2,1)} %bitcast.70, bf16[2048,256]{1,0:T(8,128)(2,1)} %bitcast.74), custom_call_target="tpu_custom_call" | custom-call | bytes 10485760 | tf_op jit(solution)/shard_map/pallas_call | solution.py:54
  92.7 0.7 constant_dynamic-slice_fusion
  93.4 2.8 collective-permute-start.11
  96.1 0.8 collective-permute-start.12
  96.9 0.9 collective-permute-start.13
  97.8 0.7 add_add_fusion
  98.5 5.1 %shard_map.121.g_ref = bf16[2048,256]{1,0:T(8,128)(2,1)} custom-call(s32[1]{0:T(128)} %bitcast.14.at_ref, bf16[2048,256]{1,0:T(8,128)(2,1)} %bitcast.79, bf16[2048,256]{1,0:T(8,128)(2,1)} %copy-done.3, bf16[2048,256]{1,0:T(8,128)(2,1)} %collective-permute-done.6.refs_2_.g2, bf16[2048,256]{1,0:T(8,128)(2,1)} %collective-permute-done.7.refs_3_.g3, ...), custom_call_target="tpu_custom_call" | custom-call | flops 1073741824 | bytes 6291456 | tf_op jit(solution)/shard_map/pallas_call | solution.py:82
  104.7 5.8 %all-to-all-start.1 = ((bf16[16,1024,128]{2,1,0:T(8,128)(2,1)}), bf16[16,1024,128]{2,1,0:T(8,128)(2,1)}, u32[]{:S(2)}, u32[]{:S(2)}) async-start(bf16[16,1024,128]{2,1,0:T(8,128)(2,1)} %bitcast.68), calls=%async_computation.1 | async-start | bytes 8388608 | tf_op jit(solution)/shard_map/all_to_all | solution.py:444
  111.1 26.9 %shard_map.122 = (bf16[2048,128]{1,0:T(8,128)(2,1)}, bf16[2048,256]{1,0:T(8,128)(2,1)}, bf16[16384,128]{1,0:T(8,128)(2,1)}, f32[2,2048,128]{2,1,0:T(8,128)}, bf1...) custom-call(s32[1]{0:T(128)} %bitcast.me_ref, s32[96]{0:T(128)} %multiply_add_fusion.slot_ref, ...), custom_call_target="tpu_custom_call" | custom-call | flops 6442450944 | bytes 16777216 | tf_op jit(solution)/shard_map/pallas_call | solution.py:191
  138.0 19.6 %all-to-all-done.1 = bf16[16,1024,128]{2,1,0:T(8,128)(2,1)} async-done(((bf16[16,1024,128]{2,1,0:T(8,128)(2,1)}), bf16[16,1024,128]{2,1,0:T(8,128)(2,1)}, u32[]{:S(2)}, u32[]{:S(2)}) %all-to-all-start.1) | async-done | bytes 4194336 | tf_op jit(solution)/shard_map/all_to_all | solution.py:444
  157.6 11.8 %all-to-all-start.2 = ((bf16[16,1024,128]{2,1,0:T(8,128)(2,1)}), bf16[16,1024,128]{2,1,0:T(8,128)(2,1)}, u32[]{:S(2)}, u32[]{:S(2)}) async-start(bf16[16,1024,128]{2,1,0:T(8,128)(2,1)} %bitcast.78), calls=%async_computation.2 | async-start | bytes 8388608 | tf_op jit(solution)/shard_map/all_to_all | solution.py:444
  169.9 1.4 collective-permute-start.16
  171.6 26.9 %shard_map.123 = (bf16[2048,128]{1,0:T(8,128)(2,1)}, bf16[2048,256]{1,0:T(8,128)(2,1)}, bf16[16384,128]{1,0:T(8,128)(2,1)}, f32[2,2048,128]{2,1,0:T(8,128)}, bf1...) custom-call(s32[1]{0:T(128)} %bitcast.me_ref, ...), custom_call_target="tpu_custom_call", output_to_operand_aliasing={{1}: (11, {})} | custom-call | flops 6442450944 | bytes 16777216 | tf_op jit(solution)/shard_map/pallas_call | solution.py:191
  198.5 3.0 collective-permute-start.15
  201.6 1.3 collective-permute-start.17
  202.9 5.3 %shard_map.124 = bf16[256,1280]{1,0:T(8,128)(2,1)} custom-call(s32[1]{0:T(128)} %bitcast.14.at_ref, bf16[2048,128]{1,0:T(8,128)(2,1)} %get-tuple-element.63.c0.refs_0_, bf16[2048,128]{1,0:T(8,128)(2,1)} %get-tuple-element.64.c1.refs_1_, bf16[2048,256]{1,0:T(8,128)(2,1)} %bitcast.80, bf16[2048,256]{1,0:T(8,128)(2,1)} %copy-done.3, ...), custom_call_target="tpu_custom_call" | custom-call | flops 1073741824 | bytes 6291456 | tf_op jit(solution)/shard_map/pallas_call | solution.py:336
  208.2 10.9 %all-to-all-done.2 = bf16[16,1024,128]{2,1,0:T(8,128)(2,1)} async-done(((bf16[16,1024,128]{2,1,0:T(8,128)(2,1)}), bf16[16,1024,128]{2,1,0:T(8,128)(2,1)}, u32[]{:S(2)}, u32[]{:S(2)}) %all-to-all-start.2) | async-done | bytes 4194336 | tf_op jit(solution)/shard_map/all_to_all | solution.py:444
  219.1 7.6 %all-to-all-start.3 = ((bf16[16,16,1280]{2,1,0:T(8,128)(2,1)}), bf16[16,16,1280]{2,1,0:T(8,128)(2,1)S(1)}, u32[]{:S(2)}, u32[]{:S(2)}) async-start(bf16[16,16,1280]{2,1,0:T(8,128)(2,1)} %bitcast.84), calls=%async_computation.3 | async-start | bytes 1310720 | tf_op jit(solution)/shard_map/all_to_all | solution.py:444
  227.5 1.3 collective-permute-start.22
  228.8 4.5 %collective-permute-start.23 = (bf16[2,64,128]{2,1,0:T(8,128)(2,1)S(1)}, bf16[2,64,128]{2,1,0:T(8,128)(2,1)S(1)}, u32[]{:S(2)}, u32[]{:S(2)}) collective-permute-start(bf16[2,64,128]{2,1,0:T(8,128)(2,1)S(1)} %get-tuple-element.111), channel_id=1, source_target_pairs={{0,4},{4,8},{8,12},{12,16},{16,20},{20,24},{24,28},{28,32},{32,36}... | collective-permute-start | bytes 98312 | tf_op jit(solution)/shard_map/ppermute | solution.py:388
  233.3 1.3 collective-permute-start.20
  234.7 4.5 %collective-permute-start.21 = (bf16[2,64,128]{2,1,0:T(8,128)(2,1)S(1)}, bf16[2,64,128]{2,1,0:T(8,128)(2,1)S(1)}, u32[]{:S(2)}, u32[]{:S(2)}) collective-permute-start(bf16[2,64,128]{2,1,0:T(8,128)(2,1)S(1)} %get-tuple-element.113), channel_id=1, source_target_pairs={{0,4},{4,8},{8,12},{12,16},{16,20},{20,24},{24,28},{28,32},{32,36}... | collective-permute-start | bytes 98312 | tf_op jit(solution)/shard_map/ppermute | solution.py:388
  239.3 0.8 copy-done.9
  240.1 5.8 %shard_map.125 = bf16[2048,256]{1,0:T(8,128)(2,1)} custom-call(bf16[2048,128]{1,0:T(8,128)(2,1)} %get-tuple-element.63.c0.refs_0_, bf16[2048,128]{1,0:T(8,128)(2,1)} %get-tuple-element.64.c1.refs_1_, bf16[2048,128]{1,0:T(8,128)(2,1)} %copy-done.6, bf16[2048,128]{1,0:T(8,128)(2,1)} %collective-permute-done.15.refs_3_, bf16[2048,128]{1,0:T(8,128)(2,1)} %copy-done.7, ...), custom_call_target="tpu_custom_call" | custom-call | flops 1073741824 | bytes 6291456 | tf_op jit(solution)/shard_map/pallas_call | solution.py:365
  246.5 5.3 %shard_map.126 = (bf16[2048,128]{1,0:T(8,128)(2,1)}, bf16[2048,128]{1,0:T(8,128)(2,1)}, f32[2,2,64,128]{3,2,1,0:T(8,128)}) custom-call(s32[128]{0:T(128)} %reshape.161.idx_ref, s32[16]{0:T(128)} %reduce_sum.56.used_ref, s32[4]{0:T(128)} %pad_add_fusion.glob_ref, f32[2,2048,128]{2,1,0:T(8,128)} %get-tuple-element.75.win_ref, ...), custom_call_target="tpu_custom_call" | custom-call | flops 4194304 | bytes 8388608 | tf_op jit(solution)/shard_map/pallas_call | solution.py:284
  252.4 11.1 %all-to-all-start.4 = ((bf16[16,1024,128]{2,1,0:T(8,128)(2,1)}), bf16[16,1024,128]{2,1,0:T(8,128)(2,1)}, u32[]{:S(2)}, u32[]{:S(2)}) async-start(bf16[16,1024,128]{2,1,0:T(8,128)(2,1)} %bitcast.77), calls=%async_computation.4 | async-start | bytes 8388608 | tf_op jit(solution)/shard_map/all_to_all | solution.py:444
  263.7 1.2 collective-permute-done.24
  265.0 64.3 %all_gather.3 = bf16[256,1280]{1,0:T(8,128)(2,1)S(1)} all-gather(bf16[16,1280]{1,0:T(8,128)(2,1)S(1)} %pad_maximum_fusion.3), channel_id=1, replica_groups=mesh['dp'=2,'ctx'=16,'tp'=4] {'ctx'}, dimensions={0}, use_global_device_ids=true | all-gather | bytes 696320 | tf_op jit(solution)/shard_map/all_gather | solution.py:492
  329.3 0.7 fusion.10
  330.0 1.1 slice_convert_fusion
  331.1 6.0 %shard_map.127 = (bf16[2048,256]{1,0:T(8,128)(2,1)}, bf16[2048,256]{1,0:T(8,128)(2,1)}) custom-call(s32[128]{0:T(128)} %reshape.161.idx_ref, s32[16]{0:T(128)} %reduce_sum.56.used_ref, s32[4]{0:T(128)} %pad_add_fusion.glob_ref, f32[2,2048,128]{2,1,0:T(8,128)} %get-tuple-element.83.win_ref, bf16[16384,128]{1,0:T(8,128)(2,1)} %bitcast.32.back_ref, ...), custom_call_target="tpu_custom_call" | custom-call | flops 4194304 | bytes 8388608 | tf_op jit(solution)/shard_map/pallas_call | solution.py:301
  (105 shorter events, 10.7 us)
Async XLA Ops:
  0.6 86.7 %copy-start = (s32[1,512,3]{1,0,2:T(1,128)S(1)}, s32[1,512,3]{1,0,2:T(1,128)}, u32[]{:S(2)}) copy-start(s32[1,512,3]{1,0,2:T(1,128)} %param.14) | copy-start | bytes 18436
  6.7 16.6 %collective-permute-start = (bf16[256,256]{1,0:T(8,128)(2,1)S(1)}, bf16[256,256]{1,0:T(8,128)(2,1)S(1)}, u32[]{:S(2)}, u32[]{:S(2)}) collective-permute-start(bf16[256,256]{1,0:T(8,128)(2,1)S(1)} %pad_maximum_fusion), channel_id=1, source_target_pairs={{0,4},{4,8},{8,12},{12,0},{16,20},{20,24},{24,28},{28,16},{32,36},... | collective-permute-start | bytes 393224 | tf_op jit(solution)/shard_map/ppermute | solution.py:396
  8.8 14.6 %collective-permute-start.1 = (bf16[256,256]{1,0:T(8,128)(2,1)S(1)}, bf16[256,256]{1,0:T(8,128)(2,1)S(1)}, u32[]{:S(2)}, u32[]{:S(2)}) collective-permute-start(bf16[256,256]{1,0:T(8,128)(2,1)S(1)} %pad_maximum_fusion), channel_id=1, source_target_pairs={{0,12},{4,0},{8,4},{12,8},{16,28},{20,16},{24,20},{28,24},{32,44},... | collective-permute-start | bytes 393224 | tf_op jit(solution)/shard_map/ppermute | solution.py:396
  11.0 12.4 %collective-permute-start.2 = (bf16[256,256]{1,0:T(8,128)(2,1)S(1)}, bf16[256,256]{1,0:T(8,128)(2,1)S(1)}, u32[]{:S(2)}, u32[]{:S(2)}) collective-permute-start(bf16[256,256]{1,0:T(8,128)(2,1)S(1)} %pad_maximum_fusion), channel_id=1, source_target_pairs={{0,8},{4,12},{8,0},{12,4},{16,24},{20,28},{24,16},{28,20},{32,40},... | collective-permute-start | bytes 393224 | tf_op jit(solution)/shard_map/ppermute | solution.py:396
  12.8 10.7 %collective-permute-start.3 = (bf16[2,64,256]{2,1,0:T(8,128)(2,1)S(1)}, bf16[2,64,256]{2,1,0:T(8,128)(2,1)S(1)}, u32[]{:S(2)}, u32[]{:S(2)}) collective-permute-start(bf16[2,64,256]{2,1,0:T(8,128)(2,1)S(1)} %pad_maximum_fusion.1), channel_id=1, source_target_pairs={{0,4},{4,8},{8,12},{12,16},{16,20},{20,24},{24,28},{28,32},{32,36}... | collective-permute-start | bytes 196616 | tf_op jit(solution)/shard_map/ppermute | solution.py:388
  15.7 7.7 %collective-permute-start.4 = (bf16[2,64,256]{2,1,0:T(8,128)(2,1)S(1)}, bf16[2,64,256]{2,1,0:T(8,128)(2,1)S(1)}, u32[]{:S(2)}, u32[]{:S(2)}) collective-permute-start(bf16[2,64,256]{2,1,0:T(8,128)(2,1)S(1)} %pad_maximum_fusion.2), channel_id=1, source_target_pairs={{4,0},{8,4},{12,8},{16,12},{20,16},{24,20},{28,24},{32,28},{36,32}... | collective-permute-start | bytes 196616 | tf_op jit(solution)/shard_map/ppermute | solution.py:388
  23.5 0.6 copy-start.20
  23.5 0.6 copy-start.21
  23.5 9.0 %copy-start.2 = (bf16[1,2048,256]{2,1,0:T(8,128)(2,1)S(1)}, bf16[1,2048,256]{2,1,0:T(8,128)(2,1)}, u32[]{:S(2)}) copy-start(bf16[1,2048,256]{2,1,0:T(8,128)(2,1)} %param.11) | copy-start | bytes 3145732
  23.5 17.7 %copy-start.19 = (s32[1,512,3]{1,0,2:T(1,128)S(1)}, s32[1,512,3]{1,0,2:T(1,128)}, u32[]{:S(2)}) copy-start(s32[1,512,3]{1,0,2:T(1,128)} %param.13) | copy-start | bytes 18436
  24.1 79.9 %all-to-all-start = ((bf16[16,1024,128]{2,1,0:T(8,128)(2,1)}), bf16[16,1024,128]{2,1,0:T(8,128)(2,1)}, u32[]{:S(2)}, u32[]{:S(2)}) async-start(bf16[16,1024,128]{2,1,0:T(8,128)(2,1)} %bitcast.67), calls=%async_computation | async-start | bytes 8388608 | tf_op jit(solution)/shard_map/all_to_all | solution.py:444
  32.5 60.2 %copy-start.1 = (bf16[256,1024]{1,0:T(8,128)(2,1)S(1)}, bf16[256,1024]{1,0:T(8,128)(2,1)}, u32[]{:S(2)}) copy-start(bf16[256,1024]{1,0:T(8,128)(2,1)} %refs_7_.1) | copy-start | bytes 1572868
  32.5 64.4 %collective-permute-start.5 = (bf16[2048,256]{1,0:T(8,128)(2,1)S(1)}, bf16[2048,256]{1,0:T(8,128)(2,1)S(1)}, u32[]{:S(2)}, u32[]{:S(2)}) collective-permute-start(bf16[2048,256]{1,0:T(8,128)(2,1)S(1)} %bitcast.81), channel_id=1, source_target_pairs={{1,0},{2,1},{3,2},{0,3},{5,4},{6,5},{7,6},{4,7},{9,8},{10,9},{11,1... | collective-permute-start | bytes 3145736 | tf_op jit(solution)/shard_map/ppermute | solution.py:381
  35.3 63.2 %collective-permute-start.6 = (bf16[2048,256]{1,0:T(8,128)(2,1)S(1)}, bf16[2048,256]{1,0:T(8,128)(2,1)}, u32[]{:S(2)}, u32[]{:S(2)}) collective-permute-start(bf16[2048,256]{1,0:T(8,128)(2,1)S(1)} %bitcast.82), channel_id=1, source_target_pairs={{2,0},{3,1},{0,2},{1,3},{6,4},{7,5},{4,6},{5,7},{10,8},{11,9},{8,1... | collective-permute-start | bytes 3145736 | tf_op jit(solution)/shard_map/ppermute | solution.py:381
  36.1 62.4 %collective-permute-start.7 = (bf16[2048,256]{1,0:T(8,128)(2,1)S(1)}, bf16[2048,256]{1,0:T(8,128)(2,1)}, u32[]{:S(2)}, u32[]{:S(2)}) collective-permute-start(bf16[2048,256]{1,0:T(8,128)(2,1)S(1)} %bitcast.83), channel_id=1, source_target_pairs={{3,0},{0,1},{1,2},{2,3},{7,4},{4,5},{5,6},{6,7},{11,8},{8,9},{9,10... | collective-permute-start | bytes 3145736 | tf_op jit(solution)/shard_map/ppermute | solution.py:381
  37.2 48.1 %collective-permute-start.10 = (bf16[256,256]{1,0:T(8,128)(2,1)S(1)}, bf16[256,256]{1,0:T(8,128)(2,1)S(1)}, u32[]{:S(2)}, u32[]{:S(2)}) collective-permute-start(bf16[256,256]{1,0:T(8,128)(2,1)S(1)} %add_add_fusion.1), channel_id=1, source_target_pairs={{0,32},{4,36},{8,40},{12,44},{16,48},{20,52},{24,56},{28,60},{32,0... | collective-permute-start | bytes 393224 | tf_op jit(solution)/shard_map/ppermute | solution.py:396
  41.3 52.1 %collective-permute-start.8 = (bf16[256,256]{1,0:T(8,128)(2,1)S(1)}, bf16[256,256]{1,0:T(8,128)(2,1)S(1)}, u32[]{:S(2)}, u32[]{:S(2)}) collective-permute-start(bf16[256,256]{1,0:T(8,128)(2,1)S(1)} %add_add_fusion.1), channel_id=1, source_target_pairs={{0,16},{4,20},{8,24},{12,28},{16,32},{20,36},{24,40},{28,44},{32,4... | collective-permute-start | bytes 393224 | tf_op jit(solution)/shard_map/ppermute | solution.py:396
  85.3 10.8 %collective-permute-start.9 = (bf16[256,256]{1,0:T(8,128)(2,1)S(1)}, bf16[256,256]{1,0:T(8,128)(2,1)S(1)}, u32[]{:S(2)}, u32[]{:S(2)}) collective-permute-start(bf16[256,256]{1,0:T(8,128)(2,1)S(1)} %add_add_fusion.1), channel_id=1, source_target_pairs={{0,48},{4,52},{8,56},{12,60},{16,0},{20,4},{24,8},{28,12},{32,16},... | collective-permute-start | bytes 393224 | tf_op jit(solution)/shard_map/ppermute | solution.py:396
  93.4 10.2 %collective-permute-start.11 = (bf16[256,256]{1,0:T(8,128)(2,1)S(1)}, bf16[256,256]{1,0:T(8,128)(2,1)S(1)}, u32[]{:S(2)}, u32[]{:S(2)}) collective-permute-start(bf16[256,256]{1,0:T(8,128)(2,1)S(1)} %get-tuple-element.108), channel_id=1, source_target_pairs={{0,3},{1,0},{2,1},{3,2},{4,7},{5,4},{6,5},{7,6},{8,11},{9,8},{10,9... | collective-permute-start | bytes 393224 | tf_op jit(solution)/shard_map/ppermute | solution.py:460
  96.1 7.5 %collective-permute-start.12 = (bf16[256,256]{1,0:T(8,128)(2,1)S(1)}, bf16[256,256]{1,0:T(8,128)(2,1)S(1)}, u32[]{:S(2)}, u32[]{:S(2)}) collective-permute-start(bf16[256,256]{1,0:T(8,128)(2,1)S(1)} %get-tuple-element.110), channel_id=1, source_target_pairs={{0,2},{1,3},{2,0},{3,1},{4,6},{5,7},{6,4},{7,5},{8,10},{9,11},{10,... | collective-permute-start | bytes 393224 | tf_op jit(solution)/shard_map/ppermute | solution.py:460
  96.9 1.6 copy-start.3
  96.9 7.1 %collective-permute-start.13 = (bf16[256,256]{1,0:T(8,128)(2,1)S(1)}, bf16[256,256]{1,0:T(8,128)(2,1)S(1)}, u32[]{:S(2)}, u32[]{:S(2)}) collective-permute-start(bf16[256,256]{1,0:T(8,128)(2,1)S(1)} %get-tuple-element.107), channel_id=1, source_target_pairs={{0,1},{1,2},{2,3},{3,0},{4,5},{5,6},{6,7},{7,4},{8,9},{9,10},{10,1... | collective-permute-start | bytes 393224 | tf_op jit(solution)/shard_map/ppermute | solution.py:460
  103.6 0.6 copy-start.10
  103.6 0.7 copy-start.11
  104.0 0.7 copy-start.12
  104.7 53.0 %all-to-all-start.1 = ((bf16[16,1024,128]{2,1,0:T(8,128)(2,1)}), bf16[16,1024,128]{2,1,0:T(8,128)(2,1)}, u32[]{:S(2)}, u32[]{:S(2)}) async-start(bf16[16,1024,128]{2,1,0:T(8,128)(2,1)} %bitcast.68), calls=%async_computation.1 | async-start | bytes 8388608 | tf_op jit(solution)/shard_map/all_to_all | solution.py:444
  157.6 11.8 %copy-start.4 = (bf16[2048,128]{1,0:T(8,128)(2,1)S(1)}, bf16[2048,128]{1,0:T(8,128)(2,1)}, u32[]{:S(2)}) copy-start(bf16[2048,128]{1,0:T(8,128)(2,1)} %get-tuple-element.63.c0.refs_0_) | copy-start | bytes 1572868
  157.6 61.4 %all-to-all-start.2 = ((bf16[16,1024,128]{2,1,0:T(8,128)(2,1)}), bf16[16,1024,128]{2,1,0:T(8,128)(2,1)}, u32[]{:S(2)}, u32[]{:S(2)}) async-start(bf16[16,1024,128]{2,1,0:T(8,128)(2,1)} %bitcast.78), calls=%async_computation.2 | async-start | bytes 8388608 | tf_op jit(solution)/shard_map/all_to_all | solution.py:444
  169.5 57.2 %collective-permute-start.14 = (bf16[2048,128]{1,0:T(8,128)(2,1)S(1)}, bf16[2048,128]{1,0:T(8,128)(2,1)S(1)}, u32[]{:S(2)}, u32[]{:S(2)}) collective-permute-start(bf16[2048,128]{1,0:T(8,128)(2,1)S(1)} %copy-done.4), channel_id=1, source_target_pairs={{1,0},{2,1},{3,2},{0,3},{5,4},{6,5},{7,6},{4,7},{9,8},{10,9},{11,1... | collective-permute-start | bytes 1572872 | tf_op jit(solution)/shard_map/ppermute | solution.py:381
  169.9 57.6 %collective-permute-start.16 = (bf16[2048,128]{1,0:T(8,128)(2,1)S(1)}, bf16[2048,128]{1,0:T(8,128)(2,1)S(1)}, u32[]{:S(2)}, u32[]{:S(2)}) collective-permute-start(bf16[2048,128]{1,0:T(8,128)(2,1)S(1)} %copy-done.4), channel_id=1, source_target_pairs={{2,0},{3,1},{0,2},{1,3},{6,4},{7,5},{4,6},{5,7},{10,8},{11,9},{8,1... | collective-permute-start | bytes 1572872 | tf_op jit(solution)/shard_map/ppermute | solution.py:381
  171.3 57.5 %collective-permute-start.18 = (bf16[2048,128]{1,0:T(8,128)(2,1)S(1)}, bf16[2048,128]{1,0:T(8,128)(2,1)S(1)}, u32[]{:S(2)}, u32[]{:S(2)}) collective-permute-start(bf16[2048,128]{1,0:T(8,128)(2,1)S(1)} %copy-done.4), channel_id=1, source_target_pairs={{3,0},{0,1},{1,2},{2,3},{7,4},{4,5},{5,6},{6,7},{11,8},{8,9},{9,10... | collective-permute-start | bytes 1572872 | tf_op jit(solution)/shard_map/ppermute | solution.py:381
  198.5 28.2 %copy-start.5 = (bf16[2048,128]{1,0:T(8,128)(2,1)S(1)}, bf16[2048,128]{1,0:T(8,128)(2,1)}, u32[]{:S(2)}) copy-start(bf16[2048,128]{1,0:T(8,128)(2,1)} %get-tuple-element.64.c1.refs_1_) | copy-start | bytes 1572868
  198.5 28.9 %copy-start.13 = (bf16[2,2,64,128]{3,2,1,0:T(8,128)(2,1)S(1)}, bf16[2,2,64,128]{3,2,1,0:T(8,128)(2,1)}, u32[]{:S(2)}) copy-start(bf16[2,2,64,128]{3,2,1,0:T(8,128)(2,1)} %get-tuple-element.77) | copy-start | bytes 196612
  198.5 28.9 %copy-start.14 = (bf16[2,2,64,128]{3,2,1,0:T(8,128)(2,1)S(1)}, bf16[2,2,64,128]{3,2,1,0:T(8,128)(2,1)}, u32[]{:S(2)}) copy-start(bf16[2,2,64,128]{3,2,1,0:T(8,128)(2,1)} %get-tuple-element.73) | copy-start | bytes 196612
  198.5 34.8 %collective-permute-start.15 = (bf16[2048,128]{1,0:T(8,128)(2,1)}, bf16[2048,128]{1,0:T(8,128)(2,1)}, u32[]{:S(2)}, u32[]{:S(2)}) collective-permute-start(bf16[2048,128]{1,0:T(8,128)(2,1)} %get-tuple-element.64.c1.refs_1_), channel_id=1, source_target_pairs={{1,0},{2,1},{3,2},{0,3},{5,4},{6,5},{7,6},{4,7},{9,8},{10,9},{11,1... | collective-permute-start | bytes 1572872 | tf_op jit(solution)/shard_map/ppermute | solution.py:381
  201.6 33.1 %collective-permute-start.17 = (bf16[2048,128]{1,0:T(8,128)(2,1)}, bf16[2048,128]{1,0:T(8,128)(2,1)}, u32[]{:S(2)}, u32[]{:S(2)}) collective-permute-start(bf16[2048,128]{1,0:T(8,128)(2,1)} %get-tuple-element.64.c1.refs_1_), channel_id=1, source_target_pairs={{2,0},{3,1},{0,2},{1,3},{6,4},{7,5},{4,6},{5,7},{10,8},{11,9},{8,1... | collective-permute-start | bytes 1572872 | tf_op jit(solution)/shard_map/ppermute | solution.py:381
  219.1 32.7 %all-to-all-start.3 = ((bf16[16,16,1280]{2,1,0:T(8,128)(2,1)}), bf16[16,16,1280]{2,1,0:T(8,128)(2,1)S(1)}, u32[]{:S(2)}, u32[]{:S(2)}) async-start(bf16[16,16,1280]{2,1,0:T(8,128)(2,1)} %bitcast.84), calls=%async_computation.3 | async-start | bytes 1310720 | tf_op jit(solution)/shard_map/all_to_all | solution.py:444
  226.7 12.5 %copy-start.6 = (bf16[2048,128]{1,0:T(8,128)(2,1)}, bf16[2048,128]{1,0:T(8,128)(2,1)S(1)}, u32[]{:S(2)}) copy-start(bf16[2048,128]{1,0:T(8,128)(2,1)S(1)} %collective-permute-done.14.refs_2_) | copy-start | bytes 1572868
  226.7 12.5 %collective-permute-start.19 = (bf16[2048,128]{1,0:T(8,128)(2,1)S(1)}, bf16[2048,128]{1,0:T(8,128)(2,1)S(1)}, u32[]{:S(2)}, u32[]{:S(2)}) collective-permute-start(bf16[2048,128]{1,0:T(8,128)(2,1)S(1)} %copy-done.5), channel_id=1, source_target_pairs={{3,0},{0,1},{1,2},{2,3},{7,4},{4,5},{5,6},{6,7},{11,8},{8,9},{9,10... | collective-permute-start | bytes 1572872 | tf_op jit(solution)/shard_map/ppermute | solution.py:381
  227.4 11.8 %copy-start.7 = (bf16[2048,128]{1,0:T(8,128)(2,1)}, bf16[2048,128]{1,0:T(8,128)(2,1)S(1)}, u32[]{:S(2)}) copy-start(bf16[2048,128]{1,0:T(8,128)(2,1)S(1)} %collective-permute-done.16.refs_4_) | copy-start | bytes 1572868
  227.5 18.4 %collective-permute-start.22 = (bf16[2,64,128]{2,1,0:T(8,128)(2,1)S(1)}, bf16[2,64,128]{2,1,0:T(8,128)(2,1)S(1)}, u32[]{:S(2)}, u32[]{:S(2)}) collective-permute-start(bf16[2,64,128]{2,1,0:T(8,128)(2,1)S(1)} %get-tuple-element.112), channel_id=1, source_target_pairs={{4,0},{8,4},{12,8},{16,12},{20,16},{24,20},{28,24},{32,28},{36,32}... | collective-permute-start | bytes 98312 | tf_op jit(solution)/shard_map/ppermute | solution.py:388
  228.8 10.5 %copy-start.8 = (bf16[2048,128]{1,0:T(8,128)(2,1)}, bf16[2048,128]{1,0:T(8,128)(2,1)S(1)}, u32[]{:S(2)}) copy-start(bf16[2048,128]{1,0:T(8,128)(2,1)S(1)} %collective-permute-done.18.refs_6_) | copy-start | bytes 1572868
  228.8 17.1 %collective-permute-start.23 = (bf16[2,64,128]{2,1,0:T(8,128)(2,1)S(1)}, bf16[2,64,128]{2,1,0:T(8,128)(2,1)S(1)}, u32[]{:S(2)}, u32[]{:S(2)}) collective-permute-start(bf16[2,64,128]{2,1,0:T(8,128)(2,1)S(1)} %get-tuple-element.111), channel_id=1, source_target_pairs={{0,4},{4,8},{8,12},{12,16},{16,20},{20,24},{24,28},{28,32},{32,36}... | collective-permute-start | bytes 98312 | tf_op jit(solution)/shard_map/ppermute | solution.py:388
  233.3 18.4 %collective-permute-start.20 = (bf16[2,64,128]{2,1,0:T(8,128)(2,1)S(1)}, bf16[2,64,128]{2,1,0:T(8,128)(2,1)S(1)}, u32[]{:S(2)}, u32[]{:S(2)}) collective-permute-start(bf16[2,64,128]{2,1,0:T(8,128)(2,1)S(1)} %get-tuple-element.114), channel_id=1, source_target_pairs={{4,0},{8,4},{12,8},{16,12},{20,16},{24,20},{28,24},{32,28},{36,32}... | collective-permute-start | bytes 98312 | tf_op jit(solution)/shard_map/ppermute | solution.py:388
  234.7 17.1 %collective-permute-start.21 = (bf16[2,64,128]{2,1,0:T(8,128)(2,1)S(1)}, bf16[2,64,128]{2,1,0:T(8,128)(2,1)S(1)}, u32[]{:S(2)}, u32[]{:S(2)}) collective-permute-start(bf16[2,64,128]{2,1,0:T(8,128)(2,1)S(1)} %get-tuple-element.113), channel_id=1, source_target_pairs={{0,4},{4,8},{8,12},{12,16},{16,20},{20,24},{24,28},{28,32},{32,36}... | collective-permute-start | bytes 98312 | tf_op jit(solution)/shard_map/ppermute | solution.py:388
  239.2 0.8 copy-start.9
  252.4 78.7 %all-to-all-start.4 = ((bf16[16,1024,128]{2,1,0:T(8,128)(2,1)}), bf16[16,1024,128]{2,1,0:T(8,128)(2,1)}, u32[]{:S(2)}, u32[]{:S(2)}) async-start(bf16[16,1024,128]{2,1,0:T(8,128)(2,1)} %bitcast.77), calls=%async_computation.4 | async-start | bytes 8388608 | tf_op jit(solution)/shard_map/all_to_all | solution.py:444
  263.6 1.3 collective-permute-start.24
  (4 other events, 2.4 us)

commit v3 on v2

v3 whole, which is shorter than its diff:
```python
import functools

import jax
import jax.numpy as jnp
from jax import lax
from jax.experimental import pallas as pl
from jax.experimental.pallas import tpu as pltpu
from jax.sharding import PartitionSpec as P

HD = 64
BLK = 64
R = 3
G = 2
LANES = 128
NEG_FILL = -1e30
VMEM_LIMIT = 56 * 1024 * 1024
CARRIED = 160

NT = (((1,), (1,)), ((), ()))
NN = (((1,), (0,)), ((), ()))
TN = (((0,), (0,)), ((), ()))


def dot(a, b, dims):
    return lax.dot_general(a, b, dims, preferred_element_type=jnp.float32)


def smem():
    return pl.BlockSpec(memory_space=pltpu.SMEM)


def whole(shape, column=None):
    if column is None:
        return pl.BlockSpec(shape, lambda i: (0,) * len(shape))
    return pl.BlockSpec(shape, lambda i: (0,) * (len(shape) - 1) + (column,))


def params(**more):
    return pltpu.CompilerParams(vmem_limit_bytes=VMEM_LIMIT, **more)


def pick_kernel(slots, idx_ref, k_ref, v_ref, out_ref):
    def body(s, _):
        src = pl.multiple_of(idx_ref[s] * BLK, BLK)
        dst = pl.multiple_of(s * 2 * BLK, 2 * BLK)
        out_ref[pl.ds(dst, BLK), :] = k_ref[pl.ds(src, BLK), :]
        out_ref[pl.ds(dst + BLK, BLK), :] = v_ref[pl.ds(src, BLK), :]
        return 0

    lax.fori_loop(0, slots, body, 0, unroll=4)


def pick_blocks(idx, keys, values, column, slots):
    rows = keys.shape[0]
    return pl.pallas_call(
        functools.partial(pick_kernel, slots),
        grid=(1,),
        in_specs=[smem(), whole((rows, LANES), column), whole((rows, LANES), column)],
        out_specs=whole((slots * 2 * BLK, LANES)),
        out_shape=jax.ShapeDtypeStruct((slots * 2 * BLK, LANES), jnp.bfloat16),
        compiler_params=params(),
        cost_estimate=pl.CostEstimate(flops=0, bytes_accessed=10 << 20, transcendentals=0),
    )(idx, keys, values)


def pick_global_kernel(blocks, glob_ref, me_ref, k_ref, v_ref, out_ref):
    owned = glob_ref[pl.program_id(0)] // blocks == me_ref[0]
    out_ref[:BLK, :] = jnp.where(owned, k_ref[...], jnp.zeros_like(k_ref))
    out_ref[BLK:, :] = jnp.where(owned, v_ref[...], jnp.zeros_like(v_ref))


def pick_global(glob, me, keys, values):
    rows, width = keys.shape
    blocks = rows // BLK
    block = pl.BlockSpec((BLK, width), lambda e, glob, me: (glob[e] % blocks, 0))
    return pl.pallas_call(
        functools.partial(pick_global_kernel, blocks),
        grid_spec=pltpu.PrefetchScalarGridSpec(
            num_scalar_prefetch=2,
            grid=(G,),
            in_specs=[block, block],
            out_specs=pl.BlockSpec((2 * BLK, width), lambda e, glob, me: (e, 0)),
        ),
        out_shape=jax.ShapeDtypeStruct((G * 2 * BLK, width), jnp.bfloat16),
        compiler_params=params(),
        cost_estimate=pl.CostEstimate(flops=0, bytes_accessed=1 << 19, transcendentals=0),
    )(glob, me, keys, values)


TILE = 512


def ring_specs(rows, width):
    last = rows // TILE // 2
    full = pl.BlockSpec((TILE, width), lambda i, *_: (i, 0))
    upper = pl.BlockSpec((TILE, width), lambda i, *_: (jnp.minimum(i, last - 1), 0))
    lower = pl.BlockSpec((TILE, width), lambda i, *_: (jnp.maximum(i - last, 0), 0))
    return [full, full, full, upper, lower]


def ring_values(refs):
    own, following, previous, upper, lower = refs
    top = pl.program_id(0) < pl.num_programs(0) // 2
    return own[...], following[...], jnp.where(top, upper[...], lower[...]), previous[...]


def grad_context_kernel(at_ref, *refs):
    del at_ref
    total = None
    for g, w in zip(ring_values(refs[:5]), refs[5:9]):
        term = dot(g, w[...], NT)
        total = term if total is None else total + term
    refs[9][...] = total.astype(jnp.bfloat16)


def grad_context_of(at, pieces, weight):
    rows, width = pieces[0].shape
    heads = weight.shape[0]
    turned = [
        pl.BlockSpec((heads, width), functools.partial(lambda j, i, at: (0, (at[0] + j) % 4), j))
        for j in range(4)
    ]
    return pl.pallas_call(
        grad_context_kernel,
        grid_spec=pltpu.PrefetchScalarGridSpec(
            num_scalar_prefetch=1,
            grid=(rows // TILE,),
            in_specs=ring_specs(rows, width) + turned,
            out_specs=pl.BlockSpec((TILE, heads), lambda i, at: (i, 0)),
        ),
        out_shape=jax.ShapeDtypeStruct((rows, heads), jnp.bfloat16),
        compiler_params=params(),
        cost_estimate=pl.CostEstimate(flops=2 * rows * 1024 * heads, bytes_accessed=16 << 20, transcendentals=0),
    )(at, *pieces, weight, weight, weight, weight)


def attend_kernel(
    blocks, last_block, me_ref, slot_ref, to_ref, valid_ref, q_ref, k_ref, v_ref, g_ref, before_ref, after_ref, glob_ref,
    fetched_ref, dq_in_ref, ctx_ref, dq_ref, win_out_ref, up_ref, down_ref, gsum_out_ref, *more,
):
    del dq_in_ref
    parts_out, (kpad, vpad, win_ref, gsum_ref) = more[:-4], more[-4:]
    if len(parts_out) == 1:
        ret_ref = parts_out[0]
    else:
        *parts_out, ret_ref = parts_out
    rows = blocks * BLK
    kpad[0:BLK, :] = before_ref[0]
    vpad[0:BLK, :] = before_ref[1]
    kpad[rows + BLK : rows + 2 * BLK, :] = after_ref[0]
    vpad[rows + BLK : rows + 2 * BLK, :] = after_ref[1]
    kpad[BLK : rows + BLK, :] = k_ref[...]
    vpad[BLK : rows + BLK, :] = v_ref[...]
    win_ref[...] = jnp.zeros_like(win_ref)
    gsum_ref[...] = jnp.zeros_like(gsum_ref)
    low = lax.broadcasted_iota(jnp.int32, (BLK, LANES), 1) < HD

    def body(i, _):
        row = pl.multiple_of(i * BLK, BLK)
        q = q_ref[pl.ds(row, BLK), :] * jnp.bfloat16(0.125)
        g = g_ref[pl.ds(row, BLK), :]
        zero = jnp.zeros_like(q)
        qbd = jnp.concatenate([jnp.where(low, q, zero), jnp.where(low, zero, q)], axis=0)
        gbd = jnp.concatenate([jnp.where(low, g, zero), jnp.where(low, zero, g)], axis=0)
        starts = [pl.multiple_of(slot_ref[i * R + r] * 2 * BLK, 2 * BLK) for r in range(R)]
        kcat = jnp.concatenate(
            [kpad[pl.ds(row, 3 * BLK), :]]
            + [fetched_ref[pl.ds(s, BLK), :] for s in starts]
            + [glob_ref[0, 0], glob_ref[1, 0]],
            axis=0,
        )
        vcat = jnp.concatenate(
            [vpad[pl.ds(row, 3 * BLK), :]]
            + [fetched_ref[pl.ds(s + BLK, BLK), :] for s in starts]
            + [glob_ref[0, 1], glob_ref[1, 1]],
            axis=0,
        )
        scores = dot(kcat, qbd, NT)
        block = me_ref[0] * blocks + i
        present = [block > 0, None, block < last_block]
        present += [valid_ref[i * R + r] == 1 for r in range(R)] + [None] * G
        parts = []
        for e, there in enumerate(present):
            part = scores[e * BLK : (e + 1) * BLK]
            parts.append(part if there is None else part + jnp.where(there, 0.0, NEG_FILL))
        scores = jnp.concatenate(parts, axis=0)
        peak = jnp.max(scores, axis=0, keepdims=True)
        terms = jnp.exp(scores - peak)
        probs = terms * (1.0 / jnp.sum(terms, axis=0, keepdims=True))
        probs_low = probs.astype(jnp.bfloat16)
        grad_probs = dot(vcat, gbd, NT)
        delta = jnp.sum(probs * grad_probs, axis=0, keepdims=True)
        grad_scores = (probs * (grad_probs - delta)).astype(jnp.bfloat16)
        context = dot(probs_low, vcat, TN)
        grad_q = dot(grad_scores, kcat, TN)
        grad_k = dot(grad_scores, qbd, NN)
        grad_v = dot(probs_low, gbd, NN)
        ctx_ref[pl.ds(row, BLK), :] = jnp.where(low, context[:BLK], context[BLK:]).astype(jnp.bfloat16)
        dq_ref[pl.ds(row, BLK), :] = (
            jnp.where(low, grad_q[:BLK], grad_q[BLK:]) * 0.125
        ).astype(jnp.bfloat16)
        win_ref[0, pl.ds(row, 3 * BLK), :] += grad_k[: 3 * BLK]
        win_ref[1, pl.ds(row, 3 * BLK), :] += grad_v[: 3 * BLK]
        for r in range(R):
            part = slice((3 + r) * BLK, (4 + r) * BLK)
            to = pl.multiple_of(to_ref[i * R + r] * 2 * BLK, 2 * BLK)
            ret_ref[pl.ds(to, BLK), :] = grad_k[part].astype(jnp.bfloat16)
            ret_ref[pl.ds(to + BLK, BLK), :] = grad_v[part].astype(jnp.bfloat16)
        for e in range(G):
            part = slice((3 + R + e) * BLK, (4 + R + e) * BLK)
            gsum_ref[e, 0] += grad_k[part]
            gsum_ref[e, 1] += grad_v[part]
        return 0

    lax.fori_loop(0, blocks, body, 0, unroll=2)
    win_out_ref[...] = win_ref[:, BLK : rows + BLK, :]
    up_ref[...] = win_ref[:, 0:BLK, :].astype(jnp.bfloat16)
    down_ref[...] = win_ref[:, rows + BLK : rows + 2 * BLK, :].astype(jnp.bfloat16)
    gsum_out_ref[...] = gsum_ref[...].reshape(G * 2 * BLK, LANES).astype(jnp.bfloat16)
    if len(parts_out) > 1:
        devices, _, lanes = parts_out[0].shape
        count = ret_ref.shape[0] // 2 // devices
        for p, part_ref in enumerate(parts_out):
            for d in range(devices):
                start = (p * devices + d) * count
                part_ref[d, 0:count, :] = ret_ref[start : start + count, :]


def attend(last_block, me, slot, to, valid, q, k, v, g, before, after, glob, fetched, dq_in, column):
    rows, width = q.shape
    blocks = rows // BLK
    half = whole((rows, LANES), column)
    first = dq_in is None
    shapes = [
        ((rows, LANES), jnp.bfloat16),
        ((rows, width), jnp.bfloat16),
        ((2, rows, LANES), jnp.float32),
        ((2, BLK, LANES), jnp.bfloat16),
        ((2, BLK, LANES), jnp.bfloat16),
        ((G * 2 * BLK, LANES), jnp.bfloat16),
    ]
    scratch = [
        pltpu.VMEM((rows + 2 * BLK, LANES), jnp.bfloat16),
        pltpu.VMEM((rows + 2 * BLK, LANES), jnp.bfloat16),
        pltpu.VMEM((2, rows + 2 * BLK, LANES), jnp.float32),
        pltpu.VMEM((G, 2, BLK, LANES), jnp.float32),
    ]
    if first:
        dq_in = jnp.zeros((16, 128), jnp.bfloat16)
        shapes.append((fetched.shape, jnp.bfloat16))
    else:
        shapes += [((16, fetched.shape[0] // 32 + CARRIED, LANES), jnp.bfloat16)] * 2
        scratch.insert(0, pltpu.VMEM(fetched.shape, jnp.bfloat16))
    specs = [whole(shape) for shape, _ in shapes]
    specs[1] = half
    return pl.pallas_call(
        functools.partial(attend_kernel, blocks, last_block),
        grid=(1,),
        in_specs=[
            smem(), smem(), smem(), smem(), half, half, half, half,
            whole((2, BLK, LANES), column),
            whole((2, BLK, LANES), column),
            whole((G, 2, BLK, LANES), column),
            whole(fetched.shape),
            pl.BlockSpec(memory_space=pl.ANY),
        ],
        out_specs=tuple(specs),
        out_shape=tuple(jax.ShapeDtypeStruct(*shape) for shape in shapes),
        scratch_shapes=scratch,
        input_output_aliases={} if first else {12: 1},
        compiler_params=params(),
        cost_estimate=pl.CostEstimate(
            flops=12 * blocks * 512 * 128 * 128 * 2, bytes_accessed=80 << 20, transcendentals=blocks * 512 * 128
        ),
    )(me, slot, to, valid, q, k, v, g, before, after, glob, fetched, dq_in)


def land(entries, idx_ref, used_ref, back_ref, acc):
    first, end, capacity = entries

    def body(a, _):
        @pl.when(used_ref[a] > 0)
        def _():
            for c in range(first, end):
                at = pl.multiple_of(idx_ref[a * capacity + c] * BLK, BLK)
                src = (c - first) * 2 * BLK
                acc[0, pl.ds(at, BLK), :] += back_ref[a, src : src + BLK, :].astype(jnp.float32)
                acc[1, pl.ds(at, BLK), :] += back_ref[a, src + BLK : src + 2 * BLK, :].astype(jnp.float32)

        return 0

    lax.fori_loop(0, back_ref.shape[0], body, 0)


def edges(up_ref, down_ref, acc):
    rows = acc.shape[1]
    acc[:, rows - BLK : rows, :] += up_ref[...].astype(jnp.float32)
    acc[:, 0:BLK, :] += down_ref[...].astype(jnp.float32)


def first_kernel(
    capacity, idx_ref, used_ref, glob_ref, win_ref, back_ref, up_ref, down_ref, dk_ref, dv_ref, kept_ref, acc
):
    acc[...] = win_ref[...]
    edges(up_ref, down_ref, acc)
    land((0, capacity, capacity), idx_ref, used_ref, back_ref, acc)
    dk_ref[...] = acc[0].astype(jnp.bfloat16)
    dv_ref[...] = acc[1].astype(jnp.bfloat16)
    blocks = acc.shape[1] // BLK
    for e in range(G):
        at = pl.multiple_of(glob_ref[e] % blocks * BLK, BLK)
        kept_ref[e] = acc[:, pl.ds(at, BLK), :]


def middle_kernel(capacity, idx_ref, used_ref, win_ref, back_ref, up_ref, down_ref, acc):
    acc[...] = win_ref[...]
    edges(up_ref, down_ref, acc)
    land((0, capacity // 2, capacity), idx_ref, used_ref, back_ref, acc)


def last_kernel(
    capacity, idx_ref, used_ref, glob_ref, me_ref, win_ref, back_ref, kept_ref, dk_in_ref, dv_in_ref,
    dk_ref, dv_ref, gw_ref, acc,
):
    acc[...] = win_ref[...]
    land((capacity // 2, capacity, capacity), idx_ref, used_ref, back_ref, acc)
    blocks = acc.shape[1] // BLK
    start = capacity * BLK
    sums = start + gw_ref.shape[1] // LANES * 16

    def total(half, e):
        found = [
            jnp.concatenate(
                [
                    back_ref[(e * 2 + t) * 4 + d, sums + half * 16 : sums + (half + 1) * 16, :].astype(jnp.float32)
                    for d in range(4)
                ]
            )
            for t in range(2)
        ]
        return jnp.stack(found)

    for e in range(G):

        @pl.when(glob_ref[e] // blocks == me_ref[0])
        def _():
            at = pl.multiple_of(glob_ref[e] % blocks * BLK, BLK)
            acc[:, pl.ds(at, BLK), :] += total(1, e)

    dk_ref[:, LANES:] = acc[0].astype(jnp.bfloat16)
    dv_ref[:, LANES:] = acc[1].astype(jnp.bfloat16)
    dk_ref[:, :LANES] = dk_in_ref[...]
    dv_ref[:, :LANES] = dv_in_ref[...]
    for e in range(G):

        @pl.when(glob_ref[e] // blocks == me_ref[0])
        def _():
            at = pl.multiple_of(glob_ref[e] % blocks * BLK, BLK)
            both = (kept_ref[e] + total(0, e)).astype(jnp.bfloat16)
            dk_ref[pl.ds(at, BLK), :LANES] = both[0]
            dv_ref[pl.ds(at, BLK), :LANES] = both[1]

    for d in range(back_ref.shape[0]):
        for j in range(gw_ref.shape[1] // LANES):
            rows = back_ref[d, start + 16 * j : start + 16 * (j + 1), :]
            gw_ref[16 * d : 16 * (d + 1), j * LANES : (j + 1) * LANES] = rows.astype(jnp.float32)


def collect_first(idx, used, glob, win, back, up, down, capacity):
    rows = win.shape[1]
    out = jax.ShapeDtypeStruct((rows, LANES), jnp.bfloat16)
    kept = jax.ShapeDtypeStruct((G, 2, BLK, LANES), jnp.float32)
    return pl.pallas_call(
        functools.partial(first_kernel, capacity),
        grid=(1,),
        in_specs=[smem()] * 3 + [whole(x.shape) for x in (win, back, up, down)],
        out_specs=(whole(out.shape), whole(out.shape), whole(kept.shape)),
        out_shape=(out, out, kept),
        scratch_shapes=[pltpu.VMEM((2, rows, LANES), jnp.float32)],
        compiler_params=params(),
        cost_estimate=pl.CostEstimate(flops=4 << 20, bytes_accessed=16 << 20, transcendentals=0),
    )(idx, used, glob, win, back, up, down)


def collect_middle(idx, used, win, back, up, down, capacity):
    return pl.pallas_call(
        functools.partial(middle_kernel, capacity),
        grid=(1,),
        in_specs=[smem()] * 2 + [whole(x.shape) for x in (win, back, up, down)],
        out_specs=whole(win.shape),
        out_shape=jax.ShapeDtypeStruct(win.shape, jnp.float32),
        compiler_params=params(),
        cost_estimate=pl.CostEstimate(flops=4 << 20, bytes_accessed=14 << 20, transcendentals=0),
    )(idx, used, win, back, up, down)


def collect_last(idx, used, glob, me, win, back, before, capacity):
    rows = win.shape[1]
    out = jax.ShapeDtypeStruct((rows, 2 * LANES), jnp.bfloat16)
    weight = jax.ShapeDtypeStruct((2 * LANES, 1024), jnp.float32)
    dk, dv, kept = before
    arrays = (win, back, kept, dk, dv)
    return pl.pallas_call(
        functools.partial(last_kernel, capacity),
        grid=(1,),
        in_specs=[smem()] * 4 + [whole(x.shape) for x in arrays],
        out_specs=(whole(out.shape), whole(out.shape), whole(weight.shape)),
        out_shape=(out, out, weight),
        scratch_shapes=[pltpu.VMEM((2, rows, LANES), jnp.float32)],
        compiler_params=params(),
        cost_estimate=pl.CostEstimate(flops=4 << 20, bytes_accessed=12 << 20, transcendentals=0),
    )(idx, used, glob, me, *arrays)


def weight_kernel(at_ref, c0, c1, *refs):
    pieces, out_ref, acc = refs[:5], refs[5], refs[6]

    @pl.when(pl.program_id(0) == 0)
    def _():
        acc[...] = jnp.zeros_like(acc)

    width = pieces[0].shape[1]
    values = ring_values(pieces)
    for r, c in enumerate((c0, c1)):
        for i, g in enumerate(values):
            acc[r * LANES : (r + 1) * LANES, i * width : (i + 1) * width] += dot(c[...], g, TN)

    @pl.when(pl.program_id(0) == pl.num_programs(0) - 1)
    def _():
        for i in range(4):
            to = pl.multiple_of(((at_ref[0] + i) % 4) * width, width)
            out_ref[:, pl.ds(to, width)] = acc[:, i * width : (i + 1) * width].astype(jnp.bfloat16)


def weight_terms(at, contexts, pieces):
    rows, width = pieces[0].shape
    shape = (2 * LANES, 4 * width)
    return pl.pallas_call(
        weight_kernel,
        grid=(rows // TILE,),
        in_specs=[smem()] + [pl.BlockSpec((TILE, LANES), lambda i: (i, 0))] * 2 + ring_specs(rows, width),
        out_specs=pl.BlockSpec(shape, lambda i: (0, 0)),
        out_shape=jax.ShapeDtypeStruct(shape, jnp.bfloat16),
        scratch_shapes=[pltpu.VMEM(shape, jnp.float32)],
        compiler_params=params(),
        cost_estimate=pl.CostEstimate(flops=2 * rows * 1024 * 256, bytes_accessed=16 << 20, transcendentals=0),
    )(at, *contexts, *pieces)


def carried_spec(devices, rows):
    return pl.BlockSpec((devices, 32, LANES), lambda i: (0, (rows - CARRIED) // 32 + i, 0))


def load_kernel(own_ref, other_ref, s0, s1, part_ref, out_ref):
    del part_ref
    devices = out_ref.shape[0]
    step = pl.program_id(0)

    @pl.when(step < pl.num_programs(0) - 1)
    def _():
        total = (own_ref[...].astype(jnp.float32) + other_ref[...].astype(jnp.float32)).astype(jnp.bfloat16)
        for d in range(devices):
            out_ref[d, 0:16, :] = total[16 * d : 16 * (d + 1), :LANES]
            out_ref[d, 16:32, :] = total[16 * d : 16 * (d + 1), LANES:]

    @pl.when(step == pl.num_programs(0) - 1)
    def _():
        for d in range(devices):
            out_ref[d, 0:16, :] = s0[16 * d : 16 * (d + 1), :]
            out_ref[d, 16:32, :] = s1[16 * d : 16 * (d + 1), :]


def load_terms(own, other, sums, part):
    devices, rows, _ = part.shape
    columns = pl.BlockSpec((own.shape[0], 2 * LANES), lambda i: (0, jnp.minimum(i, 3)))
    return pl.pallas_call(
        load_kernel,
        grid=(CARRIED // 32,),
        in_specs=[columns, columns] + [whole(x.shape) for x in sums] + [pl.BlockSpec(memory_space=pl.ANY)],
        out_specs=carried_spec(devices, rows),
        out_shape=jax.ShapeDtypeStruct(part.shape, part.dtype),
        input_output_aliases={4: 0},
        compiler_params=params(),
        cost_estimate=pl.CostEstimate(flops=1 << 18, bytes_accessed=4 << 20, transcendentals=0),
    )(own, other, *sums, part)


def sum_kernel(back_ref, part_ref, out_ref):
    del part_ref
    total = jnp.sum(back_ref[...].astype(jnp.float32), axis=0).astype(jnp.bfloat16)
    for d in range(out_ref.shape[0]):
        out_ref[d] = total


def load_sums(back, part):
    devices, rows, _ = part.shape
    return pl.pallas_call(
        sum_kernel,
        grid=(CARRIED // 32,),
        in_specs=[carried_spec(devices, rows), pl.BlockSpec(memory_space=pl.ANY)],
        out_specs=carried_spec(devices, rows),
        out_shape=jax.ShapeDtypeStruct(part.shape, part.dtype),
        input_output_aliases={1: 0},
        compiler_params=params(),
        cost_estimate=pl.CostEstimate(flops=1 << 18, bytes_accessed=4 << 20, transcendentals=0),
    )(back, part)


def project_kernel(*refs):
    weights, out_ref = refs[10:14], refs[14]
    halves = ring_values(refs[:5]), ring_values(refs[5:10])
    total = None
    for i in range(4):
        for h in range(2):
            term = dot(halves[h][i], weights[i][h * LANES : (h + 1) * LANES, :], NN)
            total = term if total is None else total + term
    out_ref[...] = total.astype(jnp.bfloat16)


def project(pieces_a, pieces_b, weights):
    rows = pieces_a[0].shape[0]
    width = weights[0].shape[1]
    return pl.pallas_call(
        project_kernel,
        grid=(rows // TILE,),
        in_specs=ring_specs(rows, LANES) * 2 + [pl.BlockSpec(w.shape, lambda i: (0, 0)) for w in weights],
        out_specs=pl.BlockSpec((TILE, width), lambda i: (i, 0)),
        out_shape=jax.ShapeDtypeStruct((rows, width), jnp.bfloat16),
        compiler_params=params(),
        cost_estimate=pl.CostEstimate(flops=2 * rows * 1024 * width, bytes_accessed=18 << 20, transcendentals=0),
    )(*pieces_a, *pieces_b, *weights)


def shifted(array, axis, by):
    size = lax.axis_size(axis)
    return lax.ppermute(array, axis, [((i + by) % size, i) for i in range(size)])


def ring_near(array, axis):
    return shifted(array, axis, 1), shifted(array, axis, -1)


def ring_far(near, axis):
    following, previous = near
    half = following.shape[0] // 2
    return shifted(following[:half], axis, 1), shifted(previous[half:], axis, -1)


def passed_along(array, axis, by):
    size = lax.axis_size(axis)
    pairs = [(i, i + by) for i in range(size) if 0 <= i + by < size]
    return lax.ppermute(array, axis, pairs)


def one_of_four(array, stride):
    span = 4 * stride
    total = array
    for by in (1, 3, 2):
        pairs = [(i, i // span * span + (i + by * stride) % span) for i in range(16)]
        total = total + lax.ppermute(array, "ctx", pairs)
    return total


def per_device(
    queries, key_vectors, value_vectors, grad_output, out_weight, random_ids, random_valid, global_ids
):
    ctx_count = lax.axis_size("ctx")
    tp_count = lax.axis_size("tp")
    me = lax.axis_index("ctx")
    tp_me = lax.axis_index("tp")
    q, k, v, g_out = queries[0], key_vectors[0], value_vectors[0], grad_output[0]
    rows, width = q.shape
    blocks = rows // BLK
    requests = blocks * R
    capacity = requests // (ctx_count * 3 // 4)
    slots = ctx_count * capacity
    barrier = lax.optimization_barrier
    at, tp_at = me.reshape(1), tp_me.reshape(1)
    glob_at = global_ids[0]

    def exchange(parts):
        return lax.all_to_all(parts, "ctx", split_axis=0, concat_axis=0, tiled=True)

    glob = one_of_four(pick_global(glob_at, at, k, v), 1)

    ids = random_ids[0].reshape(ctx_count, requests)
    owner = ids // blocks
    local = ids % blocks
    order = jnp.arange(requests, dtype=jnp.int32)
    earlier = order[None, :] < order[:, None]
    mine = owner == me
    rank = jnp.sum((mine[:, None, :] & earlier[None]).astype(jnp.int32), axis=2)
    hit = mine[:, None, :] & (rank[:, None, :] == jnp.arange(capacity, dtype=jnp.int32)[None, :, None])
    send_idx = jnp.sum(jnp.where(hit, local[:, None, :], 0), axis=2).reshape(slots)
    send_a = pick_blocks(send_idx, k, v, 0, slots)

    send_a, glob = barrier((send_a, glob))
    fetched_a = exchange(send_a.reshape(ctx_count, -1, LANES)).reshape(send_a.shape)
    near = ring_near(g_out, "tp")
    glob = one_of_four(glob, 4).reshape(G, 2, BLK, width)
    before = passed_along(jnp.stack([k[rows - BLK :], v[rows - BLK :]]), "ctx", 1)
    after = passed_along(jnp.stack([k[:BLK], v[:BLK]]), "ctx", -1)
    send_b = pick_blocks(send_idx, k, v, 1, slots)
    pieces = (g_out, *near, *ring_far(near, "tp"))
    grad_context = grad_context_of(tp_at, pieces, out_weight)
    used = jnp.sum(mine.astype(jnp.int32), axis=1)
    my_owner = lax.dynamic_index_in_dim(owner, me, 0, keepdims=False)
    my_rank = jnp.sum(((my_owner[:, None] == my_owner[None, :]) & earlier).astype(jnp.int32), axis=1)
    my_slot = my_owner * capacity + my_rank
    part_size = capacity // 2
    my_part = my_rank // part_size
    my_place = (my_part * ctx_count + my_owner) * part_size + my_rank % part_size
    valid = lax.dynamic_slice_in_dim(random_valid[0], me * blocks, blocks, 0).reshape(-1)

    ready = barrier((send_b, fetched_a, grad_context, glob, before, after, used, my_slot, my_place, valid))
    send_b, fetched_a, grad_context, glob, before, after, used, my_slot, my_place, valid = ready

    fetched_b = exchange(send_b.reshape(ctx_count, -1, LANES)).reshape(send_b.shape)
    wcols = [None] * tp_count
    for by in range(tp_count):
        part = lax.dynamic_slice_in_dim(out_weight, (tp_me + by) % tp_count * width, width, 1)
        wcols[-by % tp_count] = shifted(part, "tp", -by) if by else part
    last_block = blocks * ctx_count - 1

    def half(to, fetched, dq_in, column):
        return attend(
            last_block, at, my_slot, to, valid, q, k, v, grad_context, before, after, glob, fetched, dq_in, column
        )

    ctx_a, dq_a, win_a, up_a, down_a, gsum_a, ret_a = half(my_slot, fetched_a, None, 0)
    near_a = ring_near(ctx_a, "tp")
    ret_a, fetched_b, wcols, near_a = barrier((ret_a, fetched_b, wcols, near_a))

    back_a = exchange(ret_a.reshape(ctx_count, -1, LANES))
    pieces_a = (ctx_a, *near_a, *ring_far(near_a, "tp"))
    up_a, down_a = passed_along(up_a, "ctx", -1), passed_along(down_a, "ctx", 1)
    ctx_b, grad_q, win_b, up_b, down_b, gsum_b, ret_b, ret_c = half(my_place, fetched_b, dq_a, 1)
    near_b = ring_near(ctx_b, "tp")
    terms = weight_terms(tp_at, (ctx_a, ctx_b), pieces)
    ret_b = load_terms(terms, shifted(terms, "dp", 1), (gsum_a, gsum_b), ret_b)
    ret_b, back_a, up_a, down_a, near_b = barrier((ret_b, back_a, up_a, down_a, near_b))

    back_b = exchange(ret_b)
    up_b, down_b = passed_along(up_b, "ctx", -1), passed_along(down_b, "ctx", 1)
    pieces_b = (ctx_b, *near_b, *ring_far(near_b, "tp"))
    first = collect_first(
        send_idx, used, glob_at, win_a, back_a, up_a, down_a, capacity
    )
    ret_c = load_sums(back_b, ret_c)
    ret_c, up_b, down_b, pieces_b, first = barrier((ret_c, up_b, down_b, pieces_b, first))

    back_c = exchange(ret_c)
    projected = project(pieces_a, pieces_b, wcols)
    win_b = collect_middle(send_idx, used, win_b, back_b, up_b, down_b, capacity)
    projected, win_b, back_c = barrier((projected, win_b, back_c))
    grad_k, grad_v, grad_weight = collect_last(send_idx, used, glob_at, at, win_b, back_c, first, capacity)
    return projected[None], grad_q[None], grad_k[None], grad_v[None], grad_weight


def solution(mesh):
    tokens = P("dp", "ctx", "tp")
    in_specs = (
        tokens, tokens, tokens, tokens, P("tp", None), P("dp", None, None), P("dp", None, None), P("dp", None),
    )
    out_specs = (tokens, tokens, tokens, tokens, P("tp", None))
    return jax.shard_map(per_device, mesh=mesh, in_specs=in_specs, out_specs=out_specs, check_vma=False)
```

time: 340 us -> 309 us (0.909)
  blocking collectives: 64.3 us -> 0 us
  waiting for transfers between devices: 75.6 us -> 98 us
  Pallas kernels: 89.2 us -> 103 us
  local copies, waits for them, and re-layouts: 8.92 us -> 18 us
  starting transfers between devices: 88.3 us -> 82.8 us
    all_gather x1 -> x0, blocking collectives: 64.3 us -> none  [per_device(): share = lax.all_gather(share, 'ctx', axis=0, tiled=True)]
    ppermute x13 -> x16, waiting for transfers between devices: 1.63 us -> 38.4 us  [shifted(): lax.ppermute(array, axis, [((i + by) % size, i) for i in range(size)])]
    ppermute x6, waiting for transfers between devices: 43.4 us -> 14.5 us  [one_of_four(): total = total + lax.ppermute(array, 'ctx', pairs)]
    all_to_all x5, waiting for transfers between devices: 30.5 us -> 44.4 us  [exchange(): return lax.all_to_all(parts, 'ctx', split_axis=0, concat_axis=0, tiled=True)]
    pallas_call x4 -> x8, Pallas kernels: 22.4 us -> 35.3 us  [the longest x1 5.92 us: project(): pl.pallas_call(project_kernel, grid=(rows // TILE,), in_specs=ring_specs(...]
    all_to_all x5, starting transfers between devices: 44.8 us -> 35.2 us  [exchange(): return lax.all_to_all(parts, 'ctx', split_axis=0, concat_axis=0, tiled=True)]
    ppermute x13 -> x16, starting transfers between devices: 15.6 us -> 21.1 us  [shifted(): lax.ppermute(array, axis, [((i + by) % size, i) for i in range(size)])]
    unnamed x45 -> x63, local copies, waits for them, and re-layouts: 4.16 us -> 9.21 us
  transfers between devices with their start and end apart: 30 -> 33, of which waited for: 5 -> 14; matrix products, arithmetic and copies ran while one was open for 3% -> 5% of each run, Pallas kernels for 25% -> 31%
where the time goes in v3:
time: 309 us; the launch traced here: 308 us
  Pallas kernels  103 us (33%)
  waiting for transfers between devices  98 us (32%)
  starting transfers between devices  82.8 us (27%)
  local copies, waits for them, and re-layouts  18 us (6%)
  other arithmetic  5.24 us (2%)
    pallas_call x2, Pallas kernels, attend(): pl.pallas_call(functools.partial(attend_kernel, blocks, last_block), grid...  54.5 us
    all_to_all x5, waiting for transfers between devices, exchange(): return lax.all_to_all(parts, 'ctx', split_axis=0, concat_axis=0, tiled=True)  44.4 us
    ppermute x16, waiting for transfers between devices, shifted(): lax.ppermute(array, axis, [((i + by) % size, i) for i in range(size)])  38.4 us
    all_to_all x5, starting transfers between devices, exchange(): return lax.all_to_all(parts, 'ctx', split_axis=0, concat_axis=0, tiled=True)  35.2 us
    ppermute x16, starting transfers between devices, shifted(): lax.ppermute(array, axis, [((i + by) % size, i) for i in range(size)])  21.1 us
    ppermute x6, starting transfers between devices, passed_along(): return lax.ppermute(array, axis, pairs)  15.5 us
    ppermute x6, waiting for transfers between devices, one_of_four(): total = total + lax.ppermute(array, 'ctx', pairs)  14.5 us
    ppermute x6, starting transfers between devices, one_of_four(): total = total + lax.ppermute(array, 'ctx', pairs)  11 us
  transfers between devices with their start and end apart: 33, of which 14 were waited for; matrix products, arithmetic and copies ran while one was open for 5% of the time, Pallas kernels for 31%

profile of v3, /device:TPU:0, one launch (start us, length us, event | category | flops | bytes accessed | tf_op | source)
XLA Modules:
  0.0 307.9 jit_solution(5565144230969511163)
XLA Ops:
  0.7 2.2 shard_map.121
  2.8 2.0 collective-permute-start
  4.8 2.1 collective-permute-start.1
  7.0 1.9 collective-permute-start.2
  11.2 3.9 %shard_map.120 = bf16[16384,128]{1,0:T(8,128)(2,1)} custom-call(s32[128]{0:T(128)} %reshape.117.idx_ref, bf16[2048,256]{1,0:T(8,128)(2,1)} %bitcast.24, bf16[2048,256]{1,0:T(8,128)(2,1)} %bitcast.29), custom_call_target="tpu_custom_call" | custom-call | bytes 10485760 | tf_op jit(solution)/shard_map/pallas_call | solution.py:55
  15.2 5.7 %all-to-all-start = ((bf16[16,1024,128]{2,1,0:T(8,128)(2,1)}), bf16[16,1024,128]{2,1,0:T(8,128)(2,1)}, u32[]{:S(2)}, u32[]{:S(2)}) async-start(bf16[16,1024,128]{2,1,0:T(8,128)(2,1)} %bitcast.22), calls=%async_computation | async-start | bytes 8388608 | tf_op jit(solution)/shard_map/all_to_all | solution.py:582
  21.0 2.8 collective-permute-start.3
  24.6 1.4 fusion.6
  26.0 19.7 %collective-permute-done.3.refs_1_ = bf16[2048,256]{1,0:T(8,128)(2,1)S(1)} collective-permute-done((bf16[2048,256]{1,0:T(8,128)(2,1)}, bf16[2048,256]{1,0:T(8,128)(2,1)S(1)}, u32[]{:S(2)}, u32[]{:S(2)}) %collective-permute-start.3) | collective-permute-done | bytes 1048608 | tf_op jit(solution)/shard_map/ppermute | solution.py:536
  46.6 3.6 %collective-permute-start.5 = (bf16[1024,256]{1,0:T(8,128)(2,1)}, bf16[1024,256]{1,0:T(8,128)(2,1)S(1)}, u32[]{:S(2)}, u32[]{:S(2)}) collective-permute-start(bf16[1024,256]{1,0:T(8,128)(2,1)} %slice.44), channel_id=1, source_target_pairs={{1,0},{2,1},{3,2},{0,3},{5,4},{6,5},{7,6},{4,7},{9,8},{10,9},{11,1... | collective-permute-start | bytes 1572872 | tf_op jit(solution)/shard_map/ppermute | solution.py:536
  51.7 1.5 collective-permute-start.7
  53.2 1.7 collective-permute-start.8
  54.9 1.8 collective-permute-start.9
  56.8 4.0 %shard_map.119 = bf16[16384,128]{1,0:T(8,128)(2,1)} custom-call(s32[128]{0:T(128)} %reshape.117.idx_ref, bf16[2048,256]{1,0:T(8,128)(2,1)} %bitcast.25, bf16[2048,256]{1,0:T(8,128)(2,1)} %bitcast.30), custom_call_target="tpu_custom_call" | custom-call | bytes 10485760 | tf_op jit(solution)/shard_map/pallas_call | solution.py:55
  63.0 14.2 %collective-permute-done.7 = bf16[256,256]{1,0:T(8,128)(2,1)S(1)} collective-permute-done((bf16[256,256]{1,0:T(8,128)(2,1)S(1)}, bf16[256,256]{1,0:T(8,128)(2,1)S(1)}, u32[]{:S(2)}, u32[]{:S(2)}) %collective-permute-start.7) | collective-permute-done | bytes 131104 | tf_op jit(solution)/shard_map/ppermute | solution.py:560
  77.2 1.9 collective-permute-start.10
  80.7 1.6 add_add_fusion
  83.3 5.2 %shard_map.122.g_ref = bf16[2048,256]{1,0:T(8,128)(2,1)} custom-call(s32[1]{0:T(128)} %bitcast.6.at_ref, bf16[2048,256]{1,0:T(8,128)(2,1)} %bitcast.7.refs_0_, bf16[2048,256]{1,0:T(8,128)(2,1)} %copy-done.5, bf16[2048,256]{1,0:T(8,128)(2,1)} %copy-done.6, bf16[1024,256]{1,0:T(8,128)(2,1)} %copy-done.7, bf16[1024,256]{1,0:T(8,128)(2,1)} %copy-done.8, ...), custom_call_target="tpu_custom_call" | custom-call | flops 1073741824 | bytes 16777216 | tf_op jit(solution)/shard_map/pallas_call | solution.py:123
  89.2 9.6 %all-to-all-start.1 = ((bf16[16,1024,128]{2,1,0:T(8,128)(2,1)}), bf16[16,1024,128]{2,1,0:T(8,128)(2,1)}, u32[]{:S(2)}, u32[]{:S(2)}) async-start(bf16[16,1024,128]{2,1,0:T(8,128)(2,1)} %bitcast.21), calls=%async_computation.1 | async-start | bytes 8388608 | tf_op jit(solution)/shard_map/all_to_all | solution.py:582
  99.3 27.0 %shard_map.123 = (bf16[2048,128]{1,0:T(8,128)(2,1)}, bf16[2048,256]{1,0:T(8,128)(2,1)}, f32[2,2048,128]{2,1,0:T(8,128)}, bf16[2,64,128]{2,1,0:T(8,128)(2,1)}, bf...) custom-call(s32[1]{0:T(128)} %bitcast.me_ref, ...), custom_call_target="tpu_custom_call" | custom-call | flops 6442450944 | bytes 83886080 | tf_op jit(solution)/shard_map/pallas_call | solution.py:256
  126.3 2.8 collective-permute-start.15
  129.8 3.2 %collective-permute-start.12 = (bf16[256,256]{1,0:T(8,128)(2,1)S(1)}, bf16[256,256]{1,0:T(8,128)(2,1)S(1)}, u32[]{:S(2)}, u32[]{:S(2)}) collective-permute-start(bf16[256,256]{1,0:T(8,128)(2,1)S(1)} %get-tuple-element.134), channel_id=1, source_target_pairs={{1,0},{2,1},{3,2},{0,3},{5,4},{6,5},{7,6},{4,7},{9,8},{10,9},{11,1... | collective-permute-start | bytes 393224 | tf_op jit(solution)/shard_map/ppermute | solution.py:536
  133.9 8.6 %collective-permute-done.12.refs_11_ = bf16[256,256]{1,0:T(8,128)(2,1)S(1)} collective-permute-done((bf16[256,256]{1,0:T(8,128)(2,1)S(1)}, bf16[256,256]{1,0:T(8,128)(2,1)S(1)}, u32[]{:S(2)}, u32[]{:S(2)}) %collective-permute-start.12) | collective-permute-done | bytes 131104 | tf_op jit(solution)/shard_map/ppermute | solution.py:536
  143.7 2.2 collective-permute-done.14.refs_13_
  146.6 2.6 all-to-all-done.1
  149.2 6.1 %all-to-all-start.2 = ((bf16[16,1024,128]{2,1,0:T(8,128)(2,1)}), bf16[16,1024,128]{2,1,0:T(8,128)(2,1)}, u32[]{:S(2)}, u32[]{:S(2)}) async-start(bf16[16,1024,128]{2,1,0:T(8,128)(2,1)} %bitcast.33), calls=%async_computation.2 | async-start | bytes 8388608 | tf_op jit(solution)/shard_map/all_to_all | solution.py:582
  155.2 27.5 %shard_map.124 = (bf16[2048,128]{1,0:T(8,128)(2,1)}, bf16[2048,256]{1,0:T(8,128)(2,1)}, f32[2,2048,128]{2,1,0:T(8,128)}, bf16[2,64,128]{2,1,0:T(8,128)(2,1)}, bf...) custom-call(s32[1]{0:T(128)} %bitcast.me_ref, ...), custom_call_target="tpu_custom_call", output_to_operand_aliasing={{1}: (12, {})} | custom-call | flops 6442450944 | bytes 83886080 | tf_op jit(solution)/shard_map/pallas_call | solution.py:256
  182.8 5.3 %shard_map.125.own_ref = bf16[256,1024]{1,0:T(8,128)(2,1)} custom-call(s32[1]{0:T(128)} %bitcast.6.at_ref, bf16[2048,128]{1,0:T(8,128)(2,1)} %get-tuple-element.75.c0.refs_0_, bf16[2048,128]{1,0:T(8,128)(2,1)} %get-tuple-element.104.c1.refs_5_, bf16[2048,256]{1,0:T(8,128)(2,1)} %bitcast.7.refs_0_, bf16[2048,256]{1,0:T(8,128)(2,1)} %copy-done.5, ...), custom_call_target="tpu_custom_call" | custom-call | flops 1073741824 | bytes 16777216 | tf_op jit(solution)/shard_map/pallas_call | solution.py:438
  188.0 2.8 collective-permute-start.22
  192.2 4.5 %collective-permute-start.21 = (bf16[2,64,128]{2,1,0:T(8,128)(2,1)S(1)}, bf16[2,64,128]{2,1,0:T(8,128)(2,1)S(1)}, u32[]{:S(2)}, u32[]{:S(2)}) collective-permute-start(bf16[2,64,128]{2,1,0:T(8,128)(2,1)S(1)} %copy-done.29), channel_id=1, source_target_pairs={{0,4},{4,8},{8,12},{12,16},{16,20},{20,24},{24,28},{28,32},{32,36}... | collective-permute-start | bytes 98312 | tf_op jit(solution)/shard_map/ppermute | solution.py:552
  197.5 3.5 %shard_map.126 = bf16[16,672,128]{2,1,0:T(8,128)(2,1)} custom-call(bf16[256,1024]{1,0:T(8,128)(2,1)} %shard_map.125.own_ref, bf16[256,1024]{1,0:T(8,128)(2,1)} %copy-done.15, bf16[256,128]{1,0:T(8,128)(2,1)} %get-tuple-element.84.s0, bf16[256,128]{1,0:T(8,128)(2,1)} %get-tuple-element.85.s1, ...), custom_call_target="tpu_custom_call", output_to_operand_aliasing={{}: (4, {})} | custom-call | flops 262144 | bytes 4194304 | tf_op jit(solution)/shard_map/pallas_call | solution.py:476
  203.4 2.7 collective-permute-done.23.refs_7_
  206.2 1.4 all-to-all-done.2.back_ref
  207.5 7.1 %all-to-all-start.3 = ((bf16[16,672,128]{2,1,0:T(8,128)(2,1)}), bf16[16,672,128]{2,1,0:T(8,128)(2,1)S(1)}, u32[]{:S(2)}, u32[]{:S(2)}) async-start(bf16[16,672,128]{2,1,0:T(8,128)(2,1)} %shard_map.126), calls=%async_computation.3 | async-start | bytes 5505024 | tf_op jit(solution)/shard_map/all_to_all | solution.py:582
  215.4 2.7 collective-permute-start.26
  220.5 5.2 %collective-permute-start.25 = (bf16[2,64,128]{2,1,0:T(8,128)(2,1)}, bf16[2,64,128]{2,1,0:T(8,128)(2,1)}, u32[]{:S(2)}, u32[]{:S(2)}) collective-permute-start(bf16[2,64,128]{2,1,0:T(8,128)(2,1)} %get-tuple-element.93), channel_id=1, source_target_pairs={{0,4},{4,8},{8,12},{12,16},{16,20},{20,24},{24,28},{28,32},{32,36}... | collective-permute-start | bytes 98312 | tf_op jit(solution)/shard_map/ppermute | solution.py:552
  225.6 5.0 %shard_map.128 = (bf16[2048,128]{1,0:T(8,128)(2,1)}, bf16[2048,128]{1,0:T(8,128)(2,1)}, f32[2,2,64,128]{3,2,1,0:T(8,128)}) custom-call(s32[128]{0:T(128)} %reshape.117.idx_ref, s32[16]{0:T(128)} %reduce_sum.47.used_ref, s32[2]{0:T(128)} %bitcast.38, f32[2,2048,128]{2,1,0:T(8,128)} %get-tuple-element.97.win_ref, ...), custom_call_target="tpu_custom_call" | custom-call | flops 4194304 | bytes 16777216 | tf_op jit(solution)/shard_map/pallas_call | solution.py:373
  230.6 22.2 %all-to-all-done.3.back_ref = bf16[16,672,128]{2,1,0:T(8,128)(2,1)S(1)} async-done(((bf16[16,672,128]{2,1,0:T(8,128)(2,1)}), bf16[16,672,128]{2,1,0:T(8,128)(2,1)S(1)}, u32[]{:S(2)}, u32[]{:S(2)}) %all-to-all-start.3) | async-done | bytes 2752544 | tf_op jit(solution)/shard_map/all_to_all | solution.py:582
  252.8 1.5 copy-done.2
  254.3 3.7 %shard_map.127 = bf16[16,672,128]{2,1,0:T(8,128)(2,1)} custom-call(bf16[16,672,128]{2,1,0:T(8,128)(2,1)} %copy-done.2, bf16[16,672,128]{2,1,0:T(8,128)(2,1)} %get-tuple-element.91.part_ref), custom_call_target="tpu_custom_call", output_to_operand_aliasing={{}: (1, {})} | custom-call | flops 262144 | bytes 4194304 | tf_op jit(solution)/shard_map/pallas_call | solution.py:497
  258.8 6.7 %all-to-all-start.4 = ((bf16[16,672,128]{2,1,0:T(8,128)(2,1)}), bf16[16,672,128]{2,1,0:T(8,128)(2,1)S(1)}, u32[]{:S(2)}, u32[]{:S(2)}) async-start(bf16[16,672,128]{2,1,0:T(8,128)(2,1)} %shard_map.127), calls=%async_computation.4 | async-start | bytes 5505024 | tf_op jit(solution)/shard_map/all_to_all | solution.py:582
  265.5 2.0 collective-permute-start.17
  268.7 4.4 %shard_map.130.win_ref = f32[2,2048,128]{2,1,0:T(8,128)} custom-call(s32[128]{0:T(128)} %reshape.117.idx_ref, s32[16]{0:T(128)} %reduce_sum.47.used_ref, f32[2,2048,128]{2,1,0:T(8,128)} %get-tuple-element.113.win_ref, bf16[16,672,128]{2,1,0:T(8,128)(2,1)} %copy-done.2, bf16[2,64,128]{2,1,0:T(8,128)(2,1)} %collective-permute-done.24.up_ref, ...), custom_call_target="tpu_custom_call" | custom-call | flops 4194304 | bytes 14680064 | tf_op jit(solution)/shard_map/pallas_call | solution.py:386
  273.1 3.1 %collective-permute-done.18.refs_4_ = bf16[1024,128]{1,0:T(8,128)(2,1)S(1)} collective-permute-done((bf16[1024,128]{1,0:T(8,128)(2,1)S(1)}, bf16[1024,128]{1,0:T(8,128)(2,1)S(1)}, u32[]{:S(2)}, u32[]{:S(2)}) %collective-permute-start.18) | collective-permute-done | bytes 262176 | tf_op jit(solution)/shard_map/ppermute | solution.py:536
  276.9 5.9 %shard_map.129 = bf16[2048,256]{1,0:T(8,128)(2,1)} custom-call(bf16[2048,128]{1,0:T(8,128)(2,1)} %get-tuple-element.75.c0.refs_0_, bf16[2048,128]{1,0:T(8,128)(2,1)} %copy-done.10, bf16[2048,128]{1,0:T(8,128)(2,1)} %copy-done.12, bf16[1024,128]{1,0:T(8,128)(2,1)} %copy-done.19, bf16[1024,128]{1,0:T(8,128)(2,1)} %copy-done.20, ...), custom_call_target="tpu_custom_call" | custom-call | flops 1073741824 | bytes 18874368 | tf_op jit(solution)/shard_map/pallas_call | solution.py:523
  282.8 18.2 %all-to-all-done.4.back_ref = bf16[16,672,128]{2,1,0:T(8,128)(2,1)S(1)} async-done(((bf16[16,672,128]{2,1,0:T(8,128)(2,1)}), bf16[16,672,128]{2,1,0:T(8,128)(2,1)S(1)}, u32[]{:S(2)}, u32[]{:S(2)}) %all-to-all-start.4) | async-done | bytes 2752544 | tf_op jit(solution)/shard_map/all_to_all | solution.py:582
  301.0 1.5 copy-done.4
  302.5 5.4 %shard_map.131 = (bf16[2048,256]{1,0:T(8,128)(2,1)}, bf16[2048,256]{1,0:T(8,128)(2,1)}, f32[256,1024]{1,0:T(8,128)}) custom-call(s32[128]{0:T(128)} %reshape.117.idx_ref, s32[16]{0:T(128)} %reduce_sum.47.used_ref, s32[2]{0:T(128)} %bitcast.39, s32[1]{0:T(128)} %bitcast.me_ref, f32[2,2048,128]{2,1,0:T(8,128)} %shard_map.130.win_ref, ...), custom_call_target="tpu_custom_call" | custom-call | flops 4194304 | bytes 12582912 | tf_op jit(solution)/shard_map/pallas_call | solution.py:403
  (123 shorter events, 25.4 us)
Async XLA Ops:
  0.6 56.1 %copy-start = (s32[1,512,3]{1,0,2:T(1,128)S(1)}, s32[1,512,3]{1,0,2:T(1,128)}, u32[]{:S(2)}) copy-start(s32[1,512,3]{1,0,2:T(1,128)} %param.14) | copy-start | bytes 18436
  2.8 12.3 %collective-permute-start = (bf16[256,256]{1,0:T(8,128)(2,1)}, bf16[256,256]{1,0:T(8,128)(2,1)S(1)}, u32[]{:S(2)}, u32[]{:S(2)}) collective-permute-start(bf16[256,256]{1,0:T(8,128)(2,1)} %shard_map.121), channel_id=1, source_target_pairs={{0,4},{4,8},{8,12},{12,0},{16,20},{20,24},{24,28},{28,16},{32,36},... | collective-permute-start | bytes 393224 | tf_op jit(solution)/shard_map/ppermute | solution.py:560
  4.8 10.3 %collective-permute-start.1 = (bf16[256,256]{1,0:T(8,128)(2,1)}, bf16[256,256]{1,0:T(8,128)(2,1)S(1)}, u32[]{:S(2)}, u32[]{:S(2)}) collective-permute-start(bf16[256,256]{1,0:T(8,128)(2,1)} %shard_map.121), channel_id=1, source_target_pairs={{0,12},{4,0},{8,4},{12,8},{16,28},{20,16},{24,20},{28,24},{32,44},... | collective-permute-start | bytes 393224 | tf_op jit(solution)/shard_map/ppermute | solution.py:560
  7.0 8.2 %collective-permute-start.2 = (bf16[256,256]{1,0:T(8,128)(2,1)}, bf16[256,256]{1,0:T(8,128)(2,1)S(1)}, u32[]{:S(2)}, u32[]{:S(2)}) collective-permute-start(bf16[256,256]{1,0:T(8,128)(2,1)} %shard_map.121), channel_id=1, source_target_pairs={{0,8},{4,12},{8,0},{12,4},{16,24},{20,28},{24,16},{28,20},{32,40},... | collective-permute-start | bytes 393224 | tf_op jit(solution)/shard_map/ppermute | solution.py:560
  11.2 4.0 %copy-start.16 = (bf16[256,256]{1,0:T(8,128)(2,1)S(1)}, bf16[256,256]{1,0:T(8,128)(2,1)}, u32[]{:S(2)}) copy-start(bf16[256,256]{1,0:T(8,128)(2,1)} %shard_map.121) | copy-start | bytes 393220
  15.2 8.8 %copy-start.26 = (s32[1,512,3]{1,0,2:T(1,128)S(1)}, s32[1,512,3]{1,0,2:T(1,128)}, u32[]{:S(2)}) copy-start(s32[1,512,3]{1,0,2:T(1,128)} %param.13) | copy-start | bytes 18436
  15.2 73.3 %all-to-all-start = ((bf16[16,1024,128]{2,1,0:T(8,128)(2,1)}), bf16[16,1024,128]{2,1,0:T(8,128)(2,1)}, u32[]{:S(2)}, u32[]{:S(2)}) async-start(bf16[16,1024,128]{2,1,0:T(8,128)(2,1)} %bitcast.22), calls=%async_computation | async-start | bytes 8388608 | tf_op jit(solution)/shard_map/all_to_all | solution.py:582
  21.0 24.7 %collective-permute-start.3 = (bf16[2048,256]{1,0:T(8,128)(2,1)}, bf16[2048,256]{1,0:T(8,128)(2,1)S(1)}, u32[]{:S(2)}, u32[]{:S(2)}) collective-permute-start(bf16[2048,256]{1,0:T(8,128)(2,1)} %bitcast.7.refs_0_), channel_id=1, source_target_pairs={{1,0},{2,1},{3,2},{0,3},{5,4},{6,5},{7,6},{4,7},{9,8},{10,9},{11,1... | collective-permute-start | bytes 3145736 | tf_op jit(solution)/shard_map/ppermute | solution.py:536
  23.8 26.4 %collective-permute-start.4 = (bf16[2048,256]{1,0:T(8,128)(2,1)}, bf16[2048,256]{1,0:T(8,128)(2,1)S(1)}, u32[]{:S(2)}, u32[]{:S(2)}) collective-permute-start(bf16[2048,256]{1,0:T(8,128)(2,1)} %bitcast.7.refs_0_), channel_id=1, source_target_pairs={{3,0},{0,1},{1,2},{2,3},{7,4},{4,5},{5,6},{6,7},{11,8},{8,9},{9,10... | collective-permute-start | bytes 3145736 | tf_op jit(solution)/shard_map/ppermute | solution.py:536
  45.7 15.1 %copy-start.5 = (bf16[2048,256]{1,0:T(8,128)(2,1)}, bf16[2048,256]{1,0:T(8,128)(2,1)S(1)}, u32[]{:S(2)}) copy-start(bf16[2048,256]{1,0:T(8,128)(2,1)S(1)} %collective-permute-done.3.refs_1_) | copy-start | bytes 3145732
  46.6 35.8 %collective-permute-start.5 = (bf16[1024,256]{1,0:T(8,128)(2,1)}, bf16[1024,256]{1,0:T(8,128)(2,1)S(1)}, u32[]{:S(2)}, u32[]{:S(2)}) collective-permute-start(bf16[1024,256]{1,0:T(8,128)(2,1)} %slice.44), channel_id=1, source_target_pairs={{1,0},{2,1},{3,2},{0,3},{5,4},{6,5},{7,6},{4,7},{9,8},{10,9},{11,1... | collective-permute-start | bytes 1572872 | tf_op jit(solution)/shard_map/ppermute | solution.py:536
  50.2 10.6 %copy-start.6 = (bf16[2048,256]{1,0:T(8,128)(2,1)}, bf16[2048,256]{1,0:T(8,128)(2,1)S(1)}, u32[]{:S(2)}) copy-start(bf16[2048,256]{1,0:T(8,128)(2,1)S(1)} %collective-permute-done.4.refs_2_) | copy-start | bytes 3145732
  51.0 31.3 %collective-permute-start.6 = (bf16[1024,256]{1,0:T(8,128)(2,1)}, bf16[1024,256]{1,0:T(8,128)(2,1)S(1)}, u32[]{:S(2)}, u32[]{:S(2)}) collective-permute-start(bf16[1024,256]{1,0:T(8,128)(2,1)} %slice.45), channel_id=1, source_target_pairs={{3,0},{0,1},{1,2},{2,3},{7,4},{4,5},{5,6},{6,7},{11,8},{8,9},{9,10... | collective-permute-start | bytes 1572872 | tf_op jit(solution)/shard_map/ppermute | solution.py:536
  51.7 25.5 %collective-permute-start.7 = (bf16[256,256]{1,0:T(8,128)(2,1)S(1)}, bf16[256,256]{1,0:T(8,128)(2,1)S(1)}, u32[]{:S(2)}, u32[]{:S(2)}) collective-permute-start(bf16[256,256]{1,0:T(8,128)(2,1)S(1)} %add_add_fusion.1), channel_id=1, source_target_pairs={{0,16},{4,20},{8,24},{12,28},{16,32},{20,36},{24,40},{28,44},{32,4... | collective-permute-start | bytes 393224 | tf_op jit(solution)/shard_map/ppermute | solution.py:560
  53.2 25.9 %collective-permute-start.8 = (bf16[256,256]{1,0:T(8,128)(2,1)S(1)}, bf16[256,256]{1,0:T(8,128)(2,1)S(1)}, u32[]{:S(2)}, u32[]{:S(2)}) collective-permute-start(bf16[256,256]{1,0:T(8,128)(2,1)S(1)} %add_add_fusion.1), channel_id=1, source_target_pairs={{0,48},{4,52},{8,56},{12,60},{16,0},{20,4},{24,8},{28,12},{32,16},... | collective-permute-start | bytes 393224 | tf_op jit(solution)/shard_map/ppermute | solution.py:560
  54.9 25.8 %collective-permute-start.9 = (bf16[256,256]{1,0:T(8,128)(2,1)S(1)}, bf16[256,256]{1,0:T(8,128)(2,1)}, u32[]{:S(2)}, u32[]{:S(2)}) collective-permute-start(bf16[256,256]{1,0:T(8,128)(2,1)S(1)} %add_add_fusion.1), channel_id=1, source_target_pairs={{0,32},{4,36},{8,40},{12,44},{16,48},{20,52},{24,56},{28,60},{32,0... | collective-permute-start | bytes 393224 | tf_op jit(solution)/shard_map/ppermute | solution.py:560
  77.2 11.3 %collective-permute-start.10 = (bf16[2,64,256]{2,1,0:T(8,128)(2,1)}, bf16[2,64,256]{2,1,0:T(8,128)(2,1)S(1)}, u32[]{:S(2)}, u32[]{:S(2)}) collective-permute-start(bf16[2,64,256]{2,1,0:T(8,128)(2,1)} %pad_maximum_fusion), channel_id=1, source_target_pairs={{0,4},{4,8},{8,12},{12,16},{16,20},{20,24},{24,28},{28,32},{32,36}... | collective-permute-start | bytes 196616 | tf_op jit(solution)/shard_map/ppermute | solution.py:552
  79.1 9.4 %collective-permute-start.11 = (bf16[2,64,256]{2,1,0:T(8,128)(2,1)S(1)}, bf16[2,64,256]{2,1,0:T(8,128)(2,1)S(1)}, u32[]{:S(2)}, u32[]{:S(2)}) collective-permute-start(bf16[2,64,256]{2,1,0:T(8,128)(2,1)S(1)} %pad_maximum_fusion.1), channel_id=1, source_target_pairs={{4,0},{8,4},{12,8},{16,12},{20,16},{24,20},{28,24},{32,28},{36,32}... | collective-permute-start | bytes 196616 | tf_op jit(solution)/shard_map/ppermute | solution.py:552
  89.2 60.0 %all-to-all-start.1 = ((bf16[16,1024,128]{2,1,0:T(8,128)(2,1)}), bf16[16,1024,128]{2,1,0:T(8,128)(2,1)}, u32[]{:S(2)}, u32[]{:S(2)}) async-start(bf16[16,1024,128]{2,1,0:T(8,128)(2,1)} %bitcast.21), calls=%async_computation.1 | async-start | bytes 8388608 | tf_op jit(solution)/shard_map/all_to_all | solution.py:582
  99.3 29.7 %copy-start.3 = (bf16[256,1024]{1,0:T(8,128)(2,1)S(1)}, bf16[256,1024]{1,0:T(8,128)(2,1)}, u32[]{:S(2)}) copy-start(bf16[256,1024]{1,0:T(8,128)(2,1)} %refs_8_.1) | copy-start | bytes 1572868
  126.3 19.6 %collective-permute-start.15 = (bf16[2048,128]{1,0:T(8,128)(2,1)}, bf16[2048,128]{1,0:T(8,128)(2,1)S(1)}, u32[]{:S(2)}, u32[]{:S(2)}) collective-permute-start(bf16[2048,128]{1,0:T(8,128)(2,1)} %get-tuple-element.75.c0.refs_0_), channel_id=1, source_target_pairs={{1,0},{2,1},{3,2},{0,3},{5,4},{6,5},{7,6},{4,7},{9,8},{10,9},{11,1... | collective-permute-start | bytes 1572872 | tf_op jit(solution)/shard_map/ppermute | solution.py:536
  129.1 17.5 %collective-permute-start.16 = (bf16[2048,128]{1,0:T(8,128)(2,1)}, bf16[2048,128]{1,0:T(8,128)(2,1)S(1)}, u32[]{:S(2)}, u32[]{:S(2)}) collective-permute-start(bf16[2048,128]{1,0:T(8,128)(2,1)} %get-tuple-element.75.c0.refs_0_), channel_id=1, source_target_pairs={{3,0},{0,1},{1,2},{2,3},{7,4},{4,5},{5,6},{6,7},{11,8},{8,9},{9,10... | collective-permute-start | bytes 1572872 | tf_op jit(solution)/shard_map/ppermute | solution.py:536
  129.8 12.7 %collective-permute-start.12 = (bf16[256,256]{1,0:T(8,128)(2,1)S(1)}, bf16[256,256]{1,0:T(8,128)(2,1)S(1)}, u32[]{:S(2)}, u32[]{:S(2)}) collective-permute-start(bf16[256,256]{1,0:T(8,128)(2,1)S(1)} %get-tuple-element.134), channel_id=1, source_target_pairs={{1,0},{2,1},{3,2},{0,3},{5,4},{6,5},{7,6},{4,7},{9,8},{10,9},{11,1... | collective-permute-start | bytes 393224 | tf_op jit(solution)/shard_map/ppermute | solution.py:536
  133.0 10.6 %collective-permute-start.13 = (bf16[256,256]{1,0:T(8,128)(2,1)S(1)}, bf16[256,256]{1,0:T(8,128)(2,1)S(1)}, u32[]{:S(2)}, u32[]{:S(2)}) collective-permute-start(bf16[256,256]{1,0:T(8,128)(2,1)S(1)} %get-tuple-element.136), channel_id=1, source_target_pairs={{2,0},{3,1},{0,2},{1,3},{6,4},{7,5},{4,6},{5,7},{10,8},{11,9},{8,1... | collective-permute-start | bytes 393224 | tf_op jit(solution)/shard_map/ppermute | solution.py:536
  133.0 12.9 %collective-permute-start.14 = (bf16[256,256]{1,0:T(8,128)(2,1)S(1)}, bf16[256,256]{1,0:T(8,128)(2,1)S(1)}, u32[]{:S(2)}, u32[]{:S(2)}) collective-permute-start(bf16[256,256]{1,0:T(8,128)(2,1)S(1)} %get-tuple-element.133), channel_id=1, source_target_pairs={{3,0},{0,1},{1,2},{2,3},{7,4},{4,5},{5,6},{6,7},{11,8},{8,9},{9,10... | collective-permute-start | bytes 393224 | tf_op jit(solution)/shard_map/ppermute | solution.py:536
  142.5 3.4 %copy-start.21 = (bf16[256,256]{1,0:T(8,128)(2,1)}, bf16[256,256]{1,0:T(8,128)(2,1)S(1)}, u32[]{:S(2)}) copy-start(bf16[256,256]{1,0:T(8,128)(2,1)S(1)} %collective-permute-done.12.refs_11_) | copy-start | bytes 393220
  146.6 2.6 copy-start.10
  149.2 58.4 %all-to-all-start.2 = ((bf16[16,1024,128]{2,1,0:T(8,128)(2,1)}), bf16[16,1024,128]{2,1,0:T(8,128)(2,1)}, u32[]{:S(2)}, u32[]{:S(2)}) async-start(bf16[16,1024,128]{2,1,0:T(8,128)(2,1)} %bitcast.33), calls=%async_computation.2 | async-start | bytes 8388608 | tf_op jit(solution)/shard_map/all_to_all | solution.py:582
  182.7 5.3 %copy-start.9 = (bf16[2048,128]{1,0:T(8,128)(2,1)S(1)}, bf16[2048,128]{1,0:T(8,128)(2,1)}, u32[]{:S(2)}) copy-start(bf16[2048,128]{1,0:T(8,128)(2,1)} %get-tuple-element.104.c1.refs_5_) | copy-start | bytes 1572868
  182.7 8.1 %copy-start.30 = (bf16[2,64,128]{2,1,0:T(8,128)(2,1)S(1)}, bf16[2,64,128]{2,1,0:T(8,128)(2,1)}, u32[]{:S(2)}) copy-start(bf16[2,64,128]{2,1,0:T(8,128)(2,1)} %get-tuple-element.88) | copy-start | bytes 98308
  182.7 9.4 %copy-start.29 = (bf16[2,64,128]{2,1,0:T(8,128)(2,1)S(1)}, bf16[2,64,128]{2,1,0:T(8,128)(2,1)}, u32[]{:S(2)}) copy-start(bf16[2,64,128]{2,1,0:T(8,128)(2,1)} %get-tuple-element.89) | copy-start | bytes 98308
  188.0 8.7 %collective-permute-start.19 = (bf16[256,1024]{1,0:T(8,128)(2,1)}, bf16[256,1024]{1,0:T(8,128)(2,1)S(1)}, u32[]{:S(2)}, u32[]{:S(2)}) collective-permute-start(bf16[256,1024]{1,0:T(8,128)(2,1)} %shard_map.125.own_ref), channel_id=1, source_target_pairs={{64,0},{0,64},{65,1},{1,65},{66,2},{2,66},{67,3},{3,67},{68,4},{4,... | collective-permute-start | bytes 1572872 | tf_op jit(solution)/shard_map/ppermute | solution.py:536
  188.0 14.6 %collective-permute-start.22 = (bf16[2048,128]{1,0:T(8,128)(2,1)S(1)}, bf16[2048,128]{1,0:T(8,128)(2,1)S(1)}, u32[]{:S(2)}, u32[]{:S(2)}) collective-permute-start(bf16[2048,128]{1,0:T(8,128)(2,1)S(1)} %copy-done.9), channel_id=1, source_target_pairs={{1,0},{2,1},{3,2},{0,3},{5,4},{6,5},{7,6},{4,7},{9,8},{10,9},{11,1... | collective-permute-start | bytes 1572872 | tf_op jit(solution)/shard_map/ppermute | solution.py:536
  190.9 15.3 %collective-permute-start.23 = (bf16[2048,128]{1,0:T(8,128)(2,1)S(1)}, bf16[2048,128]{1,0:T(8,128)(2,1)}, u32[]{:S(2)}, u32[]{:S(2)}) collective-permute-start(bf16[2048,128]{1,0:T(8,128)(2,1)S(1)} %copy-done.9), channel_id=1, source_target_pairs={{3,0},{0,1},{1,2},{2,3},{7,4},{4,5},{5,6},{6,7},{11,8},{8,9},{9,10... | collective-permute-start | bytes 1572872 | tf_op jit(solution)/shard_map/ppermute | solution.py:536
  190.9 10.8 %collective-permute-start.20 = (bf16[2,64,128]{2,1,0:T(8,128)(2,1)S(1)}, bf16[2,64,128]{2,1,0:T(8,128)(2,1)S(1)}, u32[]{:S(2)}, u32[]{:S(2)}) collective-permute-start(bf16[2,64,128]{2,1,0:T(8,128)(2,1)S(1)} %copy-done.30), channel_id=1, source_target_pairs={{4,0},{8,4},{12,8},{16,12},{20,16},{24,20},{28,24},{32,28},{36,32}... | collective-permute-start | bytes 98312 | tf_op jit(solution)/shard_map/ppermute | solution.py:552
  192.2 9.5 %collective-permute-start.21 = (bf16[2,64,128]{2,1,0:T(8,128)(2,1)S(1)}, bf16[2,64,128]{2,1,0:T(8,128)(2,1)S(1)}, u32[]{:S(2)}, u32[]{:S(2)}) collective-permute-start(bf16[2,64,128]{2,1,0:T(8,128)(2,1)S(1)} %copy-done.29), channel_id=1, source_target_pairs={{0,4},{4,8},{8,12},{12,16},{16,20},{20,24},{24,28},{28,32},{32,36}... | collective-permute-start | bytes 98312 | tf_op jit(solution)/shard_map/ppermute | solution.py:552
  206.2 8.5 %copy-start.14 = (bf16[2048,128]{1,0:T(8,128)(2,1)S(1)}, bf16[2048,128]{1,0:T(8,128)(2,1)}, u32[]{:S(2)}) copy-start(bf16[2048,128]{1,0:T(8,128)(2,1)} %copy-done.13) | copy-start | bytes 1572868
  207.5 45.2 %all-to-all-start.3 = ((bf16[16,672,128]{2,1,0:T(8,128)(2,1)}), bf16[16,672,128]{2,1,0:T(8,128)(2,1)S(1)}, u32[]{:S(2)}, u32[]{:S(2)}) async-start(bf16[16,672,128]{2,1,0:T(8,128)(2,1)} %shard_map.126), calls=%async_computation.3 | async-start | bytes 5505024 | tf_op jit(solution)/shard_map/all_to_all | solution.py:582
  215.4 42.6 %collective-permute-start.26 = (bf16[1024,128]{1,0:T(8,128)(2,1)}, bf16[1024,128]{1,0:T(8,128)(2,1)S(1)}, u32[]{:S(2)}, u32[]{:S(2)}) collective-permute-start(bf16[1024,128]{1,0:T(8,128)(2,1)} %slice.42), channel_id=1, source_target_pairs={{1,0},{2,1},{3,2},{0,3},{5,4},{6,5},{7,6},{4,7},{9,8},{10,9},{11,1... | collective-permute-start | bytes 786440 | tf_op jit(solution)/shard_map/ppermute | solution.py:536
  219.1 38.9 %collective-permute-start.27 = (bf16[1024,128]{1,0:T(8,128)(2,1)S(1)}, bf16[1024,128]{1,0:T(8,128)(2,1)S(1)}, u32[]{:S(2)}, u32[]{:S(2)}) collective-permute-start(bf16[1024,128]{1,0:T(8,128)(2,1)S(1)} %slice.43), channel_id=1, source_target_pairs={{3,0},{0,1},{1,2},{2,3},{7,4},{4,5},{5,6},{6,7},{11,8},{8,9},{9,10... | collective-permute-start | bytes 786440 | tf_op jit(solution)/shard_map/ppermute | solution.py:536
  219.2 38.8 %collective-permute-start.24 = (bf16[2,64,128]{2,1,0:T(8,128)(2,1)}, bf16[2,64,128]{2,1,0:T(8,128)(2,1)}, u32[]{:S(2)}, u32[]{:S(2)}) collective-permute-start(bf16[2,64,128]{2,1,0:T(8,128)(2,1)} %get-tuple-element.92), channel_id=1, source_target_pairs={{4,0},{8,4},{12,8},{16,12},{20,16},{24,20},{28,24},{32,28},{36,32}... | collective-permute-start | bytes 98312 | tf_op jit(solution)/shard_map/ppermute | solution.py:552
  220.5 37.5 %collective-permute-start.25 = (bf16[2,64,128]{2,1,0:T(8,128)(2,1)}, bf16[2,64,128]{2,1,0:T(8,128)(2,1)}, u32[]{:S(2)}, u32[]{:S(2)}) collective-permute-start(bf16[2,64,128]{2,1,0:T(8,128)(2,1)} %get-tuple-element.93), channel_id=1, source_target_pairs={{0,4},{4,8},{8,12},{12,16},{16,20},{20,24},{24,28},{28,32},{32,36}... | collective-permute-start | bytes 98312 | tf_op jit(solution)/shard_map/ppermute | solution.py:552
  258.7 6.7 %copy-start.11 = (bf16[2048,128]{1,0:T(8,128)(2,1)S(1)}, bf16[2048,128]{1,0:T(8,128)(2,1)}, u32[]{:S(2)}) copy-start(bf16[2048,128]{1,0:T(8,128)(2,1)} %copy-done.10) | copy-start | bytes 1572868
  258.8 42.2 %all-to-all-start.4 = ((bf16[16,672,128]{2,1,0:T(8,128)(2,1)}), bf16[16,672,128]{2,1,0:T(8,128)(2,1)S(1)}, u32[]{:S(2)}, u32[]{:S(2)}) async-start(bf16[16,672,128]{2,1,0:T(8,128)(2,1)} %shard_map.127), calls=%async_computation.4 | async-start | bytes 5505024 | tf_op jit(solution)/shard_map/all_to_all | solution.py:582
  265.5 7.5 %collective-permute-start.17 = (bf16[1024,128]{1,0:T(8,128)(2,1)S(1)}, bf16[1024,128]{1,0:T(8,128)(2,1)S(1)}, u32[]{:S(2)}, u32[]{:S(2)}) collective-permute-start(bf16[1024,128]{1,0:T(8,128)(2,1)S(1)} %slice.40), channel_id=1, source_target_pairs={{1,0},{2,1},{3,2},{0,3},{5,4},{6,5},{7,6},{4,7},{9,8},{10,9},{11,1... | collective-permute-start | bytes 786440 | tf_op jit(solution)/shard_map/ppermute | solution.py:536
  268.5 7.7 %collective-permute-start.18 = (bf16[1024,128]{1,0:T(8,128)(2,1)S(1)}, bf16[1024,128]{1,0:T(8,128)(2,1)S(1)}, u32[]{:S(2)}, u32[]{:S(2)}) collective-permute-start(bf16[1024,128]{1,0:T(8,128)(2,1)S(1)} %slice.41), channel_id=1, source_target_pairs={{3,0},{0,1},{1,2},{2,3},{7,4},{4,5},{5,6},{6,7},{11,8},{8,9},{9,10... | collective-permute-start | bytes 786440 | tf_op jit(solution)/shard_map/ppermute | solution.py:536
  273.1 3.1 %copy-start.19 = (bf16[1024,128]{1,0:T(8,128)(2,1)}, bf16[1024,128]{1,0:T(8,128)(2,1)S(1)}, u32[]{:S(2)}) copy-start(bf16[1024,128]{1,0:T(8,128)(2,1)S(1)} %collective-permute-done.17.refs_3_) | copy-start | bytes 786436
  276.9 31.1 %copy-start.1 = (s32[1,512,3]{1,0,2:T(1,128)S(1)}, s32[1,512,3]{1,0,2:T(1,128)}, u32[]{:S(2)}) copy-start(s32[1,512,3]{1,0,2:T(1,128)} %param.14) | copy-start | bytes 18436
  (16 other events, 17.3 us)

commit v4 on v3

--- a/solution.py
+++ b/solution.py
@@ -63,28 +63,60 @@
     )(idx, keys, values)
 
 
-def pick_global_kernel(blocks, glob_ref, me_ref, k_ref, v_ref, out_ref):
-    owned = glob_ref[pl.program_id(0)] // blocks == me_ref[0]
-    out_ref[:BLK, :] = jnp.where(owned, k_ref[...], jnp.zeros_like(k_ref))
-    out_ref[BLK:, :] = jnp.where(owned, v_ref[...], jnp.zeros_like(v_ref))
+def pick_global_kernel(blocks, glob_ref, me_ref, k0, v0, k1, v1, k_first, v_first, k_last, v_last, up_ref, down_ref, out_ref):
+    for e, pair in enumerate(((k0, v0), (k1, v1))):
+        owned = glob_ref[e] // blocks == me_ref[0]
+        for t, x in enumerate(pair):
+            at = (e * 2 + t) * BLK
+            picked = jnp.where(owned, x[...], jnp.zeros_like(x))
+            for ref in (up_ref, down_ref, out_ref):
+                ref[at : at + BLK, :] = picked
+    at = 2 * G * BLK
+    up_ref[at : at + BLK, :] = k_last[...]
+    up_ref[at + BLK : at + 2 * BLK, :] = v_last[...]
+    down_ref[at : at + BLK, :] = k_first[...]
+    down_ref[at + BLK : at + 2 * BLK, :] = v_first[...]
 
 
 def pick_global(glob, me, keys, values):
     rows, width = keys.shape
     blocks = rows // BLK
-    block = pl.BlockSpec((BLK, width), lambda e, glob, me: (glob[e] % blocks, 0))
+
+    def block(place):
+        return [pl.BlockSpec((BLK, width), lambda i, glob, me: (place(glob), 0))] * 2
+
+    specs = block(lambda glob: glob[0] % blocks) + block(lambda glob: glob[1] % blocks)
+    specs += block(lambda glob: 0) + block(lambda glob: blocks - 1)
+    sizes = (2 * G + 2) * BLK, (2 * G + 2) * BLK, 2 * G * BLK
     return pl.pallas_call(
         functools.partial(pick_global_kernel, blocks),
         grid_spec=pltpu.PrefetchScalarGridSpec(
             num_scalar_prefetch=2,
-            grid=(G,),
-            in_specs=[block, block],
-            out_specs=pl.BlockSpec((2 * BLK, width), lambda e, glob, me: (e, 0)),
+            grid=(1,),
+            in_specs=specs,
+            out_specs=tuple(pl.BlockSpec((n, width), lambda i, glob, me: (0, 0)) for n in sizes),
         ),
-        out_shape=jax.ShapeDtypeStruct((G * 2 * BLK, width), jnp.bfloat16),
+        out_shape=tuple(jax.ShapeDtypeStruct((n, width), jnp.bfloat16) for n in sizes),
         compiler_params=params(),
         cost_estimate=pl.CostEstimate(flops=0, bytes_accessed=1 << 19, transcendentals=0),
-    )(glob, me, keys, values)
+    )(glob, me, *[keys, values] * 4)
+
+
+def sum_four_kernel(a, b, c, d, out_ref):
+    out_ref[...] = a[...] + b[...] + c[...] + d[...]
+
+
+def sum_four(arrays):
+    shape = arrays[0].shape
+    return pl.pallas_call(
+        sum_four_kernel,
+        grid=(1,),
+        in_specs=[whole(shape)] * 4,
+        out_specs=whole(shape),
+        out_shape=jax.ShapeDtypeStruct(shape, jnp.bfloat16),
+        compiler_params=params(),
+        cost_estimate=pl.CostEstimate(flops=0, bytes_accessed=60 << 20, transcendentals=0),
+    )(*arrays)
 
 
 TILE = 512
@@ -104,13 +136,33 @@
     return own[...], following[...], jnp.where(top, upper[...], lower[...]), previous[...]
 
 
+def pair_specs(rows, width):
+    last = rows // TILE // 2
+    specs = [pl.BlockSpec((TILE, width), lambda i, at: (i, 0))]
+    for d in range(2):
+        full = pl.BlockSpec((TILE, width), functools.partial(lambda d, i, at: (jnp.where(at[1] == d, i, 0), 0), d))
+        upper = functools.partial(lambda d, i, at: (jnp.where(at[1] == d, jnp.minimum(i, last - 1), 0), 0), d)
+        lower = functools.partial(lambda d, i, at: (jnp.where(at[1] == d, jnp.maximum(i - last, 0), 0), 0), d)
+        specs += [full, full, pl.BlockSpec((TILE, width), upper), pl.BlockSpec((TILE, width), lower)]
+    return specs
+
+
+def pair_values(at_ref, refs):
+    top = pl.program_id(0) < pl.num_programs(0) // 2
+    zero = at_ref[1] == 0
+
+    def chosen(j):
+        return jnp.where(zero, refs[1 + j][...], refs[5 + j][...])
+
+    return refs[0][...], chosen(0), jnp.where(top, chosen(2), chosen(3)), chosen(1)
+
+
 def grad_context_kernel(at_ref, *refs):
-    del at_ref
     total = None
-    for g, w in zip(ring_values(refs[:5]), refs[5:9]):
+    for g, w in zip(pair_values(at_ref, refs[:9]), refs[9:13]):
         term = dot(g, w[...], NT)
         total = term if total is None else total + term
-    refs[9][...] = total.astype(jnp.bfloat16)
+    refs[13][...] = total.astype(jnp.bfloat16)
 
 
 def grad_context_of(at, pieces, weight):
@@ -125,7 +177,7 @@
         grid_spec=pltpu.PrefetchScalarGridSpec(
             num_scalar_prefetch=1,
             grid=(rows // TILE,),
-            in_specs=ring_specs(rows, width) + turned,
+            in_specs=pair_specs(rows, width) + turned,
             out_specs=pl.BlockSpec((TILE, heads), lambda i, at: (i, 0)),
         ),
         out_shape=jax.ShapeDtypeStruct((rows, heads), jnp.bfloat16),
@@ -145,10 +197,10 @@
     else:
         *parts_out, ret_ref = parts_out
     rows = blocks * BLK
-    kpad[0:BLK, :] = before_ref[0]
-    vpad[0:BLK, :] = before_ref[1]
-    kpad[rows + BLK : rows + 2 * BLK, :] = after_ref[0]
-    vpad[rows + BLK : rows + 2 * BLK, :] = after_ref[1]
+    kpad[0:BLK, :] = before_ref[0:BLK, :]
+    vpad[0:BLK, :] = before_ref[BLK : 2 * BLK, :]
+    kpad[rows + BLK : rows + 2 * BLK, :] = after_ref[0:BLK, :]
+    vpad[rows + BLK : rows + 2 * BLK, :] = after_ref[BLK : 2 * BLK, :]
     kpad[BLK : rows + BLK, :] = k_ref[...]
     vpad[BLK : rows + BLK, :] = v_ref[...]
     win_ref[...] = jnp.zeros_like(win_ref)
@@ -223,7 +275,7 @@
         for p, part_ref in enumerate(parts_out):
             for d in range(devices):
                 start = (p * devices + d) * count
-                part_ref[d, 0:count, :] = ret_ref[start : start + count, :]
+                part_ref[d, CARRIED : CARRIED + count, :] = ret_ref[start : start + count, :]
 
 
 def attend(last_block, me, slot, to, valid, q, k, v, g, before, after, glob, fetched, dq_in, column):
@@ -258,8 +310,8 @@
         grid=(1,),
         in_specs=[
             smem(), smem(), smem(), smem(), half, half, half, half,
-            whole((2, BLK, LANES), column),
-            whole((2, BLK, LANES), column),
+            pl.BlockSpec((2 * BLK, LANES), lambda i: (G, column)),
+            pl.BlockSpec((2 * BLK, LANES), lambda i: (G, column)),
             whole((G, 2, BLK, LANES), column),
             whole(fetched.shape),
             pl.BlockSpec(memory_space=pl.ANY),
@@ -276,14 +328,14 @@
 
 
 def land(entries, idx_ref, used_ref, back_ref, acc):
-    first, end, capacity = entries
+    first, end, capacity, skipped = entries
 
     def body(a, _):
         @pl.when(used_ref[a] > 0)
         def _():
             for c in range(first, end):
                 at = pl.multiple_of(idx_ref[a * capacity + c] * BLK, BLK)
-                src = (c - first) * 2 * BLK
+                src = skipped + (c - first) * 2 * BLK
                 acc[0, pl.ds(at, BLK), :] += back_ref[a, src : src + BLK, :].astype(jnp.float32)
                 acc[1, pl.ds(at, BLK), :] += back_ref[a, src + BLK : src + 2 * BLK, :].astype(jnp.float32)
 
@@ -303,7 +355,7 @@
 ):
     acc[...] = win_ref[...]
     edges(up_ref, down_ref, acc)
-    land((0, capacity, capacity), idx_ref, used_ref, back_ref, acc)
+    land((0, capacity, capacity, 0), idx_ref, used_ref, back_ref, acc)
     dk_ref[...] = acc[0].astype(jnp.bfloat16)
     dv_ref[...] = acc[1].astype(jnp.bfloat16)
     blocks = acc.shape[1] // BLK
@@ -315,18 +367,17 @@
 def middle_kernel(capacity, idx_ref, used_ref, win_ref, back_ref, up_ref, down_ref, acc):
     acc[...] = win_ref[...]
     edges(up_ref, down_ref, acc)
-    land((0, capacity // 2, capacity), idx_ref, used_ref, back_ref, acc)
+    land((0, capacity // 2, capacity, CARRIED), idx_ref, used_ref, back_ref, acc)
 
 
 def last_kernel(
     capacity, idx_ref, used_ref, glob_ref, me_ref, win_ref, back_ref, kept_ref, dk_in_ref, dv_in_ref,
-    dk_ref, dv_ref, gw_ref, acc,
+    dk_ref, dv_ref, acc,
 ):
     acc[...] = win_ref[...]
-    land((capacity // 2, capacity, capacity), idx_ref, used_ref, back_ref, acc)
+    land((capacity // 2, capacity, capacity, CARRIED), idx_ref, used_ref, back_ref, acc)
     blocks = acc.shape[1] // BLK
-    start = capacity * BLK
-    sums = start + gw_ref.shape[1] // LANES * 16
+    sums = CARRIED - 32
 
     def total(half, e):
         found = [
@@ -360,11 +411,6 @@
             dk_ref[pl.ds(at, BLK), :LANES] = both[0]
             dv_ref[pl.ds(at, BLK), :LANES] = both[1]
 
-    for d in range(back_ref.shape[0]):
-        for j in range(gw_ref.shape[1] // LANES):
-            rows = back_ref[d, start + 16 * j : start + 16 * (j + 1), :]
-            gw_ref[16 * d : 16 * (d + 1), j * LANES : (j + 1) * LANES] = rows.astype(jnp.float32)
-
 
 def collect_first(idx, used, glob, win, back, up, down, capacity):
     rows = win.shape[1]
@@ -397,15 +443,14 @@
 def collect_last(idx, used, glob, me, win, back, before, capacity):
     rows = win.shape[1]
     out = jax.ShapeDtypeStruct((rows, 2 * LANES), jnp.bfloat16)
-    weight = jax.ShapeDtypeStruct((2 * LANES, 1024), jnp.float32)
     dk, dv, kept = before
     arrays = (win, back, kept, dk, dv)
     return pl.pallas_call(
         functools.partial(last_kernel, capacity),
         grid=(1,),
         in_specs=[smem()] * 4 + [whole(x.shape) for x in arrays],
-        out_specs=(whole(out.shape), whole(out.shape), whole(weight.shape)),
-        out_shape=(out, out, weight),
+        out_specs=(whole(out.shape), whole(out.shape)),
+        out_shape=(out, out),
         scratch_shapes=[pltpu.VMEM((2, rows, LANES), jnp.float32)],
         compiler_params=params(),
         cost_estimate=pl.CostEstimate(flops=4 << 20, bytes_accessed=12 << 20, transcendentals=0),
@@ -413,14 +458,14 @@
 
 
 def weight_kernel(at_ref, c0, c1, *refs):
-    pieces, out_ref, acc = refs[:5], refs[5], refs[6]
+    pieces, out_ref, acc = refs[:9], refs[9], refs[10]
 
     @pl.when(pl.program_id(0) == 0)
     def _():
         acc[...] = jnp.zeros_like(acc)
 
     width = pieces[0].shape[1]
-    values = ring_values(pieces)
+    values = pair_values(at_ref, pieces)
     for r, c in enumerate((c0, c1)):
         for i, g in enumerate(values):
             acc[r * LANES : (r + 1) * LANES, i * width : (i + 1) * width] += dot(c[...], g, TN)
@@ -437,52 +482,44 @@
     shape = (2 * LANES, 4 * width)
     return pl.pallas_call(
         weight_kernel,
-        grid=(rows // TILE,),
-        in_specs=[smem()] + [pl.BlockSpec((TILE, LANES), lambda i: (i, 0))] * 2 + ring_specs(rows, width),
-        out_specs=pl.BlockSpec(shape, lambda i: (0, 0)),
+        grid_spec=pltpu.PrefetchScalarGridSpec(
+            num_scalar_prefetch=1,
+            grid=(rows // TILE,),
+            in_specs=[pl.BlockSpec((TILE, LANES), lambda i, at: (i, 0))] * 2 + pair_specs(rows, width),
+            out_specs=pl.BlockSpec(shape, lambda i, at: (0, 0)),
+            scratch_shapes=[pltpu.VMEM(shape, jnp.float32)],
+        ),
         out_shape=jax.ShapeDtypeStruct(shape, jnp.bfloat16),
-        scratch_shapes=[pltpu.VMEM(shape, jnp.float32)],
         compiler_params=params(),
         cost_estimate=pl.CostEstimate(flops=2 * rows * 1024 * 256, bytes_accessed=16 << 20, transcendentals=0),
     )(at, *contexts, *pieces)
 
 
-def carried_spec(devices, rows):
-    return pl.BlockSpec((devices, 32, LANES), lambda i: (0, (rows - CARRIED) // 32 + i, 0))
-
-
-def load_kernel(own_ref, other_ref, s0, s1, part_ref, out_ref):
+def carried(array):
+    return whole((array.shape[0], CARRIED, LANES))
+
+
+def load_kernel(terms_ref, s0, s1, part_ref, out_ref):
     del part_ref
-    devices = out_ref.shape[0]
-    step = pl.program_id(0)
-
-    @pl.when(step < pl.num_programs(0) - 1)
-    def _():
-        total = (own_ref[...].astype(jnp.float32) + other_ref[...].astype(jnp.float32)).astype(jnp.bfloat16)
-        for d in range(devices):
-            out_ref[d, 0:16, :] = total[16 * d : 16 * (d + 1), :LANES]
-            out_ref[d, 16:32, :] = total[16 * d : 16 * (d + 1), LANES:]
-
-    @pl.when(step == pl.num_programs(0) - 1)
-    def _():
-        for d in range(devices):
-            out_ref[d, 0:16, :] = s0[16 * d : 16 * (d + 1), :]
-            out_ref[d, 16:32, :] = s1[16 * d : 16 * (d + 1), :]
-
-
-def load_terms(own, other, sums, part):
-    devices, rows, _ = part.shape
-    columns = pl.BlockSpec((own.shape[0], 2 * LANES), lambda i: (0, jnp.minimum(i, 3)))
+    for d in range(out_ref.shape[0]):
+        rows = slice(16 * d, 16 * (d + 1))
+        for j in range(terms_ref.shape[1] // LANES):
+            out_ref[d, 16 * j : 16 * (j + 1), :] = terms_ref[rows, j * LANES : (j + 1) * LANES]
+        out_ref[d, CARRIED - 32 : CARRIED - 16, :] = s0[rows, :]
+        out_ref[d, CARRIED - 16 :, :] = s1[rows, :]
+
+
+def load_terms(terms, sums, part):
     return pl.pallas_call(
         load_kernel,
-        grid=(CARRIED // 32,),
-        in_specs=[columns, columns] + [whole(x.shape) for x in sums] + [pl.BlockSpec(memory_space=pl.ANY)],
-        out_specs=carried_spec(devices, rows),
+        grid=(1,),
+        in_specs=[whole(x.shape) for x in (terms, *sums)] + [pl.BlockSpec(memory_space=pl.ANY)],
+        out_specs=carried(part),
         out_shape=jax.ShapeDtypeStruct(part.shape, part.dtype),
-        input_output_aliases={4: 0},
+        input_output_aliases={3: 0},
         compiler_params=params(),
         cost_estimate=pl.CostEstimate(flops=1 << 18, bytes_accessed=4 << 20, transcendentals=0),
-    )(own, other, *sums, part)
+    )(terms, *sums, part)
 
 
 def sum_kernel(back_ref, part_ref, out_ref):
@@ -493,17 +530,36 @@
 
 
 def load_sums(back, part):
-    devices, rows, _ = part.shape
     return pl.pallas_call(
         sum_kernel,
-        grid=(CARRIED // 32,),
-        in_specs=[carried_spec(devices, rows), pl.BlockSpec(memory_space=pl.ANY)],
-        out_specs=carried_spec(devices, rows),
+        grid=(1,),
+        in_specs=[carried(back), pl.BlockSpec(memory_space=pl.ANY)],
+        out_specs=carried(part),
         out_shape=jax.ShapeDtypeStruct(part.shape, part.dtype),
         input_output_aliases={1: 0},
         compiler_params=params(),
         cost_estimate=pl.CostEstimate(flops=1 << 18, bytes_accessed=4 << 20, transcendentals=0),
     )(back, part)
+
+
+def weight_sum_kernel(own_ref, other_ref, out_ref):
+    total = own_ref[...].astype(jnp.float32) + other_ref[...].astype(jnp.float32)
+    for d in range(total.shape[0]):
+        for j in range(out_ref.shape[1] // LANES):
+            out_ref[16 * d : 16 * (d + 1), j * LANES : (j + 1) * LANES] = total[d, 16 * j : 16 * (j + 1), :]
+
+
+def weight_sum(own, other):
+    shape = (2 * LANES, 1024)
+    return pl.pallas_call(
+        weight_sum_kernel,
+        grid=(1,),
+        in_specs=[whole(own.shape), whole(other.shape)],
+        out_specs=whole(shape),
+        out_shape=jax.ShapeDtypeStruct(shape, jnp.float32),
+        compiler_params=params(),
+        cost_estimate=pl.CostEstimate(flops=1 << 18, bytes_accessed=2 << 20, transcendentals=0),
+    )(own, other)
 
 
 def project_kernel(*refs):
@@ -552,13 +608,15 @@
     return lax.ppermute(array, axis, pairs)
 
 
-def one_of_four(array, stride):
-    span = 4 * stride
-    total = array
-    for by in (1, 3, 2):
-        pairs = [(i, i // span * span + (i + by * stride) % span) for i in range(16)]
-        total = total + lax.ppermute(array, "ctx", pairs)
-    return total
+def core_ring(array, d):
+    size = lax.axis_size("tp")
+
+    def moved(x, by):
+        return lax.ppermute(x, ("dp", "tp"), [(d * size + (i + by) % size, d * size + i) for i in range(size)])
+
+    half = array.shape[0] // 2
+    following, previous = moved(array, 1), moved(array, -1)
+    return following, previous, moved(following[:half], 1), moved(previous[half:], -1)
 
 
 def per_device(
@@ -575,13 +633,16 @@
     capacity = requests // (ctx_count * 3 // 4)
     slots = ctx_count * capacity
     barrier = lax.optimization_barrier
-    at, tp_at = me.reshape(1), tp_me.reshape(1)
+    at = me.reshape(1)
+    tp_at = jnp.stack([tp_me, lax.axis_index("dp")])
     glob_at = global_ids[0]
 
     def exchange(parts):
         return lax.all_to_all(parts, "ctx", split_axis=0, concat_axis=0, tiled=True)
 
-    glob = one_of_four(pick_global(glob_at, at, k, v), 1)
+    up, down, picked = pick_global(glob_at, at, k, v)
+    before, after = shifted(up, "ctx", -1), shifted(down, "ctx", 1)
+    glob = sum_four((picked, before, after, shifted(picked, "ctx", 2)))
 
     ids = random_ids[0].reshape(ctx_count, requests)
     owner = ids // blocks
@@ -594,15 +655,12 @@
     send_idx = jnp.sum(jnp.where(hit, local[:, None, :], 0), axis=2).reshape(slots)
     send_a = pick_blocks(send_idx, k, v, 0, slots)
 
-    send_a, glob = barrier((send_a, glob))
+    later = core_ring(g_out, 1)
+    send_a, glob, before, after, later, g_now = barrier((send_a, glob, before, after, later, g_out))
     fetched_a = exchange(send_a.reshape(ctx_count, -1, LANES)).reshape(send_a.shape)
-    near = ring_near(g_out, "tp")
-    glob = one_of_four(glob, 4).reshape(G, 2, BLK, width)
-    before = passed_along(jnp.stack([k[rows - BLK :], v[rows - BLK :]]), "ctx", 1)
-    after = passed_along(jnp.stack([k[:BLK], v[:BLK]]), "ctx", -1)
+    pieces = (g_out, *core_ring(g_now, 0), *later)
+    glob = sum_four((glob, *[shifted(glob, "ctx", 4 * by) for by in (1, 3, 2)])).reshape(G, 2, BLK, width)
     send_b = pick_blocks(send_idx, k, v, 1, slots)
-    pieces = (g_out, *near, *ring_far(near, "tp"))
-    grad_context = grad_context_of(tp_at, pieces, out_weight)
     used = jnp.sum(mine.astype(jnp.int32), axis=1)
     my_owner = lax.dynamic_index_in_dim(owner, me, 0, keepdims=False)
     my_rank = jnp.sum(((my_owner[:, None] == my_owner[None, :]) & earlier).astype(jnp.int32), axis=1)
@@ -612,8 +670,9 @@
     my_place = (my_part * ctx_count + my_owner) * part_size + my_rank % part_size
     valid = lax.dynamic_slice_in_dim(random_valid[0], me * blocks, blocks, 0).reshape(-1)
 
-    ready = barrier((send_b, fetched_a, grad_context, glob, before, after, used, my_slot, my_place, valid))
-    send_b, fetched_a, grad_context, glob, before, after, used, my_slot, my_place, valid = ready
+    ready = barrier((send_b, fetched_a, pieces, glob, used, my_slot, my_place, valid))
+    send_b, fetched_a, pieces, glob, used, my_slot, my_place, valid = ready
+    grad_context = grad_context_of(tp_at, pieces, out_weight)
 
     fetched_b = exchange(send_b.reshape(ctx_count, -1, LANES)).reshape(send_b.shape)
     wcols = [None] * tp_count
@@ -637,7 +696,7 @@
     ctx_b, grad_q, win_b, up_b, down_b, gsum_b, ret_b, ret_c = half(my_place, fetched_b, dq_a, 1)
     near_b = ring_near(ctx_b, "tp")
     terms = weight_terms(tp_at, (ctx_a, ctx_b), pieces)
-    ret_b = load_terms(terms, shifted(terms, "dp", 1), (gsum_a, gsum_b), ret_b)
+    ret_b = load_terms(terms, (gsum_a, gsum_b), ret_b)
     ret_b, back_a, up_a, down_a, near_b = barrier((ret_b, back_a, up_a, down_a, near_b))
 
     back_b = exchange(ret_b)
@@ -653,7 +712,9 @@
     projected = project(pieces_a, pieces_b, wcols)
     win_b = collect_middle(send_idx, used, win_b, back_b, up_b, down_b, capacity)
     projected, win_b, back_c = barrier((projected, win_b, back_c))
-    grad_k, grad_v, grad_weight = collect_last(send_idx, used, glob_at, at, win_b, back_c, first, capacity)
+    weight_own = back_c[:, : CARRIED - 32]
+    grad_weight = weight_sum(weight_own, shifted(weight_own, "dp", 1))
+    grad_k, grad_v = collect_last(send_idx, used, glob_at, at, win_b, back_c, first, capacity)
     return projected[None], grad_q[None], grad_k[None], grad_v[None], grad_weight
 
 

time: 309 us -> 313 us (1.013)
  waiting for transfers between devices: 98 us -> 74.2 us
  starting transfers between devices: 82.8 us -> 104 us
  Pallas kernels: 103 us -> 108 us
    ppermute x16 -> x18, starting transfers between devices: 21.1 us -> 38.3 us  [shifted(): lax.ppermute(array, axis, [((i + by) % size, i) for i in range(size)])]
    ppermute x16 -> x18, waiting for transfers between devices: 38.4 us -> 24.2 us  [shifted(): lax.ppermute(array, axis, [((i + by) % size, i) for i in range(size)])]
    ppermute x6 -> x8, waiting for transfers between devices: 14.5 us -> 6.29 us  [moved(): lax.ppermute(x, ('dp', 'tp'), [(d * size + (i + by) % size, d * size + i)...]
    ppermute x6 -> x8, starting transfers between devices: 11 us -> 17 us  [moved(): lax.ppermute(x, ('dp', 'tp'), [(d * size + (i + by) % size, d * size + i)...]
    pallas_call x3 -> x6, Pallas kernels: 12.4 us -> 16.3 us  [the longest x1 6.43 us: weight_terms(): pl.pallas_call(weight_kernel, grid_spec=pltpu.PrefetchScalarGridSpec(num_...]
    ppermute x6 -> x4, starting transfers between devices: 15.5 us -> 12.9 us  [passed_along(): return lax.ppermute(array, axis, pairs)]
    unnamed x63 -> x65, local copies, waits for them, and re-layouts: 9.21 us -> 9.43 us
  transfers between devices with their start and end apart: 33 -> 35, of which waited for: 14 -> 8; matrix products, arithmetic and copies ran while one was open for 5% -> 4% of each run, Pallas kernels for 31% -> 34%
where the time goes in v4:
time: 313 us; the launch traced here: 310 us
  Pallas kernels  108 us (35%)
  starting transfers between devices  104 us (33%)
  waiting for transfers between devices  74.2 us (24%)
  local copies, waits for them, and re-layouts  20.4 us (7%)
    pallas_call x2, Pallas kernels, attend(): pl.pallas_call(functools.partial(attend_kernel, blocks, last_block), grid...  54.5 us
    all_to_all x5, waiting for transfers between devices, exchange(): return lax.all_to_all(parts, 'ctx', split_axis=0, concat_axis=0, tiled=True)  43.7 us
    ppermute x18, starting transfers between devices, shifted(): lax.ppermute(array, axis, [((i + by) % size, i) for i in range(size)])  38.3 us
    all_to_all x5, starting transfers between devices, exchange(): return lax.all_to_all(parts, 'ctx', split_axis=0, concat_axis=0, tiled=True)  35.8 us
    ppermute x18, waiting for transfers between devices, shifted(): lax.ppermute(array, axis, [((i + by) % size, i) for i in range(size)])  24.2 us
    ppermute x8, starting transfers between devices, moved(): lax.ppermute(x, ('dp', 'tp'), [(d * size + (i + by) % size, d * size + i)...  17 us
    ppermute x4, starting transfers between devices, passed_along(): return lax.ppermute(array, axis, pairs)  12.9 us
    unnamed x65, local copies, waits for them, and re-layouts  9.43 us
  transfers between devices with their start and end apart: 35, of which 8 were waited for; matrix products, arithmetic and copies ran while one was open for 4% of the time, Pallas kernels for 34%

profile of v4, /device:TPU:0, one launch (start us, length us, event | category | flops | bytes accessed | tf_op | source)
XLA Modules:
  0.0 310.4 jit_solution(1136253851979635394)
XLA Ops:
  2.1 2.4 shard_map.121
  4.5 2.0 collective-permute-start
  6.5 4.6 %collective-permute-start.1 = (bf16[384,256]{1,0:T(8,128)(2,1)}, bf16[384,256]{1,0:T(8,128)(2,1)}, u32[]{:S(2)}, u32[]{:S(2)}) collective-permute-start(bf16[384,256]{1,0:T(8,128)(2,1)} %get-tuple-element.83), channel_id=1, source_target_pairs={{4,0},{8,4},{12,8},{16,12},{20,16},{24,20},{28,24},{32,28},{36,32}... | collective-permute-start | bytes 589832 | tf_op jit(solution)/shard_map/ppermute | solution.py:592
  11.1 1.9 collective-permute-start.2
  17.9 3.9 %shard_map.120 = bf16[16384,128]{1,0:T(8,128)(2,1)} custom-call(s32[128]{0:T(128)} %reshape.106.idx_ref, bf16[2048,256]{1,0:T(8,128)(2,1)} %bitcast.26, bf16[2048,256]{1,0:T(8,128)(2,1)} %bitcast.34), custom_call_target="tpu_custom_call" | custom-call | bytes 10485760 | tf_op jit(solution)/shard_map/pallas_call | solution.py:55
  22.5 1.8 shard_map.122.a
  25.3 4.5 %all-to-all-start = ((bf16[16,1024,128]{2,1,0:T(8,128)(2,1)}), bf16[16,1024,128]{2,1,0:T(8,128)(2,1)}, u32[]{:S(2)}, u32[]{:S(2)}) async-start(bf16[16,1024,128]{2,1,0:T(8,128)(2,1)} %bitcast.39), calls=%async_computation | async-start | bytes 8388608 | tf_op jit(solution)/shard_map/all_to_all | solution.py:641
  29.9 3.5 %collective-permute-start.8 = (bf16[2048,256]{1,0:T(8,128)(2,1)}, bf16[2048,256]{1,0:T(8,128)(2,1)S(1)}, u32[]{:S(2)}, u32[]{:S(2)}) collective-permute-start(bf16[2048,256]{1,0:T(8,128)(2,1)} %bitcast.4.refs_0_), channel_id=1, source_target_pairs={{3,0},{0,1},{1,2},{2,3},{7,4},{4,5},{5,6},{6,7},{11,8},{8,9},{9,10... | collective-permute-start | bytes 3145736 | tf_op jit(solution)/shard_map/ppermute | solution.py:615
  33.4 3.7 %collective-permute-start.7 = (bf16[2048,256]{1,0:T(8,128)(2,1)}, bf16[2048,256]{1,0:T(8,128)(2,1)S(1)}, u32[]{:S(2)}, u32[]{:S(2)}) collective-permute-start(bf16[2048,256]{1,0:T(8,128)(2,1)} %bitcast.4.refs_0_), channel_id=1, source_target_pairs={{1,0},{2,1},{3,2},{0,3},{5,4},{6,5},{7,6},{4,7},{9,8},{10,9},{11,1... | collective-permute-start | bytes 3145736 | tf_op jit(solution)/shard_map/ppermute | solution.py:615
  37.1 3.9 %shard_map.119 = bf16[16384,128]{1,0:T(8,128)(2,1)} custom-call(s32[128]{0:T(128)} %reshape.106.idx_ref, bf16[2048,256]{1,0:T(8,128)(2,1)} %bitcast.27, bf16[2048,256]{1,0:T(8,128)(2,1)} %bitcast.35), custom_call_target="tpu_custom_call" | custom-call | bytes 10485760 | tf_op jit(solution)/shard_map/pallas_call | solution.py:55
  41.8 6.3 %collective-permute-done.8.refs_2_ = bf16[2048,256]{1,0:T(8,128)(2,1)S(1)} collective-permute-done((bf16[2048,256]{1,0:T(8,128)(2,1)}, bf16[2048,256]{1,0:T(8,128)(2,1)S(1)}, u32[]{:S(2)}, u32[]{:S(2)}) %collective-permute-start.8) | collective-permute-done | bytes 1048608 | tf_op jit(solution)/shard_map/ppermute | solution.py:615
  49.0 2.2 collective-permute-start.10
  52.1 4.9 %collective-permute-start.9 = (bf16[1024,256]{1,0:T(8,128)(2,1)}, bf16[1024,256]{1,0:T(8,128)(2,1)S(1)}, u32[]{:S(2)}, u32[]{:S(2)}) collective-permute-start(bf16[1024,256]{1,0:T(8,128)(2,1)} %slice.38), channel_id=1, source_target_pairs={{1,0},{2,1},{3,2},{0,3},{5,4},{6,5},{7,6},{4,7},{9,8},{10,9},{11,1... | collective-permute-start | bytes 1572872 | tf_op jit(solution)/shard_map/ppermute | solution.py:615
  58.0 3.1 collective-permute-start.11
  61.1 2.3 collective-permute-start.13
  63.9 12.8 %collective-permute-done.11.b = bf16[256,256]{1,0:T(8,128)(2,1)S(1)} collective-permute-done((bf16[256,256]{1,0:T(8,128)(2,1)S(1)}, bf16[256,256]{1,0:T(8,128)(2,1)S(1)}, u32[]{:S(2)}, u32[]{:S(2)}) %collective-permute-start.11) | collective-permute-done | bytes 131104 | tf_op jit(solution)/shard_map/ppermute | solution.py:592
  78.6 1.8 shard_map.123
  81.4 5.0 %all-to-all-start.1 = ((bf16[16,1024,128]{2,1,0:T(8,128)(2,1)}), bf16[16,1024,128]{2,1,0:T(8,128)(2,1)}, u32[]{:S(2)}, u32[]{:S(2)}) async-start(bf16[16,1024,128]{2,1,0:T(8,128)(2,1)} %bitcast.38), calls=%async_computation.1 | async-start | bytes 8388608 | tf_op jit(solution)/shard_map/all_to_all | solution.py:641
  87.0 6.3 %shard_map.124.g_ref = bf16[2048,256]{1,0:T(8,128)(2,1)} custom-call(s32[2]{0:T(128)} %pad_add_fusion.at_ref, bf16[2048,256]{1,0:T(8,128)(2,1)} %bitcast.4.refs_0_, bf16[2048,256]{1,0:T(8,128)(2,1)} %copy-done.8, bf16[2048,256]{1,0:T(8,128)(2,1)} %copy-done.7, bf16[1024,256]{1,0:T(8,128)(2,1)} %copy-done.13, bf16[1024,256]{1,0:T(8,128)(2,1)} %copy-done.12, ...), custom_call_target="tpu_custom_call" | custom-call | flops 1073741824 | bytes 16777216 | tf_op jit(solution)/shard_map/pallas_call | solution.py:175
  94.0 27.0 %shard_map.125 = (bf16[2048,128]{1,0:T(8,128)(2,1)}, bf16[2048,256]{1,0:T(8,128)(2,1)}, f32[2,2048,128]{2,1,0:T(8,128)}, bf16[2,64,128]{2,1,0:T(8,128)(2,1)}, bf...) custom-call(s32[1]{0:T(128)} %bitcast.me_ref, ...), custom_call_target="tpu_custom_call" | custom-call | flops 6442450944 | bytes 83886080 | tf_op jit(solution)/shard_map/pallas_call | solution.py:308
  120.9 4.0 %collective-permute-start.17 = (bf16[2048,128]{1,0:T(8,128)(2,1)}, bf16[2048,128]{1,0:T(8,128)(2,1)S(1)}, u32[]{:S(2)}, u32[]{:S(2)}) collective-permute-start(bf16[2048,128]{1,0:T(8,128)(2,1)} %get-tuple-element.106.c0.refs_0_), channel_id=1, source_target_pairs={{1,0},{2,1},{3,2},{0,3},{5,4},{6,5},{7,6},{4,7},{9,8},{10,9},{11,1... | collective-permute-start | bytes 1572872 | tf_op jit(solution)/shard_map/ppermute | solution.py:592
  127.0 6.5 %collective-permute-start.14 = (bf16[256,256]{1,0:T(8,128)(2,1)S(1)}, bf16[256,256]{1,0:T(8,128)(2,1)S(1)}, u32[]{:S(2)}, u32[]{:S(2)}) collective-permute-start(bf16[256,256]{1,0:T(8,128)(2,1)S(1)} %get-tuple-element.160), channel_id=1, source_target_pairs={{1,0},{2,1},{3,2},{0,3},{5,4},{6,5},{7,6},{4,7},{9,8},{10,9},{11,1... | collective-permute-start | bytes 393224 | tf_op jit(solution)/shard_map/ppermute | solution.py:592
  133.5 1.5 collective-permute-start.15
  136.4 6.7 %collective-permute-done.15.refs_12_ = bf16[256,256]{1,0:T(8,128)(2,1)S(1)} collective-permute-done((bf16[256,256]{1,0:T(8,128)(2,1)S(1)}, bf16[256,256]{1,0:T(8,128)(2,1)S(1)}, u32[]{:S(2)}, u32[]{:S(2)}) %collective-permute-start.15) | collective-permute-done | bytes 131104 | tf_op jit(solution)/shard_map/ppermute | solution.py:592
  144.0 7.0 %all-to-all-start.2 = ((bf16[16,1024,128]{2,1,0:T(8,128)(2,1)}), bf16[16,1024,128]{2,1,0:T(8,128)(2,1)}, u32[]{:S(2)}, u32[]{:S(2)}) async-start(bf16[16,1024,128]{2,1,0:T(8,128)(2,1)} %bitcast.40), calls=%async_computation.2 | async-start | bytes 8388608 | tf_op jit(solution)/shard_map/all_to_all | solution.py:641
  151.1 27.5 %shard_map.126 = (bf16[2048,128]{1,0:T(8,128)(2,1)}, bf16[2048,256]{1,0:T(8,128)(2,1)}, f32[2,2048,128]{2,1,0:T(8,128)}, bf16[2,64,128]{2,1,0:T(8,128)(2,1)}, bf...) custom-call(s32[1]{0:T(128)} %bitcast.me_ref, ...), custom_call_target="tpu_custom_call", output_to_operand_aliasing={{1}: (12, {})} | custom-call | flops 6442450944 | bytes 83886080 | tf_op jit(solution)/shard_map/pallas_call | solution.py:308
  178.6 3.3 %collective-permute-start.23 = (bf16[2048,128]{1,0:T(8,128)(2,1)}, bf16[2048,128]{1,0:T(8,128)(2,1)}, u32[]{:S(2)}, u32[]{:S(2)}) collective-permute-start(bf16[2048,128]{1,0:T(8,128)(2,1)} %get-tuple-element.135.c1.refs_5_), channel_id=1, source_target_pairs={{1,0},{2,1},{3,2},{0,3},{5,4},{6,5},{7,6},{4,7},{9,8},{10,9},{11,1... | collective-permute-start | bytes 1572872 | tf_op jit(solution)/shard_map/ppermute | solution.py:592
  183.2 5.1 %collective-permute-start.22 = (bf16[2,64,128]{2,1,0:T(8,128)(2,1)S(1)}, bf16[2,64,128]{2,1,0:T(8,128)(2,1)}, u32[]{:S(2)}, u32[]{:S(2)}) collective-permute-start(bf16[2,64,128]{2,1,0:T(8,128)(2,1)S(1)} %copy-done.30), channel_id=1, source_target_pairs={{0,4},{4,8},{8,12},{12,16},{16,20},{20,24},{24,28},{28,32},{32,36}... | collective-permute-start | bytes 98312 | tf_op jit(solution)/shard_map/ppermute | solution.py:608
  188.3 6.4 %shard_map.127.terms_ref = bf16[256,1024]{1,0:T(8,128)(2,1)} custom-call(s32[2]{0:T(128)} %pad_add_fusion.at_ref, bf16[2048,128]{1,0:T(8,128)(2,1)} %get-tuple-element.106.c0.refs_0_, bf16[2048,128]{1,0:T(8,128)(2,1)} %get-tuple-element.135.c1.refs_5_, bf16[2048,256]{1,0:T(8,128)(2,1)} %bitcast.4.refs_0_, bf16[2048,256]{1,0:T(8,128)(2,1)} %copy-done.8, ...), custom_call_target="tpu_custom_call" | custom-call | flops 1073741824 | bytes 16777216 | tf_op jit(solution)/shard_map/pallas_call | solution.py:483
  194.8 2.0 shard_map.128
  196.8 3.3 %all-to-all-done.2.back_ref = bf16[16,1024,128]{2,1,0:T(8,128)(2,1)} async-done(((bf16[16,1024,128]{2,1,0:T(8,128)(2,1)}), bf16[16,1024,128]{2,1,0:T(8,128)(2,1)}, u32[]{:S(2)}, u32[]{:S(2)}) %all-to-all-start.2) | async-done | bytes 4194336 | tf_op jit(solution)/shard_map/all_to_all | solution.py:641
  200.1 12.2 %all-to-all-start.3 = ((bf16[16,672,128]{2,1,0:T(8,128)(2,1)}), bf16[16,672,128]{2,1,0:T(8,128)(2,1)S(1)}, u32[]{:S(2)}, u32[]{:S(2)}) async-start(bf16[16,672,128]{2,1,0:T(8,128)(2,1)} %shard_map.128), calls=%async_computation.3 | async-start | bytes 5505024 | tf_op jit(solution)/shard_map/all_to_all | solution.py:641
  212.4 1.7 slice.33
  214.0 1.7 collective-permute-start.27
  215.7 1.7 slice.34
  219.4 5.2 %collective-permute-start.26 = (bf16[2,64,128]{2,1,0:T(8,128)(2,1)}, bf16[2,64,128]{2,1,0:T(8,128)(2,1)}, u32[]{:S(2)}, u32[]{:S(2)}) collective-permute-start(bf16[2,64,128]{2,1,0:T(8,128)(2,1)} %get-tuple-element.124), channel_id=1, source_target_pairs={{0,4},{4,8},{8,12},{12,16},{16,20},{20,24},{24,28},{28,32},{32,36}... | collective-permute-start | bytes 98312 | tf_op jit(solution)/shard_map/ppermute | solution.py:608
  224.5 5.0 %shard_map.130 = (bf16[2048,128]{1,0:T(8,128)(2,1)}, bf16[2048,128]{1,0:T(8,128)(2,1)}, f32[2,2,64,128]{3,2,1,0:T(8,128)}) custom-call(s32[128]{0:T(128)} %reshape.106.idx_ref, s32[16]{0:T(128)} %reduce_sum.47.used_ref, s32[2]{0:T(128)} %bitcast.45, f32[2,2048,128]{2,1,0:T(8,128)} %get-tuple-element.128.win_ref, ...), custom_call_target="tpu_custom_call" | custom-call | flops 4194304 | bytes 16777216 | tf_op jit(solution)/shard_map/pallas_call | solution.py:419
  229.5 20.2 %all-to-all-done.3.back_ref = bf16[16,672,128]{2,1,0:T(8,128)(2,1)S(1)} async-done(((bf16[16,672,128]{2,1,0:T(8,128)(2,1)}), bf16[16,672,128]{2,1,0:T(8,128)(2,1)S(1)}, u32[]{:S(2)}, u32[]{:S(2)}) %all-to-all-start.3) | async-done | bytes 2752544 | tf_op jit(solution)/shard_map/all_to_all | solution.py:641
  251.2 2.1 shard_map.129
  254.0 7.0 %all-to-all-start.4 = ((bf16[16,672,128]{2,1,0:T(8,128)(2,1)}), bf16[16,672,128]{2,1,0:T(8,128)(2,1)S(1)}, u32[]{:S(2)}, u32[]{:S(2)}) async-start(bf16[16,672,128]{2,1,0:T(8,128)(2,1)} %shard_map.129), calls=%async_computation.4 | async-start | bytes 5505024 | tf_op jit(solution)/shard_map/all_to_all | solution.py:641
  261.1 1.8 collective-permute-start.19
  263.8 2.2 collective-permute-start.20
  266.0 4.5 %shard_map.132.win_ref = f32[2,2048,128]{2,1,0:T(8,128)} custom-call(s32[128]{0:T(128)} %reshape.106.idx_ref, s32[16]{0:T(128)} %reduce_sum.47.used_ref, f32[2,2048,128]{2,1,0:T(8,128)} %get-tuple-element.144.win_ref, bf16[16,672,128]{2,1,0:T(8,128)(2,1)} %copy-done.2, bf16[2,64,128]{2,1,0:T(8,128)(2,1)} %collective-permute-done.25.up_ref, ...), custom_call_target="tpu_custom_call" | custom-call | flops 4194304 | bytes 14680064 | tf_op jit(solution)/shard_map/pallas_call | solution.py:432
  270.5 3.5 %collective-permute-done.20.refs_4_ = bf16[1024,128]{1,0:T(8,128)(2,1)S(1)} collective-permute-done((bf16[1024,128]{1,0:T(8,128)(2,1)S(1)}, bf16[1024,128]{1,0:T(8,128)(2,1)S(1)}, u32[]{:S(2)}, u32[]{:S(2)}) %collective-permute-start.20) | collective-permute-done | bytes 262176 | tf_op jit(solution)/shard_map/ppermute | solution.py:592
  274.6 5.9 %shard_map.131 = bf16[2048,256]{1,0:T(8,128)(2,1)} custom-call(bf16[2048,128]{1,0:T(8,128)(2,1)} %get-tuple-element.106.c0.refs_0_, bf16[2048,128]{1,0:T(8,128)(2,1)} %copy-done.14, bf16[2048,128]{1,0:T(8,128)(2,1)} %copy-done.15, bf16[1024,128]{1,0:T(8,128)(2,1)} %copy-done.19, bf16[1024,128]{1,0:T(8,128)(2,1)} %copy-done.20, ...), custom_call_target="tpu_custom_call" | custom-call | flops 1073741824 | bytes 18874368 | tf_op jit(solution)/shard_map/pallas_call | solution.py:579
  280.5 20.2 %all-to-all-done.4.back_ref = bf16[16,672,128]{2,1,0:T(8,128)(2,1)S(1)} async-done(((bf16[16,672,128]{2,1,0:T(8,128)(2,1)}), bf16[16,672,128]{2,1,0:T(8,128)(2,1)S(1)}, u32[]{:S(2)}, u32[]{:S(2)}) %all-to-all-start.4) | async-done | bytes 2752544 | tf_op jit(solution)/shard_map/all_to_all | solution.py:641
  302.2 5.1 %shard_map.133 = (bf16[2048,256]{1,0:T(8,128)(2,1)}, bf16[2048,256]{1,0:T(8,128)(2,1)}) custom-call(s32[128]{0:T(128)} %reshape.106.idx_ref, s32[16]{0:T(128)} %reduce_sum.47.used_ref, s32[2]{0:T(128)} %bitcast.46, s32[1]{0:T(128)} %bitcast.me_ref, f32[2,2048,128]{2,1,0:T(8,128)} %shard_map.132.win_ref, bf16[16,672,128]{2,1,0:T(8,128)(2,1)} %copy-done.3, ...), custom_call_target="tpu_custom_call" | custom-call | flops 4194304 | bytes 12582912 | tf_op jit(solution)/shard_map/pallas_call | solution.py:448
  308.1 2.3 shard_map.134
  (131 shorter events, 30.1 us)
Async XLA Ops:
  0.6 40.3 %copy-start = (s32[1,512,3]{1,0,2:T(1,128)S(1)}, s32[1,512,3]{1,0,2:T(1,128)}, u32[]{:S(2)}) copy-start(s32[1,512,3]{1,0,2:T(1,128)} %param.14) | copy-start | bytes 18436
  0.6 12.6 %collective-permute-start.3 = (bf16[2048,256]{1,0:T(8,128)(2,1)}, bf16[2048,256]{1,0:T(8,128)(2,1)S(1)}, u32[]{:S(2)}, u32[]{:S(2)}) collective-permute-start(bf16[2048,256]{1,0:T(8,128)(2,1)} %bitcast.4.refs_0_), channel_id=1, source_target_pairs={{65,64},{66,65},{67,66},{64,67},{69,68},{70,69},{71,70},{68,71},{7... | collective-permute-start | bytes 3145736 | tf_op jit(solution)/shard_map/ppermute | solution.py:615
  1.4 13.5 %collective-permute-start.4 = (bf16[2048,256]{1,0:T(8,128)(2,1)}, bf16[2048,256]{1,0:T(8,128)(2,1)S(1)}, u32[]{:S(2)}, u32[]{:S(2)}) collective-permute-start(bf16[2048,256]{1,0:T(8,128)(2,1)} %bitcast.4.refs_0_), channel_id=1, source_target_pairs={{67,64},{64,65},{65,66},{66,67},{71,68},{68,69},{69,70},{70,71},{7... | collective-permute-start | bytes 3145736 | tf_op jit(solution)/shard_map/ppermute | solution.py:615
  2.1 10.8 %copy-start.29 = (s32[1,512,3]{1,0,2:T(1,128)S(1)}, s32[1,512,3]{1,0,2:T(1,128)}, u32[]{:S(2)}) copy-start(s32[1,512,3]{1,0,2:T(1,128)} %param.13) | copy-start | bytes 18436
  4.5 17.3 %collective-permute-start = (bf16[384,256]{1,0:T(8,128)(2,1)}, bf16[384,256]{1,0:T(8,128)(2,1)S(1)}, u32[]{:S(2)}, u32[]{:S(2)}) collective-permute-start(bf16[384,256]{1,0:T(8,128)(2,1)} %get-tuple-element.82), channel_id=1, source_target_pairs={{60,0},{0,4},{4,8},{8,12},{12,16},{16,20},{20,24},{24,28},{28,32},... | collective-permute-start | bytes 589832 | tf_op jit(solution)/shard_map/ppermute | solution.py:592
  6.5 15.3 %collective-permute-start.1 = (bf16[384,256]{1,0:T(8,128)(2,1)}, bf16[384,256]{1,0:T(8,128)(2,1)}, u32[]{:S(2)}, u32[]{:S(2)}) collective-permute-start(bf16[384,256]{1,0:T(8,128)(2,1)} %get-tuple-element.83), channel_id=1, source_target_pairs={{4,0},{8,4},{12,8},{16,12},{20,16},{24,20},{28,24},{32,28},{36,32}... | collective-permute-start | bytes 589832 | tf_op jit(solution)/shard_map/ppermute | solution.py:592
  11.1 10.7 %collective-permute-start.2 = (bf16[256,256]{1,0:T(8,128)(2,1)}, bf16[256,256]{1,0:T(8,128)(2,1)S(1)}, u32[]{:S(2)}, u32[]{:S(2)}) collective-permute-start(bf16[256,256]{1,0:T(8,128)(2,1)} %get-tuple-element.81.a), channel_id=1, source_target_pairs={{8,0},{12,4},{16,8},{20,12},{24,16},{28,20},{32,24},{36,28},{40,32... | collective-permute-start | bytes 393224 | tf_op jit(solution)/shard_map/ppermute | solution.py:592
  13.3 8.5 %copy-start.5 = (bf16[2048,256]{1,0:T(8,128)(2,1)}, bf16[2048,256]{1,0:T(8,128)(2,1)S(1)}, u32[]{:S(2)}) copy-start(bf16[2048,256]{1,0:T(8,128)(2,1)S(1)} %collective-permute-done.3.refs_5_) | copy-start | bytes 3145732
  14.2 10.1 %collective-permute-start.5 = (bf16[1024,256]{1,0:T(8,128)(2,1)}, bf16[1024,256]{1,0:T(8,128)(2,1)S(1)}, u32[]{:S(2)}, u32[]{:S(2)}) collective-permute-start(bf16[1024,256]{1,0:T(8,128)(2,1)} %slice.36), channel_id=1, source_target_pairs={{65,64},{66,65},{67,66},{64,67},{69,68},{70,69},{71,70},{68,71},{7... | collective-permute-start | bytes 1572872 | tf_op jit(solution)/shard_map/ppermute | solution.py:615
  14.9 6.9 %copy-start.6 = (bf16[2048,256]{1,0:T(8,128)(2,1)}, bf16[2048,256]{1,0:T(8,128)(2,1)S(1)}, u32[]{:S(2)}) copy-start(bf16[2048,256]{1,0:T(8,128)(2,1)S(1)} %collective-permute-done.4.refs_6_) | copy-start | bytes 3145732
  15.8 8.5 %collective-permute-start.6 = (bf16[1024,256]{1,0:T(8,128)(2,1)}, bf16[1024,256]{1,0:T(8,128)(2,1)S(1)}, u32[]{:S(2)}, u32[]{:S(2)}) collective-permute-start(bf16[1024,256]{1,0:T(8,128)(2,1)} %slice.37), channel_id=1, source_target_pairs={{67,64},{64,65},{65,66},{66,67},{71,68},{68,69},{69,70},{70,71},{7... | collective-permute-start | bytes 1572872 | tf_op jit(solution)/shard_map/ppermute | solution.py:615
  25.3 55.1 %all-to-all-start = ((bf16[16,1024,128]{2,1,0:T(8,128)(2,1)}), bf16[16,1024,128]{2,1,0:T(8,128)(2,1)}, u32[]{:S(2)}, u32[]{:S(2)}) async-start(bf16[16,1024,128]{2,1,0:T(8,128)(2,1)} %bitcast.39), calls=%async_computation | async-start | bytes 8388608 | tf_op jit(solution)/shard_map/all_to_all | solution.py:641
  29.8 28.1 %copy-start.16 = (bf16[256,256]{1,0:T(8,128)(2,1)S(1)}, bf16[256,256]{1,0:T(8,128)(2,1)}, u32[]{:S(2)}) copy-start(bf16[256,256]{1,0:T(8,128)(2,1)} %shard_map.122.a) | copy-start | bytes 393220
  29.9 18.2 %collective-permute-start.8 = (bf16[2048,256]{1,0:T(8,128)(2,1)}, bf16[2048,256]{1,0:T(8,128)(2,1)S(1)}, u32[]{:S(2)}, u32[]{:S(2)}) collective-permute-start(bf16[2048,256]{1,0:T(8,128)(2,1)} %bitcast.4.refs_0_), channel_id=1, source_target_pairs={{3,0},{0,1},{1,2},{2,3},{7,4},{4,5},{5,6},{6,7},{11,8},{8,9},{9,10... | collective-permute-start | bytes 3145736 | tf_op jit(solution)/shard_map/ppermute | solution.py:615
  33.4 17.8 %collective-permute-start.7 = (bf16[2048,256]{1,0:T(8,128)(2,1)}, bf16[2048,256]{1,0:T(8,128)(2,1)S(1)}, u32[]{:S(2)}, u32[]{:S(2)}) collective-permute-start(bf16[2048,256]{1,0:T(8,128)(2,1)} %bitcast.4.refs_0_), channel_id=1, source_target_pairs={{1,0},{2,1},{3,2},{0,3},{5,4},{6,5},{7,6},{4,7},{9,8},{10,9},{11,1... | collective-permute-start | bytes 3145736 | tf_op jit(solution)/shard_map/ppermute | solution.py:615
  48.1 32.3 %copy-start.7 = (bf16[2048,256]{1,0:T(8,128)(2,1)}, bf16[2048,256]{1,0:T(8,128)(2,1)S(1)}, u32[]{:S(2)}) copy-start(bf16[2048,256]{1,0:T(8,128)(2,1)S(1)} %collective-permute-done.8.refs_2_) | copy-start | bytes 3145732
  49.0 31.4 %collective-permute-start.10 = (bf16[1024,256]{1,0:T(8,128)(2,1)}, bf16[1024,256]{1,0:T(8,128)(2,1)S(1)}, u32[]{:S(2)}, u32[]{:S(2)}) collective-permute-start(bf16[1024,256]{1,0:T(8,128)(2,1)} %slice.39), channel_id=1, source_target_pairs={{3,0},{0,1},{1,2},{2,3},{7,4},{4,5},{5,6},{6,7},{11,8},{8,9},{9,10... | collective-permute-start | bytes 1572872 | tf_op jit(solution)/shard_map/ppermute | solution.py:615
  51.2 29.3 %copy-start.8 = (bf16[2048,256]{1,0:T(8,128)(2,1)}, bf16[2048,256]{1,0:T(8,128)(2,1)S(1)}, u32[]{:S(2)}) copy-start(bf16[2048,256]{1,0:T(8,128)(2,1)S(1)} %collective-permute-done.7.refs_1_) | copy-start | bytes 3145732
  52.1 28.3 %collective-permute-start.9 = (bf16[1024,256]{1,0:T(8,128)(2,1)}, bf16[1024,256]{1,0:T(8,128)(2,1)S(1)}, u32[]{:S(2)}, u32[]{:S(2)}) collective-permute-start(bf16[1024,256]{1,0:T(8,128)(2,1)} %slice.38), channel_id=1, source_target_pairs={{1,0},{2,1},{3,2},{0,3},{5,4},{6,5},{7,6},{4,7},{9,8},{10,9},{11,1... | collective-permute-start | bytes 1572872 | tf_op jit(solution)/shard_map/ppermute | solution.py:615
  58.0 18.8 %collective-permute-start.11 = (bf16[256,256]{1,0:T(8,128)(2,1)S(1)}, bf16[256,256]{1,0:T(8,128)(2,1)S(1)}, u32[]{:S(2)}, u32[]{:S(2)}) collective-permute-start(bf16[256,256]{1,0:T(8,128)(2,1)S(1)} %copy-done.16), channel_id=1, source_target_pairs={{16,0},{20,4},{24,8},{28,12},{32,16},{36,20},{40,24},{44,28},{48,3... | collective-permute-start | bytes 393224 | tf_op jit(solution)/shard_map/ppermute | solution.py:592
  61.0 15.7 %collective-permute-start.12 = (bf16[256,256]{1,0:T(8,128)(2,1)S(1)}, bf16[256,256]{1,0:T(8,128)(2,1)S(1)}, u32[]{:S(2)}, u32[]{:S(2)}) collective-permute-start(bf16[256,256]{1,0:T(8,128)(2,1)S(1)} %copy-done.16), channel_id=1, source_target_pairs={{48,0},{52,4},{56,8},{60,12},{0,16},{4,20},{8,24},{12,28},{16,32},... | collective-permute-start | bytes 393224 | tf_op jit(solution)/shard_map/ppermute | solution.py:592
  61.1 16.9 %collective-permute-start.13 = (bf16[256,256]{1,0:T(8,128)(2,1)S(1)}, bf16[256,256]{1,0:T(8,128)(2,1)S(1)}, u32[]{:S(2)}, u32[]{:S(2)}) collective-permute-start(bf16[256,256]{1,0:T(8,128)(2,1)S(1)} %copy-done.16), channel_id=1, source_target_pairs={{32,0},{36,4},{40,8},{44,12},{48,16},{52,20},{56,24},{60,28},{0,32... | collective-permute-start | bytes 393224 | tf_op jit(solution)/shard_map/ppermute | solution.py:592
  81.4 61.8 %all-to-all-start.1 = ((bf16[16,1024,128]{2,1,0:T(8,128)(2,1)}), bf16[16,1024,128]{2,1,0:T(8,128)(2,1)}, u32[]{:S(2)}, u32[]{:S(2)}) async-start(bf16[16,1024,128]{2,1,0:T(8,128)(2,1)} %bitcast.38), calls=%async_computation.1 | async-start | bytes 8388608 | tf_op jit(solution)/shard_map/all_to_all | solution.py:641
  94.0 32.3 %copy-start.4 = (bf16[256,1024]{1,0:T(8,128)(2,1)S(1)}, bf16[256,1024]{1,0:T(8,128)(2,1)}, u32[]{:S(2)}) copy-start(bf16[256,1024]{1,0:T(8,128)(2,1)} %refs_12_.1) | copy-start | bytes 1572868
  120.9 22.2 %collective-permute-start.17 = (bf16[2048,128]{1,0:T(8,128)(2,1)}, bf16[2048,128]{1,0:T(8,128)(2,1)S(1)}, u32[]{:S(2)}, u32[]{:S(2)}) collective-permute-start(bf16[2048,128]{1,0:T(8,128)(2,1)} %get-tuple-element.106.c0.refs_0_), channel_id=1, source_target_pairs={{1,0},{2,1},{3,2},{0,3},{5,4},{6,5},{7,6},{4,7},{9,8},{10,9},{11,1... | collective-permute-start | bytes 1572872 | tf_op jit(solution)/shard_map/ppermute | solution.py:592
  124.9 18.2 %collective-permute-start.18 = (bf16[2048,128]{1,0:T(8,128)(2,1)}, bf16[2048,128]{1,0:T(8,128)(2,1)S(1)}, u32[]{:S(2)}, u32[]{:S(2)}) collective-permute-start(bf16[2048,128]{1,0:T(8,128)(2,1)} %get-tuple-element.106.c0.refs_0_), channel_id=1, source_target_pairs={{3,0},{0,1},{1,2},{2,3},{7,4},{4,5},{5,6},{6,7},{11,8},{8,9},{9,10... | collective-permute-start | bytes 1572872 | tf_op jit(solution)/shard_map/ppermute | solution.py:592
  127.0 9.4 %collective-permute-start.14 = (bf16[256,256]{1,0:T(8,128)(2,1)S(1)}, bf16[256,256]{1,0:T(8,128)(2,1)S(1)}, u32[]{:S(2)}, u32[]{:S(2)}) collective-permute-start(bf16[256,256]{1,0:T(8,128)(2,1)S(1)} %get-tuple-element.160), channel_id=1, source_target_pairs={{1,0},{2,1},{3,2},{0,3},{5,4},{6,5},{7,6},{4,7},{9,8},{10,9},{11,1... | collective-permute-start | bytes 393224 | tf_op jit(solution)/shard_map/ppermute | solution.py:592
  133.5 9.6 %collective-permute-start.15 = (bf16[256,256]{1,0:T(8,128)(2,1)S(1)}, bf16[256,256]{1,0:T(8,128)(2,1)S(1)}, u32[]{:S(2)}, u32[]{:S(2)}) collective-permute-start(bf16[256,256]{1,0:T(8,128)(2,1)S(1)} %get-tuple-element.162), channel_id=1, source_target_pairs={{2,0},{3,1},{0,2},{1,3},{6,4},{7,5},{4,6},{5,7},{10,8},{11,9},{8,1... | collective-permute-start | bytes 393224 | tf_op jit(solution)/shard_map/ppermute | solution.py:592
  135.1 8.1 %collective-permute-start.16 = (bf16[256,256]{1,0:T(8,128)(2,1)S(1)}, bf16[256,256]{1,0:T(8,128)(2,1)S(1)}, u32[]{:S(2)}, u32[]{:S(2)}) collective-permute-start(bf16[256,256]{1,0:T(8,128)(2,1)S(1)} %get-tuple-element.159), channel_id=1, source_target_pairs={{3,0},{0,1},{1,2},{2,3},{7,4},{4,5},{5,6},{6,7},{11,8},{8,9},{9,10... | collective-permute-start | bytes 393224 | tf_op jit(solution)/shard_map/ppermute | solution.py:592
  136.4 6.8 %copy-start.22 = (bf16[256,256]{1,0:T(8,128)(2,1)}, bf16[256,256]{1,0:T(8,128)(2,1)S(1)}, u32[]{:S(2)}) copy-start(bf16[256,256]{1,0:T(8,128)(2,1)S(1)} %collective-permute-done.14.refs_11_) | copy-start | bytes 393220
  143.2 117.9 %copy-start.14 = (bf16[2048,128]{1,0:T(8,128)(2,1)}, bf16[2048,128]{1,0:T(8,128)(2,1)S(1)}, u32[]{:S(2)}) copy-start(bf16[2048,128]{1,0:T(8,128)(2,1)S(1)} %collective-permute-done.17.refs_1_) | copy-start | bytes 1572868
  144.0 56.1 %all-to-all-start.2 = ((bf16[16,1024,128]{2,1,0:T(8,128)(2,1)}), bf16[16,1024,128]{2,1,0:T(8,128)(2,1)}, u32[]{:S(2)}, u32[]{:S(2)}) async-start(bf16[16,1024,128]{2,1,0:T(8,128)(2,1)} %bitcast.40), calls=%async_computation.2 | async-start | bytes 8388608 | tf_op jit(solution)/shard_map/all_to_all | solution.py:641
  151.1 30.8 %copy-start.31 = (bf16[2,64,128]{2,1,0:T(8,128)(2,1)S(1)}, bf16[2,64,128]{2,1,0:T(8,128)(2,1)}, u32[]{:S(2)}) copy-start(bf16[2,64,128]{2,1,0:T(8,128)(2,1)} %get-tuple-element.119) | copy-start | bytes 98308
  151.1 32.1 %copy-start.30 = (bf16[2,64,128]{2,1,0:T(8,128)(2,1)S(1)}, bf16[2,64,128]{2,1,0:T(8,128)(2,1)}, u32[]{:S(2)}) copy-start(bf16[2,64,128]{2,1,0:T(8,128)(2,1)} %get-tuple-element.120) | copy-start | bytes 98308
  178.6 18.2 %collective-permute-start.23 = (bf16[2048,128]{1,0:T(8,128)(2,1)}, bf16[2048,128]{1,0:T(8,128)(2,1)}, u32[]{:S(2)}, u32[]{:S(2)}) collective-permute-start(bf16[2048,128]{1,0:T(8,128)(2,1)} %get-tuple-element.135.c1.refs_5_), channel_id=1, source_target_pairs={{1,0},{2,1},{3,2},{0,3},{5,4},{6,5},{7,6},{4,7},{9,8},{10,9},{11,1... | collective-permute-start | bytes 1572872 | tf_op jit(solution)/shard_map/ppermute | solution.py:592
  181.9 14.9 %collective-permute-start.24 = (bf16[2048,128]{1,0:T(8,128)(2,1)}, bf16[2048,128]{1,0:T(8,128)(2,1)}, u32[]{:S(2)}, u32[]{:S(2)}) collective-permute-start(bf16[2048,128]{1,0:T(8,128)(2,1)} %get-tuple-element.135.c1.refs_5_), channel_id=1, source_target_pairs={{3,0},{0,1},{1,2},{2,3},{7,4},{4,5},{5,6},{6,7},{11,8},{8,9},{9,10... | collective-permute-start | bytes 1572872 | tf_op jit(solution)/shard_map/ppermute | solution.py:592
  181.9 14.9 %collective-permute-start.21 = (bf16[2,64,128]{2,1,0:T(8,128)(2,1)S(1)}, bf16[2,64,128]{2,1,0:T(8,128)(2,1)}, u32[]{:S(2)}, u32[]{:S(2)}) collective-permute-start(bf16[2,64,128]{2,1,0:T(8,128)(2,1)S(1)} %copy-done.31), channel_id=1, source_target_pairs={{4,0},{8,4},{12,8},{16,12},{20,16},{24,20},{28,24},{32,28},{36,32}... | collective-permute-start | bytes 98312 | tf_op jit(solution)/shard_map/ppermute | solution.py:608
  183.2 13.6 %collective-permute-start.22 = (bf16[2,64,128]{2,1,0:T(8,128)(2,1)S(1)}, bf16[2,64,128]{2,1,0:T(8,128)(2,1)}, u32[]{:S(2)}, u32[]{:S(2)}) collective-permute-start(bf16[2,64,128]{2,1,0:T(8,128)(2,1)S(1)} %copy-done.30), channel_id=1, source_target_pairs={{0,4},{4,8},{8,12},{12,16},{16,20},{20,24},{24,28},{28,32},{32,36}... | collective-permute-start | bytes 98312 | tf_op jit(solution)/shard_map/ppermute | solution.py:608
  200.1 49.6 %all-to-all-start.3 = ((bf16[16,672,128]{2,1,0:T(8,128)(2,1)}), bf16[16,672,128]{2,1,0:T(8,128)(2,1)S(1)}, u32[]{:S(2)}, u32[]{:S(2)}) async-start(bf16[16,672,128]{2,1,0:T(8,128)(2,1)} %shard_map.128), calls=%async_computation.3 | async-start | bytes 5505024 | tf_op jit(solution)/shard_map/all_to_all | solution.py:641
  214.0 39.3 %collective-permute-start.27 = (bf16[1024,128]{1,0:T(8,128)(2,1)}, bf16[1024,128]{1,0:T(8,128)(2,1)S(1)}, u32[]{:S(2)}, u32[]{:S(2)}) collective-permute-start(bf16[1024,128]{1,0:T(8,128)(2,1)} %slice.33), channel_id=1, source_target_pairs={{1,0},{2,1},{3,2},{0,3},{5,4},{6,5},{7,6},{4,7},{9,8},{10,9},{11,1... | collective-permute-start | bytes 786440 | tf_op jit(solution)/shard_map/ppermute | solution.py:592
  217.4 36.0 %collective-permute-start.28 = (bf16[1024,128]{1,0:T(8,128)(2,1)}, bf16[1024,128]{1,0:T(8,128)(2,1)}, u32[]{:S(2)}, u32[]{:S(2)}) collective-permute-start(bf16[1024,128]{1,0:T(8,128)(2,1)} %slice.34), channel_id=1, source_target_pairs={{3,0},{0,1},{1,2},{2,3},{7,4},{4,5},{5,6},{6,7},{11,8},{8,9},{9,10... | collective-permute-start | bytes 786440 | tf_op jit(solution)/shard_map/ppermute | solution.py:592
  218.1 35.2 %collective-permute-start.25 = (bf16[2,64,128]{2,1,0:T(8,128)(2,1)}, bf16[2,64,128]{2,1,0:T(8,128)(2,1)}, u32[]{:S(2)}, u32[]{:S(2)}) collective-permute-start(bf16[2,64,128]{2,1,0:T(8,128)(2,1)} %get-tuple-element.123), channel_id=1, source_target_pairs={{4,0},{8,4},{12,8},{16,12},{20,16},{24,20},{28,24},{32,28},{36,32}... | collective-permute-start | bytes 98312 | tf_op jit(solution)/shard_map/ppermute | solution.py:608
  219.4 33.9 %collective-permute-start.26 = (bf16[2,64,128]{2,1,0:T(8,128)(2,1)}, bf16[2,64,128]{2,1,0:T(8,128)(2,1)}, u32[]{:S(2)}, u32[]{:S(2)}) collective-permute-start(bf16[2,64,128]{2,1,0:T(8,128)(2,1)} %get-tuple-element.124), channel_id=1, source_target_pairs={{0,4},{4,8},{8,12},{12,16},{16,20},{20,24},{24,28},{28,32},{32,36}... | collective-permute-start | bytes 98312 | tf_op jit(solution)/shard_map/ppermute | solution.py:608
  254.0 46.7 %all-to-all-start.4 = ((bf16[16,672,128]{2,1,0:T(8,128)(2,1)}), bf16[16,672,128]{2,1,0:T(8,128)(2,1)S(1)}, u32[]{:S(2)}, u32[]{:S(2)}) async-start(bf16[16,672,128]{2,1,0:T(8,128)(2,1)} %shard_map.129), calls=%async_computation.4 | async-start | bytes 5505024 | tf_op jit(solution)/shard_map/all_to_all | solution.py:641
  261.1 9.4 %collective-permute-start.19 = (bf16[1024,128]{1,0:T(8,128)(2,1)S(1)}, bf16[1024,128]{1,0:T(8,128)(2,1)S(1)}, u32[]{:S(2)}, u32[]{:S(2)}) collective-permute-start(bf16[1024,128]{1,0:T(8,128)(2,1)S(1)} %slice.31), channel_id=1, source_target_pairs={{1,0},{2,1},{3,2},{0,3},{5,4},{6,5},{7,6},{4,7},{9,8},{10,9},{11,1... | collective-permute-start | bytes 786440 | tf_op jit(solution)/shard_map/ppermute | solution.py:592
  263.8 10.1 %collective-permute-start.20 = (bf16[1024,128]{1,0:T(8,128)(2,1)S(1)}, bf16[1024,128]{1,0:T(8,128)(2,1)S(1)}, u32[]{:S(2)}, u32[]{:S(2)}) collective-permute-start(bf16[1024,128]{1,0:T(8,128)(2,1)S(1)} %slice.32), channel_id=1, source_target_pairs={{3,0},{0,1},{1,2},{2,3},{7,4},{4,5},{5,6},{6,7},{11,8},{8,9},{9,10... | collective-permute-start | bytes 786440 | tf_op jit(solution)/shard_map/ppermute | solution.py:592
  300.7 9.7 %copy-start.1 = (s32[1,512,3]{1,0,2:T(1,128)S(1)}, s32[1,512,3]{1,0,2:T(1,128)}, u32[]{:S(2)}) copy-start(s32[1,512,3]{1,0,2:T(1,128)} %param.14) | copy-start | bytes 18436
  300.8 6.5 %collective-permute-start.29 = (bf16[16,128,128]{2,1,0:T(8,128)(2,1)S(1)}, bf16[16,128,128]{2,1,0:T(8,128)(2,1)S(1)}, u32[]{:S(2)}, u32[]{:S(2)}) collective-permute-start(bf16[16,128,128]{2,1,0:T(8,128)(2,1)S(1)} %slice.35.own_ref), channel_id=1, source_target_pairs={{64,0},{0,64},{65,1},{1,65},{66,2},{2,66},{67,3},{3,67},{68,4},{4,... | collective-permute-start | bytes 1572872 | tf_op jit(solution)/shard_map/ppermute | solution.py:592
  (19 other events, 25.7 us)

commit v5 on v4

--- a/solution.py
+++ b/solution.py
@@ -563,7 +563,7 @@
 
 
 def project_kernel(*refs):
-    weights, out_ref = refs[10:14], refs[14]
+    weights, out_ref = [refs[10][...]] + [refs[10 + j][...] + refs[13 + j][...] for j in range(1, 4)], refs[17]
     halves = ring_values(refs[:5]), ring_values(refs[5:10])
     total = None
     for i in range(4):
@@ -608,15 +608,15 @@
     return lax.ppermute(array, axis, pairs)
 
 
+def core_shifted(array, d, by):
+    size = lax.axis_size("tp")
+    return lax.ppermute(array, ("dp", "tp"), [(d * size + (i + by) % size, d * size + i) for i in range(size)])
+
+
 def core_ring(array, d):
-    size = lax.axis_size("tp")
-
-    def moved(x, by):
-        return lax.ppermute(x, ("dp", "tp"), [(d * size + (i + by) % size, d * size + i) for i in range(size)])
-
     half = array.shape[0] // 2
-    following, previous = moved(array, 1), moved(array, -1)
-    return following, previous, moved(following[:half], 1), moved(previous[half:], -1)
+    following, previous = core_shifted(array, d, 1), core_shifted(array, d, -1)
+    return following, previous, core_shifted(following[:half], d, 1), core_shifted(previous[half:], d, -1)
 
 
 def per_device(
@@ -642,7 +642,7 @@
 
     up, down, picked = pick_global(glob_at, at, k, v)
     before, after = shifted(up, "ctx", -1), shifted(down, "ctx", 1)
-    glob = sum_four((picked, before, after, shifted(picked, "ctx", 2)))
+    across = shifted(picked, "ctx", 2)
 
     ids = random_ids[0].reshape(ctx_count, requests)
     owner = ids // blocks
@@ -656,9 +656,14 @@
     send_a = pick_blocks(send_idx, k, v, 0, slots)
 
     later = core_ring(g_out, 1)
-    send_a, glob, before, after, later, g_now = barrier((send_a, glob, before, after, later, g_out))
+    wparts = [lax.dynamic_slice_in_dim(out_weight, (tp_me + by) % tp_count * width, width, 1) for by in range(tp_count)]
+    wparts, later = barrier((wparts, later))
+    wcols_later = [core_shifted(wparts[-j % tp_count], 1, j) for j in range(1, tp_count)]
+    ready = barrier((send_a, picked, across, before, after, later, wcols_later, g_out))
+    send_a, picked, across, before, after, later, wcols_later, g_now = ready
     fetched_a = exchange(send_a.reshape(ctx_count, -1, LANES)).reshape(send_a.shape)
     pieces = (g_out, *core_ring(g_now, 0), *later)
+    glob = sum_four((picked, before, after, across))
     glob = sum_four((glob, *[shifted(glob, "ctx", 4 * by) for by in (1, 3, 2)])).reshape(G, 2, BLK, width)
     send_b = pick_blocks(send_idx, k, v, 1, slots)
     used = jnp.sum(mine.astype(jnp.int32), axis=1)
@@ -675,10 +680,7 @@
     grad_context = grad_context_of(tp_at, pieces, out_weight)
 
     fetched_b = exchange(send_b.reshape(ctx_count, -1, LANES)).reshape(send_b.shape)
-    wcols = [None] * tp_count
-    for by in range(tp_count):
-        part = lax.dynamic_slice_in_dim(out_weight, (tp_me + by) % tp_count * width, width, 1)
-        wcols[-by % tp_count] = shifted(part, "tp", -by) if by else part
+    wcols = [wparts[0]] + [core_shifted(wparts[-j % tp_count], 0, j) for j in range(1, tp_count)] + wcols_later
     last_block = blocks * ctx_count - 1
 
     def half(to, fetched, dq_in, column):

time: 313 us -> 311 us (level)
  the two profiles are of different devices: /device:TPU:0 before, /device:TPU:85 now
where the time goes in v5:
time: 311 us; the launch traced here: 309 us
  Pallas kernels  107 us (34%)
  starting transfers between devices  94.5 us (30%)
  waiting for transfers between devices  86.1 us (28%)
  local copies, waits for them, and re-layouts  17.3 us (6%)
    pallas_call x2, Pallas kernels, attend(): pl.pallas_call(functools.partial(attend_kernel, blocks, last_block), grid...  54.5 us
    all_to_all x5, waiting for transfers between devices, exchange(): return lax.all_to_all(parts, 'ctx', split_axis=0, concat_axis=0, tiled=True)  47.5 us
    all_to_all x5, starting transfers between devices, exchange(): return lax.all_to_all(parts, 'ctx', split_axis=0, concat_axis=0, tiled=True)  41.8 us
    ppermute x14, starting transfers between devices, core_shifted(): lax.ppermute(array, ('dp', 'tp'), [(d * size + (i + by) % size, d * size...  29.5 us
    ppermute x15, waiting for transfers between devices, shifted(): lax.ppermute(array, axis, [((i + by) % size, i) for i in range(size)])  27.8 us
    ppermute x15, starting transfers between devices, shifted(): lax.ppermute(array, axis, [((i + by) % size, i) for i in range(size)])  12.5 us
    ppermute x14, waiting for transfers between devices, core_shifted(): lax.ppermute(array, ('dp', 'tp'), [(d * size + (i + by) % size, d * size...  10.8 us
    ppermute x4, starting transfers between devices, passed_along(): return lax.ppermute(array, axis, pairs)  10.7 us
  transfers between devices with their start and end apart: 38, of which 12 were waited for; matrix products, arithmetic and copies ran while one was open for 4% of the time, Pallas kernels for 34%

profile of v5, /device:TPU:85, one launch (start us, length us, event | category | flops | bytes accessed | tf_op | source)
XLA Modules:
  0.0 309.2 jit_solution(13280837815657740706)
XLA Ops:
  0.6 2.2 collective-permute-start.3
  2.8 3.1 %collective-permute-start.4 = (bf16[2048,256]{1,0:T(8,128)(2,1)}, bf16[2048,256]{1,0:T(8,128)(2,1)S(1)}, u32[]{:S(2)}, u32[]{:S(2)}) collective-permute-start(bf16[2048,256]{1,0:T(8,128)(2,1)} %bitcast.42), channel_id=1, source_target_pairs={{67,64},{64,65},{65,66},{66,67},{71,68},{68,69},{69,70},{70,71},{7... | collective-permute-start | bytes 3145736 | tf_op jit(solution)/shard_map/ppermute | solution.py:613
  6.0 2.4 shard_map.121
  8.3 1.6 collective-permute-start.1
  11.1 5.3 %collective-permute-done.3.refs_5_ = bf16[2048,256]{1,0:T(8,128)(2,1)S(1)} collective-permute-done((bf16[2048,256]{1,0:T(8,128)(2,1)}, bf16[2048,256]{1,0:T(8,128)(2,1)S(1)}, u32[]{:S(2)}, u32[]{:S(2)}) %collective-permute-start.3) | collective-permute-done | bytes 1048608 | tf_op jit(solution)/shard_map/ppermute | solution.py:613
  17.3 2.2 collective-permute-start.5
  20.4 3.8 %collective-permute-start.6 = (bf16[1024,256]{1,0:T(8,128)(2,1)}, bf16[1024,256]{1,0:T(8,128)(2,1)}, u32[]{:S(2)}, u32[]{:S(2)}) collective-permute-start(bf16[1024,256]{1,0:T(8,128)(2,1)} %slice.37), channel_id=1, source_target_pairs={{67,64},{64,65},{65,66},{66,67},{71,68},{68,69},{69,70},{70,71},{7... | collective-permute-start | bytes 1572872 | tf_op jit(solution)/shard_map/ppermute | solution.py:613
  25.2 2.9 collective-permute-done.5.refs_7_
  28.1 2.5 collective-permute-done.6.refs_8_
  30.6 4.4 %collective-permute-start.7 = (bf16[256,256]{1,0:T(8,128)(2,1)}, bf16[256,256]{1,0:T(8,128)(2,1)S(1)}, u32[]{:S(2)}, u32[]{:S(2)}) collective-permute-start(bf16[256,256]{1,0:T(8,128)(2,1)} %get-tuple-element.103), channel_id=1, source_target_pairs={{65,64},{66,65},{67,66},{64,67},{69,68},{70,69},{71,70},{68,71},{7... | collective-permute-start | bytes 393224 | tf_op jit(solution)/shard_map/ppermute | solution.py:613
  35.0 4.3 %collective-permute-start.8 = (bf16[256,256]{1,0:T(8,128)(2,1)}, bf16[256,256]{1,0:T(8,128)(2,1)S(1)}, u32[]{:S(2)}, u32[]{:S(2)}) collective-permute-start(bf16[256,256]{1,0:T(8,128)(2,1)} %get-tuple-element.104), channel_id=1, source_target_pairs={{66,64},{67,65},{64,66},{65,67},{70,68},{71,69},{68,70},{69,71},{7... | collective-permute-start | bytes 393224 | tf_op jit(solution)/shard_map/ppermute | solution.py:613
  39.3 4.0 %collective-permute-start.9 = (bf16[256,256]{1,0:T(8,128)(2,1)}, bf16[256,256]{1,0:T(8,128)(2,1)S(1)}, u32[]{:S(2)}, u32[]{:S(2)}) collective-permute-start(bf16[256,256]{1,0:T(8,128)(2,1)} %get-tuple-element.105), channel_id=1, source_target_pairs={{67,64},{64,65},{65,66},{66,67},{71,68},{68,69},{69,70},{70,71},{7... | collective-permute-start | bytes 393224 | tf_op jit(solution)/shard_map/ppermute | solution.py:613
  44.6 3.9 %shard_map.120 = bf16[16384,128]{1,0:T(8,128)(2,1)} custom-call(s32[128]{0:T(128)} %reshape.106.idx_ref, bf16[2048,256]{1,0:T(8,128)(2,1)} %bitcast.26, bf16[2048,256]{1,0:T(8,128)(2,1)} %bitcast.34), custom_call_target="tpu_custom_call" | custom-call | bytes 10485760 | tf_op jit(solution)/shard_map/pallas_call | solution.py:55
  49.4 7.5 %all-to-all-start = ((bf16[16,1024,128]{2,1,0:T(8,128)(2,1)}), bf16[16,1024,128]{2,1,0:T(8,128)(2,1)}, u32[]{:S(2)}, u32[]{:S(2)}) async-start(bf16[16,1024,128]{2,1,0:T(8,128)(2,1)} %bitcast.39), calls=%async_computation | async-start | bytes 8388608 | tf_op jit(solution)/shard_map/all_to_all | solution.py:641
  58.4 3.9 %shard_map.119 = bf16[16384,128]{1,0:T(8,128)(2,1)} custom-call(s32[128]{0:T(128)} %reshape.106.idx_ref, bf16[2048,256]{1,0:T(8,128)(2,1)} %bitcast.27, bf16[2048,256]{1,0:T(8,128)(2,1)} %bitcast.35), custom_call_target="tpu_custom_call" | custom-call | bytes 10485760 | tf_op jit(solution)/shard_map/pallas_call | solution.py:55
  64.0 1.5 collective-permute-start.12
  67.1 1.8 shard_map.122.a
  72.1 17.0 %collective-permute-done.14.b = bf16[256,256]{1,0:T(8,128)(2,1)S(1)} collective-permute-done((bf16[256,256]{1,0:T(8,128)(2,1)}, bf16[256,256]{1,0:T(8,128)(2,1)S(1)}, u32[]{:S(2)}, u32[]{:S(2)}) %collective-permute-start.14) | collective-permute-done | bytes 131104 | tf_op jit(solution)/shard_map/ppermute | solution.py:592
  89.1 3.4 %collective-permute-done.16.d = bf16[256,256]{1,0:T(8,128)(2,1)S(1)} collective-permute-done((bf16[256,256]{1,0:T(8,128)(2,1)}, bf16[256,256]{1,0:T(8,128)(2,1)S(1)}, u32[]{:S(2)}, u32[]{:S(2)}) %collective-permute-start.16) | collective-permute-done | bytes 131104 | tf_op jit(solution)/shard_map/ppermute | solution.py:592
  93.2 1.8 shard_map.123
  95.7 11.6 %all-to-all-start.1 = ((bf16[16,1024,128]{2,1,0:T(8,128)(2,1)}), bf16[16,1024,128]{2,1,0:T(8,128)(2,1)}, u32[]{:S(2)}, u32[]{:S(2)}) async-start(bf16[16,1024,128]{2,1,0:T(8,128)(2,1)} %bitcast.38), calls=%async_computation.1 | async-start | bytes 8388608 | tf_op jit(solution)/shard_map/all_to_all | solution.py:641
  108.0 6.3 %shard_map.124.g_ref = bf16[2048,256]{1,0:T(8,128)(2,1)} custom-call(s32[2]{0:T(128)} %pad_add_fusion.at_ref, bf16[2048,256]{1,0:T(8,128)(2,1)} %bitcast.43, bf16[2048,256]{1,0:T(8,128)(2,1)} %copy-done.7, bf16[2048,256]{1,0:T(8,128)(2,1)} %copy-done.8, bf16[1024,256]{1,0:T(8,128)(2,1)} %collective-permute-done.12.refs_3_, bf16[1024,256]{1,0:T(8,128)(2,1)} %copy-done.12, ...), custom_call_target="tpu_custom_call" | custom-call | flops 1073741824 | bytes 16777216 | tf_op jit(solution)/shard_map/pallas_call | solution.py:175
  114.9 27.1 %shard_map.125 = (bf16[2048,128]{1,0:T(8,128)(2,1)}, bf16[2048,256]{1,0:T(8,128)(2,1)}, f32[2,2048,128]{2,1,0:T(8,128)}, bf16[2,64,128]{2,1,0:T(8,128)(2,1)}, bf...) custom-call(s32[1]{0:T(128)} %bitcast.me_ref, ...), custom_call_target="tpu_custom_call" | custom-call | flops 6442450944 | bytes 83886080 | tf_op jit(solution)/shard_map/pallas_call | solution.py:308
  145.5 4.7 %collective-permute-done.20.refs_1_ = bf16[2048,128]{1,0:T(8,128)(2,1)S(1)} collective-permute-done((bf16[2048,128]{1,0:T(8,128)(2,1)}, bf16[2048,128]{1,0:T(8,128)(2,1)S(1)}, u32[]{:S(2)}, u32[]{:S(2)}) %collective-permute-start.20) | collective-permute-done | bytes 524320 | tf_op jit(solution)/shard_map/ppermute | solution.py:592
  150.4 6.7 %all-to-all-start.2 = ((bf16[16,1024,128]{2,1,0:T(8,128)(2,1)}), bf16[16,1024,128]{2,1,0:T(8,128)(2,1)}, u32[]{:S(2)}, u32[]{:S(2)}) async-start(bf16[16,1024,128]{2,1,0:T(8,128)(2,1)} %bitcast.40), calls=%async_computation.2 | async-start | bytes 8388608 | tf_op jit(solution)/shard_map/all_to_all | solution.py:641
  157.1 27.5 %shard_map.126 = (bf16[2048,128]{1,0:T(8,128)(2,1)}, bf16[2048,256]{1,0:T(8,128)(2,1)}, f32[2,2048,128]{2,1,0:T(8,128)}, bf16[2,64,128]{2,1,0:T(8,128)(2,1)}, bf...) custom-call(s32[1]{0:T(128)} %bitcast.me_ref, ...), custom_call_target="tpu_custom_call", output_to_operand_aliasing={{1}: (12, {})} | custom-call | flops 6442450944 | bytes 83886080 | tf_op jit(solution)/shard_map/pallas_call | solution.py:308
  186.3 2.2 collective-permute-start.24
  188.5 3.3 %collective-permute-start.25 = (bf16[2,64,128]{2,1,0:T(8,128)(2,1)S(1)}, bf16[2,64,128]{2,1,0:T(8,128)(2,1)}, u32[]{:S(2)}, u32[]{:S(2)}) collective-permute-start(bf16[2,64,128]{2,1,0:T(8,128)(2,1)S(1)} %copy-done.29), channel_id=1, source_target_pairs={{0,4},{4,8},{8,12},{12,16},{16,20},{20,24},{24,28},{28,32},{32,36}... | collective-permute-start | bytes 98312 | tf_op jit(solution)/shard_map/ppermute | solution.py:608
  191.8 6.4 %shard_map.127.terms_ref = bf16[256,1024]{1,0:T(8,128)(2,1)} custom-call(s32[2]{0:T(128)} %pad_add_fusion.at_ref, bf16[2048,128]{1,0:T(8,128)(2,1)} %get-tuple-element.129.c0.refs_0_, bf16[2048,128]{1,0:T(8,128)(2,1)} %get-tuple-element.162.c1.refs_5_, bf16[2048,256]{1,0:T(8,128)(2,1)} %bitcast.44, bf16[2048,256]{1,0:T(8,128)(2,1)} %copy-done.7, ...), custom_call_target="tpu_custom_call" | custom-call | flops 1073741824 | bytes 16777216 | tf_op jit(solution)/shard_map/pallas_call | solution.py:483
  198.2 2.1 shard_map.128
  200.3 3.7 %all-to-all-done.2.back_ref = bf16[16,1024,128]{2,1,0:T(8,128)(2,1)} async-done(((bf16[16,1024,128]{2,1,0:T(8,128)(2,1)}), bf16[16,1024,128]{2,1,0:T(8,128)(2,1)}, u32[]{:S(2)}, u32[]{:S(2)}) %all-to-all-start.2) | async-done | bytes 4194336 | tf_op jit(solution)/shard_map/all_to_all | solution.py:641
  204.0 8.9 %all-to-all-start.3 = ((bf16[16,672,128]{2,1,0:T(8,128)(2,1)}), bf16[16,672,128]{2,1,0:T(8,128)(2,1)S(1)}, u32[]{:S(2)}, u32[]{:S(2)}) async-start(bf16[16,672,128]{2,1,0:T(8,128)(2,1)} %shard_map.128), calls=%async_computation.3 | async-start | bytes 5505024 | tf_op jit(solution)/shard_map/all_to_all | solution.py:641
  212.9 1.7 slice.33
  215.9 1.7 slice.34
  218.3 2.2 collective-permute-start.28
  220.5 3.1 %collective-permute-start.29 = (bf16[2,64,128]{2,1,0:T(8,128)(2,1)}, bf16[2,64,128]{2,1,0:T(8,128)(2,1)}, u32[]{:S(2)}, u32[]{:S(2)}) collective-permute-start(bf16[2,64,128]{2,1,0:T(8,128)(2,1)} %get-tuple-element.151), channel_id=1, source_target_pairs={{0,4},{4,8},{8,12},{12,16},{16,20},{20,24},{24,28},{28,32},{32,36}... | collective-permute-start | bytes 98312 | tf_op jit(solution)/shard_map/ppermute | solution.py:608
  223.6 4.7 %shard_map.130 = (bf16[2048,128]{1,0:T(8,128)(2,1)}, bf16[2048,128]{1,0:T(8,128)(2,1)}, f32[2,2,64,128]{3,2,1,0:T(8,128)}) custom-call(s32[128]{0:T(128)} %reshape.106.idx_ref, s32[16]{0:T(128)} %reduce_sum.47.used_ref, s32[2]{0:T(128)} %bitcast.51, f32[2,2048,128]{2,1,0:T(8,128)} %get-tuple-element.155.win_ref, ...), custom_call_target="tpu_custom_call" | custom-call | flops 4194304 | bytes 16777216 | tf_op jit(solution)/shard_map/pallas_call | solution.py:419
  228.3 19.3 %all-to-all-done.3.back_ref = bf16[16,672,128]{2,1,0:T(8,128)(2,1)S(1)} async-done(((bf16[16,672,128]{2,1,0:T(8,128)(2,1)}), bf16[16,672,128]{2,1,0:T(8,128)(2,1)S(1)}, u32[]{:S(2)}, u32[]{:S(2)}) %all-to-all-start.3) | async-done | bytes 2752544 | tf_op jit(solution)/shard_map/all_to_all | solution.py:641
  247.6 1.5 copy-done.2
  249.1 2.0 shard_map.129
  251.9 7.1 %all-to-all-start.4 = ((bf16[16,672,128]{2,1,0:T(8,128)(2,1)}), bf16[16,672,128]{2,1,0:T(8,128)(2,1)S(1)}, u32[]{:S(2)}, u32[]{:S(2)}) async-start(bf16[16,672,128]{2,1,0:T(8,128)(2,1)} %shard_map.129), calls=%async_computation.4 | async-start | bytes 5505024 | tf_op jit(solution)/shard_map/all_to_all | solution.py:641
  260.1 1.5 collective-permute-start.23
  261.6 4.3 %shard_map.132.win_ref = f32[2,2048,128]{2,1,0:T(8,128)} custom-call(s32[128]{0:T(128)} %reshape.106.idx_ref, s32[16]{0:T(128)} %reduce_sum.47.used_ref, f32[2,2048,128]{2,1,0:T(8,128)} %get-tuple-element.174.win_ref, bf16[16,672,128]{2,1,0:T(8,128)(2,1)} %copy-done.2, bf16[2,64,128]{2,1,0:T(8,128)(2,1)} %collective-permute-done.28.up_ref, ...), custom_call_target="tpu_custom_call" | custom-call | flops 4194304 | bytes 14680064 | tf_op jit(solution)/shard_map/pallas_call | solution.py:432
  265.9 1.4 collective-permute-done.22.refs_3_
  269.1 6.1 %shard_map.131 = bf16[2048,256]{1,0:T(8,128)(2,1)} custom-call(bf16[2048,128]{1,0:T(8,128)(2,1)} %get-tuple-element.129.c0.refs_0_, bf16[2048,128]{1,0:T(8,128)(2,1)} %copy-done.13, bf16[2048,128]{1,0:T(8,128)(2,1)} %collective-permute-done.21.refs_2_, bf16[1024,128]{1,0:T(8,128)(2,1)} %copy-done.16, bf16[1024,128]{1,0:T(8,128)(2,1)} %copy-done.17, ...), custom_call_target="tpu_custom_call" | custom-call | flops 1073741824 | bytes 18874368 | tf_op jit(solution)/shard_map/pallas_call | solution.py:579
  275.2 24.5 %all-to-all-done.4.back_ref = bf16[16,672,128]{2,1,0:T(8,128)(2,1)S(1)} async-done(((bf16[16,672,128]{2,1,0:T(8,128)(2,1)}), bf16[16,672,128]{2,1,0:T(8,128)(2,1)S(1)}, u32[]{:S(2)}, u32[]{:S(2)}) %all-to-all-start.4) | async-done | bytes 2752544 | tf_op jit(solution)/shard_map/all_to_all | solution.py:641
  301.2 4.9 %shard_map.133 = (bf16[2048,256]{1,0:T(8,128)(2,1)}, bf16[2048,256]{1,0:T(8,128)(2,1)}) custom-call(s32[128]{0:T(128)} %reshape.106.idx_ref, s32[16]{0:T(128)} %reduce_sum.47.used_ref, s32[2]{0:T(128)} %bitcast.52, s32[1]{0:T(128)} %bitcast.me_ref, f32[2,2048,128]{2,1,0:T(8,128)} %shard_map.132.win_ref, bf16[16,672,128]{2,1,0:T(8,128)(2,1)} %copy-done.3, ...), custom_call_target="tpu_custom_call" | custom-call | flops 4194304 | bytes 12582912 | tf_op jit(solution)/shard_map/pallas_call | solution.py:448
  306.9 2.3 shard_map.134
  (135 shorter events, 29.9 us)
Async XLA Ops:
  0.6 61.7 %copy-start = (s32[1,512,3]{1,0,2:T(1,128)S(1)}, s32[1,512,3]{1,0,2:T(1,128)}, u32[]{:S(2)}) copy-start(s32[1,512,3]{1,0,2:T(1,128)} %param.14) | copy-start | bytes 18436
  0.6 15.8 %collective-permute-start.3 = (bf16[2048,256]{1,0:T(8,128)(2,1)}, bf16[2048,256]{1,0:T(8,128)(2,1)S(1)}, u32[]{:S(2)}, u32[]{:S(2)}) collective-permute-start(bf16[2048,256]{1,0:T(8,128)(2,1)} %bitcast.41), channel_id=1, source_target_pairs={{65,64},{66,65},{67,66},{64,67},{69,68},{70,69},{71,70},{68,71},{7... | collective-permute-start | bytes 3145736 | tf_op jit(solution)/shard_map/ppermute | solution.py:613
  2.8 16.6 %collective-permute-start.4 = (bf16[2048,256]{1,0:T(8,128)(2,1)}, bf16[2048,256]{1,0:T(8,128)(2,1)S(1)}, u32[]{:S(2)}, u32[]{:S(2)}) collective-permute-start(bf16[2048,256]{1,0:T(8,128)(2,1)} %bitcast.42), channel_id=1, source_target_pairs={{67,64},{64,65},{65,66},{66,67},{71,68},{68,69},{69,70},{70,71},{7... | collective-permute-start | bytes 3145736 | tf_op jit(solution)/shard_map/ppermute | solution.py:613
  8.3 16.0 %copy-start.4 = (bf16[256,1024]{1,0:T(8,128)(2,1)S(1)}, bf16[256,1024]{1,0:T(8,128)(2,1)}, u32[]{:S(2)}) copy-start(bf16[256,1024]{1,0:T(8,128)(2,1)} %refs_12_.1) | copy-start | bytes 1572868
  8.3 31.0 %collective-permute-start = (bf16[256,256]{1,0:T(8,128)(2,1)}, bf16[256,256]{1,0:T(8,128)(2,1)}, u32[]{:S(2)}, u32[]{:S(2)}) collective-permute-start(bf16[256,256]{1,0:T(8,128)(2,1)} %get-tuple-element.112.a), channel_id=1, source_target_pairs={{8,0},{12,4},{16,8},{20,12},{24,16},{28,20},{32,24},{36,28},{40,32... | collective-permute-start | bytes 393224 | tf_op jit(solution)/shard_map/ppermute | solution.py:592
  8.3 40.2 %collective-permute-start.1 = (bf16[384,256]{1,0:T(8,128)(2,1)}, bf16[384,256]{1,0:T(8,128)(2,1)S(1)}, u32[]{:S(2)}, u32[]{:S(2)}) collective-permute-start(bf16[384,256]{1,0:T(8,128)(2,1)} %get-tuple-element.97), channel_id=1, source_target_pairs={{60,0},{0,4},{4,8},{8,12},{12,16},{16,20},{20,24},{24,28},{28,32},... | collective-permute-start | bytes 589832 | tf_op jit(solution)/shard_map/ppermute | solution.py:592
  10.0 38.6 %collective-permute-start.2 = (bf16[384,256]{1,0:T(8,128)(2,1)}, bf16[384,256]{1,0:T(8,128)(2,1)}, u32[]{:S(2)}, u32[]{:S(2)}) collective-permute-start(bf16[384,256]{1,0:T(8,128)(2,1)} %get-tuple-element.98), channel_id=1, source_target_pairs={{4,0},{8,4},{12,8},{16,12},{20,16},{24,20},{28,24},{32,28},{36,32}... | collective-permute-start | bytes 589832 | tf_op jit(solution)/shard_map/ppermute | solution.py:592
  16.4 32.1 %copy-start.5 = (bf16[2048,256]{1,0:T(8,128)(2,1)}, bf16[2048,256]{1,0:T(8,128)(2,1)S(1)}, u32[]{:S(2)}) copy-start(bf16[2048,256]{1,0:T(8,128)(2,1)S(1)} %collective-permute-done.3.refs_5_) | copy-start | bytes 3145732
  17.3 10.8 %collective-permute-start.5 = (bf16[1024,256]{1,0:T(8,128)(2,1)}, bf16[1024,256]{1,0:T(8,128)(2,1)S(1)}, u32[]{:S(2)}, u32[]{:S(2)}) collective-permute-start(bf16[1024,256]{1,0:T(8,128)(2,1)} %slice.36), channel_id=1, source_target_pairs={{65,64},{66,65},{67,66},{64,67},{69,68},{70,69},{71,70},{68,71},{7... | collective-permute-start | bytes 1572872 | tf_op jit(solution)/shard_map/ppermute | solution.py:613
  19.5 29.0 %copy-start.6 = (bf16[2048,256]{1,0:T(8,128)(2,1)}, bf16[2048,256]{1,0:T(8,128)(2,1)S(1)}, u32[]{:S(2)}) copy-start(bf16[2048,256]{1,0:T(8,128)(2,1)S(1)} %collective-permute-done.4.refs_6_) | copy-start | bytes 3145732
  20.4 10.2 %collective-permute-start.6 = (bf16[1024,256]{1,0:T(8,128)(2,1)}, bf16[1024,256]{1,0:T(8,128)(2,1)}, u32[]{:S(2)}, u32[]{:S(2)}) collective-permute-start(bf16[1024,256]{1,0:T(8,128)(2,1)} %slice.37), channel_id=1, source_target_pairs={{67,64},{64,65},{65,66},{66,67},{71,68},{68,69},{69,70},{70,71},{7... | collective-permute-start | bytes 1572872 | tf_op jit(solution)/shard_map/ppermute | solution.py:613
  28.1 20.4 %copy-start.11 = (bf16[1024,256]{1,0:T(8,128)(2,1)}, bf16[1024,256]{1,0:T(8,128)(2,1)S(1)}, u32[]{:S(2)}) copy-start(bf16[1024,256]{1,0:T(8,128)(2,1)S(1)} %collective-permute-done.5.refs_7_) | copy-start | bytes 1572868
  30.6 17.9 %collective-permute-start.7 = (bf16[256,256]{1,0:T(8,128)(2,1)}, bf16[256,256]{1,0:T(8,128)(2,1)S(1)}, u32[]{:S(2)}, u32[]{:S(2)}) collective-permute-start(bf16[256,256]{1,0:T(8,128)(2,1)} %get-tuple-element.103), channel_id=1, source_target_pairs={{65,64},{66,65},{67,66},{64,67},{69,68},{70,69},{71,70},{68,71},{7... | collective-permute-start | bytes 393224 | tf_op jit(solution)/shard_map/ppermute | solution.py:613
  35.0 13.6 %collective-permute-start.8 = (bf16[256,256]{1,0:T(8,128)(2,1)}, bf16[256,256]{1,0:T(8,128)(2,1)S(1)}, u32[]{:S(2)}, u32[]{:S(2)}) collective-permute-start(bf16[256,256]{1,0:T(8,128)(2,1)} %get-tuple-element.104), channel_id=1, source_target_pairs={{66,64},{67,65},{64,66},{65,67},{70,68},{71,69},{68,70},{69,71},{7... | collective-permute-start | bytes 393224 | tf_op jit(solution)/shard_map/ppermute | solution.py:613
  39.3 9.3 %collective-permute-start.9 = (bf16[256,256]{1,0:T(8,128)(2,1)}, bf16[256,256]{1,0:T(8,128)(2,1)S(1)}, u32[]{:S(2)}, u32[]{:S(2)}) collective-permute-start(bf16[256,256]{1,0:T(8,128)(2,1)} %get-tuple-element.105), channel_id=1, source_target_pairs={{67,64},{64,65},{65,66},{66,67},{71,68},{68,69},{69,70},{70,71},{7... | collective-permute-start | bytes 393224 | tf_op jit(solution)/shard_map/ppermute | solution.py:613
  49.4 45.6 %all-to-all-start = ((bf16[16,1024,128]{2,1,0:T(8,128)(2,1)}), bf16[16,1024,128]{2,1,0:T(8,128)(2,1)}, u32[]{:S(2)}, u32[]{:S(2)}) async-start(bf16[16,1024,128]{2,1,0:T(8,128)(2,1)} %bitcast.39), calls=%async_computation | async-start | bytes 8388608 | tf_op jit(solution)/shard_map/all_to_all | solution.py:641
  56.9 6.2 %collective-permute-start.10 = (bf16[2048,256]{1,0:T(8,128)(2,1)S(1)}, bf16[2048,256]{1,0:T(8,128)(2,1)S(1)}, u32[]{:S(2)}, u32[]{:S(2)}) collective-permute-start(bf16[2048,256]{1,0:T(8,128)(2,1)S(1)} %bitcast.45), channel_id=1, source_target_pairs={{1,0},{2,1},{3,2},{0,3},{5,4},{6,5},{7,6},{4,7},{9,8},{10,9},{11,1... | collective-permute-start | bytes 3145736 | tf_op jit(solution)/shard_map/ppermute | solution.py:613
  57.6 7.8 %collective-permute-start.11 = (bf16[2048,256]{1,0:T(8,128)(2,1)S(1)}, bf16[2048,256]{1,0:T(8,128)(2,1)S(1)}, u32[]{:S(2)}, u32[]{:S(2)}) collective-permute-start(bf16[2048,256]{1,0:T(8,128)(2,1)S(1)} %bitcast.46), channel_id=1, source_target_pairs={{3,0},{0,1},{1,2},{2,3},{7,4},{4,5},{5,6},{6,7},{11,8},{8,9},{9,10... | collective-permute-start | bytes 3145736 | tf_op jit(solution)/shard_map/ppermute | solution.py:613
  63.1 31.9 %copy-start.7 = (bf16[2048,256]{1,0:T(8,128)(2,1)}, bf16[2048,256]{1,0:T(8,128)(2,1)S(1)}, u32[]{:S(2)}) copy-start(bf16[2048,256]{1,0:T(8,128)(2,1)S(1)} %collective-permute-done.10.refs_1_) | copy-start | bytes 3145732
  64.0 31.0 %collective-permute-start.12 = (bf16[1024,256]{1,0:T(8,128)(2,1)}, bf16[1024,256]{1,0:T(8,128)(2,1)}, u32[]{:S(2)}, u32[]{:S(2)}) collective-permute-start(bf16[1024,256]{1,0:T(8,128)(2,1)} %slice.38), channel_id=1, source_target_pairs={{1,0},{2,1},{3,2},{0,3},{5,4},{6,5},{7,6},{4,7},{9,8},{10,9},{11,1... | collective-permute-start | bytes 1572872 | tf_op jit(solution)/shard_map/ppermute | solution.py:613
  65.4 29.5 %copy-start.8 = (bf16[2048,256]{1,0:T(8,128)(2,1)}, bf16[2048,256]{1,0:T(8,128)(2,1)S(1)}, u32[]{:S(2)}) copy-start(bf16[2048,256]{1,0:T(8,128)(2,1)S(1)} %collective-permute-done.11.refs_2_) | copy-start | bytes 3145732
  65.5 29.5 %collective-permute-start.13 = (bf16[1024,256]{1,0:T(8,128)(2,1)S(1)}, bf16[1024,256]{1,0:T(8,128)(2,1)S(1)}, u32[]{:S(2)}, u32[]{:S(2)}) collective-permute-start(bf16[1024,256]{1,0:T(8,128)(2,1)S(1)} %slice.39), channel_id=1, source_target_pairs={{3,0},{0,1},{1,2},{2,3},{7,4},{4,5},{5,6},{6,7},{11,8},{8,9},{9,10... | collective-permute-start | bytes 1572872 | tf_op jit(solution)/shard_map/ppermute | solution.py:613
  68.9 20.2 %collective-permute-start.14 = (bf16[256,256]{1,0:T(8,128)(2,1)}, bf16[256,256]{1,0:T(8,128)(2,1)S(1)}, u32[]{:S(2)}, u32[]{:S(2)}) collective-permute-start(bf16[256,256]{1,0:T(8,128)(2,1)} %shard_map.122.a), channel_id=1, source_target_pairs={{16,0},{20,4},{24,8},{28,12},{32,16},{36,20},{40,24},{44,28},{48,3... | collective-permute-start | bytes 393224 | tf_op jit(solution)/shard_map/ppermute | solution.py:592
  69.2 19.9 %collective-permute-start.15 = (bf16[256,256]{1,0:T(8,128)(2,1)}, bf16[256,256]{1,0:T(8,128)(2,1)S(1)}, u32[]{:S(2)}, u32[]{:S(2)}) collective-permute-start(bf16[256,256]{1,0:T(8,128)(2,1)} %shard_map.122.a), channel_id=1, source_target_pairs={{48,0},{52,4},{56,8},{60,12},{0,16},{4,20},{8,24},{12,28},{16,32},... | collective-permute-start | bytes 393224 | tf_op jit(solution)/shard_map/ppermute | solution.py:592
  70.3 22.2 %collective-permute-start.16 = (bf16[256,256]{1,0:T(8,128)(2,1)}, bf16[256,256]{1,0:T(8,128)(2,1)S(1)}, u32[]{:S(2)}, u32[]{:S(2)}) collective-permute-start(bf16[256,256]{1,0:T(8,128)(2,1)} %shard_map.122.a), channel_id=1, source_target_pairs={{32,0},{36,4},{40,8},{44,12},{48,16},{52,20},{56,24},{60,28},{0,32... | collective-permute-start | bytes 393224 | tf_op jit(solution)/shard_map/ppermute | solution.py:592
  95.7 54.6 %all-to-all-start.1 = ((bf16[16,1024,128]{2,1,0:T(8,128)(2,1)}), bf16[16,1024,128]{2,1,0:T(8,128)(2,1)}, u32[]{:S(2)}, u32[]{:S(2)}) async-start(bf16[16,1024,128]{2,1,0:T(8,128)(2,1)} %bitcast.38), calls=%async_computation.1 | async-start | bytes 8388608 | tf_op jit(solution)/shard_map/all_to_all | solution.py:641
  141.9 8.2 %collective-permute-start.20 = (bf16[2048,128]{1,0:T(8,128)(2,1)}, bf16[2048,128]{1,0:T(8,128)(2,1)S(1)}, u32[]{:S(2)}, u32[]{:S(2)}) collective-permute-start(bf16[2048,128]{1,0:T(8,128)(2,1)} %get-tuple-element.129.c0.refs_0_), channel_id=1, source_target_pairs={{1,0},{2,1},{3,2},{0,3},{5,4},{6,5},{7,6},{4,7},{9,8},{10,9},{11,1... | collective-permute-start | bytes 1572872 | tf_op jit(solution)/shard_map/ppermute | solution.py:592
  142.0 8.3 %collective-permute-start.21 = (bf16[2048,128]{1,0:T(8,128)(2,1)}, bf16[2048,128]{1,0:T(8,128)(2,1)}, u32[]{:S(2)}, u32[]{:S(2)}) collective-permute-start(bf16[2048,128]{1,0:T(8,128)(2,1)} %get-tuple-element.129.c0.refs_0_), channel_id=1, source_target_pairs={{3,0},{0,1},{1,2},{2,3},{7,4},{4,5},{5,6},{6,7},{11,8},{8,9},{9,10... | collective-permute-start | bytes 1572872 | tf_op jit(solution)/shard_map/ppermute | solution.py:592
  143.4 2.0 collective-permute-start.17
  144.1 1.4 collective-permute-start.18
  144.7 0.7 collective-permute-start.19
  150.2 108.8 %copy-start.13 = (bf16[2048,128]{1,0:T(8,128)(2,1)}, bf16[2048,128]{1,0:T(8,128)(2,1)S(1)}, u32[]{:S(2)}) copy-start(bf16[2048,128]{1,0:T(8,128)(2,1)S(1)} %collective-permute-done.20.refs_1_) | copy-start | bytes 1572868
  150.4 53.6 %all-to-all-start.2 = ((bf16[16,1024,128]{2,1,0:T(8,128)(2,1)}), bf16[16,1024,128]{2,1,0:T(8,128)(2,1)}, u32[]{:S(2)}, u32[]{:S(2)}) async-start(bf16[16,1024,128]{2,1,0:T(8,128)(2,1)} %bitcast.40), calls=%async_computation.2 | async-start | bytes 8388608 | tf_op jit(solution)/shard_map/all_to_all | solution.py:641
  157.0 29.3 %copy-start.30 = (bf16[2,64,128]{2,1,0:T(8,128)(2,1)S(1)}, bf16[2,64,128]{2,1,0:T(8,128)(2,1)}, u32[]{:S(2)}) copy-start(bf16[2,64,128]{2,1,0:T(8,128)(2,1)} %get-tuple-element.146) | copy-start | bytes 98308
  157.0 31.5 %copy-start.29 = (bf16[2,64,128]{2,1,0:T(8,128)(2,1)S(1)}, bf16[2,64,128]{2,1,0:T(8,128)(2,1)}, u32[]{:S(2)}) copy-start(bf16[2,64,128]{2,1,0:T(8,128)(2,1)} %get-tuple-element.147) | copy-start | bytes 98308
  184.5 15.7 %collective-permute-start.26 = (bf16[2048,128]{1,0:T(8,128)(2,1)}, bf16[2048,128]{1,0:T(8,128)(2,1)}, u32[]{:S(2)}, u32[]{:S(2)}) collective-permute-start(bf16[2048,128]{1,0:T(8,128)(2,1)} %get-tuple-element.162.c1.refs_5_), channel_id=1, source_target_pairs={{1,0},{2,1},{3,2},{0,3},{5,4},{6,5},{7,6},{4,7},{9,8},{10,9},{11,1... | collective-permute-start | bytes 1572872 | tf_op jit(solution)/shard_map/ppermute | solution.py:592
  185.4 14.8 %collective-permute-start.27 = (bf16[2048,128]{1,0:T(8,128)(2,1)}, bf16[2048,128]{1,0:T(8,128)(2,1)}, u32[]{:S(2)}, u32[]{:S(2)}) collective-permute-start(bf16[2048,128]{1,0:T(8,128)(2,1)} %get-tuple-element.162.c1.refs_5_), channel_id=1, source_target_pairs={{3,0},{0,1},{1,2},{2,3},{7,4},{4,5},{5,6},{6,7},{11,8},{8,9},{9,10... | collective-permute-start | bytes 1572872 | tf_op jit(solution)/shard_map/ppermute | solution.py:592
  186.3 14.0 %collective-permute-start.24 = (bf16[2,64,128]{2,1,0:T(8,128)(2,1)S(1)}, bf16[2,64,128]{2,1,0:T(8,128)(2,1)}, u32[]{:S(2)}, u32[]{:S(2)}) collective-permute-start(bf16[2,64,128]{2,1,0:T(8,128)(2,1)S(1)} %copy-done.30), channel_id=1, source_target_pairs={{4,0},{8,4},{12,8},{16,12},{20,16},{24,20},{28,24},{32,28},{36,32}... | collective-permute-start | bytes 98312 | tf_op jit(solution)/shard_map/ppermute | solution.py:608
  188.5 11.8 %collective-permute-start.25 = (bf16[2,64,128]{2,1,0:T(8,128)(2,1)S(1)}, bf16[2,64,128]{2,1,0:T(8,128)(2,1)}, u32[]{:S(2)}, u32[]{:S(2)}) collective-permute-start(bf16[2,64,128]{2,1,0:T(8,128)(2,1)S(1)} %copy-done.29), channel_id=1, source_target_pairs={{0,4},{4,8},{8,12},{12,16},{16,20},{20,24},{24,28},{28,32},{32,36}... | collective-permute-start | bytes 98312 | tf_op jit(solution)/shard_map/ppermute | solution.py:608
  204.0 43.6 %all-to-all-start.3 = ((bf16[16,672,128]{2,1,0:T(8,128)(2,1)}), bf16[16,672,128]{2,1,0:T(8,128)(2,1)S(1)}, u32[]{:S(2)}, u32[]{:S(2)}) async-start(bf16[16,672,128]{2,1,0:T(8,128)(2,1)} %shard_map.128), calls=%async_computation.3 | async-start | bytes 5505024 | tf_op jit(solution)/shard_map/all_to_all | solution.py:641
  214.5 36.7 %collective-permute-start.30 = (bf16[1024,128]{1,0:T(8,128)(2,1)}, bf16[1024,128]{1,0:T(8,128)(2,1)S(1)}, u32[]{:S(2)}, u32[]{:S(2)}) collective-permute-start(bf16[1024,128]{1,0:T(8,128)(2,1)} %slice.33), channel_id=1, source_target_pairs={{1,0},{2,1},{3,2},{0,3},{5,4},{6,5},{7,6},{4,7},{9,8},{10,9},{11,1... | collective-permute-start | bytes 786440 | tf_op jit(solution)/shard_map/ppermute | solution.py:592
  217.6 33.6 %collective-permute-start.31 = (bf16[1024,128]{1,0:T(8,128)(2,1)}, bf16[1024,128]{1,0:T(8,128)(2,1)}, u32[]{:S(2)}, u32[]{:S(2)}) collective-permute-start(bf16[1024,128]{1,0:T(8,128)(2,1)} %slice.34), channel_id=1, source_target_pairs={{3,0},{0,1},{1,2},{2,3},{7,4},{4,5},{5,6},{6,7},{11,8},{8,9},{9,10... | collective-permute-start | bytes 786440 | tf_op jit(solution)/shard_map/ppermute | solution.py:592
  218.3 32.9 %collective-permute-start.28 = (bf16[2,64,128]{2,1,0:T(8,128)(2,1)}, bf16[2,64,128]{2,1,0:T(8,128)(2,1)}, u32[]{:S(2)}, u32[]{:S(2)}) collective-permute-start(bf16[2,64,128]{2,1,0:T(8,128)(2,1)} %get-tuple-element.150), channel_id=1, source_target_pairs={{4,0},{8,4},{12,8},{16,12},{20,16},{24,20},{28,24},{32,28},{36,32}... | collective-permute-start | bytes 98312 | tf_op jit(solution)/shard_map/ppermute | solution.py:608
  220.5 30.7 %collective-permute-start.29 = (bf16[2,64,128]{2,1,0:T(8,128)(2,1)}, bf16[2,64,128]{2,1,0:T(8,128)(2,1)}, u32[]{:S(2)}, u32[]{:S(2)}) collective-permute-start(bf16[2,64,128]{2,1,0:T(8,128)(2,1)} %get-tuple-element.151), channel_id=1, source_target_pairs={{0,4},{4,8},{8,12},{12,16},{16,20},{20,24},{24,28},{28,32},{32,36}... | collective-permute-start | bytes 98312 | tf_op jit(solution)/shard_map/ppermute | solution.py:608
  251.9 47.8 %all-to-all-start.4 = ((bf16[16,672,128]{2,1,0:T(8,128)(2,1)}), bf16[16,672,128]{2,1,0:T(8,128)(2,1)S(1)}, u32[]{:S(2)}, u32[]{:S(2)}) async-start(bf16[16,672,128]{2,1,0:T(8,128)(2,1)} %shard_map.129), calls=%async_computation.4 | async-start | bytes 5505024 | tf_op jit(solution)/shard_map/all_to_all | solution.py:641
  259.0 8.3 %collective-permute-start.22 = (bf16[1024,128]{1,0:T(8,128)(2,1)S(1)}, bf16[1024,128]{1,0:T(8,128)(2,1)S(1)}, u32[]{:S(2)}, u32[]{:S(2)}) collective-permute-start(bf16[1024,128]{1,0:T(8,128)(2,1)S(1)} %slice.31), channel_id=1, source_target_pairs={{1,0},{2,1},{3,2},{0,3},{5,4},{6,5},{7,6},{4,7},{9,8},{10,9},{11,1... | collective-permute-start | bytes 786440 | tf_op jit(solution)/shard_map/ppermute | solution.py:592
  260.1 8.3 %collective-permute-start.23 = (bf16[1024,128]{1,0:T(8,128)(2,1)S(1)}, bf16[1024,128]{1,0:T(8,128)(2,1)S(1)}, u32[]{:S(2)}, u32[]{:S(2)}) collective-permute-start(bf16[1024,128]{1,0:T(8,128)(2,1)S(1)} %slice.32), channel_id=1, source_target_pairs={{3,0},{0,1},{1,2},{2,3},{7,4},{4,5},{5,6},{6,7},{11,8},{8,9},{9,10... | collective-permute-start | bytes 786440 | tf_op jit(solution)/shard_map/ppermute | solution.py:592
  299.7 6.4 %collective-permute-start.32 = (bf16[16,128,128]{2,1,0:T(8,128)(2,1)S(1)}, bf16[16,128,128]{2,1,0:T(8,128)(2,1)S(1)}, u32[]{:S(2)}, u32[]{:S(2)}) collective-permute-start(bf16[16,128,128]{2,1,0:T(8,128)(2,1)S(1)} %slice.35.own_ref), channel_id=1, source_target_pairs={{64,0},{0,64},{65,1},{1,65},{66,2},{2,66},{67,3},{3,67},{68,4},{4,... | collective-permute-start | bytes 1572872 | tf_op jit(solution)/shard_map/ppermute | solution.py:592
  (21 other events, 60.7 us)

commit v6 on v4

--- a/solution.py
+++ b/solution.py
@@ -136,33 +136,13 @@
     return own[...], following[...], jnp.where(top, upper[...], lower[...]), previous[...]
 
 
-def pair_specs(rows, width):
-    last = rows // TILE // 2
-    specs = [pl.BlockSpec((TILE, width), lambda i, at: (i, 0))]
-    for d in range(2):
-        full = pl.BlockSpec((TILE, width), functools.partial(lambda d, i, at: (jnp.where(at[1] == d, i, 0), 0), d))
-        upper = functools.partial(lambda d, i, at: (jnp.where(at[1] == d, jnp.minimum(i, last - 1), 0), 0), d)
-        lower = functools.partial(lambda d, i, at: (jnp.where(at[1] == d, jnp.maximum(i - last, 0), 0), 0), d)
-        specs += [full, full, pl.BlockSpec((TILE, width), upper), pl.BlockSpec((TILE, width), lower)]
-    return specs
-
-
-def pair_values(at_ref, refs):
-    top = pl.program_id(0) < pl.num_programs(0) // 2
-    zero = at_ref[1] == 0
-
-    def chosen(j):
-        return jnp.where(zero, refs[1 + j][...], refs[5 + j][...])
-
-    return refs[0][...], chosen(0), jnp.where(top, chosen(2), chosen(3)), chosen(1)
-
-
 def grad_context_kernel(at_ref, *refs):
+    del at_ref
     total = None
-    for g, w in zip(pair_values(at_ref, refs[:9]), refs[9:13]):
+    for g, w in zip(ring_values(refs[:5]), refs[5:9]):
         term = dot(g, w[...], NT)
         total = term if total is None else total + term
-    refs[13][...] = total.astype(jnp.bfloat16)
+    refs[9][...] = total.astype(jnp.bfloat16)
 
 
 def grad_context_of(at, pieces, weight):
@@ -177,7 +157,7 @@
         grid_spec=pltpu.PrefetchScalarGridSpec(
             num_scalar_prefetch=1,
             grid=(rows // TILE,),
-            in_specs=pair_specs(rows, width) + turned,
+            in_specs=ring_specs(rows, width) + turned,
             out_specs=pl.BlockSpec((TILE, heads), lambda i, at: (i, 0)),
         ),
         out_shape=jax.ShapeDtypeStruct((rows, heads), jnp.bfloat16),
@@ -372,7 +352,7 @@
 
 def last_kernel(
     capacity, idx_ref, used_ref, glob_ref, me_ref, win_ref, back_ref, kept_ref, dk_in_ref, dv_in_ref,
-    dk_ref, dv_ref, acc,
+    dk_ref, dv_ref, gw_ref, acc,
 ):
     acc[...] = win_ref[...]
     land((capacity // 2, capacity, capacity, CARRIED), idx_ref, used_ref, back_ref, acc)
@@ -411,6 +391,11 @@
             dk_ref[pl.ds(at, BLK), :LANES] = both[0]
             dv_ref[pl.ds(at, BLK), :LANES] = both[1]
 
+    for d in range(back_ref.shape[0]):
+        for j in range(gw_ref.shape[1] // LANES):
+            rows = back_ref[d, 16 * j : 16 * (j + 1), :]
+            gw_ref[16 * d : 16 * (d + 1), j * LANES : (j + 1) * LANES] = rows.astype(jnp.float32)
+
 
 def collect_first(idx, used, glob, win, back, up, down, capacity):
     rows = win.shape[1]
@@ -443,14 +428,15 @@
 def collect_last(idx, used, glob, me, win, back, before, capacity):
     rows = win.shape[1]
     out = jax.ShapeDtypeStruct((rows, 2 * LANES), jnp.bfloat16)
+    weight = jax.ShapeDtypeStruct((2 * LANES, 1024), jnp.float32)
     dk, dv, kept = before
     arrays = (win, back, kept, dk, dv)
     return pl.pallas_call(
         functools.partial(last_kernel, capacity),
         grid=(1,),
         in_specs=[smem()] * 4 + [whole(x.shape) for x in arrays],
-        out_specs=(whole(out.shape), whole(out.shape)),
-        out_shape=(out, out),
+        out_specs=(whole(out.shape), whole(out.shape), whole(weight.shape)),
+        out_shape=(out, out, weight),
         scratch_shapes=[pltpu.VMEM((2, rows, LANES), jnp.float32)],
         compiler_params=params(),
         cost_estimate=pl.CostEstimate(flops=4 << 20, bytes_accessed=12 << 20, transcendentals=0),
@@ -458,14 +444,14 @@
 
 
 def weight_kernel(at_ref, c0, c1, *refs):
-    pieces, out_ref, acc = refs[:9], refs[9], refs[10]
+    pieces, out_ref, acc = refs[:5], refs[5], refs[6]
 
     @pl.when(pl.program_id(0) == 0)
     def _():
         acc[...] = jnp.zeros_like(acc)
 
     width = pieces[0].shape[1]
-    values = pair_values(at_ref, pieces)
+    values = ring_values(pieces)
     for r, c in enumerate((c0, c1)):
         for i, g in enumerate(values):
             acc[r * LANES : (r + 1) * LANES, i * width : (i + 1) * width] += dot(c[...], g, TN)
@@ -485,7 +471,7 @@
         grid_spec=pltpu.PrefetchScalarGridSpec(
             num_scalar_prefetch=1,
             grid=(rows // TILE,),
-            in_specs=[pl.BlockSpec((TILE, LANES), lambda i, at: (i, 0))] * 2 + pair_specs(rows, width),
+            in_specs=[pl.BlockSpec((TILE, LANES), lambda i, at: (i, 0))] * 2 + ring_specs(rows, width),
             out_specs=pl.BlockSpec(shape, lambda i, at: (0, 0)),
             scratch_shapes=[pltpu.VMEM(shape, jnp.float32)],
         ),
@@ -499,27 +485,28 @@
     return whole((array.shape[0], CARRIED, LANES))
 
 
-def load_kernel(terms_ref, s0, s1, part_ref, out_ref):
+def load_kernel(own_ref, other_ref, s0, s1, part_ref, out_ref):
     del part_ref
+    terms = (own_ref[...].astype(jnp.float32) + other_ref[...].astype(jnp.float32)).astype(jnp.bfloat16)
     for d in range(out_ref.shape[0]):
         rows = slice(16 * d, 16 * (d + 1))
-        for j in range(terms_ref.shape[1] // LANES):
-            out_ref[d, 16 * j : 16 * (j + 1), :] = terms_ref[rows, j * LANES : (j + 1) * LANES]
+        for j in range(terms.shape[1] // LANES):
+            out_ref[d, 16 * j : 16 * (j + 1), :] = terms[rows, j * LANES : (j + 1) * LANES]
         out_ref[d, CARRIED - 32 : CARRIED - 16, :] = s0[rows, :]
         out_ref[d, CARRIED - 16 :, :] = s1[rows, :]
 
 
-def load_terms(terms, sums, part):
+def load_terms(own, other, sums, part):
     return pl.pallas_call(
         load_kernel,
         grid=(1,),
-        in_specs=[whole(x.shape) for x in (terms, *sums)] + [pl.BlockSpec(memory_space=pl.ANY)],
+        in_specs=[whole(x.shape) for x in (own, other, *sums)] + [pl.BlockSpec(memory_space=pl.ANY)],
         out_specs=carried(part),
         out_shape=jax.ShapeDtypeStruct(part.shape, part.dtype),
-        input_output_aliases={3: 0},
+        input_output_aliases={4: 0},
         compiler_params=params(),
         cost_estimate=pl.CostEstimate(flops=1 << 18, bytes_accessed=4 << 20, transcendentals=0),
-    )(terms, *sums, part)
+    )(own, other, *sums, part)
 
 
 def sum_kernel(back_ref, part_ref, out_ref):
@@ -540,26 +527,6 @@
         compiler_params=params(),
         cost_estimate=pl.CostEstimate(flops=1 << 18, bytes_accessed=4 << 20, transcendentals=0),
     )(back, part)
-
-
-def weight_sum_kernel(own_ref, other_ref, out_ref):
-    total = own_ref[...].astype(jnp.float32) + other_ref[...].astype(jnp.float32)
-    for d in range(total.shape[0]):
-        for j in range(out_ref.shape[1] // LANES):
-            out_ref[16 * d : 16 * (d + 1), j * LANES : (j + 1) * LANES] = total[d, 16 * j : 16 * (j + 1), :]
-
-
-def weight_sum(own, other):
-    shape = (2 * LANES, 1024)
-    return pl.pallas_call(
-        weight_sum_kernel,
-        grid=(1,),
-        in_specs=[whole(own.shape), whole(other.shape)],
-        out_specs=whole(shape),
-        out_shape=jax.ShapeDtypeStruct(shape, jnp.float32),
-        compiler_params=params(),
-        cost_estimate=pl.CostEstimate(flops=1 << 18, bytes_accessed=2 << 20, transcendentals=0),
-    )(own, other)
 
 
 def project_kernel(*refs):
@@ -606,17 +573,6 @@
     size = lax.axis_size(axis)
     pairs = [(i, i + by) for i in range(size) if 0 <= i + by < size]
     return lax.ppermute(array, axis, pairs)
-
-
-def core_ring(array, d):
-    size = lax.axis_size("tp")
-
-    def moved(x, by):
-        return lax.ppermute(x, ("dp", "tp"), [(d * size + (i + by) % size, d * size + i) for i in range(size)])
-
-    half = array.shape[0] // 2
-    following, previous = moved(array, 1), moved(array, -1)
-    return following, previous, moved(following[:half], 1), moved(previous[half:], -1)
 
 
 def per_device(
@@ -634,7 +590,7 @@
     slots = ctx_count * capacity
     barrier = lax.optimization_barrier
     at = me.reshape(1)
-    tp_at = jnp.stack([tp_me, lax.axis_index("dp")])
+    tp_at = tp_me.reshape(1)
     glob_at = global_ids[0]
 
     def exchange(parts):
@@ -642,7 +598,7 @@
 
     up, down, picked = pick_global(glob_at, at, k, v)
     before, after = shifted(up, "ctx", -1), shifted(down, "ctx", 1)
-    glob = sum_four((picked, before, after, shifted(picked, "ctx", 2)))
+    across = shifted(picked, "ctx", 2)
 
     ids = random_ids[0].reshape(ctx_count, requests)
     owner = ids // blocks
@@ -655,10 +611,11 @@
     send_idx = jnp.sum(jnp.where(hit, local[:, None, :], 0), axis=2).reshape(slots)
     send_a = pick_blocks(send_idx, k, v, 0, slots)
 
-    later = core_ring(g_out, 1)
-    send_a, glob, before, after, later, g_now = barrier((send_a, glob, before, after, later, g_out))
+    send_a, picked, across, before, after, g_now = barrier((send_a, picked, across, before, after, g_out))
     fetched_a = exchange(send_a.reshape(ctx_count, -1, LANES)).reshape(send_a.shape)
-    pieces = (g_out, *core_ring(g_now, 0), *later)
+    near = ring_near(g_now, "tp")
+    pieces = (g_out, *near, *ring_far(near, "tp"))
+    glob = sum_four((picked, before, after, across))
     glob = sum_four((glob, *[shifted(glob, "ctx", 4 * by) for by in (1, 3, 2)])).reshape(G, 2, BLK, width)
     send_b = pick_blocks(send_idx, k, v, 1, slots)
     used = jnp.sum(mine.astype(jnp.int32), axis=1)
@@ -696,7 +653,7 @@
     ctx_b, grad_q, win_b, up_b, down_b, gsum_b, ret_b, ret_c = half(my_place, fetched_b, dq_a, 1)
     near_b = ring_near(ctx_b, "tp")
     terms = weight_terms(tp_at, (ctx_a, ctx_b), pieces)
-    ret_b = load_terms(terms, (gsum_a, gsum_b), ret_b)
+    ret_b = load_terms(terms, shifted(terms, "dp", 1), (gsum_a, gsum_b), ret_b)
     ret_b, back_a, up_a, down_a, near_b = barrier((ret_b, back_a, up_a, down_a, near_b))
 
     back_b = exchange(ret_b)
@@ -712,9 +669,7 @@
     projected = project(pieces_a, pieces_b, wcols)
     win_b = collect_middle(send_idx, used, win_b, back_b, up_b, down_b, capacity)
     projected, win_b, back_c = barrier((projected, win_b, back_c))
-    weight_own = back_c[:, : CARRIED - 32]
-    grad_weight = weight_sum(weight_own, shifted(weight_own, "dp", 1))
-    grad_k, grad_v = collect_last(send_idx, used, glob_at, at, win_b, back_c, first, capacity)
+    grad_k, grad_v, grad_weight = collect_last(send_idx, used, glob_at, at, win_b, back_c, first, capacity)
     return projected[None], grad_q[None], grad_k[None], grad_v[None], grad_weight
 
 

time: 313 us -> 307 us (0.981)
  waiting for transfers between devices: 74.2 us -> 97.5 us
  starting transfers between devices: 104 us -> 82.4 us
  Pallas kernels: 108 us -> 103 us
    ppermute x18 -> x22, waiting for transfers between devices: 24.2 us -> 51.8 us  [shifted(): lax.ppermute(array, axis, [((i + by) % size, i) for i in range(size)])]
    ppermute x8 -> x0, starting transfers between devices: 17 us -> none  [moved(): lax.ppermute(x, ('dp', 'tp'), [(d * size + (i + by) % size, d * size + i)...]
    ppermute x8 -> x0, waiting for transfers between devices: 6.29 us -> none  [moved(): lax.ppermute(x, ('dp', 'tp'), [(d * size + (i + by) % size, d * size + i)...]
    slice x5 -> x0, local copies, waits for them, and re-layouts: 3.61 us -> none  [the longest x2 1.79 us: core_ring(): previous[half:]]
    ppermute x18 -> x22, starting transfers between devices: 38.3 us -> 36.4 us  [shifted(): lax.ppermute(array, axis, [((i + by) % size, i) for i in range(size)])]
    unnamed x65 -> x69, local copies, waits for them, and re-layouts: 9.43 us -> 10.3 us
  transfers between devices with their start and end apart: 35 -> 31, of which waited for: 8 -> 13; matrix products, arithmetic and copies ran while one was open for 4% -> 4% of each run, Pallas kernels for 34% -> 31%
where the time goes in v6:
time: 307 us; the launch traced here: 306 us
  Pallas kernels  103 us (34%)
  waiting for transfers between devices  97.5 us (32%)
  starting transfers between devices  82.4 us (27%)
  local copies, waits for them, and re-layouts  18.4 us (6%)
  other arithmetic  3.43 us (1%)
    pallas_call x2, Pallas kernels, attend(): pl.pallas_call(functools.partial(attend_kernel, blocks, last_block), grid...  54.5 us
    ppermute x22, waiting for transfers between devices, shifted(): lax.ppermute(array, axis, [((i + by) % size, i) for i in range(size)])  51.8 us
    all_to_all x5, waiting for transfers between devices, exchange(): return lax.all_to_all(parts, 'ctx', split_axis=0, concat_axis=0, tiled=True)  43.1 us
    ppermute x22, starting transfers between devices, shifted(): lax.ppermute(array, axis, [((i + by) % size, i) for i in range(size)])  36.4 us
    all_to_all x5, starting transfers between devices, exchange(): return lax.all_to_all(parts, 'ctx', split_axis=0, concat_axis=0, tiled=True)  33.8 us
    ppermute x4, starting transfers between devices, passed_along(): return lax.ppermute(array, axis, pairs)  12.3 us
    unnamed x69, local copies, waits for them, and re-layouts  10.3 us
    pallas_call x2, Pallas kernels, pick_blocks(): pl.pallas_call(functools.partial(pick_kernel, slots), grid=(1,), in_specs...  7.81 us
  transfers between devices with their start and end apart: 31, of which 13 were waited for; matrix products, arithmetic and copies ran while one was open for 4% of the time, Pallas kernels for 31%

profile of v6, /device:TPU:0, one launch (start us, length us, event | category | flops | bytes accessed | tf_op | source)
XLA Modules:
  0.0 306.1 jit_solution(9758334704654605721)
XLA Ops:
  0.7 2.4 shard_map.121
  3.0 6.4 %collective-permute-start = (bf16[256,256]{1,0:T(8,128)(2,1)}, bf16[256,256]{1,0:T(8,128)(2,1)S(1)}, u32[]{:S(2)}, u32[]{:S(2)}) collective-permute-start(bf16[256,256]{1,0:T(8,128)(2,1)} %get-tuple-element.80.a), channel_id=1, source_target_pairs={{8,0},{12,4},{16,8},{20,12},{24,16},{28,20},{32,24},{36,28},{40,32... | collective-permute-start | bytes 393224 | tf_op jit(solution)/shard_map/ppermute | solution.py:559
  10.5 4.3 %collective-permute-start.2 = (bf16[384,256]{1,0:T(8,128)(2,1)}, bf16[384,256]{1,0:T(8,128)(2,1)S(1)}, u32[]{:S(2)}, u32[]{:S(2)}) collective-permute-start(bf16[384,256]{1,0:T(8,128)(2,1)} %get-tuple-element.77), channel_id=1, source_target_pairs={{4,0},{8,4},{12,8},{16,12},{20,16},{24,20},{28,24},{32,28},{36,32}... | collective-permute-start | bytes 589832 | tf_op jit(solution)/shard_map/ppermute | solution.py:559
  17.1 3.9 %shard_map.120 = bf16[16384,128]{1,0:T(8,128)(2,1)} custom-call(s32[128]{0:T(128)} %reshape.109.idx_ref, bf16[2048,256]{1,0:T(8,128)(2,1)} %bitcast.25, bf16[2048,256]{1,0:T(8,128)(2,1)} %bitcast.33), custom_call_target="tpu_custom_call" | custom-call | bytes 10485760 | tf_op jit(solution)/shard_map/pallas_call | solution.py:55
  21.9 4.6 %all-to-all-start = ((bf16[16,1024,128]{2,1,0:T(8,128)(2,1)}), bf16[16,1024,128]{2,1,0:T(8,128)(2,1)}, u32[]{:S(2)}, u32[]{:S(2)}) async-start(bf16[16,1024,128]{2,1,0:T(8,128)(2,1)} %bitcast.38), calls=%async_computation | async-start | bytes 8388608 | tf_op jit(solution)/shard_map/all_to_all | solution.py:597
  26.5 2.8 collective-permute-start.3
  29.3 3.9 %shard_map.119 = bf16[16384,128]{1,0:T(8,128)(2,1)} custom-call(s32[128]{0:T(128)} %reshape.109.idx_ref, bf16[2048,256]{1,0:T(8,128)(2,1)} %bitcast.26, bf16[2048,256]{1,0:T(8,128)(2,1)} %bitcast.34), custom_call_target="tpu_custom_call" | custom-call | bytes 10485760 | tf_op jit(solution)/shard_map/pallas_call | solution.py:55
  34.1 17.0 %collective-permute-done.3.refs_1_ = bf16[2048,256]{1,0:T(8,128)(2,1)S(1)} collective-permute-done((bf16[2048,256]{1,0:T(8,128)(2,1)}, bf16[2048,256]{1,0:T(8,128)(2,1)S(1)}, u32[]{:S(2)}, u32[]{:S(2)}) %collective-permute-start.3) | collective-permute-done | bytes 1048608 | tf_op jit(solution)/shard_map/ppermute | solution.py:559
  52.0 3.6 %collective-permute-start.5 = (bf16[1024,256]{1,0:T(8,128)(2,1)}, bf16[1024,256]{1,0:T(8,128)(2,1)S(1)}, u32[]{:S(2)}, u32[]{:S(2)}) collective-permute-start(bf16[1024,256]{1,0:T(8,128)(2,1)} %slice.24), channel_id=1, source_target_pairs={{1,0},{2,1},{3,2},{0,3},{5,4},{6,5},{7,6},{4,7},{9,8},{10,9},{11,1... | collective-permute-start | bytes 1572872 | tf_op jit(solution)/shard_map/ppermute | solution.py:559
  58.1 1.8 shard_map.122.a
  59.9 2.7 collective-permute-start.7
  62.6 2.3 collective-permute-start.9
  64.9 1.2 fusion.4
  66.1 13.3 %collective-permute-done.7.b = bf16[256,256]{1,0:T(8,128)(2,1)S(1)} collective-permute-done((bf16[256,256]{1,0:T(8,128)(2,1)}, bf16[256,256]{1,0:T(8,128)(2,1)S(1)}, u32[]{:S(2)}, u32[]{:S(2)}) %collective-permute-start.7) | collective-permute-done | bytes 131104 | tf_op jit(solution)/shard_map/ppermute | solution.py:559
  79.4 2.7 collective-permute-done.8.c
  82.0 2.7 collective-permute-done.9.d
  85.4 1.8 shard_map.123
  88.2 5.6 %all-to-all-start.1 = ((bf16[16,1024,128]{2,1,0:T(8,128)(2,1)}), bf16[16,1024,128]{2,1,0:T(8,128)(2,1)}, u32[]{:S(2)}, u32[]{:S(2)}) async-start(bf16[16,1024,128]{2,1,0:T(8,128)(2,1)} %bitcast.37), calls=%async_computation.1 | async-start | bytes 8388608 | tf_op jit(solution)/shard_map/all_to_all | solution.py:597
  93.8 5.2 %shard_map.124.g_ref = bf16[2048,256]{1,0:T(8,128)(2,1)} custom-call(s32[1]{0:T(128)} %bitcast.10.at_ref, bf16[2048,256]{1,0:T(8,128)(2,1)} %bitcast.4.refs_0_, bf16[2048,256]{1,0:T(8,128)(2,1)} %copy-done.5, bf16[2048,256]{1,0:T(8,128)(2,1)} %copy-done.6, bf16[1024,256]{1,0:T(8,128)(2,1)} %copy-done.7, bf16[1024,256]{1,0:T(8,128)(2,1)} %copy-done.8, ...), custom_call_target="tpu_custom_call" | custom-call | flops 1073741824 | bytes 16777216 | tf_op jit(solution)/shard_map/pallas_call | solution.py:155
  99.7 27.0 %shard_map.125 = (bf16[2048,128]{1,0:T(8,128)(2,1)}, bf16[2048,256]{1,0:T(8,128)(2,1)}, f32[2,2048,128]{2,1,0:T(8,128)}, bf16[2,64,128]{2,1,0:T(8,128)(2,1)}, bf...) custom-call(s32[1]{0:T(128)} %bitcast.me_ref, ...), custom_call_target="tpu_custom_call" | custom-call | flops 6442450944 | bytes 83886080 | tf_op jit(solution)/shard_map/pallas_call | solution.py:288
  126.6 2.8 collective-permute-start.13
  130.1 3.2 %collective-permute-start.10 = (bf16[256,256]{1,0:T(8,128)(2,1)S(1)}, bf16[256,256]{1,0:T(8,128)(2,1)S(1)}, u32[]{:S(2)}, u32[]{:S(2)}) collective-permute-start(bf16[256,256]{1,0:T(8,128)(2,1)S(1)} %get-tuple-element.148), channel_id=1, source_target_pairs={{1,0},{2,1},{3,2},{0,3},{5,4},{6,5},{7,6},{4,7},{9,8},{10,9},{11,1... | collective-permute-start | bytes 393224 | tf_op jit(solution)/shard_map/ppermute | solution.py:559
  134.2 9.9 %collective-permute-done.10.refs_11_ = bf16[256,256]{1,0:T(8,128)(2,1)S(1)} collective-permute-done((bf16[256,256]{1,0:T(8,128)(2,1)S(1)}, bf16[256,256]{1,0:T(8,128)(2,1)S(1)}, u32[]{:S(2)}, u32[]{:S(2)}) %collective-permute-start.10) | collective-permute-done | bytes 131104 | tf_op jit(solution)/shard_map/ppermute | solution.py:559
  145.1 2.4 collective-permute-done.12.refs_13_
  149.1 6.9 %all-to-all-start.2 = ((bf16[16,1024,128]{2,1,0:T(8,128)(2,1)}), bf16[16,1024,128]{2,1,0:T(8,128)(2,1)}, u32[]{:S(2)}, u32[]{:S(2)}) async-start(bf16[16,1024,128]{2,1,0:T(8,128)(2,1)} %bitcast.39), calls=%async_computation.2 | async-start | bytes 8388608 | tf_op jit(solution)/shard_map/all_to_all | solution.py:597
  156.0 27.5 %shard_map.126 = (bf16[2048,128]{1,0:T(8,128)(2,1)}, bf16[2048,256]{1,0:T(8,128)(2,1)}, f32[2,2048,128]{2,1,0:T(8,128)}, bf16[2,64,128]{2,1,0:T(8,128)(2,1)}, bf...) custom-call(s32[1]{0:T(128)} %bitcast.me_ref, ...), custom_call_target="tpu_custom_call", output_to_operand_aliasing={{1}: (12, {})} | custom-call | flops 6442450944 | bytes 83886080 | tf_op jit(solution)/shard_map/pallas_call | solution.py:288
  183.6 5.3 %shard_map.127.own_ref = bf16[256,1024]{1,0:T(8,128)(2,1)} custom-call(s32[1]{0:T(128)} %bitcast.10.at_ref, bf16[2048,128]{1,0:T(8,128)(2,1)} %get-tuple-element.93.c0.refs_0_, bf16[2048,128]{1,0:T(8,128)(2,1)} %get-tuple-element.122.c1.refs_5_, bf16[2048,256]{1,0:T(8,128)(2,1)} %bitcast.4.refs_0_, bf16[2048,256]{1,0:T(8,128)(2,1)} %copy-done.5, ...), custom_call_target="tpu_custom_call" | custom-call | flops 1073741824 | bytes 16777216 | tf_op jit(solution)/shard_map/pallas_call | solution.py:469
  189.3 1.6 collective-permute-start.21
  191.0 1.3 collective-permute-start.18
  192.3 4.5 %collective-permute-start.19 = (bf16[2,64,128]{2,1,0:T(8,128)(2,1)S(1)}, bf16[2,64,128]{2,1,0:T(8,128)(2,1)S(1)}, u32[]{:S(2)}, u32[]{:S(2)}) collective-permute-start(bf16[2,64,128]{2,1,0:T(8,128)(2,1)S(1)} %copy-done.32), channel_id=1, source_target_pairs={{0,4},{4,8},{8,12},{12,16},{16,20},{20,24},{24,28},{28,32},{32,36}... | collective-permute-start | bytes 98312 | tf_op jit(solution)/shard_map/ppermute | solution.py:575
  197.6 2.2 shard_map.128
  199.8 2.6 collective-permute-done.18.up_ref
  204.6 9.2 %all-to-all-start.3 = ((bf16[16,672,128]{2,1,0:T(8,128)(2,1)}), bf16[16,672,128]{2,1,0:T(8,128)(2,1)S(1)}, u32[]{:S(2)}, u32[]{:S(2)}) async-start(bf16[16,672,128]{2,1,0:T(8,128)(2,1)} %shard_map.128), calls=%async_computation.3 | async-start | bytes 5505024 | tf_op jit(solution)/shard_map/all_to_all | solution.py:597
  215.7 1.9 collective-permute-start.25
  217.6 1.3 collective-permute-start.22
  218.9 5.2 %collective-permute-start.23 = (bf16[2,64,128]{2,1,0:T(8,128)(2,1)}, bf16[2,64,128]{2,1,0:T(8,128)(2,1)}, u32[]{:S(2)}, u32[]{:S(2)}) collective-permute-start(bf16[2,64,128]{2,1,0:T(8,128)(2,1)} %get-tuple-element.111), channel_id=1, source_target_pairs={{0,4},{4,8},{8,12},{12,16},{16,20},{20,24},{24,28},{28,32},{32,36}... | collective-permute-start | bytes 98312 | tf_op jit(solution)/shard_map/ppermute | solution.py:575
  224.1 4.8 %shard_map.130 = (bf16[2048,128]{1,0:T(8,128)(2,1)}, bf16[2048,128]{1,0:T(8,128)(2,1)}, f32[2,2,64,128]{3,2,1,0:T(8,128)}) custom-call(s32[128]{0:T(128)} %reshape.109.idx_ref, s32[16]{0:T(128)} %reduce_sum.47.used_ref, s32[2]{0:T(128)} %bitcast.44, f32[2,2048,128]{2,1,0:T(8,128)} %get-tuple-element.115.win_ref, ...), custom_call_target="tpu_custom_call" | custom-call | flops 4194304 | bytes 16777216 | tf_op jit(solution)/shard_map/pallas_call | solution.py:404
  228.9 23.0 %all-to-all-done.3.back_ref = bf16[16,672,128]{2,1,0:T(8,128)(2,1)S(1)} async-done(((bf16[16,672,128]{2,1,0:T(8,128)(2,1)}), bf16[16,672,128]{2,1,0:T(8,128)(2,1)S(1)}, u32[]{:S(2)}, u32[]{:S(2)}) %all-to-all-start.3) | async-done | bytes 2752544 | tf_op jit(solution)/shard_map/all_to_all | solution.py:597
  251.9 1.5 copy-done.2
  253.4 2.0 shard_map.129
  256.3 7.4 %all-to-all-start.4 = ((bf16[16,672,128]{2,1,0:T(8,128)(2,1)}), bf16[16,672,128]{2,1,0:T(8,128)(2,1)S(1)}, u32[]{:S(2)}, u32[]{:S(2)}) async-start(bf16[16,672,128]{2,1,0:T(8,128)(2,1)} %shard_map.129), calls=%async_computation.4 | async-start | bytes 5505024 | tf_op jit(solution)/shard_map/all_to_all | solution.py:597
  264.9 1.9 collective-permute-start.16
  266.8 4.3 %shard_map.132.win_ref = f32[2,2048,128]{2,1,0:T(8,128)} custom-call(s32[128]{0:T(128)} %reshape.109.idx_ref, s32[16]{0:T(128)} %reduce_sum.47.used_ref, f32[2,2048,128]{2,1,0:T(8,128)} %get-tuple-element.131.win_ref, bf16[16,672,128]{2,1,0:T(8,128)(2,1)} %copy-done.2, bf16[2,64,128]{2,1,0:T(8,128)(2,1)} %collective-permute-done.22.up_ref, ...), custom_call_target="tpu_custom_call" | custom-call | flops 4194304 | bytes 14680064 | tf_op jit(solution)/shard_map/pallas_call | solution.py:417
  271.2 1.4 collective-permute-done.16.refs_4_
  273.3 5.9 %shard_map.131 = bf16[2048,256]{1,0:T(8,128)(2,1)} custom-call(bf16[2048,128]{1,0:T(8,128)(2,1)} %get-tuple-element.93.c0.refs_0_, bf16[2048,128]{1,0:T(8,128)(2,1)} %copy-done.10, bf16[2048,128]{1,0:T(8,128)(2,1)} %copy-done.12, bf16[1024,128]{1,0:T(8,128)(2,1)} %copy-done.18, bf16[1024,128]{1,0:T(8,128)(2,1)} %copy-done.19, ...), custom_call_target="tpu_custom_call" | custom-call | flops 1073741824 | bytes 18874368 | tf_op jit(solution)/shard_map/pallas_call | solution.py:546
  279.2 20.1 %all-to-all-done.4.back_ref = bf16[16,672,128]{2,1,0:T(8,128)(2,1)S(1)} async-done(((bf16[16,672,128]{2,1,0:T(8,128)(2,1)}), bf16[16,672,128]{2,1,0:T(8,128)(2,1)S(1)}, u32[]{:S(2)}, u32[]{:S(2)}) %all-to-all-start.4) | async-done | bytes 2752544 | tf_op jit(solution)/shard_map/all_to_all | solution.py:597
  299.3 1.5 copy-done.4
  300.8 5.3 %shard_map.133 = (bf16[2048,256]{1,0:T(8,128)(2,1)}, bf16[2048,256]{1,0:T(8,128)(2,1)}, f32[256,1024]{1,0:T(8,128)}) custom-call(s32[128]{0:T(128)} %reshape.109.idx_ref, s32[16]{0:T(128)} %reduce_sum.47.used_ref, s32[2]{0:T(128)} %bitcast.45, s32[1]{0:T(128)} %bitcast.me_ref, f32[2,2048,128]{2,1,0:T(8,128)} %shard_map.132.win_ref, ...), custom_call_target="tpu_custom_call" | custom-call | flops 4194304 | bytes 12582912 | tf_op jit(solution)/shard_map/pallas_call | solution.py:434
  (122 shorter events, 23.0 us)
Async XLA Ops:
  0.6 32.6 %copy-start = (s32[1,512,3]{1,0,2:T(1,128)S(1)}, s32[1,512,3]{1,0,2:T(1,128)}, u32[]{:S(2)}) copy-start(s32[1,512,3]{1,0,2:T(1,128)} %param.14) | copy-start | bytes 18436
  0.7 14.2 %copy-start.31 = (s32[1,512,3]{1,0,2:T(1,128)S(1)}, s32[1,512,3]{1,0,2:T(1,128)}, u32[]{:S(2)}) copy-start(s32[1,512,3]{1,0,2:T(1,128)} %param.13) | copy-start | bytes 18436
  3.0 18.0 %collective-permute-start = (bf16[256,256]{1,0:T(8,128)(2,1)}, bf16[256,256]{1,0:T(8,128)(2,1)S(1)}, u32[]{:S(2)}, u32[]{:S(2)}) collective-permute-start(bf16[256,256]{1,0:T(8,128)(2,1)} %get-tuple-element.80.a), channel_id=1, source_target_pairs={{8,0},{12,4},{16,8},{20,12},{24,16},{28,20},{32,24},{36,28},{40,32... | collective-permute-start | bytes 393224 | tf_op jit(solution)/shard_map/ppermute | solution.py:559
  9.4 11.6 %collective-permute-start.1 = (bf16[384,256]{1,0:T(8,128)(2,1)}, bf16[384,256]{1,0:T(8,128)(2,1)S(1)}, u32[]{:S(2)}, u32[]{:S(2)}) collective-permute-start(bf16[384,256]{1,0:T(8,128)(2,1)} %get-tuple-element.76), channel_id=1, source_target_pairs={{60,0},{0,4},{4,8},{8,12},{12,16},{16,20},{20,24},{24,28},{28,32},... | collective-permute-start | bytes 589832 | tf_op jit(solution)/shard_map/ppermute | solution.py:559
  10.5 10.6 %collective-permute-start.2 = (bf16[384,256]{1,0:T(8,128)(2,1)}, bf16[384,256]{1,0:T(8,128)(2,1)S(1)}, u32[]{:S(2)}, u32[]{:S(2)}) collective-permute-start(bf16[384,256]{1,0:T(8,128)(2,1)} %get-tuple-element.77), channel_id=1, source_target_pairs={{4,0},{8,4},{12,8},{16,12},{20,16},{24,20},{28,24},{32,28},{36,32}... | collective-permute-start | bytes 589832 | tf_op jit(solution)/shard_map/ppermute | solution.py:559
  21.9 65.3 %all-to-all-start = ((bf16[16,1024,128]{2,1,0:T(8,128)(2,1)}), bf16[16,1024,128]{2,1,0:T(8,128)(2,1)}, u32[]{:S(2)}, u32[]{:S(2)}) async-start(bf16[16,1024,128]{2,1,0:T(8,128)(2,1)} %bitcast.38), calls=%async_computation | async-start | bytes 8388608 | tf_op jit(solution)/shard_map/all_to_all | solution.py:597
  26.5 24.6 %collective-permute-start.3 = (bf16[2048,256]{1,0:T(8,128)(2,1)}, bf16[2048,256]{1,0:T(8,128)(2,1)S(1)}, u32[]{:S(2)}, u32[]{:S(2)}) collective-permute-start(bf16[2048,256]{1,0:T(8,128)(2,1)} %bitcast.4.refs_0_), channel_id=1, source_target_pairs={{1,0},{2,1},{3,2},{0,3},{5,4},{6,5},{7,6},{4,7},{9,8},{10,9},{11,1... | collective-permute-start | bytes 3145736 | tf_op jit(solution)/shard_map/ppermute | solution.py:559
  29.3 26.3 %collective-permute-start.4 = (bf16[2048,256]{1,0:T(8,128)(2,1)}, bf16[2048,256]{1,0:T(8,128)(2,1)S(1)}, u32[]{:S(2)}, u32[]{:S(2)}) collective-permute-start(bf16[2048,256]{1,0:T(8,128)(2,1)} %bitcast.4.refs_0_), channel_id=1, source_target_pairs={{3,0},{0,1},{1,2},{2,3},{7,4},{4,5},{5,6},{6,7},{11,8},{8,9},{9,10... | collective-permute-start | bytes 3145736 | tf_op jit(solution)/shard_map/ppermute | solution.py:559
  51.1 36.1 %copy-start.5 = (bf16[2048,256]{1,0:T(8,128)(2,1)}, bf16[2048,256]{1,0:T(8,128)(2,1)S(1)}, u32[]{:S(2)}) copy-start(bf16[2048,256]{1,0:T(8,128)(2,1)S(1)} %collective-permute-done.3.refs_1_) | copy-start | bytes 3145732
  52.0 35.2 %collective-permute-start.5 = (bf16[1024,256]{1,0:T(8,128)(2,1)}, bf16[1024,256]{1,0:T(8,128)(2,1)S(1)}, u32[]{:S(2)}, u32[]{:S(2)}) collective-permute-start(bf16[1024,256]{1,0:T(8,128)(2,1)} %slice.24), channel_id=1, source_target_pairs={{1,0},{2,1},{3,2},{0,3},{5,4},{6,5},{7,6},{4,7},{9,8},{10,9},{11,1... | collective-permute-start | bytes 1572872 | tf_op jit(solution)/shard_map/ppermute | solution.py:559
  55.6 31.6 %copy-start.6 = (bf16[2048,256]{1,0:T(8,128)(2,1)}, bf16[2048,256]{1,0:T(8,128)(2,1)S(1)}, u32[]{:S(2)}) copy-start(bf16[2048,256]{1,0:T(8,128)(2,1)S(1)} %collective-permute-done.4.refs_2_) | copy-start | bytes 3145732
  56.5 30.7 %collective-permute-start.6 = (bf16[1024,256]{1,0:T(8,128)(2,1)}, bf16[1024,256]{1,0:T(8,128)(2,1)S(1)}, u32[]{:S(2)}, u32[]{:S(2)}) collective-permute-start(bf16[1024,256]{1,0:T(8,128)(2,1)} %slice.25), channel_id=1, source_target_pairs={{3,0},{0,1},{1,2},{2,3},{7,4},{4,5},{5,6},{6,7},{11,8},{8,9},{9,10... | collective-permute-start | bytes 1572872 | tf_op jit(solution)/shard_map/ppermute | solution.py:559
  59.9 19.5 %collective-permute-start.7 = (bf16[256,256]{1,0:T(8,128)(2,1)}, bf16[256,256]{1,0:T(8,128)(2,1)S(1)}, u32[]{:S(2)}, u32[]{:S(2)}) collective-permute-start(bf16[256,256]{1,0:T(8,128)(2,1)} %shard_map.122.a), channel_id=1, source_target_pairs={{16,0},{20,4},{24,8},{28,12},{32,16},{36,20},{40,24},{44,28},{48,3... | collective-permute-start | bytes 393224 | tf_op jit(solution)/shard_map/ppermute | solution.py:559
  62.6 19.5 %collective-permute-start.8 = (bf16[256,256]{1,0:T(8,128)(2,1)}, bf16[256,256]{1,0:T(8,128)(2,1)S(1)}, u32[]{:S(2)}, u32[]{:S(2)}) collective-permute-start(bf16[256,256]{1,0:T(8,128)(2,1)} %shard_map.122.a), channel_id=1, source_target_pairs={{48,0},{52,4},{56,8},{60,12},{0,16},{4,20},{8,24},{12,28},{16,32},... | collective-permute-start | bytes 393224 | tf_op jit(solution)/shard_map/ppermute | solution.py:559
  62.6 22.2 %collective-permute-start.9 = (bf16[256,256]{1,0:T(8,128)(2,1)}, bf16[256,256]{1,0:T(8,128)(2,1)S(1)}, u32[]{:S(2)}, u32[]{:S(2)}) collective-permute-start(bf16[256,256]{1,0:T(8,128)(2,1)} %shard_map.122.a), channel_id=1, source_target_pairs={{32,0},{36,4},{40,8},{44,12},{48,16},{52,20},{56,24},{60,28},{0,32... | collective-permute-start | bytes 393224 | tf_op jit(solution)/shard_map/ppermute | solution.py:559
  79.4 5.4 %copy-start.25 = (bf16[256,256]{1,0:T(8,128)(2,1)}, bf16[256,256]{1,0:T(8,128)(2,1)S(1)}, u32[]{:S(2)}) copy-start(bf16[256,256]{1,0:T(8,128)(2,1)S(1)} %collective-permute-done.7.b) | copy-start | bytes 393220
  82.0 2.7 copy-start.26
  88.2 59.9 %all-to-all-start.1 = ((bf16[16,1024,128]{2,1,0:T(8,128)(2,1)}), bf16[16,1024,128]{2,1,0:T(8,128)(2,1)}, u32[]{:S(2)}, u32[]{:S(2)}) async-start(bf16[16,1024,128]{2,1,0:T(8,128)(2,1)} %bitcast.37), calls=%async_computation.1 | async-start | bytes 8388608 | tf_op jit(solution)/shard_map/all_to_all | solution.py:597
  99.7 29.7 %copy-start.3 = (bf16[256,1024]{1,0:T(8,128)(2,1)S(1)}, bf16[256,1024]{1,0:T(8,128)(2,1)}, u32[]{:S(2)}) copy-start(bf16[256,1024]{1,0:T(8,128)(2,1)} %refs_8_.1) | copy-start | bytes 1572868
  126.6 20.9 %collective-permute-start.13 = (bf16[2048,128]{1,0:T(8,128)(2,1)}, bf16[2048,128]{1,0:T(8,128)(2,1)S(1)}, u32[]{:S(2)}, u32[]{:S(2)}) collective-permute-start(bf16[2048,128]{1,0:T(8,128)(2,1)} %get-tuple-element.93.c0.refs_0_), channel_id=1, source_target_pairs={{1,0},{2,1},{3,2},{0,3},{5,4},{6,5},{7,6},{4,7},{9,8},{10,9},{11,1... | collective-permute-start | bytes 1572872 | tf_op jit(solution)/shard_map/ppermute | solution.py:559
  129.4 18.8 %collective-permute-start.14 = (bf16[2048,128]{1,0:T(8,128)(2,1)}, bf16[2048,128]{1,0:T(8,128)(2,1)S(1)}, u32[]{:S(2)}, u32[]{:S(2)}) collective-permute-start(bf16[2048,128]{1,0:T(8,128)(2,1)} %get-tuple-element.93.c0.refs_0_), channel_id=1, source_target_pairs={{3,0},{0,1},{1,2},{2,3},{7,4},{4,5},{5,6},{6,7},{11,8},{8,9},{9,10... | collective-permute-start | bytes 1572872 | tf_op jit(solution)/shard_map/ppermute | solution.py:559
  130.1 14.0 %collective-permute-start.10 = (bf16[256,256]{1,0:T(8,128)(2,1)S(1)}, bf16[256,256]{1,0:T(8,128)(2,1)S(1)}, u32[]{:S(2)}, u32[]{:S(2)}) collective-permute-start(bf16[256,256]{1,0:T(8,128)(2,1)S(1)} %get-tuple-element.148), channel_id=1, source_target_pairs={{1,0},{2,1},{3,2},{0,3},{5,4},{6,5},{7,6},{4,7},{9,8},{10,9},{11,1... | collective-permute-start | bytes 393224 | tf_op jit(solution)/shard_map/ppermute | solution.py:559
  133.3 11.8 %collective-permute-start.11 = (bf16[256,256]{1,0:T(8,128)(2,1)S(1)}, bf16[256,256]{1,0:T(8,128)(2,1)S(1)}, u32[]{:S(2)}, u32[]{:S(2)}) collective-permute-start(bf16[256,256]{1,0:T(8,128)(2,1)S(1)} %get-tuple-element.150), channel_id=1, source_target_pairs={{2,0},{3,1},{0,2},{1,3},{6,4},{7,5},{4,6},{5,7},{10,8},{11,9},{8,1... | collective-permute-start | bytes 393224 | tf_op jit(solution)/shard_map/ppermute | solution.py:559
  133.3 14.1 %collective-permute-start.12 = (bf16[256,256]{1,0:T(8,128)(2,1)S(1)}, bf16[256,256]{1,0:T(8,128)(2,1)S(1)}, u32[]{:S(2)}, u32[]{:S(2)}) collective-permute-start(bf16[256,256]{1,0:T(8,128)(2,1)S(1)} %get-tuple-element.147), channel_id=1, source_target_pairs={{3,0},{0,1},{1,2},{2,3},{7,4},{4,5},{5,6},{6,7},{11,8},{8,9},{9,10... | collective-permute-start | bytes 393224 | tf_op jit(solution)/shard_map/ppermute | solution.py:559
  144.1 3.4 %copy-start.22 = (bf16[256,256]{1,0:T(8,128)(2,1)}, bf16[256,256]{1,0:T(8,128)(2,1)S(1)}, u32[]{:S(2)}) copy-start(bf16[256,256]{1,0:T(8,128)(2,1)S(1)} %collective-permute-done.10.refs_11_) | copy-start | bytes 393220
  145.1 2.4 copy-start.23
  149.1 55.5 %all-to-all-start.2 = ((bf16[16,1024,128]{2,1,0:T(8,128)(2,1)}), bf16[16,1024,128]{2,1,0:T(8,128)(2,1)}, u32[]{:S(2)}, u32[]{:S(2)}) async-start(bf16[16,1024,128]{2,1,0:T(8,128)(2,1)} %bitcast.39), calls=%async_computation.2 | async-start | bytes 8388608 | tf_op jit(solution)/shard_map/all_to_all | solution.py:597
  183.6 5.3 %copy-start.9 = (bf16[2048,128]{1,0:T(8,128)(2,1)S(1)}, bf16[2048,128]{1,0:T(8,128)(2,1)}, u32[]{:S(2)}) copy-start(bf16[2048,128]{1,0:T(8,128)(2,1)} %get-tuple-element.122.c1.refs_5_) | copy-start | bytes 1572868
  183.6 7.4 %copy-start.33 = (bf16[2,64,128]{2,1,0:T(8,128)(2,1)S(1)}, bf16[2,64,128]{2,1,0:T(8,128)(2,1)}, u32[]{:S(2)}) copy-start(bf16[2,64,128]{2,1,0:T(8,128)(2,1)} %get-tuple-element.106) | copy-start | bytes 98308
  183.6 8.7 %copy-start.32 = (bf16[2,64,128]{2,1,0:T(8,128)(2,1)S(1)}, bf16[2,64,128]{2,1,0:T(8,128)(2,1)}, u32[]{:S(2)}) copy-start(bf16[2,64,128]{2,1,0:T(8,128)(2,1)} %get-tuple-element.107) | copy-start | bytes 98308
  188.9 8.0 %collective-permute-start.17 = (bf16[256,1024]{1,0:T(8,128)(2,1)}, bf16[256,1024]{1,0:T(8,128)(2,1)S(1)}, u32[]{:S(2)}, u32[]{:S(2)}) collective-permute-start(bf16[256,1024]{1,0:T(8,128)(2,1)} %shard_map.127.own_ref), channel_id=1, source_target_pairs={{64,0},{0,64},{65,1},{1,65},{66,2},{2,66},{67,3},{3,67},{68,4},{4,... | collective-permute-start | bytes 1572872 | tf_op jit(solution)/shard_map/ppermute | solution.py:559
  188.9 14.3 %collective-permute-start.20 = (bf16[2048,128]{1,0:T(8,128)(2,1)S(1)}, bf16[2048,128]{1,0:T(8,128)(2,1)S(1)}, u32[]{:S(2)}, u32[]{:S(2)}) collective-permute-start(bf16[2048,128]{1,0:T(8,128)(2,1)S(1)} %copy-done.9), channel_id=1, source_target_pairs={{1,0},{2,1},{3,2},{0,3},{5,4},{6,5},{7,6},{4,7},{9,8},{10,9},{11,1... | collective-permute-start | bytes 1572872 | tf_op jit(solution)/shard_map/ppermute | solution.py:559
  189.3 15.3 %collective-permute-start.21 = (bf16[2048,128]{1,0:T(8,128)(2,1)S(1)}, bf16[2048,128]{1,0:T(8,128)(2,1)}, u32[]{:S(2)}, u32[]{:S(2)}) collective-permute-start(bf16[2048,128]{1,0:T(8,128)(2,1)S(1)} %copy-done.9), channel_id=1, source_target_pairs={{3,0},{0,1},{1,2},{2,3},{7,4},{4,5},{5,6},{6,7},{11,8},{8,9},{9,10... | collective-permute-start | bytes 1572872 | tf_op jit(solution)/shard_map/ppermute | solution.py:559
  191.0 11.4 %collective-permute-start.18 = (bf16[2,64,128]{2,1,0:T(8,128)(2,1)S(1)}, bf16[2,64,128]{2,1,0:T(8,128)(2,1)S(1)}, u32[]{:S(2)}, u32[]{:S(2)}) collective-permute-start(bf16[2,64,128]{2,1,0:T(8,128)(2,1)S(1)} %copy-done.33), channel_id=1, source_target_pairs={{4,0},{8,4},{12,8},{16,12},{20,16},{24,20},{28,24},{32,28},{36,32}... | collective-permute-start | bytes 98312 | tf_op jit(solution)/shard_map/ppermute | solution.py:575
  192.3 10.1 %collective-permute-start.19 = (bf16[2,64,128]{2,1,0:T(8,128)(2,1)S(1)}, bf16[2,64,128]{2,1,0:T(8,128)(2,1)S(1)}, u32[]{:S(2)}, u32[]{:S(2)}) collective-permute-start(bf16[2,64,128]{2,1,0:T(8,128)(2,1)S(1)} %copy-done.32), channel_id=1, source_target_pairs={{0,4},{4,8},{8,12},{12,16},{16,20},{20,24},{24,28},{28,32},{32,36}... | collective-permute-start | bytes 98312 | tf_op jit(solution)/shard_map/ppermute | solution.py:575
  204.6 9.2 %copy-start.14 = (bf16[2048,128]{1,0:T(8,128)(2,1)S(1)}, bf16[2048,128]{1,0:T(8,128)(2,1)}, u32[]{:S(2)}) copy-start(bf16[2048,128]{1,0:T(8,128)(2,1)} %copy-done.13) | copy-start | bytes 1572868
  204.6 47.3 %all-to-all-start.3 = ((bf16[16,672,128]{2,1,0:T(8,128)(2,1)}), bf16[16,672,128]{2,1,0:T(8,128)(2,1)S(1)}, u32[]{:S(2)}, u32[]{:S(2)}) async-start(bf16[16,672,128]{2,1,0:T(8,128)(2,1)} %shard_map.128), calls=%async_computation.3 | async-start | bytes 5505024 | tf_op jit(solution)/shard_map/all_to_all | solution.py:597
  214.6 40.9 %collective-permute-start.24 = (bf16[1024,128]{1,0:T(8,128)(2,1)}, bf16[1024,128]{1,0:T(8,128)(2,1)S(1)}, u32[]{:S(2)}, u32[]{:S(2)}) collective-permute-start(bf16[1024,128]{1,0:T(8,128)(2,1)} %slice.22), channel_id=1, source_target_pairs={{1,0},{2,1},{3,2},{0,3},{5,4},{6,5},{7,6},{4,7},{9,8},{10,9},{11,1... | collective-permute-start | bytes 786440 | tf_op jit(solution)/shard_map/ppermute | solution.py:559
  215.7 39.7 %collective-permute-start.25 = (bf16[1024,128]{1,0:T(8,128)(2,1)S(1)}, bf16[1024,128]{1,0:T(8,128)(2,1)S(1)}, u32[]{:S(2)}, u32[]{:S(2)}) collective-permute-start(bf16[1024,128]{1,0:T(8,128)(2,1)S(1)} %slice.23), channel_id=1, source_target_pairs={{3,0},{0,1},{1,2},{2,3},{7,4},{4,5},{5,6},{6,7},{11,8},{8,9},{9,10... | collective-permute-start | bytes 786440 | tf_op jit(solution)/shard_map/ppermute | solution.py:559
  217.6 37.8 %collective-permute-start.22 = (bf16[2,64,128]{2,1,0:T(8,128)(2,1)}, bf16[2,64,128]{2,1,0:T(8,128)(2,1)}, u32[]{:S(2)}, u32[]{:S(2)}) collective-permute-start(bf16[2,64,128]{2,1,0:T(8,128)(2,1)} %get-tuple-element.110), channel_id=1, source_target_pairs={{4,0},{8,4},{12,8},{16,12},{20,16},{24,20},{28,24},{32,28},{36,32}... | collective-permute-start | bytes 98312 | tf_op jit(solution)/shard_map/ppermute | solution.py:575
  218.9 36.5 %collective-permute-start.23 = (bf16[2,64,128]{2,1,0:T(8,128)(2,1)}, bf16[2,64,128]{2,1,0:T(8,128)(2,1)}, u32[]{:S(2)}, u32[]{:S(2)}) collective-permute-start(bf16[2,64,128]{2,1,0:T(8,128)(2,1)} %get-tuple-element.111), channel_id=1, source_target_pairs={{0,4},{4,8},{8,12},{12,16},{16,20},{20,24},{24,28},{28,32},{32,36}... | collective-permute-start | bytes 98312 | tf_op jit(solution)/shard_map/ppermute | solution.py:575
  251.9 1.5 copy-start.2
  256.2 7.4 %copy-start.11 = (bf16[2048,128]{1,0:T(8,128)(2,1)S(1)}, bf16[2048,128]{1,0:T(8,128)(2,1)}, u32[]{:S(2)}) copy-start(bf16[2048,128]{1,0:T(8,128)(2,1)} %copy-done.10) | copy-start | bytes 1572868
  256.3 43.0 %all-to-all-start.4 = ((bf16[16,672,128]{2,1,0:T(8,128)(2,1)}), bf16[16,672,128]{2,1,0:T(8,128)(2,1)S(1)}, u32[]{:S(2)}, u32[]{:S(2)}) async-start(bf16[16,672,128]{2,1,0:T(8,128)(2,1)} %shard_map.129), calls=%async_computation.4 | async-start | bytes 5505024 | tf_op jit(solution)/shard_map/all_to_all | solution.py:597
  263.7 7.5 %collective-permute-start.15 = (bf16[1024,128]{1,0:T(8,128)(2,1)S(1)}, bf16[1024,128]{1,0:T(8,128)(2,1)S(1)}, u32[]{:S(2)}, u32[]{:S(2)}) collective-permute-start(bf16[1024,128]{1,0:T(8,128)(2,1)S(1)} %slice.20), channel_id=1, source_target_pairs={{1,0},{2,1},{3,2},{0,3},{5,4},{6,5},{7,6},{4,7},{9,8},{10,9},{11,1... | collective-permute-start | bytes 786440 | tf_op jit(solution)/shard_map/ppermute | solution.py:559
  264.9 7.7 %collective-permute-start.16 = (bf16[1024,128]{1,0:T(8,128)(2,1)S(1)}, bf16[1024,128]{1,0:T(8,128)(2,1)S(1)}, u32[]{:S(2)}, u32[]{:S(2)}) collective-permute-start(bf16[1024,128]{1,0:T(8,128)(2,1)S(1)} %slice.21), channel_id=1, source_target_pairs={{3,0},{0,1},{1,2},{2,3},{7,4},{4,5},{5,6},{6,7},{11,8},{8,9},{9,10... | collective-permute-start | bytes 786440 | tf_op jit(solution)/shard_map/ppermute | solution.py:559
  273.3 32.8 %copy-start.1 = (s32[1,512,3]{1,0,2:T(1,128)S(1)}, s32[1,512,3]{1,0,2:T(1,128)}, u32[]{:S(2)}) copy-start(s32[1,512,3]{1,0,2:T(1,128)} %param.14) | copy-start | bytes 18436
  299.3 1.5 copy-start.4
  (17 other events, 13.9 us)

commit v7 on v6

--- a/solution.py
+++ b/solution.py
@@ -13,7 +13,7 @@
 G = 2
 LANES = 128
 NEG_FILL = -1e30
-VMEM_LIMIT = 56 * 1024 * 1024
+VMEM_LIMIT = 60 * 1024 * 1024
 CARRIED = 160
 
 NT = (((1,), (1,)), ((), ()))
@@ -614,7 +614,6 @@
     send_a, picked, across, before, after, g_now = barrier((send_a, picked, across, before, after, g_out))
     fetched_a = exchange(send_a.reshape(ctx_count, -1, LANES)).reshape(send_a.shape)
     near = ring_near(g_now, "tp")
-    pieces = (g_out, *near, *ring_far(near, "tp"))
     glob = sum_four((picked, before, after, across))
     glob = sum_four((glob, *[shifted(glob, "ctx", 4 * by) for by in (1, 3, 2)])).reshape(G, 2, BLK, width)
     send_b = pick_blocks(send_idx, k, v, 1, slots)
@@ -627,8 +626,9 @@
     my_place = (my_part * ctx_count + my_owner) * part_size + my_rank % part_size
     valid = lax.dynamic_slice_in_dim(random_valid[0], me * blocks, blocks, 0).reshape(-1)
 
-    ready = barrier((send_b, fetched_a, pieces, glob, used, my_slot, my_place, valid))
-    send_b, fetched_a, pieces, glob, used, my_slot, my_place, valid = ready
+    ready = barrier((send_b, fetched_a, near, glob, used, my_slot, my_place, valid))
+    send_b, fetched_a, near, glob, used, my_slot, my_place, valid = ready
+    pieces = (g_out, *near, *ring_far(near, "tp"))
     grad_context = grad_context_of(tp_at, pieces, out_weight)
 
     fetched_b = exchange(send_b.reshape(ctx_count, -1, LANES)).reshape(send_b.shape)

time: 307 us -> 313 us (1.020); the launches traced: 306 us -> 308 us
  waiting for transfers between devices: 97.5 us -> 105 us
    ppermute x22, waiting for transfers between devices: 51.8 us -> 70.5 us  [shifted(): lax.ppermute(array, axis, [((i + by) % size, i) for i in range(size)])]
    all_to_all x5, waiting for transfers between devices: 43.1 us -> 33.7 us  [exchange(): return lax.all_to_all(parts, 'ctx', split_axis=0, concat_axis=0, tiled=True)]
  transfers between devices with their start and end apart: 31 -> 31, of which waited for: 13 -> 13; matrix products, arithmetic and copies ran while one was open for 4% -> 3% of each run, Pallas kernels for 31% -> 31%
where the time goes in v7:
time: 313 us; the launch traced here: 308 us
  waiting for transfers between devices  105 us (34%)
  Pallas kernels  104 us (33%)
  starting transfers between devices  80 us (26%)
  local copies, waits for them, and re-layouts  16.5 us (5%)
    ppermute x22, waiting for transfers between devices, shifted(): lax.ppermute(array, axis, [((i + by) % size, i) for i in range(size)])  70.5 us
    pallas_call x2, Pallas kernels, attend(): pl.pallas_call(functools.partial(attend_kernel, blocks, last_block), grid...  54.4 us
    ppermute x22, starting transfers between devices, shifted(): lax.ppermute(array, axis, [((i + by) % size, i) for i in range(size)])  36.7 us
    all_to_all x5, waiting for transfers between devices, exchange(): return lax.all_to_all(parts, 'ctx', split_axis=0, concat_axis=0, tiled=True)  33.7 us
    all_to_all x5, starting transfers between devices, exchange(): return lax.all_to_all(parts, 'ctx', split_axis=0, concat_axis=0, tiled=True)  31.1 us
    ppermute x4, starting transfers between devices, passed_along(): return lax.ppermute(array, axis, pairs)  12.3 us
    unnamed x69, local copies, waits for them, and re-layouts  10.7 us
    pallas_call x2, Pallas kernels, pick_blocks(): pl.pallas_call(functools.partial(pick_kernel, slots), grid=(1,), in_specs...  7.87 us
  transfers between devices with their start and end apart: 31, of which 13 were waited for; matrix products, arithmetic and copies ran while one was open for 3% of the time, Pallas kernels for 31%

profile of v7, /device:TPU:0, one launch (start us, length us, event | category | flops | bytes accessed | tf_op | source)
XLA Modules:
  0.0 308.5 jit_solution(13979097705985181799)
XLA Ops:
  0.7 2.4 shard_map.121
  3.0 6.4 %collective-permute-start = (bf16[256,256]{1,0:T(8,128)(2,1)}, bf16[256,256]{1,0:T(8,128)(2,1)S(1)}, u32[]{:S(2)}, u32[]{:S(2)}) collective-permute-start(bf16[256,256]{1,0:T(8,128)(2,1)} %get-tuple-element.77.a), channel_id=1, source_target_pairs={{8,0},{12,4},{16,8},{20,12},{24,16},{28,20},{32,24},{36,28},{40,32... | collective-permute-start | bytes 393224 | tf_op jit(solution)/shard_map/ppermute | solution.py:559
  10.5 4.3 %collective-permute-start.2 = (bf16[384,256]{1,0:T(8,128)(2,1)}, bf16[384,256]{1,0:T(8,128)(2,1)S(1)}, u32[]{:S(2)}, u32[]{:S(2)}) collective-permute-start(bf16[384,256]{1,0:T(8,128)(2,1)} %get-tuple-element.74), channel_id=1, source_target_pairs={{4,0},{8,4},{12,8},{16,12},{20,16},{24,20},{28,24},{32,28},{36,32}... | collective-permute-start | bytes 589832 | tf_op jit(solution)/shard_map/ppermute | solution.py:559
  16.6 3.9 %shard_map.120 = bf16[16384,128]{1,0:T(8,128)(2,1)} custom-call(s32[128]{0:T(128)} %reshape.109.idx_ref, bf16[2048,256]{1,0:T(8,128)(2,1)} %bitcast.25, bf16[2048,256]{1,0:T(8,128)(2,1)} %bitcast.33), custom_call_target="tpu_custom_call" | custom-call | bytes 10485760 | tf_op jit(solution)/shard_map/pallas_call | solution.py:55
  21.2 5.3 %all-to-all-start = ((bf16[16,1024,128]{2,1,0:T(8,128)(2,1)}), bf16[16,1024,128]{2,1,0:T(8,128)(2,1)}, u32[]{:S(2)}, u32[]{:S(2)}) async-start(bf16[16,1024,128]{2,1,0:T(8,128)(2,1)} %bitcast.38), calls=%async_computation | async-start | bytes 8388608 | tf_op jit(solution)/shard_map/all_to_all | solution.py:597
  26.5 2.8 collective-permute-start.3
  29.3 4.0 %shard_map.119 = bf16[16384,128]{1,0:T(8,128)(2,1)} custom-call(s32[128]{0:T(128)} %reshape.109.idx_ref, bf16[2048,256]{1,0:T(8,128)(2,1)} %bitcast.26, bf16[2048,256]{1,0:T(8,128)(2,1)} %bitcast.34), custom_call_target="tpu_custom_call" | custom-call | bytes 10485760 | tf_op jit(solution)/shard_map/pallas_call | solution.py:55
  35.1 1.8 shard_map.122.a
  36.9 3.0 collective-permute-start.5
  40.0 2.3 collective-permute-start.7
  42.8 34.9 %collective-permute-done.5.b = bf16[256,256]{1,0:T(8,128)(2,1)S(1)} collective-permute-done((bf16[256,256]{1,0:T(8,128)(2,1)}, bf16[256,256]{1,0:T(8,128)(2,1)S(1)}, u32[]{:S(2)}, u32[]{:S(2)}) %collective-permute-start.5) | collective-permute-done | bytes 131104 | tf_op jit(solution)/shard_map/ppermute | solution.py:559
  77.7 3.5 %collective-permute-done.6.c = bf16[256,256]{1,0:T(8,128)(2,1)S(1)} collective-permute-done((bf16[256,256]{1,0:T(8,128)(2,1)}, bf16[256,256]{1,0:T(8,128)(2,1)S(1)}, u32[]{:S(2)}, u32[]{:S(2)}) %collective-permute-start.6) | collective-permute-done | bytes 131104 | tf_op jit(solution)/shard_map/ppermute | solution.py:559
  82.5 1.8 shard_map.123
  84.3 4.9 %all-to-all-start.1 = ((bf16[16,1024,128]{2,1,0:T(8,128)(2,1)}), bf16[16,1024,128]{2,1,0:T(8,128)(2,1)}, u32[]{:S(2)}, u32[]{:S(2)}) async-start(bf16[16,1024,128]{2,1,0:T(8,128)(2,1)} %bitcast.37), calls=%async_computation.1 | async-start | bytes 8388608 | tf_op jit(solution)/shard_map/all_to_all | solution.py:597
  89.2 2.8 collective-permute-start.8
  92.2 8.8 %collective-permute-done.8.refs_3_ = bf16[1024,256]{1,0:T(8,128)(2,1)S(1)} collective-permute-done((bf16[1024,256]{1,0:T(8,128)(2,1)S(1)}, bf16[1024,256]{1,0:T(8,128)(2,1)S(1)}, u32[]{:S(2)}, u32[]{:S(2)}) %collective-permute-start.8) | collective-permute-done | bytes 524320 | tf_op jit(solution)/shard_map/ppermute | solution.py:559
  101.0 3.5 %collective-permute-done.9.refs_4_ = bf16[1024,256]{1,0:T(8,128)(2,1)S(1)} collective-permute-done((bf16[1024,256]{1,0:T(8,128)(2,1)S(1)}, bf16[1024,256]{1,0:T(8,128)(2,1)S(1)}, u32[]{:S(2)}, u32[]{:S(2)}) %collective-permute-start.9) | collective-permute-done | bytes 524320 | tf_op jit(solution)/shard_map/ppermute | solution.py:559
  105.4 5.2 %shard_map.124.g_ref = bf16[2048,256]{1,0:T(8,128)(2,1)} custom-call(s32[1]{0:T(128)} %bitcast.10.at_ref, bf16[2048,256]{1,0:T(8,128)(2,1)} %bitcast.4.refs_0_, bf16[2048,256]{1,0:T(8,128)(2,1)} %copy-done.5, bf16[2048,256]{1,0:T(8,128)(2,1)} %copy-done.6, bf16[1024,256]{1,0:T(8,128)(2,1)} %copy-done.7, bf16[1024,256]{1,0:T(8,128)(2,1)} %copy-done.8, ...), custom_call_target="tpu_custom_call" | custom-call | flops 1073741824 | bytes 16777216 | tf_op jit(solution)/shard_map/pallas_call | solution.py:155
  111.2 27.0 %shard_map.125 = (bf16[2048,128]{1,0:T(8,128)(2,1)}, bf16[2048,256]{1,0:T(8,128)(2,1)}, f32[2,2048,128]{2,1,0:T(8,128)}, bf16[2,64,128]{2,1,0:T(8,128)(2,1)}, bf...) custom-call(s32[1]{0:T(128)} %bitcast.me_ref, ...), custom_call_target="tpu_custom_call" | custom-call | flops 6442450944 | bytes 83886080 | tf_op jit(solution)/shard_map/pallas_call | solution.py:288
  138.5 1.7 collective-permute-start.14
  140.9 1.6 collective-permute-start.10
  143.3 9.6 %collective-permute-done.10.refs_11_ = bf16[256,256]{1,0:T(8,128)(2,1)S(1)} collective-permute-done((bf16[256,256]{1,0:T(8,128)(2,1)S(1)}, bf16[256,256]{1,0:T(8,128)(2,1)S(1)}, u32[]{:S(2)}, u32[]{:S(2)}) %collective-permute-start.10) | collective-permute-done | bytes 131104 | tf_op jit(solution)/shard_map/ppermute | solution.py:559
  153.1 2.7 collective-permute-done.12.refs_13_
  157.5 6.6 %all-to-all-start.2 = ((bf16[16,1024,128]{2,1,0:T(8,128)(2,1)}), bf16[16,1024,128]{2,1,0:T(8,128)(2,1)}, u32[]{:S(2)}, u32[]{:S(2)}) async-start(bf16[16,1024,128]{2,1,0:T(8,128)(2,1)} %bitcast.39), calls=%async_computation.2 | async-start | bytes 8388608 | tf_op jit(solution)/shard_map/all_to_all | solution.py:597
  164.0 27.5 %shard_map.126 = (bf16[2048,128]{1,0:T(8,128)(2,1)}, bf16[2048,256]{1,0:T(8,128)(2,1)}, f32[2,2048,128]{2,1,0:T(8,128)}, bf16[2,64,128]{2,1,0:T(8,128)(2,1)}, bf...) custom-call(s32[1]{0:T(128)} %bitcast.me_ref, ...), custom_call_target="tpu_custom_call", output_to_operand_aliasing={{1}: (12, {})} | custom-call | flops 6442450944 | bytes 83886080 | tf_op jit(solution)/shard_map/pallas_call | solution.py:288
  191.5 5.3 %shard_map.127.own_ref = bf16[256,1024]{1,0:T(8,128)(2,1)} custom-call(s32[1]{0:T(128)} %bitcast.10.at_ref, bf16[2048,128]{1,0:T(8,128)(2,1)} %get-tuple-element.87.c0.refs_0_, bf16[2048,128]{1,0:T(8,128)(2,1)} %get-tuple-element.116.c1.refs_5_, bf16[2048,256]{1,0:T(8,128)(2,1)} %bitcast.4.refs_0_, bf16[2048,256]{1,0:T(8,128)(2,1)} %copy-done.5, ...), custom_call_target="tpu_custom_call" | custom-call | flops 1073741824 | bytes 16777216 | tf_op jit(solution)/shard_map/pallas_call | solution.py:469
  196.8 1.4 collective-permute-start.20
  198.9 1.3 collective-permute-start.18
  200.2 4.5 %collective-permute-start.19 = (bf16[2,64,128]{2,1,0:T(8,128)(2,1)S(1)}, bf16[2,64,128]{2,1,0:T(8,128)(2,1)S(1)}, u32[]{:S(2)}, u32[]{:S(2)}) collective-permute-start(bf16[2,64,128]{2,1,0:T(8,128)(2,1)S(1)} %copy-done.32), channel_id=1, source_target_pairs={{0,4},{4,8},{8,12},{12,16},{16,20},{20,24},{24,28},{28,32},{32,36}... | collective-permute-start | bytes 98312 | tf_op jit(solution)/shard_map/ppermute | solution.py:575
  205.6 2.2 shard_map.128
  208.6 2.6 collective-permute-done.20.refs_6_
  211.9 1.5 collective-permute-done.21.refs_7_
  213.5 9.0 %all-to-all-start.3 = ((bf16[16,672,128]{2,1,0:T(8,128)(2,1)}), bf16[16,672,128]{2,1,0:T(8,128)(2,1)S(1)}, u32[]{:S(2)}, u32[]{:S(2)}) async-start(bf16[16,672,128]{2,1,0:T(8,128)(2,1)} %shard_map.128), calls=%async_computation.3 | async-start | bytes 5505024 | tf_op jit(solution)/shard_map/all_to_all | solution.py:597
  224.2 2.1 collective-permute-start.25
  226.3 1.3 collective-permute-start.22
  227.6 5.2 %collective-permute-start.23 = (bf16[2,64,128]{2,1,0:T(8,128)(2,1)}, bf16[2,64,128]{2,1,0:T(8,128)(2,1)}, u32[]{:S(2)}, u32[]{:S(2)}) collective-permute-start(bf16[2,64,128]{2,1,0:T(8,128)(2,1)} %get-tuple-element.105), channel_id=1, source_target_pairs={{0,4},{4,8},{8,12},{12,16},{16,20},{20,24},{24,28},{28,32},{32,36}... | collective-permute-start | bytes 98312 | tf_op jit(solution)/shard_map/ppermute | solution.py:575
  232.8 5.0 %shard_map.130 = (bf16[2048,128]{1,0:T(8,128)(2,1)}, bf16[2048,128]{1,0:T(8,128)(2,1)}, f32[2,2,64,128]{3,2,1,0:T(8,128)}) custom-call(s32[128]{0:T(128)} %reshape.109.idx_ref, s32[16]{0:T(128)} %reduce_sum.47.used_ref, s32[2]{0:T(128)} %bitcast.44, f32[2,2048,128]{2,1,0:T(8,128)} %get-tuple-element.109.win_ref, ...), custom_call_target="tpu_custom_call" | custom-call | flops 4194304 | bytes 16777216 | tf_op jit(solution)/shard_map/pallas_call | solution.py:404
  237.8 19.7 %all-to-all-done.3.back_ref = bf16[16,672,128]{2,1,0:T(8,128)(2,1)S(1)} async-done(((bf16[16,672,128]{2,1,0:T(8,128)(2,1)}), bf16[16,672,128]{2,1,0:T(8,128)(2,1)S(1)}, u32[]{:S(2)}, u32[]{:S(2)}) %all-to-all-start.3) | async-done | bytes 2752544 | tf_op jit(solution)/shard_map/all_to_all | solution.py:597
  257.4 1.5 copy-done.2
  258.9 2.0 shard_map.129
  261.8 5.4 %all-to-all-start.4 = ((bf16[16,672,128]{2,1,0:T(8,128)(2,1)}), bf16[16,672,128]{2,1,0:T(8,128)(2,1)S(1)}, u32[]{:S(2)}, u32[]{:S(2)}) async-start(bf16[16,672,128]{2,1,0:T(8,128)(2,1)} %shard_map.129), calls=%async_computation.4 | async-start | bytes 5505024 | tf_op jit(solution)/shard_map/all_to_all | solution.py:597
  267.2 5.1 %collective-permute-start.15 = (bf16[1024,128]{1,0:T(8,128)(2,1)S(1)}, bf16[1024,128]{1,0:T(8,128)(2,1)S(1)}, u32[]{:S(2)}, u32[]{:S(2)}) collective-permute-start(bf16[1024,128]{1,0:T(8,128)(2,1)S(1)} %slice.20), channel_id=1, source_target_pairs={{1,0},{2,1},{3,2},{0,3},{5,4},{6,5},{7,6},{4,7},{9,8},{10,9},{11,1... | collective-permute-start | bytes 786440 | tf_op jit(solution)/shard_map/ppermute | solution.py:559
  273.4 4.4 %shard_map.132.win_ref = f32[2,2048,128]{2,1,0:T(8,128)} custom-call(s32[128]{0:T(128)} %reshape.109.idx_ref, s32[16]{0:T(128)} %reduce_sum.47.used_ref, f32[2,2048,128]{2,1,0:T(8,128)} %get-tuple-element.125.win_ref, bf16[16,672,128]{2,1,0:T(8,128)(2,1)} %copy-done.2, bf16[2,64,128]{2,1,0:T(8,128)(2,1)} %collective-permute-done.22.up_ref, ...), custom_call_target="tpu_custom_call" | custom-call | flops 4194304 | bytes 14680064 | tf_op jit(solution)/shard_map/pallas_call | solution.py:417
  277.8 3.1 %collective-permute-done.16.refs_4_ = bf16[1024,128]{1,0:T(8,128)(2,1)S(1)} collective-permute-done((bf16[1024,128]{1,0:T(8,128)(2,1)S(1)}, bf16[1024,128]{1,0:T(8,128)(2,1)S(1)}, u32[]{:S(2)}, u32[]{:S(2)}) %collective-permute-start.16) | collective-permute-done | bytes 262176 | tf_op jit(solution)/shard_map/ppermute | solution.py:559
  281.7 5.9 %shard_map.131 = bf16[2048,256]{1,0:T(8,128)(2,1)} custom-call(bf16[2048,128]{1,0:T(8,128)(2,1)} %get-tuple-element.87.c0.refs_0_, bf16[2048,128]{1,0:T(8,128)(2,1)} %copy-done.10, bf16[2048,128]{1,0:T(8,128)(2,1)} %copy-done.12, bf16[1024,128]{1,0:T(8,128)(2,1)} %copy-done.18, bf16[1024,128]{1,0:T(8,128)(2,1)} %copy-done.19, ...), custom_call_target="tpu_custom_call" | custom-call | flops 1073741824 | bytes 18874368 | tf_op jit(solution)/shard_map/pallas_call | solution.py:546
  287.6 14.0 %all-to-all-done.4.back_ref = bf16[16,672,128]{2,1,0:T(8,128)(2,1)S(1)} async-done(((bf16[16,672,128]{2,1,0:T(8,128)(2,1)}), bf16[16,672,128]{2,1,0:T(8,128)(2,1)S(1)}, u32[]{:S(2)}, u32[]{:S(2)}) %all-to-all-start.4) | async-done | bytes 2752544 | tf_op jit(solution)/shard_map/all_to_all | solution.py:597
  301.6 1.5 copy-done.4
  303.1 5.4 %shard_map.133 = (bf16[2048,256]{1,0:T(8,128)(2,1)}, bf16[2048,256]{1,0:T(8,128)(2,1)}, f32[256,1024]{1,0:T(8,128)}) custom-call(s32[128]{0:T(128)} %reshape.109.idx_ref, s32[16]{0:T(128)} %reduce_sum.47.used_ref, s32[2]{0:T(128)} %bitcast.45, s32[1]{0:T(128)} %bitcast.me_ref, f32[2,2048,128]{2,1,0:T(8,128)} %shard_map.132.win_ref, ...), custom_call_target="tpu_custom_call" | custom-call | flops 4194304 | bytes 12582912 | tf_op jit(solution)/shard_map/pallas_call | solution.py:434
  (122 shorter events, 19.9 us)
Async XLA Ops:
  0.6 32.7 %copy-start = (s32[1,512,3]{1,0,2:T(1,128)S(1)}, s32[1,512,3]{1,0,2:T(1,128)}, u32[]{:S(2)}) copy-start(s32[1,512,3]{1,0,2:T(1,128)} %param.14) | copy-start | bytes 18436
  0.7 14.2 %copy-start.31 = (s32[1,512,3]{1,0,2:T(1,128)S(1)}, s32[1,512,3]{1,0,2:T(1,128)}, u32[]{:S(2)}) copy-start(s32[1,512,3]{1,0,2:T(1,128)} %param.13) | copy-start | bytes 18436
  3.0 17.4 %collective-permute-start = (bf16[256,256]{1,0:T(8,128)(2,1)}, bf16[256,256]{1,0:T(8,128)(2,1)S(1)}, u32[]{:S(2)}, u32[]{:S(2)}) collective-permute-start(bf16[256,256]{1,0:T(8,128)(2,1)} %get-tuple-element.77.a), channel_id=1, source_target_pairs={{8,0},{12,4},{16,8},{20,12},{24,16},{28,20},{32,24},{36,28},{40,32... | collective-permute-start | bytes 393224 | tf_op jit(solution)/shard_map/ppermute | solution.py:559
  9.4 11.0 %collective-permute-start.1 = (bf16[384,256]{1,0:T(8,128)(2,1)}, bf16[384,256]{1,0:T(8,128)(2,1)S(1)}, u32[]{:S(2)}, u32[]{:S(2)}) collective-permute-start(bf16[384,256]{1,0:T(8,128)(2,1)} %get-tuple-element.73), channel_id=1, source_target_pairs={{60,0},{0,4},{4,8},{8,12},{12,16},{16,20},{20,24},{24,28},{28,32},... | collective-permute-start | bytes 589832 | tf_op jit(solution)/shard_map/ppermute | solution.py:559
  10.5 10.0 %collective-permute-start.2 = (bf16[384,256]{1,0:T(8,128)(2,1)}, bf16[384,256]{1,0:T(8,128)(2,1)S(1)}, u32[]{:S(2)}, u32[]{:S(2)}) collective-permute-start(bf16[384,256]{1,0:T(8,128)(2,1)} %get-tuple-element.74), channel_id=1, source_target_pairs={{4,0},{8,4},{12,8},{16,12},{20,16},{24,20},{28,24},{32,28},{36,32}... | collective-permute-start | bytes 589832 | tf_op jit(solution)/shard_map/ppermute | solution.py:559
  21.2 63.0 %all-to-all-start = ((bf16[16,1024,128]{2,1,0:T(8,128)(2,1)}), bf16[16,1024,128]{2,1,0:T(8,128)(2,1)}, u32[]{:S(2)}, u32[]{:S(2)}) async-start(bf16[16,1024,128]{2,1,0:T(8,128)(2,1)} %bitcast.38), calls=%async_computation | async-start | bytes 8388608 | tf_op jit(solution)/shard_map/all_to_all | solution.py:597
  26.5 57.7 %collective-permute-start.3 = (bf16[2048,256]{1,0:T(8,128)(2,1)}, bf16[2048,256]{1,0:T(8,128)(2,1)S(1)}, u32[]{:S(2)}, u32[]{:S(2)}) collective-permute-start(bf16[2048,256]{1,0:T(8,128)(2,1)} %bitcast.4.refs_0_), channel_id=1, source_target_pairs={{1,0},{2,1},{3,2},{0,3},{5,4},{6,5},{7,6},{4,7},{9,8},{10,9},{11,1... | collective-permute-start | bytes 3145736 | tf_op jit(solution)/shard_map/ppermute | solution.py:559
  29.3 54.9 %collective-permute-start.4 = (bf16[2048,256]{1,0:T(8,128)(2,1)}, bf16[2048,256]{1,0:T(8,128)(2,1)S(1)}, u32[]{:S(2)}, u32[]{:S(2)}) collective-permute-start(bf16[2048,256]{1,0:T(8,128)(2,1)} %bitcast.4.refs_0_), channel_id=1, source_target_pairs={{3,0},{0,1},{1,2},{2,3},{7,4},{4,5},{5,6},{6,7},{11,8},{8,9},{9,10... | collective-permute-start | bytes 3145736 | tf_op jit(solution)/shard_map/ppermute | solution.py:559
  36.9 40.8 %collective-permute-start.5 = (bf16[256,256]{1,0:T(8,128)(2,1)}, bf16[256,256]{1,0:T(8,128)(2,1)S(1)}, u32[]{:S(2)}, u32[]{:S(2)}) collective-permute-start(bf16[256,256]{1,0:T(8,128)(2,1)} %shard_map.122.a), channel_id=1, source_target_pairs={{16,0},{20,4},{24,8},{28,12},{32,16},{36,20},{40,24},{44,28},{48,3... | collective-permute-start | bytes 393224 | tf_op jit(solution)/shard_map/ppermute | solution.py:559
  40.0 41.2 %collective-permute-start.6 = (bf16[256,256]{1,0:T(8,128)(2,1)}, bf16[256,256]{1,0:T(8,128)(2,1)S(1)}, u32[]{:S(2)}, u32[]{:S(2)}) collective-permute-start(bf16[256,256]{1,0:T(8,128)(2,1)} %shard_map.122.a), channel_id=1, source_target_pairs={{48,0},{52,4},{56,8},{60,12},{0,16},{4,20},{8,24},{12,28},{16,32},... | collective-permute-start | bytes 393224 | tf_op jit(solution)/shard_map/ppermute | solution.py:559
  40.0 41.2 %collective-permute-start.7 = (bf16[256,256]{1,0:T(8,128)(2,1)}, bf16[256,256]{1,0:T(8,128)(2,1)S(1)}, u32[]{:S(2)}, u32[]{:S(2)}) collective-permute-start(bf16[256,256]{1,0:T(8,128)(2,1)} %shard_map.122.a), channel_id=1, source_target_pairs={{32,0},{36,4},{40,8},{44,12},{48,16},{52,20},{56,24},{60,28},{0,32... | collective-permute-start | bytes 393224 | tf_op jit(solution)/shard_map/ppermute | solution.py:559
  77.7 3.5 %copy-start.25 = (bf16[256,256]{1,0:T(8,128)(2,1)}, bf16[256,256]{1,0:T(8,128)(2,1)S(1)}, u32[]{:S(2)}) copy-start(bf16[256,256]{1,0:T(8,128)(2,1)S(1)} %collective-permute-done.5.b) | copy-start | bytes 393220
  84.2 4.9 %copy-start.5 = (bf16[2048,256]{1,0:T(8,128)(2,1)}, bf16[2048,256]{1,0:T(8,128)(2,1)S(1)}, u32[]{:S(2)}) copy-start(bf16[2048,256]{1,0:T(8,128)(2,1)S(1)} %collective-permute-done.3.refs_1_) | copy-start | bytes 3145732
  84.3 7.8 %copy-start.6 = (bf16[2048,256]{1,0:T(8,128)(2,1)}, bf16[2048,256]{1,0:T(8,128)(2,1)S(1)}, u32[]{:S(2)}) copy-start(bf16[2048,256]{1,0:T(8,128)(2,1)S(1)} %collective-permute-done.4.refs_2_) | copy-start | bytes 3145732
  84.3 72.2 %all-to-all-start.1 = ((bf16[16,1024,128]{2,1,0:T(8,128)(2,1)}), bf16[16,1024,128]{2,1,0:T(8,128)(2,1)}, u32[]{:S(2)}, u32[]{:S(2)}) async-start(bf16[16,1024,128]{2,1,0:T(8,128)(2,1)} %bitcast.37), calls=%async_computation.1 | async-start | bytes 8388608 | tf_op jit(solution)/shard_map/all_to_all | solution.py:597
  89.2 11.8 %collective-permute-start.8 = (bf16[1024,256]{1,0:T(8,128)(2,1)S(1)}, bf16[1024,256]{1,0:T(8,128)(2,1)S(1)}, u32[]{:S(2)}, u32[]{:S(2)}) collective-permute-start(bf16[1024,256]{1,0:T(8,128)(2,1)S(1)} %slice.18), channel_id=1, source_target_pairs={{1,0},{2,1},{3,2},{0,3},{5,4},{6,5},{7,6},{4,7},{9,8},{10,9},{11,1... | collective-permute-start | bytes 1572872 | tf_op jit(solution)/shard_map/ppermute | solution.py:559
  92.1 12.5 %collective-permute-start.9 = (bf16[1024,256]{1,0:T(8,128)(2,1)S(1)}, bf16[1024,256]{1,0:T(8,128)(2,1)S(1)}, u32[]{:S(2)}, u32[]{:S(2)}) collective-permute-start(bf16[1024,256]{1,0:T(8,128)(2,1)S(1)} %slice.19), channel_id=1, source_target_pairs={{3,0},{0,1},{1,2},{2,3},{7,4},{4,5},{5,6},{6,7},{11,8},{8,9},{9,10... | collective-permute-start | bytes 1572872 | tf_op jit(solution)/shard_map/ppermute | solution.py:559
  101.0 3.5 %copy-start.7 = (bf16[1024,256]{1,0:T(8,128)(2,1)}, bf16[1024,256]{1,0:T(8,128)(2,1)S(1)}, u32[]{:S(2)}) copy-start(bf16[1024,256]{1,0:T(8,128)(2,1)S(1)} %collective-permute-done.8.refs_3_) | copy-start | bytes 1572868
  111.2 29.0 %copy-start.3 = (bf16[256,1024]{1,0:T(8,128)(2,1)S(1)}, bf16[256,1024]{1,0:T(8,128)(2,1)}, u32[]{:S(2)}) copy-start(bf16[256,1024]{1,0:T(8,128)(2,1)} %refs_8_.1) | copy-start | bytes 1572868
  138.1 17.7 %collective-permute-start.13 = (bf16[2048,128]{1,0:T(8,128)(2,1)}, bf16[2048,128]{1,0:T(8,128)(2,1)S(1)}, u32[]{:S(2)}, u32[]{:S(2)}) collective-permute-start(bf16[2048,128]{1,0:T(8,128)(2,1)} %get-tuple-element.87.c0.refs_0_), channel_id=1, source_target_pairs={{1,0},{2,1},{3,2},{0,3},{5,4},{6,5},{7,6},{4,7},{9,8},{10,9},{11,1... | collective-permute-start | bytes 1572872 | tf_op jit(solution)/shard_map/ppermute | solution.py:559
  138.5 18.0 %collective-permute-start.14 = (bf16[2048,128]{1,0:T(8,128)(2,1)}, bf16[2048,128]{1,0:T(8,128)(2,1)S(1)}, u32[]{:S(2)}, u32[]{:S(2)}) collective-permute-start(bf16[2048,128]{1,0:T(8,128)(2,1)} %get-tuple-element.87.c0.refs_0_), channel_id=1, source_target_pairs={{3,0},{0,1},{1,2},{2,3},{7,4},{4,5},{5,6},{6,7},{11,8},{8,9},{9,10... | collective-permute-start | bytes 1572872 | tf_op jit(solution)/shard_map/ppermute | solution.py:559
  140.9 12.0 %collective-permute-start.10 = (bf16[256,256]{1,0:T(8,128)(2,1)S(1)}, bf16[256,256]{1,0:T(8,128)(2,1)S(1)}, u32[]{:S(2)}, u32[]{:S(2)}) collective-permute-start(bf16[256,256]{1,0:T(8,128)(2,1)S(1)} %get-tuple-element.142), channel_id=1, source_target_pairs={{1,0},{2,1},{3,2},{0,3},{5,4},{6,5},{7,6},{4,7},{9,8},{10,9},{11,1... | collective-permute-start | bytes 393224 | tf_op jit(solution)/shard_map/ppermute | solution.py:559
  142.4 10.7 %collective-permute-start.11 = (bf16[256,256]{1,0:T(8,128)(2,1)S(1)}, bf16[256,256]{1,0:T(8,128)(2,1)S(1)}, u32[]{:S(2)}, u32[]{:S(2)}) collective-permute-start(bf16[256,256]{1,0:T(8,128)(2,1)S(1)} %get-tuple-element.144), channel_id=1, source_target_pairs={{2,0},{3,1},{0,2},{1,3},{6,4},{7,5},{4,6},{5,7},{10,8},{11,9},{8,1... | collective-permute-start | bytes 393224 | tf_op jit(solution)/shard_map/ppermute | solution.py:559
  142.9 12.9 %collective-permute-start.12 = (bf16[256,256]{1,0:T(8,128)(2,1)S(1)}, bf16[256,256]{1,0:T(8,128)(2,1)S(1)}, u32[]{:S(2)}, u32[]{:S(2)}) collective-permute-start(bf16[256,256]{1,0:T(8,128)(2,1)S(1)} %get-tuple-element.141), channel_id=1, source_target_pairs={{3,0},{0,1},{1,2},{2,3},{7,4},{4,5},{5,6},{6,7},{11,8},{8,9},{9,10... | collective-permute-start | bytes 393224 | tf_op jit(solution)/shard_map/ppermute | solution.py:559
  152.9 3.0 copy-start.22
  157.5 56.0 %all-to-all-start.2 = ((bf16[16,1024,128]{2,1,0:T(8,128)(2,1)}), bf16[16,1024,128]{2,1,0:T(8,128)(2,1)}, u32[]{:S(2)}, u32[]{:S(2)}) async-start(bf16[16,1024,128]{2,1,0:T(8,128)(2,1)} %bitcast.39), calls=%async_computation.2 | async-start | bytes 8388608 | tf_op jit(solution)/shard_map/all_to_all | solution.py:597
  191.5 5.3 %copy-start.9 = (bf16[2048,128]{1,0:T(8,128)(2,1)S(1)}, bf16[2048,128]{1,0:T(8,128)(2,1)}, u32[]{:S(2)}) copy-start(bf16[2048,128]{1,0:T(8,128)(2,1)} %get-tuple-element.116.c1.refs_5_) | copy-start | bytes 1572868
  191.5 7.4 %copy-start.33 = (bf16[2,64,128]{2,1,0:T(8,128)(2,1)S(1)}, bf16[2,64,128]{2,1,0:T(8,128)(2,1)}, u32[]{:S(2)}) copy-start(bf16[2,64,128]{2,1,0:T(8,128)(2,1)} %get-tuple-element.100) | copy-start | bytes 98308
  191.5 8.7 %copy-start.32 = (bf16[2,64,128]{2,1,0:T(8,128)(2,1)S(1)}, bf16[2,64,128]{2,1,0:T(8,128)(2,1)}, u32[]{:S(2)}) copy-start(bf16[2,64,128]{2,1,0:T(8,128)(2,1)} %get-tuple-element.101) | copy-start | bytes 98308
  196.8 8.0 %collective-permute-start.17 = (bf16[256,1024]{1,0:T(8,128)(2,1)}, bf16[256,1024]{1,0:T(8,128)(2,1)S(1)}, u32[]{:S(2)}, u32[]{:S(2)}) collective-permute-start(bf16[256,1024]{1,0:T(8,128)(2,1)} %shard_map.127.own_ref), channel_id=1, source_target_pairs={{64,0},{0,64},{65,1},{1,65},{66,2},{2,66},{67,3},{3,67},{68,4},{4,... | collective-permute-start | bytes 1572872 | tf_op jit(solution)/shard_map/ppermute | solution.py:559
  196.8 14.3 %collective-permute-start.20 = (bf16[2048,128]{1,0:T(8,128)(2,1)S(1)}, bf16[2048,128]{1,0:T(8,128)(2,1)S(1)}, u32[]{:S(2)}, u32[]{:S(2)}) collective-permute-start(bf16[2048,128]{1,0:T(8,128)(2,1)S(1)} %copy-done.9), channel_id=1, source_target_pairs={{1,0},{2,1},{3,2},{0,3},{5,4},{6,5},{7,6},{4,7},{9,8},{10,9},{11,1... | collective-permute-start | bytes 1572872 | tf_op jit(solution)/shard_map/ppermute | solution.py:559
  198.2 15.3 %collective-permute-start.21 = (bf16[2048,128]{1,0:T(8,128)(2,1)S(1)}, bf16[2048,128]{1,0:T(8,128)(2,1)}, u32[]{:S(2)}, u32[]{:S(2)}) collective-permute-start(bf16[2048,128]{1,0:T(8,128)(2,1)S(1)} %copy-done.9), channel_id=1, source_target_pairs={{3,0},{0,1},{1,2},{2,3},{7,4},{4,5},{5,6},{6,7},{11,8},{8,9},{9,10... | collective-permute-start | bytes 1572872 | tf_op jit(solution)/shard_map/ppermute | solution.py:559
  198.9 8.8 %collective-permute-start.18 = (bf16[2,64,128]{2,1,0:T(8,128)(2,1)S(1)}, bf16[2,64,128]{2,1,0:T(8,128)(2,1)S(1)}, u32[]{:S(2)}, u32[]{:S(2)}) collective-permute-start(bf16[2,64,128]{2,1,0:T(8,128)(2,1)S(1)} %copy-done.33), channel_id=1, source_target_pairs={{4,0},{8,4},{12,8},{16,12},{20,16},{24,20},{28,24},{32,28},{36,32}... | collective-permute-start | bytes 98312 | tf_op jit(solution)/shard_map/ppermute | solution.py:575
  200.2 8.4 %collective-permute-start.19 = (bf16[2,64,128]{2,1,0:T(8,128)(2,1)S(1)}, bf16[2,64,128]{2,1,0:T(8,128)(2,1)S(1)}, u32[]{:S(2)}, u32[]{:S(2)}) collective-permute-start(bf16[2,64,128]{2,1,0:T(8,128)(2,1)S(1)} %copy-done.32), channel_id=1, source_target_pairs={{0,4},{4,8},{8,12},{12,16},{16,20},{20,24},{24,28},{28,32},{32,36}... | collective-permute-start | bytes 98312 | tf_op jit(solution)/shard_map/ppermute | solution.py:575
  207.8 5.7 %copy-start.29 = (bf16[2,64,128]{2,1,0:T(8,128)(2,1)}, bf16[2,64,128]{2,1,0:T(8,128)(2,1)S(1)}, u32[]{:S(2)}) copy-start(bf16[2,64,128]{2,1,0:T(8,128)(2,1)S(1)} %collective-permute-done.18.up_ref) | copy-start | bytes 98308
  208.6 4.9 %copy-start.30 = (bf16[2,64,128]{2,1,0:T(8,128)(2,1)}, bf16[2,64,128]{2,1,0:T(8,128)(2,1)S(1)}, u32[]{:S(2)}) copy-start(bf16[2,64,128]{2,1,0:T(8,128)(2,1)S(1)} %collective-permute-done.19.down_ref) | copy-start | bytes 98308
  213.5 9.0 %copy-start.14 = (bf16[2048,128]{1,0:T(8,128)(2,1)S(1)}, bf16[2048,128]{1,0:T(8,128)(2,1)}, u32[]{:S(2)}) copy-start(bf16[2048,128]{1,0:T(8,128)(2,1)} %copy-done.13) | copy-start | bytes 1572868
  213.5 43.9 %all-to-all-start.3 = ((bf16[16,672,128]{2,1,0:T(8,128)(2,1)}), bf16[16,672,128]{2,1,0:T(8,128)(2,1)S(1)}, u32[]{:S(2)}, u32[]{:S(2)}) async-start(bf16[16,672,128]{2,1,0:T(8,128)(2,1)} %shard_map.128), calls=%async_computation.3 | async-start | bytes 5505024 | tf_op jit(solution)/shard_map/all_to_all | solution.py:597
  223.3 37.7 %collective-permute-start.24 = (bf16[1024,128]{1,0:T(8,128)(2,1)}, bf16[1024,128]{1,0:T(8,128)(2,1)S(1)}, u32[]{:S(2)}, u32[]{:S(2)}) collective-permute-start(bf16[1024,128]{1,0:T(8,128)(2,1)} %slice.22), channel_id=1, source_target_pairs={{1,0},{2,1},{3,2},{0,3},{5,4},{6,5},{7,6},{4,7},{9,8},{10,9},{11,1... | collective-permute-start | bytes 786440 | tf_op jit(solution)/shard_map/ppermute | solution.py:559
  224.2 36.8 %collective-permute-start.25 = (bf16[1024,128]{1,0:T(8,128)(2,1)S(1)}, bf16[1024,128]{1,0:T(8,128)(2,1)S(1)}, u32[]{:S(2)}, u32[]{:S(2)}) collective-permute-start(bf16[1024,128]{1,0:T(8,128)(2,1)S(1)} %slice.23), channel_id=1, source_target_pairs={{3,0},{0,1},{1,2},{2,3},{7,4},{4,5},{5,6},{6,7},{11,8},{8,9},{9,10... | collective-permute-start | bytes 786440 | tf_op jit(solution)/shard_map/ppermute | solution.py:559
  226.3 34.7 %collective-permute-start.22 = (bf16[2,64,128]{2,1,0:T(8,128)(2,1)}, bf16[2,64,128]{2,1,0:T(8,128)(2,1)}, u32[]{:S(2)}, u32[]{:S(2)}) collective-permute-start(bf16[2,64,128]{2,1,0:T(8,128)(2,1)} %get-tuple-element.104), channel_id=1, source_target_pairs={{4,0},{8,4},{12,8},{16,12},{20,16},{24,20},{28,24},{32,28},{36,32}... | collective-permute-start | bytes 98312 | tf_op jit(solution)/shard_map/ppermute | solution.py:575
  227.6 33.4 %collective-permute-start.23 = (bf16[2,64,128]{2,1,0:T(8,128)(2,1)}, bf16[2,64,128]{2,1,0:T(8,128)(2,1)}, u32[]{:S(2)}, u32[]{:S(2)}) collective-permute-start(bf16[2,64,128]{2,1,0:T(8,128)(2,1)} %get-tuple-element.105), channel_id=1, source_target_pairs={{0,4},{4,8},{8,12},{12,16},{16,20},{20,24},{24,28},{28,32},{32,36}... | collective-permute-start | bytes 98312 | tf_op jit(solution)/shard_map/ppermute | solution.py:575
  261.7 5.4 %copy-start.11 = (bf16[2048,128]{1,0:T(8,128)(2,1)S(1)}, bf16[2048,128]{1,0:T(8,128)(2,1)}, u32[]{:S(2)}) copy-start(bf16[2048,128]{1,0:T(8,128)(2,1)} %copy-done.10) | copy-start | bytes 1572868
  261.8 39.8 %all-to-all-start.4 = ((bf16[16,672,128]{2,1,0:T(8,128)(2,1)}), bf16[16,672,128]{2,1,0:T(8,128)(2,1)S(1)}, u32[]{:S(2)}, u32[]{:S(2)}) async-start(bf16[16,672,128]{2,1,0:T(8,128)(2,1)} %shard_map.129), calls=%async_computation.4 | async-start | bytes 5505024 | tf_op jit(solution)/shard_map/all_to_all | solution.py:597
  267.2 10.6 %collective-permute-start.15 = (bf16[1024,128]{1,0:T(8,128)(2,1)S(1)}, bf16[1024,128]{1,0:T(8,128)(2,1)S(1)}, u32[]{:S(2)}, u32[]{:S(2)}) collective-permute-start(bf16[1024,128]{1,0:T(8,128)(2,1)S(1)} %slice.20), channel_id=1, source_target_pairs={{1,0},{2,1},{3,2},{0,3},{5,4},{6,5},{7,6},{4,7},{9,8},{10,9},{11,1... | collective-permute-start | bytes 786440 | tf_op jit(solution)/shard_map/ppermute | solution.py:559
  273.3 7.7 %collective-permute-start.16 = (bf16[1024,128]{1,0:T(8,128)(2,1)S(1)}, bf16[1024,128]{1,0:T(8,128)(2,1)S(1)}, u32[]{:S(2)}, u32[]{:S(2)}) collective-permute-start(bf16[1024,128]{1,0:T(8,128)(2,1)S(1)} %slice.21), channel_id=1, source_target_pairs={{3,0},{0,1},{1,2},{2,3},{7,4},{4,5},{5,6},{6,7},{11,8},{8,9},{9,10... | collective-permute-start | bytes 786440 | tf_op jit(solution)/shard_map/ppermute | solution.py:559
  277.8 3.1 %copy-start.18 = (bf16[1024,128]{1,0:T(8,128)(2,1)}, bf16[1024,128]{1,0:T(8,128)(2,1)S(1)}, u32[]{:S(2)}) copy-start(bf16[1024,128]{1,0:T(8,128)(2,1)S(1)} %collective-permute-done.15.refs_3_) | copy-start | bytes 786436
  281.7 26.8 %copy-start.1 = (s32[1,512,3]{1,0,2:T(1,128)S(1)}, s32[1,512,3]{1,0,2:T(1,128)}, u32[]{:S(2)}) copy-start(s32[1,512,3]{1,0,2:T(1,128)} %param.14) | copy-start | bytes 18436
  (17 other events, 16.2 us)

commit v8 on v7

--- a/solution.py
+++ b/solution.py
@@ -167,10 +167,10 @@
 
 
 def attend_kernel(
-    blocks, last_block, me_ref, slot_ref, to_ref, valid_ref, q_ref, k_ref, v_ref, g_ref, before_ref, after_ref, glob_ref,
-    fetched_ref, dq_in_ref, ctx_ref, dq_ref, win_out_ref, up_ref, down_ref, gsum_out_ref, *more,
+    blocks, last_block, handed_on, me_ref, slot_ref, to_ref, valid_ref, q_ref, k_ref, v_ref, g_ref, before_ref,
+    after_ref, glob_ref, fetched_ref, *more,
 ):
-    del dq_in_ref
+    ctx_ref, dq_ref, win_out_ref, up_ref, down_ref, gsum_out_ref, *more = more[handed_on:]
     parts_out, (kpad, vpad, win_ref, gsum_ref) = more[:-4], more[-4:]
     if len(parts_out) == 1:
         ret_ref = parts_out[0]
@@ -258,17 +258,16 @@
                 part_ref[d, CARRIED : CARRIED + count, :] = ret_ref[start : start + count, :]
 
 
-def attend(last_block, me, slot, to, valid, q, k, v, g, before, after, glob, fetched, dq_in, column):
+def attend(last_block, me, slot, to, valid, q, k, v, g, before, after, glob, fetched, handed, column):
     rows, width = q.shape
     blocks = rows // BLK
     half = whole((rows, LANES), column)
-    first = dq_in is None
     shapes = [
-        ((rows, LANES), jnp.bfloat16),
+        ((rows, width), jnp.bfloat16),
         ((rows, width), jnp.bfloat16),
         ((2, rows, LANES), jnp.float32),
-        ((2, BLK, LANES), jnp.bfloat16),
-        ((2, BLK, LANES), jnp.bfloat16),
+        ((2, BLK, width), jnp.bfloat16),
+        ((2, BLK, width), jnp.bfloat16),
         ((G * 2 * BLK, LANES), jnp.bfloat16),
     ]
     scratch = [
@@ -277,16 +276,16 @@
         pltpu.VMEM((2, rows + 2 * BLK, LANES), jnp.float32),
         pltpu.VMEM((G, 2, BLK, LANES), jnp.float32),
     ]
-    if first:
-        dq_in = jnp.zeros((16, 128), jnp.bfloat16)
+    if not handed:
         shapes.append((fetched.shape, jnp.bfloat16))
     else:
         shapes += [((16, fetched.shape[0] // 32 + CARRIED, LANES), jnp.bfloat16)] * 2
         scratch.insert(0, pltpu.VMEM(fetched.shape, jnp.bfloat16))
     specs = [whole(shape) for shape, _ in shapes]
-    specs[1] = half
-    return pl.pallas_call(
-        functools.partial(attend_kernel, blocks, last_block),
+    specs[0] = specs[1] = half
+    specs[3] = specs[4] = whole((2, BLK, LANES), column)
+    return pl.pallas_call(
+        functools.partial(attend_kernel, blocks, last_block, len(handed)),
         grid=(1,),
         in_specs=[
             smem(), smem(), smem(), smem(), half, half, half, half,
@@ -294,17 +293,17 @@
             pl.BlockSpec((2 * BLK, LANES), lambda i: (G, column)),
             whole((G, 2, BLK, LANES), column),
             whole(fetched.shape),
-            pl.BlockSpec(memory_space=pl.ANY),
-        ],
+        ]
+        + [pl.BlockSpec(memory_space=pl.ANY)] * len(handed),
         out_specs=tuple(specs),
         out_shape=tuple(jax.ShapeDtypeStruct(*shape) for shape in shapes),
         scratch_shapes=scratch,
-        input_output_aliases={} if first else {12: 1},
+        input_output_aliases={12: 0, 13: 1, 14: 3, 15: 4} if handed else {},
         compiler_params=params(),
         cost_estimate=pl.CostEstimate(
             flops=12 * blocks * 512 * 128 * 128 * 2, bytes_accessed=80 << 20, transcendentals=blocks * 512 * 128
         ),
-    )(me, slot, to, valid, q, k, v, g, before, after, glob, fetched, dq_in)
+    )(me, slot, to, valid, q, k, v, g, before, after, glob, fetched, *handed)
 
 
 def land(entries, idx_ref, used_ref, back_ref, acc):
@@ -404,7 +403,7 @@
     return pl.pallas_call(
         functools.partial(first_kernel, capacity),
         grid=(1,),
-        in_specs=[smem()] * 3 + [whole(x.shape) for x in (win, back, up, down)],
+        in_specs=[smem()] * 3 + [whole(x.shape) for x in (win, back)] + [whole((2, BLK, LANES), 0)] * 2,
         out_specs=(whole(out.shape), whole(out.shape), whole(kept.shape)),
         out_shape=(out, out, kept),
         scratch_shapes=[pltpu.VMEM((2, rows, LANES), jnp.float32)],
@@ -417,7 +416,7 @@
     return pl.pallas_call(
         functools.partial(middle_kernel, capacity),
         grid=(1,),
-        in_specs=[smem()] * 2 + [whole(x.shape) for x in (win, back, up, down)],
+        in_specs=[smem()] * 2 + [whole(x.shape) for x in (win, back)] + [whole((2, BLK, LANES), 1)] * 2,
         out_specs=whole(win.shape),
         out_shape=jax.ShapeDtypeStruct(win.shape, jnp.float32),
         compiler_params=params(),
@@ -443,7 +442,7 @@
     )(idx, used, glob, me, *arrays)
 
 
-def weight_kernel(at_ref, c0, c1, *refs):
+def weight_kernel(at_ref, c_ref, *refs):
     pieces, out_ref, acc = refs[:5], refs[5], refs[6]
 
     @pl.when(pl.program_id(0) == 0)
@@ -452,9 +451,8 @@
 
     width = pieces[0].shape[1]
     values = ring_values(pieces)
-    for r, c in enumerate((c0, c1)):
-        for i, g in enumerate(values):
-            acc[r * LANES : (r + 1) * LANES, i * width : (i + 1) * width] += dot(c[...], g, TN)
+    for i, g in enumerate(values):
+        acc[:, i * width : (i + 1) * width] += dot(c_ref[...], g, TN)
 
     @pl.when(pl.program_id(0) == pl.num_programs(0) - 1)
     def _():
@@ -463,7 +461,7 @@
             out_ref[:, pl.ds(to, width)] = acc[:, i * width : (i + 1) * width].astype(jnp.bfloat16)
 
 
-def weight_terms(at, contexts, pieces):
+def weight_terms(at, context, pieces):
     rows, width = pieces[0].shape
     shape = (2 * LANES, 4 * width)
     return pl.pallas_call(
@@ -471,14 +469,14 @@
         grid_spec=pltpu.PrefetchScalarGridSpec(
             num_scalar_prefetch=1,
             grid=(rows // TILE,),
-            in_specs=[pl.BlockSpec((TILE, LANES), lambda i, at: (i, 0))] * 2 + ring_specs(rows, width),
+            in_specs=[pl.BlockSpec((TILE, width), lambda i, at: (i, 0))] + ring_specs(rows, width),
             out_specs=pl.BlockSpec(shape, lambda i, at: (0, 0)),
             scratch_shapes=[pltpu.VMEM(shape, jnp.float32)],
         ),
         out_shape=jax.ShapeDtypeStruct(shape, jnp.bfloat16),
         compiler_params=params(),
         cost_estimate=pl.CostEstimate(flops=2 * rows * 1024 * 256, bytes_accessed=16 << 20, transcendentals=0),
-    )(at, *contexts, *pieces)
+    )(at, context, *pieces)
 
 
 def carried(array):
@@ -530,28 +528,24 @@
 
 
 def project_kernel(*refs):
-    weights, out_ref = refs[10:14], refs[14]
-    halves = ring_values(refs[:5]), ring_values(refs[5:10])
     total = None
-    for i in range(4):
-        for h in range(2):
-            term = dot(halves[h][i], weights[i][h * LANES : (h + 1) * LANES, :], NN)
-            total = term if total is None else total + term
-    out_ref[...] = total.astype(jnp.bfloat16)
-
-
-def project(pieces_a, pieces_b, weights):
-    rows = pieces_a[0].shape[0]
-    width = weights[0].shape[1]
+    for c, w in zip(ring_values(refs[:5]), refs[5:9]):
+        term = dot(c, w[...], NN)
+        total = term if total is None else total + term
+    refs[9][...] = total.astype(jnp.bfloat16)
+
+
+def project(pieces, weights):
+    rows, width = pieces[0].shape
     return pl.pallas_call(
         project_kernel,
         grid=(rows // TILE,),
-        in_specs=ring_specs(rows, LANES) * 2 + [pl.BlockSpec(w.shape, lambda i: (0, 0)) for w in weights],
+        in_specs=ring_specs(rows, width) + [pl.BlockSpec(w.shape, lambda i: (0, 0)) for w in weights],
         out_specs=pl.BlockSpec((TILE, width), lambda i: (i, 0)),
         out_shape=jax.ShapeDtypeStruct((rows, width), jnp.bfloat16),
         compiler_params=params(),
         cost_estimate=pl.CostEstimate(flops=2 * rows * 1024 * width, bytes_accessed=18 << 20, transcendentals=0),
-    )(*pieces_a, *pieces_b, *weights)
+    )(*pieces, *weights)
 
 
 def shifted(array, axis, by):
@@ -632,43 +626,37 @@
     grad_context = grad_context_of(tp_at, pieces, out_weight)
 
     fetched_b = exchange(send_b.reshape(ctx_count, -1, LANES)).reshape(send_b.shape)
+    last_block = blocks * ctx_count - 1
+
+    def half(to, fetched, handed, column):
+        return attend(
+            last_block, at, my_slot, to, valid, q, k, v, grad_context, before, after, glob, fetched, handed, column
+        )
+
+    context, grad_q, win_a, up, down, gsum_a, ret_a = half(my_slot, fetched_a, (), 0)
+    ret_a, fetched_b = barrier((ret_a, fetched_b))
+
+    back_a = exchange(ret_a.reshape(ctx_count, -1, LANES))
+    context, grad_q, win_b, up, down, gsum_b, ret_b, ret_c = half(my_place, fetched_b, (context, grad_q, up, down), 1)
+    terms = weight_terms(tp_at, context, pieces)
+    ret_b = load_terms(terms, shifted(terms, "dp", 1), (gsum_a, gsum_b), ret_b)
+    ret_b, back_a = barrier((ret_b, back_a))
+
+    back_b = exchange(ret_b)
+    near = ring_near(context, "tp")
+    up, down = passed_along(up, "ctx", -1), passed_along(down, "ctx", 1)
+    ret_c = load_sums(back_b, ret_c)
+    ret_c, up, down, near, w_now = barrier((ret_c, up, down, near, out_weight))
+
+    back_c = exchange(ret_c)
+    first = collect_first(send_idx, used, glob_at, win_a, back_a, up, down, capacity)
+    win_b = collect_middle(send_idx, used, win_b, back_b, up, down, capacity)
     wcols = [None] * tp_count
     for by in range(tp_count):
-        part = lax.dynamic_slice_in_dim(out_weight, (tp_me + by) % tp_count * width, width, 1)
+        part = lax.dynamic_slice_in_dim(w_now, (tp_me + by) % tp_count * width, width, 1)
         wcols[-by % tp_count] = shifted(part, "tp", -by) if by else part
-    last_block = blocks * ctx_count - 1
-
-    def half(to, fetched, dq_in, column):
-        return attend(
-            last_block, at, my_slot, to, valid, q, k, v, grad_context, before, after, glob, fetched, dq_in, column
-        )
-
-    ctx_a, dq_a, win_a, up_a, down_a, gsum_a, ret_a = half(my_slot, fetched_a, None, 0)
-    near_a = ring_near(ctx_a, "tp")
-    ret_a, fetched_b, wcols, near_a = barrier((ret_a, fetched_b, wcols, near_a))
-
-    back_a = exchange(ret_a.reshape(ctx_count, -1, LANES))
-    pieces_a = (ctx_a, *near_a, *ring_far(near_a, "tp"))
-    up_a, down_a = passed_along(up_a, "ctx", -1), passed_along(down_a, "ctx", 1)
-    ctx_b, grad_q, win_b, up_b, down_b, gsum_b, ret_b, ret_c = half(my_place, fetched_b, dq_a, 1)
-    near_b = ring_near(ctx_b, "tp")
-    terms = weight_terms(tp_at, (ctx_a, ctx_b), pieces)
-    ret_b = load_terms(terms, shifted(terms, "dp", 1), (gsum_a, gsum_b), ret_b)
-    ret_b, back_a, up_a, down_a, near_b = barrier((ret_b, back_a, up_a, down_a, near_b))
-
-    back_b = exchange(ret_b)
-    up_b, down_b = passed_along(up_b, "ctx", -1), passed_along(down_b, "ctx", 1)
-    pieces_b = (ctx_b, *near_b, *ring_far(near_b, "tp"))
-    first = collect_first(
-        send_idx, used, glob_at, win_a, back_a, up_a, down_a, capacity
-    )
-    ret_c = load_sums(back_b, ret_c)
-    ret_c, up_b, down_b, pieces_b, first = barrier((ret_c, up_b, down_b, pieces_b, first))
-
-    back_c = exchange(ret_c)
-    projected = project(pieces_a, pieces_b, wcols)
-    win_b = collect_middle(send_idx, used, win_b, back_b, up_b, down_b, capacity)
-    projected, win_b, back_c = barrier((projected, win_b, back_c))
+    projected = project((context, *near, *ring_far(near, "tp")), wcols)
+    projected, win_b, first, back_c = barrier((projected, win_b, first, back_c))
     grad_k, grad_v, grad_weight = collect_last(send_idx, used, glob_at, at, win_b, back_c, first, capacity)
     return projected[None], grad_q[None], grad_k[None], grad_v[None], grad_weight
 

time: 313 us -> 293 us (0.936); the launches traced: 308 us -> 292 us
  starting transfers between devices: 80 us -> 64.8 us
    all_to_all x5, waiting for transfers between devices: 33.7 us -> 48.9 us  [exchange(): return lax.all_to_all(parts, 'ctx', split_axis=0, concat_axis=0, tiled=True)]
    ppermute x22 -> x18, waiting for transfers between devices: 70.5 us -> 57 us  [shifted(): lax.ppermute(array, axis, [((i + by) % size, i) for i in range(size)])]
    ppermute x4 -> x2, starting transfers between devices: 12.3 us -> 5.83 us  [passed_along(): return lax.ppermute(array, axis, pairs)]
    all_to_all x5, starting transfers between devices: 31.1 us -> 26.4 us  [exchange(): return lax.all_to_all(parts, 'ctx', split_axis=0, concat_axis=0, tiled=True)]
    ppermute x22 -> x18, starting transfers between devices: 36.7 us -> 32.6 us  [shifted(): lax.ppermute(array, axis, [((i + by) % size, i) for i in range(size)])]
    unnamed x69 -> x51, local copies, waits for them, and re-layouts: 10.7 us -> 7.51 us
  transfers between devices with their start and end apart: 31 -> 25, of which waited for: 13 -> 12; matrix products, arithmetic and copies ran while one was open for 3% -> 4% of each run, Pallas kernels for 31% -> 32%
where the time goes in v8:
time: 293 us; the launch traced here: 292 us
  waiting for transfers between devices  106 us (36%)
  Pallas kernels  102 us (35%)
  starting transfers between devices  64.8 us (22%)
  local copies, waits for them, and re-layouts  14.4 us (5%)
  other arithmetic  3.46 us (1%)
    ppermute x18, waiting for transfers between devices, shifted(): lax.ppermute(array, axis, [((i + by) % size, i) for i in range(size)])  57 us
    pallas_call x2, Pallas kernels, attend(): pl.pallas_call(functools.partial(attend_kernel, blocks, last_block, len(h...  54.4 us
    all_to_all x5, waiting for transfers between devices, exchange(): return lax.all_to_all(parts, 'ctx', split_axis=0, concat_axis=0, tiled=True)  48.9 us
    ppermute x18, starting transfers between devices, shifted(): lax.ppermute(array, axis, [((i + by) % size, i) for i in range(size)])  32.6 us
    all_to_all x5, starting transfers between devices, exchange(): return lax.all_to_all(parts, 'ctx', split_axis=0, concat_axis=0, tiled=True)  26.4 us
    pallas_call x2, Pallas kernels, pick_blocks(): pl.pallas_call(functools.partial(pick_kernel, slots), grid=(1,), in_specs...  7.75 us
    unnamed x51, local copies, waits for them, and re-layouts  7.51 us
  transfers between devices with their start and end apart: 25, of which 12 were waited for; matrix products, arithmetic and copies ran while one was open for 4% of the time, Pallas kernels for 32%

profile of v8, /device:TPU:0, one launch (start us, length us, event | category | flops | bytes accessed | tf_op | source)
XLA Modules:
  0.0 291.9 jit_solution(6552162549318302998)
XLA Ops:
  0.7 2.4 shard_map.121
  3.0 6.4 %collective-permute-start = (bf16[256,256]{1,0:T(8,128)(2,1)}, bf16[256,256]{1,0:T(8,128)(2,1)S(1)}, u32[]{:S(2)}, u32[]{:S(2)}) collective-permute-start(bf16[256,256]{1,0:T(8,128)(2,1)} %get-tuple-element.65.a), channel_id=1, source_target_pairs={{8,0},{12,4},{16,8},{20,12},{24,16},{28,20},{32,24},{36,28},{40,32... | collective-permute-start | bytes 393224 | tf_op jit(solution)/shard_map/ppermute | solution.py:553
  9.4 1.0 collective-permute-start.1
  10.5 4.3 %collective-permute-start.2 = (bf16[384,256]{1,0:T(8,128)(2,1)}, bf16[384,256]{1,0:T(8,128)(2,1)S(1)}, u32[]{:S(2)}, u32[]{:S(2)}) collective-permute-start(bf16[384,256]{1,0:T(8,128)(2,1)} %get-tuple-element.62), channel_id=1, source_target_pairs={{4,0},{8,4},{12,8},{16,12},{20,16},{24,20},{28,24},{32,28},{36,32}... | collective-permute-start | bytes 589832 | tf_op jit(solution)/shard_map/ppermute | solution.py:553
  17.0 3.9 %shard_map.120 = bf16[16384,128]{1,0:T(8,128)(2,1)} custom-call(s32[128]{0:T(128)} %reshape.109.idx_ref, bf16[2048,256]{1,0:T(8,128)(2,1)} %bitcast.25, bf16[2048,256]{1,0:T(8,128)(2,1)} %bitcast.33), custom_call_target="tpu_custom_call" | custom-call | bytes 10485760 | tf_op jit(solution)/shard_map/pallas_call | solution.py:55
  21.8 4.8 %all-to-all-start = ((bf16[16,1024,128]{2,1,0:T(8,128)(2,1)}), bf16[16,1024,128]{2,1,0:T(8,128)(2,1)}, u32[]{:S(2)}, u32[]{:S(2)}) async-start(bf16[16,1024,128]{2,1,0:T(8,128)(2,1)} %bitcast.38), calls=%async_computation | async-start | bytes 8388608 | tf_op jit(solution)/shard_map/all_to_all | solution.py:591
  26.5 2.8 collective-permute-start.3
  29.4 3.8 %shard_map.119 = bf16[16384,128]{1,0:T(8,128)(2,1)} custom-call(s32[128]{0:T(128)} %reshape.109.idx_ref, bf16[2048,256]{1,0:T(8,128)(2,1)} %bitcast.26, bf16[2048,256]{1,0:T(8,128)(2,1)} %bitcast.34), custom_call_target="tpu_custom_call" | custom-call | bytes 10485760 | tf_op jit(solution)/shard_map/pallas_call | solution.py:55
  35.6 1.8 shard_map.122.a
  37.4 3.1 %collective-permute-start.5 = (bf16[256,256]{1,0:T(8,128)(2,1)}, bf16[256,256]{1,0:T(8,128)(2,1)S(1)}, u32[]{:S(2)}, u32[]{:S(2)}) collective-permute-start(bf16[256,256]{1,0:T(8,128)(2,1)} %shard_map.122.a), channel_id=1, source_target_pairs={{16,0},{20,4},{24,8},{28,12},{32,16},{36,20},{40,24},{44,28},{48,3... | collective-permute-start | bytes 393224 | tf_op jit(solution)/shard_map/ppermute | solution.py:553
  40.5 2.3 collective-permute-start.7
  42.8 1.3 fusion.4
  44.1 34.8 %collective-permute-done.5.b = bf16[256,256]{1,0:T(8,128)(2,1)S(1)} collective-permute-done((bf16[256,256]{1,0:T(8,128)(2,1)}, bf16[256,256]{1,0:T(8,128)(2,1)S(1)}, u32[]{:S(2)}, u32[]{:S(2)}) %collective-permute-start.5) | collective-permute-done | bytes 131104 | tf_op jit(solution)/shard_map/ppermute | solution.py:553
  78.9 2.3 collective-permute-done.6.c
  81.2 2.6 collective-permute-done.7.d
  84.4 1.8 shard_map.123
  86.3 5.9 %all-to-all-start.1 = ((bf16[16,1024,128]{2,1,0:T(8,128)(2,1)}), bf16[16,1024,128]{2,1,0:T(8,128)(2,1)}, u32[]{:S(2)}, u32[]{:S(2)}) async-start(bf16[16,1024,128]{2,1,0:T(8,128)(2,1)} %bitcast.37), calls=%async_computation.1 | async-start | bytes 8388608 | tf_op jit(solution)/shard_map/all_to_all | solution.py:591
  92.2 2.8 collective-permute-start.8
  95.2 8.5 %collective-permute-done.8.refs_3_ = bf16[1024,256]{1,0:T(8,128)(2,1)S(1)} collective-permute-done((bf16[1024,256]{1,0:T(8,128)(2,1)S(1)}, bf16[1024,256]{1,0:T(8,128)(2,1)S(1)}, u32[]{:S(2)}, u32[]{:S(2)}) %collective-permute-start.8) | collective-permute-done | bytes 524320 | tf_op jit(solution)/shard_map/ppermute | solution.py:553
  103.7 3.5 %collective-permute-done.9.refs_4_ = bf16[1024,256]{1,0:T(8,128)(2,1)S(1)} collective-permute-done((bf16[1024,256]{1,0:T(8,128)(2,1)S(1)}, bf16[1024,256]{1,0:T(8,128)(2,1)S(1)}, u32[]{:S(2)}, u32[]{:S(2)}) %collective-permute-start.9) | collective-permute-done | bytes 524320 | tf_op jit(solution)/shard_map/ppermute | solution.py:553
  108.0 5.2 %shard_map.124.g_ref = bf16[2048,256]{1,0:T(8,128)(2,1)} custom-call(s32[1]{0:T(128)} %bitcast.10.at_ref, bf16[2048,256]{1,0:T(8,128)(2,1)} %bitcast.40, bf16[2048,256]{1,0:T(8,128)(2,1)} %copy-done.5, bf16[2048,256]{1,0:T(8,128)(2,1)} %copy-done.6, bf16[1024,256]{1,0:T(8,128)(2,1)} %copy-done.8, bf16[1024,256]{1,0:T(8,128)(2,1)} %copy-done.9, ...), custom_call_target="tpu_custom_call" | custom-call | flops 1073741824 | bytes 16777216 | tf_op jit(solution)/shard_map/pallas_call | solution.py:155
  113.2 27.0 %shard_map.125 = (bf16[2048,256]{1,0:T(8,128)(2,1)}, bf16[2048,256]{1,0:T(8,128)(2,1)}, f32[2,2048,128]{2,1,0:T(8,128)}, bf16[2,64,256]{2,1,0:T(8,128)(2,1)}, bf...) custom-call(s32[1]{0:T(128)} %bitcast.me_ref, ...), custom_call_target="tpu_custom_call" | custom-call | flops 6442450944 | bytes 83886080 | tf_op jit(solution)/shard_map/pallas_call | solution.py:287
  140.2 4.6 %all-to-all-done.1 = bf16[16,1024,128]{2,1,0:T(8,128)(2,1)} async-done(((bf16[16,1024,128]{2,1,0:T(8,128)(2,1)}), bf16[16,1024,128]{2,1,0:T(8,128)(2,1)}, u32[]{:S(2)}, u32[]{:S(2)}) %all-to-all-start.1) | async-done | bytes 4194336 | tf_op jit(solution)/shard_map/all_to_all | solution.py:591
  144.8 4.9 %all-to-all-start.2 = ((bf16[16,1024,128]{2,1,0:T(8,128)(2,1)}), bf16[16,1024,128]{2,1,0:T(8,128)(2,1)}, u32[]{:S(2)}, u32[]{:S(2)}) async-start(bf16[16,1024,128]{2,1,0:T(8,128)(2,1)} %bitcast.39), calls=%async_computation.2 | async-start | bytes 8388608 | tf_op jit(solution)/shard_map/all_to_all | solution.py:591
  149.7 27.4 %shard_map.126 = (bf16[2048,256]{1,0:T(8,128)(2,1)}, bf16[2048,256]{1,0:T(8,128)(2,1)}, f32[2,2048,128]{2,1,0:T(8,128)}, bf16[2,64,256]{2,1,0:T(8,128)(2,1)}, bf...) custom-call(s32[1]{0:T(128)} %bitcast.me_ref, ...), custom_call_target="tpu_custom_call", output_to_operand_aliasing={{0}: (12, {}), {1}: (13, {}), {3}: (14, {}), {4}: (15, {})} | custom-call | flops 6442450944 | bytes 83886080 | tf_op jit(solution)/shard_map/pallas_call | solution.py:287
  177.1 5.2 %shard_map.127.own_ref = bf16[256,1024]{1,0:T(8,128)(2,1)} custom-call(s32[1]{0:T(128)} %bitcast.10.at_ref, bf16[2048,256]{1,0:T(8,128)(2,1)} %get-tuple-element.83.c_ref.refs_0_, bf16[2048,256]{1,0:T(8,128)(2,1)} %bitcast.41, bf16[2048,256]{1,0:T(8,128)(2,1)} %copy-done.5, bf16[2048,256]{1,0:T(8,128)(2,1)} %copy-done.6, bf16[1024,256]{1,0:T(8,128)(2,1)} %copy-done.8, ...), custom_call_target="tpu_custom_call" | custom-call | flops 1073741824 | bytes 16777216 | tf_op jit(solution)/shard_map/pallas_call | solution.py:467
  182.3 2.1 collective-permute-done.10.other_ref
  185.2 2.2 shard_map.128
  187.4 13.7 %all-to-all-done.2.back_ref = bf16[16,1024,128]{2,1,0:T(8,128)(2,1)} async-done(((bf16[16,1024,128]{2,1,0:T(8,128)(2,1)}), bf16[16,1024,128]{2,1,0:T(8,128)(2,1)}, u32[]{:S(2)}, u32[]{:S(2)}) %all-to-all-start.2) | async-done | bytes 4194336 | tf_op jit(solution)/shard_map/all_to_all | solution.py:591
  201.1 5.2 %all-to-all-start.3 = ((bf16[16,672,128]{2,1,0:T(8,128)(2,1)}), bf16[16,672,128]{2,1,0:T(8,128)(2,1)S(1)}, u32[]{:S(2)}, u32[]{:S(2)}) async-start(bf16[16,672,128]{2,1,0:T(8,128)(2,1)} %shard_map.128), calls=%async_computation.3 | async-start | bytes 5505024 | tf_op jit(solution)/shard_map/all_to_all | solution.py:591
  206.3 2.8 collective-permute-start.13
  209.1 1.3 collective-permute-start.11
  210.4 4.5 %collective-permute-start.12 = (bf16[2,64,256]{2,1,0:T(8,128)(2,1)S(1)}, bf16[2,64,256]{2,1,0:T(8,128)(2,1)S(1)}, u32[]{:S(2)}, u32[]{:S(2)}) collective-permute-start(bf16[2,64,256]{2,1,0:T(8,128)(2,1)S(1)} %copy-done.24), channel_id=1, source_target_pairs={{0,4},{4,8},{8,12},{12,16},{16,20},{20,24},{24,28},{28,32},{32,36}... | collective-permute-start | bytes 196616 | tf_op jit(solution)/shard_map/ppermute | solution.py:569
  215.0 25.8 %all-to-all-done.3.back_ref = bf16[16,672,128]{2,1,0:T(8,128)(2,1)S(1)} async-done(((bf16[16,672,128]{2,1,0:T(8,128)(2,1)}), bf16[16,672,128]{2,1,0:T(8,128)(2,1)S(1)}, u32[]{:S(2)}, u32[]{:S(2)}) %all-to-all-start.3) | async-done | bytes 2752544 | tf_op jit(solution)/shard_map/all_to_all | solution.py:591
  240.7 1.6 copy-done.2
  242.3 2.0 shard_map.129
  245.0 5.6 %all-to-all-start.4 = ((bf16[16,672,128]{2,1,0:T(8,128)(2,1)}), bf16[16,672,128]{2,1,0:T(8,128)(2,1)S(1)}, u32[]{:S(2)}, u32[]{:S(2)}) async-start(bf16[16,672,128]{2,1,0:T(8,128)(2,1)} %shard_map.129), calls=%async_computation.4 | async-start | bytes 5505024 | tf_op jit(solution)/shard_map/all_to_all | solution.py:591
  250.6 1.9 slice.14
  252.5 2.8 collective-permute-start.15
  255.2 1.9 slice.15
  257.8 3.2 %collective-permute-start.17 = (bf16[256,256]{1,0:T(8,128)(2,1)S(1)}, bf16[256,256]{1,0:T(8,128)(2,1)S(1)}, u32[]{:S(2)}, u32[]{:S(2)}) collective-permute-start(bf16[256,256]{1,0:T(8,128)(2,1)S(1)} %get-tuple-element.119), channel_id=1, source_target_pairs={{1,0},{2,1},{3,2},{0,3},{5,4},{6,5},{7,6},{4,7},{9,8},{10,9},{11,1... | collective-permute-start | bytes 393224 | tf_op jit(solution)/shard_map/ppermute | solution.py:553
  261.9 4.9 %shard_map.132 = (bf16[2048,128]{1,0:T(8,128)(2,1)}, bf16[2048,128]{1,0:T(8,128)(2,1)}, f32[2,2,64,128]{3,2,1,0:T(8,128)}) custom-call(s32[128]{0:T(128)} %reshape.109.idx_ref, s32[16]{0:T(128)} %reduce_sum.47.used_ref, s32[2]{0:T(128)} %bitcast.48, f32[2,2048,128]{2,1,0:T(8,128)} %get-tuple-element.99.win_ref, ...), custom_call_target="tpu_custom_call" | custom-call | flops 4194304 | bytes 16777216 | tf_op jit(solution)/shard_map/pallas_call | solution.py:403
  266.8 4.4 %shard_map.131.win_ref = f32[2,2048,128]{2,1,0:T(8,128)} custom-call(s32[128]{0:T(128)} %reshape.109.idx_ref, s32[16]{0:T(128)} %reduce_sum.47.used_ref, f32[2,2048,128]{2,1,0:T(8,128)} %get-tuple-element.96.win_ref, bf16[16,672,128]{2,1,0:T(8,128)(2,1)} %copy-done.2, bf16[2,64,256]{2,1,0:T(8,128)(2,1)} %copy-done.11, bf16[2,64,256]{2,1,0:T(8,128)(2,1)} %copy-done.12), custom_call_target="tpu_custom_call" | custom-call | flops 4194304 | bytes 14680064 | tf_op jit(solution)/shard_map/pallas_call | solution.py:416
  272.1 2.3 collective-permute-done.19.refs_8_
  275.0 5.1 %shard_map.130 = bf16[2048,256]{1,0:T(8,128)(2,1)} custom-call(bf16[2048,256]{1,0:T(8,128)(2,1)} %get-tuple-element.83.c_ref.refs_0_, bf16[2048,256]{1,0:T(8,128)(2,1)} %collective-permute-done.13.refs_1_, bf16[2048,256]{1,0:T(8,128)(2,1)} %collective-permute-done.14.refs_2_, bf16[1024,256]{1,0:T(8,128)(2,1)} %collective-permute-done.15.refs_3_, ...), custom_call_target="tpu_custom_call" | custom-call | flops 1073741824 | bytes 18874368 | tf_op jit(solution)/shard_map/pallas_call | solution.py:540
  280.1 4.9 %all-to-all-done.4.back_ref = bf16[16,672,128]{2,1,0:T(8,128)(2,1)S(1)} async-done(((bf16[16,672,128]{2,1,0:T(8,128)(2,1)}), bf16[16,672,128]{2,1,0:T(8,128)(2,1)S(1)}, u32[]{:S(2)}, u32[]{:S(2)}) %all-to-all-start.4) | async-done | bytes 2752544 | tf_op jit(solution)/shard_map/all_to_all | solution.py:591
  285.0 1.5 copy-done.4
  286.5 5.4 %shard_map.133 = (bf16[2048,256]{1,0:T(8,128)(2,1)}, bf16[2048,256]{1,0:T(8,128)(2,1)}, f32[256,1024]{1,0:T(8,128)}) custom-call(s32[128]{0:T(128)} %reshape.109.idx_ref, s32[16]{0:T(128)} %reduce_sum.47.used_ref, s32[2]{0:T(128)} %bitcast.49, s32[1]{0:T(128)} %bitcast.me_ref, f32[2,2048,128]{2,1,0:T(8,128)} %shard_map.131.win_ref, ...), custom_call_target="tpu_custom_call" | custom-call | flops 4194304 | bytes 12582912 | tf_op jit(solution)/shard_map/pallas_call | solution.py:433
  (89 shorter events, 11.6 us)
Async XLA Ops:
  0.6 32.6 %copy-start = (s32[1,512,3]{1,0,2:T(1,128)S(1)}, s32[1,512,3]{1,0,2:T(1,128)}, u32[]{:S(2)}) copy-start(s32[1,512,3]{1,0,2:T(1,128)} %param.14) | copy-start | bytes 18436
  0.7 14.2 %copy-start.22 = (s32[1,512,3]{1,0,2:T(1,128)S(1)}, s32[1,512,3]{1,0,2:T(1,128)}, u32[]{:S(2)}) copy-start(s32[1,512,3]{1,0,2:T(1,128)} %param.13) | copy-start | bytes 18436
  3.0 17.9 %collective-permute-start = (bf16[256,256]{1,0:T(8,128)(2,1)}, bf16[256,256]{1,0:T(8,128)(2,1)S(1)}, u32[]{:S(2)}, u32[]{:S(2)}) collective-permute-start(bf16[256,256]{1,0:T(8,128)(2,1)} %get-tuple-element.65.a), channel_id=1, source_target_pairs={{8,0},{12,4},{16,8},{20,12},{24,16},{28,20},{32,24},{36,28},{40,32... | collective-permute-start | bytes 393224 | tf_op jit(solution)/shard_map/ppermute | solution.py:553
  9.4 11.5 %collective-permute-start.1 = (bf16[384,256]{1,0:T(8,128)(2,1)}, bf16[384,256]{1,0:T(8,128)(2,1)S(1)}, u32[]{:S(2)}, u32[]{:S(2)}) collective-permute-start(bf16[384,256]{1,0:T(8,128)(2,1)} %get-tuple-element.61), channel_id=1, source_target_pairs={{60,0},{0,4},{4,8},{8,12},{12,16},{16,20},{20,24},{24,28},{28,32},... | collective-permute-start | bytes 589832 | tf_op jit(solution)/shard_map/ppermute | solution.py:553
  10.5 10.5 %collective-permute-start.2 = (bf16[384,256]{1,0:T(8,128)(2,1)}, bf16[384,256]{1,0:T(8,128)(2,1)S(1)}, u32[]{:S(2)}, u32[]{:S(2)}) collective-permute-start(bf16[384,256]{1,0:T(8,128)(2,1)} %get-tuple-element.62), channel_id=1, source_target_pairs={{4,0},{8,4},{12,8},{16,12},{20,16},{24,20},{28,24},{32,28},{36,32}... | collective-permute-start | bytes 589832 | tf_op jit(solution)/shard_map/ppermute | solution.py:553
  21.0 0.7 copy-start.21
  21.0 0.7 copy-start.13
  21.0 0.8 copy-start.14
  21.0 5.5 %copy-start.7 = (bf16[1,2048,256]{2,1,0:T(8,128)(2,1)S(1)}, bf16[1,2048,256]{2,1,0:T(8,128)(2,1)}, u32[]{:S(2)}) copy-start(bf16[1,2048,256]{2,1,0:T(8,128)(2,1)} %param.11) | copy-start | bytes 3145732
  21.8 64.5 %all-to-all-start = ((bf16[16,1024,128]{2,1,0:T(8,128)(2,1)}), bf16[16,1024,128]{2,1,0:T(8,128)(2,1)}, u32[]{:S(2)}, u32[]{:S(2)}) async-start(bf16[16,1024,128]{2,1,0:T(8,128)(2,1)} %bitcast.38), calls=%async_computation | async-start | bytes 8388608 | tf_op jit(solution)/shard_map/all_to_all | solution.py:591
  26.5 59.7 %collective-permute-start.3 = (bf16[2048,256]{1,0:T(8,128)(2,1)S(1)}, bf16[2048,256]{1,0:T(8,128)(2,1)S(1)}, u32[]{:S(2)}, u32[]{:S(2)}) collective-permute-start(bf16[2048,256]{1,0:T(8,128)(2,1)S(1)} %bitcast.42), channel_id=1, source_target_pairs={{1,0},{2,1},{3,2},{0,3},{5,4},{6,5},{7,6},{4,7},{9,8},{10,9},{11,1... | collective-permute-start | bytes 3145736 | tf_op jit(solution)/shard_map/ppermute | solution.py:553
  29.4 56.9 %collective-permute-start.4 = (bf16[2048,256]{1,0:T(8,128)(2,1)S(1)}, bf16[2048,256]{1,0:T(8,128)(2,1)S(1)}, u32[]{:S(2)}, u32[]{:S(2)}) collective-permute-start(bf16[2048,256]{1,0:T(8,128)(2,1)S(1)} %bitcast.43), channel_id=1, source_target_pairs={{3,0},{0,1},{1,2},{2,3},{7,4},{4,5},{5,6},{6,7},{11,8},{8,9},{9,10... | collective-permute-start | bytes 3145736 | tf_op jit(solution)/shard_map/ppermute | solution.py:553
  37.4 41.5 %collective-permute-start.5 = (bf16[256,256]{1,0:T(8,128)(2,1)}, bf16[256,256]{1,0:T(8,128)(2,1)S(1)}, u32[]{:S(2)}, u32[]{:S(2)}) collective-permute-start(bf16[256,256]{1,0:T(8,128)(2,1)} %shard_map.122.a), channel_id=1, source_target_pairs={{16,0},{20,4},{24,8},{28,12},{32,16},{36,20},{40,24},{44,28},{48,3... | collective-permute-start | bytes 393224 | tf_op jit(solution)/shard_map/ppermute | solution.py:553
  40.5 40.7 %collective-permute-start.6 = (bf16[256,256]{1,0:T(8,128)(2,1)}, bf16[256,256]{1,0:T(8,128)(2,1)S(1)}, u32[]{:S(2)}, u32[]{:S(2)}) collective-permute-start(bf16[256,256]{1,0:T(8,128)(2,1)} %shard_map.122.a), channel_id=1, source_target_pairs={{48,0},{52,4},{56,8},{60,12},{0,16},{4,20},{8,24},{12,28},{16,32},... | collective-permute-start | bytes 393224 | tf_op jit(solution)/shard_map/ppermute | solution.py:553
  40.5 43.2 %collective-permute-start.7 = (bf16[256,256]{1,0:T(8,128)(2,1)}, bf16[256,256]{1,0:T(8,128)(2,1)S(1)}, u32[]{:S(2)}, u32[]{:S(2)}) collective-permute-start(bf16[256,256]{1,0:T(8,128)(2,1)} %shard_map.122.a), channel_id=1, source_target_pairs={{32,0},{36,4},{40,8},{44,12},{48,16},{52,20},{56,24},{60,28},{0,32... | collective-permute-start | bytes 393224 | tf_op jit(solution)/shard_map/ppermute | solution.py:553
  78.9 4.8 %copy-start.18 = (bf16[256,256]{1,0:T(8,128)(2,1)}, bf16[256,256]{1,0:T(8,128)(2,1)S(1)}, u32[]{:S(2)}) copy-start(bf16[256,256]{1,0:T(8,128)(2,1)S(1)} %collective-permute-done.5.b) | copy-start | bytes 393220
  81.2 2.6 copy-start.19
  83.8 0.7 copy-start.20
  86.2 5.9 %copy-start.5 = (bf16[2048,256]{1,0:T(8,128)(2,1)}, bf16[2048,256]{1,0:T(8,128)(2,1)S(1)}, u32[]{:S(2)}) copy-start(bf16[2048,256]{1,0:T(8,128)(2,1)S(1)} %collective-permute-done.3.refs_1_) | copy-start | bytes 3145732
  86.2 8.8 %copy-start.6 = (bf16[2048,256]{1,0:T(8,128)(2,1)}, bf16[2048,256]{1,0:T(8,128)(2,1)S(1)}, u32[]{:S(2)}) copy-start(bf16[2048,256]{1,0:T(8,128)(2,1)S(1)} %collective-permute-done.4.refs_2_) | copy-start | bytes 3145732
  86.3 58.6 %all-to-all-start.1 = ((bf16[16,1024,128]{2,1,0:T(8,128)(2,1)}), bf16[16,1024,128]{2,1,0:T(8,128)(2,1)}, u32[]{:S(2)}, u32[]{:S(2)}) async-start(bf16[16,1024,128]{2,1,0:T(8,128)(2,1)} %bitcast.37), calls=%async_computation.1 | async-start | bytes 8388608 | tf_op jit(solution)/shard_map/all_to_all | solution.py:591
  92.2 11.5 %collective-permute-start.8 = (bf16[1024,256]{1,0:T(8,128)(2,1)S(1)}, bf16[1024,256]{1,0:T(8,128)(2,1)S(1)}, u32[]{:S(2)}, u32[]{:S(2)}) collective-permute-start(bf16[1024,256]{1,0:T(8,128)(2,1)S(1)} %slice.12), channel_id=1, source_target_pairs={{1,0},{2,1},{3,2},{0,3},{5,4},{6,5},{7,6},{4,7},{9,8},{10,9},{11,1... | collective-permute-start | bytes 1572872 | tf_op jit(solution)/shard_map/ppermute | solution.py:553
  95.1 12.1 %collective-permute-start.9 = (bf16[1024,256]{1,0:T(8,128)(2,1)S(1)}, bf16[1024,256]{1,0:T(8,128)(2,1)S(1)}, u32[]{:S(2)}, u32[]{:S(2)}) collective-permute-start(bf16[1024,256]{1,0:T(8,128)(2,1)S(1)} %slice.13), channel_id=1, source_target_pairs={{3,0},{0,1},{1,2},{2,3},{7,4},{4,5},{5,6},{6,7},{11,8},{8,9},{9,10... | collective-permute-start | bytes 1572872 | tf_op jit(solution)/shard_map/ppermute | solution.py:553
  103.7 3.5 %copy-start.8 = (bf16[1024,256]{1,0:T(8,128)(2,1)}, bf16[1024,256]{1,0:T(8,128)(2,1)S(1)}, u32[]{:S(2)}) copy-start(bf16[1024,256]{1,0:T(8,128)(2,1)S(1)} %collective-permute-done.8.refs_3_) | copy-start | bytes 1572868
  107.2 0.8 copy-start.9
  144.8 56.2 %all-to-all-start.2 = ((bf16[16,1024,128]{2,1,0:T(8,128)(2,1)}), bf16[16,1024,128]{2,1,0:T(8,128)(2,1)}, u32[]{:S(2)}, u32[]{:S(2)}) async-start(bf16[16,1024,128]{2,1,0:T(8,128)(2,1)} %bitcast.39), calls=%async_computation.2 | async-start | bytes 8388608 | tf_op jit(solution)/shard_map/all_to_all | solution.py:591
  182.3 2.1 collective-permute-start.10
  184.4 0.8 copy-start.10
  187.4 21.7 %copy-start.23 = (bf16[2,64,256]{2,1,0:T(8,128)(2,1)S(1)}, bf16[2,64,256]{2,1,0:T(8,128)(2,1)}, u32[]{:S(2)}) copy-start(bf16[2,64,256]{2,1,0:T(8,128)(2,1)} %get-tuple-element.90) | copy-start | bytes 196612
  187.4 23.0 %copy-start.24 = (bf16[2,64,256]{2,1,0:T(8,128)(2,1)S(1)}, bf16[2,64,256]{2,1,0:T(8,128)(2,1)}, u32[]{:S(2)}) copy-start(bf16[2,64,256]{2,1,0:T(8,128)(2,1)} %get-tuple-element.91) | copy-start | bytes 196612
  201.1 39.7 %all-to-all-start.3 = ((bf16[16,672,128]{2,1,0:T(8,128)(2,1)}), bf16[16,672,128]{2,1,0:T(8,128)(2,1)S(1)}, u32[]{:S(2)}, u32[]{:S(2)}) async-start(bf16[16,672,128]{2,1,0:T(8,128)(2,1)} %shard_map.128), calls=%async_computation.3 | async-start | bytes 5505024 | tf_op jit(solution)/shard_map/all_to_all | solution.py:591
  206.3 38.1 %collective-permute-start.13 = (bf16[2048,256]{1,0:T(8,128)(2,1)}, bf16[2048,256]{1,0:T(8,128)(2,1)}, u32[]{:S(2)}, u32[]{:S(2)}) collective-permute-start(bf16[2048,256]{1,0:T(8,128)(2,1)} %get-tuple-element.83.c_ref.refs_0_), channel_id=1, source_target_pairs={{1,0},{2,1},{3,2},{0,3},{5,4},{6,5},{7,6},{4,7},{9,8},{10,9},{11,1... | collective-permute-start | bytes 3145736 | tf_op jit(solution)/shard_map/ppermute | solution.py:553
  209.1 35.3 %collective-permute-start.14 = (bf16[2048,256]{1,0:T(8,128)(2,1)}, bf16[2048,256]{1,0:T(8,128)(2,1)}, u32[]{:S(2)}, u32[]{:S(2)}) collective-permute-start(bf16[2048,256]{1,0:T(8,128)(2,1)} %get-tuple-element.83.c_ref.refs_0_), channel_id=1, source_target_pairs={{3,0},{0,1},{1,2},{2,3},{7,4},{4,5},{5,6},{6,7},{11,8},{8,9},{9,10... | collective-permute-start | bytes 3145736 | tf_op jit(solution)/shard_map/ppermute | solution.py:553
  209.1 35.2 %collective-permute-start.11 = (bf16[2,64,256]{2,1,0:T(8,128)(2,1)S(1)}, bf16[2,64,256]{2,1,0:T(8,128)(2,1)S(1)}, u32[]{:S(2)}, u32[]{:S(2)}) collective-permute-start(bf16[2,64,256]{2,1,0:T(8,128)(2,1)S(1)} %copy-done.23), channel_id=1, source_target_pairs={{4,0},{8,4},{12,8},{16,12},{20,16},{24,20},{28,24},{32,28},{36,32}... | collective-permute-start | bytes 196616 | tf_op jit(solution)/shard_map/ppermute | solution.py:569
  210.4 33.9 %collective-permute-start.12 = (bf16[2,64,256]{2,1,0:T(8,128)(2,1)S(1)}, bf16[2,64,256]{2,1,0:T(8,128)(2,1)S(1)}, u32[]{:S(2)}, u32[]{:S(2)}) collective-permute-start(bf16[2,64,256]{2,1,0:T(8,128)(2,1)S(1)} %copy-done.24), channel_id=1, source_target_pairs={{0,4},{4,8},{8,12},{12,16},{16,20},{20,24},{24,28},{28,32},{32,36}... | collective-permute-start | bytes 196616 | tf_op jit(solution)/shard_map/ppermute | solution.py:569
  240.7 1.6 copy-start.2
  244.3 12.7 %copy-start.3 = (bf16[256,1024]{1,0:T(8,128)(2,1)S(1)}, bf16[256,1024]{1,0:T(8,128)(2,1)}, u32[]{:S(2)}) copy-start(bf16[256,1024]{1,0:T(8,128)(2,1)} %refs_8_.1) | copy-start | bytes 1572868
  245.0 40.0 %all-to-all-start.4 = ((bf16[16,672,128]{2,1,0:T(8,128)(2,1)}), bf16[16,672,128]{2,1,0:T(8,128)(2,1)S(1)}, u32[]{:S(2)}, u32[]{:S(2)}) async-start(bf16[16,672,128]{2,1,0:T(8,128)(2,1)} %shard_map.129), calls=%async_computation.4 | async-start | bytes 5505024 | tf_op jit(solution)/shard_map/all_to_all | solution.py:591
  252.5 21.9 %collective-permute-start.15 = (bf16[1024,256]{1,0:T(8,128)(2,1)}, bf16[1024,256]{1,0:T(8,128)(2,1)}, u32[]{:S(2)}, u32[]{:S(2)}) collective-permute-start(bf16[1024,256]{1,0:T(8,128)(2,1)} %slice.14), channel_id=1, source_target_pairs={{1,0},{2,1},{3,2},{0,3},{5,4},{6,5},{7,6},{4,7},{9,8},{10,9},{11,1... | collective-permute-start | bytes 1572872 | tf_op jit(solution)/shard_map/ppermute | solution.py:553
  257.1 17.3 %collective-permute-start.16 = (bf16[1024,256]{1,0:T(8,128)(2,1)}, bf16[1024,256]{1,0:T(8,128)(2,1)}, u32[]{:S(2)}, u32[]{:S(2)}) collective-permute-start(bf16[1024,256]{1,0:T(8,128)(2,1)} %slice.15), channel_id=1, source_target_pairs={{3,0},{0,1},{1,2},{2,3},{7,4},{4,5},{5,6},{6,7},{11,8},{8,9},{9,10... | collective-permute-start | bytes 1572872 | tf_op jit(solution)/shard_map/ppermute | solution.py:553
  257.8 13.4 %collective-permute-start.17 = (bf16[256,256]{1,0:T(8,128)(2,1)S(1)}, bf16[256,256]{1,0:T(8,128)(2,1)S(1)}, u32[]{:S(2)}, u32[]{:S(2)}) collective-permute-start(bf16[256,256]{1,0:T(8,128)(2,1)S(1)} %get-tuple-element.119), channel_id=1, source_target_pairs={{1,0},{2,1},{3,2},{0,3},{5,4},{6,5},{7,6},{4,7},{9,8},{10,9},{11,1... | collective-permute-start | bytes 393224 | tf_op jit(solution)/shard_map/ppermute | solution.py:553
  261.0 11.0 %collective-permute-start.18 = (bf16[256,256]{1,0:T(8,128)(2,1)S(1)}, bf16[256,256]{1,0:T(8,128)(2,1)S(1)}, u32[]{:S(2)}, u32[]{:S(2)}) collective-permute-start(bf16[256,256]{1,0:T(8,128)(2,1)S(1)} %get-tuple-element.118), channel_id=1, source_target_pairs={{2,0},{3,1},{0,2},{1,3},{6,4},{7,5},{4,6},{5,7},{10,8},{11,9},{8,1... | collective-permute-start | bytes 393224 | tf_op jit(solution)/shard_map/ppermute | solution.py:553
  261.0 13.3 %collective-permute-start.19 = (bf16[256,256]{1,0:T(8,128)(2,1)S(1)}, bf16[256,256]{1,0:T(8,128)(2,1)S(1)}, u32[]{:S(2)}, u32[]{:S(2)}) collective-permute-start(bf16[256,256]{1,0:T(8,128)(2,1)S(1)} %get-tuple-element.117), channel_id=1, source_target_pairs={{3,0},{0,1},{1,2},{2,3},{7,4},{4,5},{5,6},{6,7},{11,8},{8,9},{9,10... | collective-permute-start | bytes 393224 | tf_op jit(solution)/shard_map/ppermute | solution.py:553
  271.2 3.2 %copy-start.15 = (bf16[256,256]{1,0:T(8,128)(2,1)}, bf16[256,256]{1,0:T(8,128)(2,1)S(1)}, u32[]{:S(2)}) copy-start(bf16[256,256]{1,0:T(8,128)(2,1)S(1)} %collective-permute-done.17.refs_6_) | copy-start | bytes 393220
  272.1 2.3 copy-start.16
  274.3 0.6 copy-start.17
  285.0 1.5 copy-start.4
  285.0 6.9 %copy-start.1 = (s32[1,512,3]{1,0,2:T(1,128)S(1)}, s32[1,512,3]{1,0,2:T(1,128)}, u32[]{:S(2)}) copy-start(s32[1,512,3]{1,0,2:T(1,128)} %param.14) | copy-start | bytes 18436
  (2 other events, 1.3 us)

commit v9 on v8

--- a/solution.py
+++ b/solution.py
@@ -40,8 +40,10 @@
 
 
 def pick_kernel(slots, idx_ref, k_ref, v_ref, out_ref):
+    first = pl.program_id(0) * slots
+
     def body(s, _):
-        src = pl.multiple_of(idx_ref[s] * BLK, BLK)
+        src = pl.multiple_of(idx_ref[first + s] * BLK, BLK)
         dst = pl.multiple_of(s * 2 * BLK, 2 * BLK)
         out_ref[pl.ds(dst, BLK), :] = k_ref[pl.ds(src, BLK), :]
         out_ref[pl.ds(dst + BLK, BLK), :] = v_ref[pl.ds(src, BLK), :]
@@ -53,10 +55,10 @@
 def pick_blocks(idx, keys, values, column, slots):
     rows = keys.shape[0]
     return pl.pallas_call(
-        functools.partial(pick_kernel, slots),
-        grid=(1,),
+        functools.partial(pick_kernel, slots // 4),
+        grid=(4,),
         in_specs=[smem(), whole((rows, LANES), column), whole((rows, LANES), column)],
-        out_specs=whole((slots * 2 * BLK, LANES)),
+        out_specs=pl.BlockSpec((slots // 4 * 2 * BLK, LANES), lambda i: (i, 0)),
         out_shape=jax.ShapeDtypeStruct((slots * 2 * BLK, LANES), jnp.bfloat16),
         compiler_params=params(),
         cost_estimate=pl.CostEstimate(flops=0, bytes_accessed=10 << 20, transcendentals=0),
@@ -507,24 +509,10 @@
     )(own, other, *sums, part)
 
 
-def sum_kernel(back_ref, part_ref, out_ref):
-    del part_ref
-    total = jnp.sum(back_ref[...].astype(jnp.float32), axis=0).astype(jnp.bfloat16)
-    for d in range(out_ref.shape[0]):
-        out_ref[d] = total
-
-
 def load_sums(back, part):
-    return pl.pallas_call(
-        sum_kernel,
-        grid=(1,),
-        in_specs=[carried(back), pl.BlockSpec(memory_space=pl.ANY)],
-        out_specs=carried(part),
-        out_shape=jax.ShapeDtypeStruct(part.shape, part.dtype),
-        input_output_aliases={1: 0},
-        compiler_params=params(),
-        cost_estimate=pl.CostEstimate(flops=1 << 18, bytes_accessed=4 << 20, transcendentals=0),
-    )(back, part)
+    total = jnp.sum(back[:, :CARRIED].astype(jnp.float32), axis=0).astype(jnp.bfloat16)
+    spread = jnp.broadcast_to(total[None], (part.shape[0], CARRIED, LANES))
+    return lax.dynamic_update_slice_in_dim(part, spread, 0, 1)
 
 
 def project_kernel(*refs):
@@ -609,7 +597,7 @@
     fetched_a = exchange(send_a.reshape(ctx_count, -1, LANES)).reshape(send_a.shape)
     near = ring_near(g_now, "tp")
     glob = sum_four((picked, before, after, across))
-    glob = sum_four((glob, *[shifted(glob, "ctx", 4 * by) for by in (1, 3, 2)])).reshape(G, 2, BLK, width)
+    globs = [glob] + [shifted(glob, "ctx", 4 * by) for by in (1, 3, 2)]
     send_b = pick_blocks(send_idx, k, v, 1, slots)
     used = jnp.sum(mine.astype(jnp.int32), axis=1)
     my_owner = lax.dynamic_index_in_dim(owner, me, 0, keepdims=False)
@@ -620,8 +608,9 @@
     my_place = (my_part * ctx_count + my_owner) * part_size + my_rank % part_size
     valid = lax.dynamic_slice_in_dim(random_valid[0], me * blocks, blocks, 0).reshape(-1)
 
-    ready = barrier((send_b, fetched_a, near, glob, used, my_slot, my_place, valid))
-    send_b, fetched_a, near, glob, used, my_slot, my_place, valid = ready
+    ready = barrier((send_b, fetched_a, near, globs, used, my_slot, my_place, valid))
+    send_b, fetched_a, near, globs, used, my_slot, my_place, valid = ready
+    glob = sum_four(globs).reshape(G, 2, BLK, width)
     pieces = (g_out, *near, *ring_far(near, "tp"))
     grad_context = grad_context_of(tp_at, pieces, out_weight)
 

time: 293 us -> 290 us (0.990)
  local copies, waits for them, and re-layouts: 14.4 us -> 11.3 us
    unnamed x51 -> x53, local copies, waits for them, and re-layouts: 7.51 us -> 4.71 us
    pallas_call x3 -> x2, Pallas kernels: 9.79 us -> 7.88 us  [pick_blocks(): pl.pallas_call(functools.partial(pick_kernel, slots // 4), grid=(4,), in_...]
where the time goes in v9:
time: 290 us; the launch traced here: 289 us
  waiting for transfers between devices  105 us (36%)
  Pallas kernels  101 us (35%)
  starting transfers between devices  67.2 us (23%)
  local copies, waits for them, and re-layouts  11.3 us (4%)
  other arithmetic  3.61 us (1%)
    ppermute x18, waiting for transfers between devices, shifted(): lax.ppermute(array, axis, [((i + by) % size, i) for i in range(size)])  56.9 us
    pallas_call x2, Pallas kernels, attend(): pl.pallas_call(functools.partial(attend_kernel, blocks, last_block, len(h...  54.4 us
    all_to_all x5, waiting for transfers between devices, exchange(): return lax.all_to_all(parts, 'ctx', split_axis=0, concat_axis=0, tiled=True)  48.4 us
    ppermute x18, starting transfers between devices, shifted(): lax.ppermute(array, axis, [((i + by) % size, i) for i in range(size)])  32.6 us
    all_to_all x5, starting transfers between devices, exchange(): return lax.all_to_all(parts, 'ctx', split_axis=0, concat_axis=0, tiled=True)  28.6 us
    pallas_call x2, Pallas kernels, pick_blocks(): pl.pallas_call(functools.partial(pick_kernel, slots // 4), grid=(4,), in_...  7.88 us
    ppermute x2, starting transfers between devices, passed_along(): return lax.ppermute(array, axis, pairs)  6.01 us
  transfers between devices with their start and end apart: 25, of which 12 were waited for; matrix products, arithmetic and copies ran while one was open for 4% of the time, Pallas kernels for 32%

profile of v9, /device:TPU:0, one launch (start us, length us, event | category | flops | bytes accessed | tf_op | source)
XLA Modules:
  0.0 289.1 jit_solution(12917000754858994011)
XLA Ops:
  0.7 2.4 shard_map.121
  3.0 6.4 %collective-permute-start = (bf16[256,256]{1,0:T(8,128)(2,1)}, bf16[256,256]{1,0:T(8,128)(2,1)S(1)}, u32[]{:S(2)}, u32[]{:S(2)}) collective-permute-start(bf16[256,256]{1,0:T(8,128)(2,1)} %get-tuple-element.68.a), channel_id=1, source_target_pairs={{8,0},{12,4},{16,8},{20,12},{24,16},{28,20},{32,24},{36,28},{40,32... | collective-permute-start | bytes 393224 | tf_op jit(solution)/shard_map/ppermute | solution.py:541
  9.4 1.0 collective-permute-start.1
  10.5 4.3 %collective-permute-start.2 = (bf16[384,256]{1,0:T(8,128)(2,1)}, bf16[384,256]{1,0:T(8,128)(2,1)S(1)}, u32[]{:S(2)}, u32[]{:S(2)}) collective-permute-start(bf16[384,256]{1,0:T(8,128)(2,1)} %get-tuple-element.65), channel_id=1, source_target_pairs={{4,0},{8,4},{12,8},{16,12},{20,16},{24,20},{28,24},{32,28},{36,32}... | collective-permute-start | bytes 589832 | tf_op jit(solution)/shard_map/ppermute | solution.py:541
  17.1 4.0 %shard_map.120 = bf16[16384,128]{1,0:T(8,128)(2,1)} custom-call(s32[128]{0:T(128)} %reshape.110.idx_ref, bf16[2048,256]{1,0:T(8,128)(2,1)} %bitcast.25, bf16[2048,256]{1,0:T(8,128)(2,1)} %bitcast.33), custom_call_target="tpu_custom_call" | custom-call | bytes 10485760 | tf_op jit(solution)/shard_map/pallas_call | solution.py:57
  21.9 4.6 %all-to-all-start = ((bf16[16,1024,128]{2,1,0:T(8,128)(2,1)}), bf16[16,1024,128]{2,1,0:T(8,128)(2,1)}, u32[]{:S(2)}, u32[]{:S(2)}) async-start(bf16[16,1024,128]{2,1,0:T(8,128)(2,1)} %bitcast.38), calls=%async_computation | async-start | bytes 8388608 | tf_op jit(solution)/shard_map/all_to_all | solution.py:579
  26.5 2.8 collective-permute-start.3
  29.4 3.9 %shard_map.119 = bf16[16384,128]{1,0:T(8,128)(2,1)} custom-call(s32[128]{0:T(128)} %reshape.110.idx_ref, bf16[2048,256]{1,0:T(8,128)(2,1)} %bitcast.26, bf16[2048,256]{1,0:T(8,128)(2,1)} %bitcast.34), custom_call_target="tpu_custom_call" | custom-call | bytes 10485760 | tf_op jit(solution)/shard_map/pallas_call | solution.py:57
  35.8 1.8 shard_map.122.a
  37.6 3.1 %collective-permute-start.5 = (bf16[256,256]{1,0:T(8,128)(2,1)}, bf16[256,256]{1,0:T(8,128)(2,1)S(1)}, u32[]{:S(2)}, u32[]{:S(2)}) collective-permute-start(bf16[256,256]{1,0:T(8,128)(2,1)} %shard_map.122.a), channel_id=1, source_target_pairs={{16,0},{20,4},{24,8},{28,12},{32,16},{36,20},{40,24},{44,28},{48,3... | collective-permute-start | bytes 393224 | tf_op jit(solution)/shard_map/ppermute | solution.py:541
  40.7 2.3 collective-permute-start.7
  43.0 1.3 fusion.4
  44.2 35.4 %collective-permute-done.5.b = bf16[256,256]{1,0:T(8,128)(2,1)S(1)} collective-permute-done((bf16[256,256]{1,0:T(8,128)(2,1)}, bf16[256,256]{1,0:T(8,128)(2,1)S(1)}, u32[]{:S(2)}, u32[]{:S(2)}) %collective-permute-start.5) | collective-permute-done | bytes 131104 | tf_op jit(solution)/shard_map/ppermute | solution.py:541
  79.6 3.4 %collective-permute-done.6.c = bf16[256,256]{1,0:T(8,128)(2,1)S(1)} collective-permute-done((bf16[256,256]{1,0:T(8,128)(2,1)}, bf16[256,256]{1,0:T(8,128)(2,1)S(1)}, u32[]{:S(2)}, u32[]{:S(2)}) %collective-permute-start.6) | collective-permute-done | bytes 131104 | tf_op jit(solution)/shard_map/ppermute | solution.py:541
  83.1 2.2 collective-permute-done.7.d
  85.9 6.1 %all-to-all-start.1 = ((bf16[16,1024,128]{2,1,0:T(8,128)(2,1)}), bf16[16,1024,128]{2,1,0:T(8,128)(2,1)}, u32[]{:S(2)}, u32[]{:S(2)}) async-start(bf16[16,1024,128]{2,1,0:T(8,128)(2,1)} %bitcast.37), calls=%async_computation.1 | async-start | bytes 8388608 | tf_op jit(solution)/shard_map/all_to_all | solution.py:579
  92.1 2.8 collective-permute-start.8
  95.0 1.8 shard_map.124
  96.8 6.9 %collective-permute-done.8.refs_3_ = bf16[1024,256]{1,0:T(8,128)(2,1)S(1)} collective-permute-done((bf16[1024,256]{1,0:T(8,128)(2,1)S(1)}, bf16[1024,256]{1,0:T(8,128)(2,1)S(1)}, u32[]{:S(2)}, u32[]{:S(2)}) %collective-permute-start.8) | collective-permute-done | bytes 524320 | tf_op jit(solution)/shard_map/ppermute | solution.py:541
  103.7 3.5 %collective-permute-done.9.refs_4_ = bf16[1024,256]{1,0:T(8,128)(2,1)S(1)} collective-permute-done((bf16[1024,256]{1,0:T(8,128)(2,1)S(1)}, bf16[1024,256]{1,0:T(8,128)(2,1)S(1)}, u32[]{:S(2)}, u32[]{:S(2)}) %collective-permute-start.9) | collective-permute-done | bytes 524320 | tf_op jit(solution)/shard_map/ppermute | solution.py:541
  108.0 5.2 %shard_map.123.g_ref = bf16[2048,256]{1,0:T(8,128)(2,1)} custom-call(s32[1]{0:T(128)} %bitcast.9.at_ref, bf16[2048,256]{1,0:T(8,128)(2,1)} %bitcast.40, bf16[2048,256]{1,0:T(8,128)(2,1)} %copy-done.4, bf16[2048,256]{1,0:T(8,128)(2,1)} %copy-done.5, bf16[1024,256]{1,0:T(8,128)(2,1)} %copy-done.7, bf16[1024,256]{1,0:T(8,128)(2,1)} %copy-done.8, ...), custom_call_target="tpu_custom_call" | custom-call | flops 1073741824 | bytes 16777216 | tf_op jit(solution)/shard_map/pallas_call | solution.py:157
  113.2 27.0 %shard_map.125 = (bf16[2048,256]{1,0:T(8,128)(2,1)}, bf16[2048,256]{1,0:T(8,128)(2,1)}, f32[2,2048,128]{2,1,0:T(8,128)}, bf16[2,64,256]{2,1,0:T(8,128)(2,1)}, bf...) custom-call(s32[1]{0:T(128)} %bitcast.me_ref, ...), custom_call_target="tpu_custom_call" | custom-call | flops 6442450944 | bytes 83886080 | tf_op jit(solution)/shard_map/pallas_call | solution.py:289
  140.2 4.8 %all-to-all-done.1 = bf16[16,1024,128]{2,1,0:T(8,128)(2,1)} async-done(((bf16[16,1024,128]{2,1,0:T(8,128)(2,1)}), bf16[16,1024,128]{2,1,0:T(8,128)(2,1)}, u32[]{:S(2)}, u32[]{:S(2)}) %all-to-all-start.1) | async-done | bytes 4194336 | tf_op jit(solution)/shard_map/all_to_all | solution.py:579
  145.0 5.8 %all-to-all-start.2 = ((bf16[16,1024,128]{2,1,0:T(8,128)(2,1)}), bf16[16,1024,128]{2,1,0:T(8,128)(2,1)}, u32[]{:S(2)}, u32[]{:S(2)}) async-start(bf16[16,1024,128]{2,1,0:T(8,128)(2,1)} %bitcast.39), calls=%async_computation.2 | async-start | bytes 8388608 | tf_op jit(solution)/shard_map/all_to_all | solution.py:579
  150.8 27.4 %shard_map.126 = (bf16[2048,256]{1,0:T(8,128)(2,1)}, bf16[2048,256]{1,0:T(8,128)(2,1)}, f32[2,2048,128]{2,1,0:T(8,128)}, bf16[2,64,256]{2,1,0:T(8,128)(2,1)}, bf...) custom-call(s32[1]{0:T(128)} %bitcast.me_ref, ...), custom_call_target="tpu_custom_call", output_to_operand_aliasing={{0}: (12, {}), {1}: (13, {}), {3}: (14, {}), {4}: (15, {})} | custom-call | flops 6442450944 | bytes 83886080 | tf_op jit(solution)/shard_map/pallas_call | solution.py:289
  178.2 5.1 %shard_map.127.own_ref = bf16[256,1024]{1,0:T(8,128)(2,1)} custom-call(s32[1]{0:T(128)} %bitcast.9.at_ref, bf16[2048,256]{1,0:T(8,128)(2,1)} %get-tuple-element.89.c_ref.refs_0_, bf16[2048,256]{1,0:T(8,128)(2,1)} %bitcast.41, bf16[2048,256]{1,0:T(8,128)(2,1)} %copy-done.4, bf16[2048,256]{1,0:T(8,128)(2,1)} %copy-done.5, bf16[1024,256]{1,0:T(8,128)(2,1)} %copy-done.7, ...), custom_call_target="tpu_custom_call" | custom-call | flops 1073741824 | bytes 16777216 | tf_op jit(solution)/shard_map/pallas_call | solution.py:469
  183.3 2.1 collective-permute-done.10.other_ref
  186.2 2.2 shard_map.128
  188.4 12.1 %all-to-all-done.2.back_ref = bf16[16,1024,128]{2,1,0:T(8,128)(2,1)} async-done(((bf16[16,1024,128]{2,1,0:T(8,128)(2,1)}), bf16[16,1024,128]{2,1,0:T(8,128)(2,1)}, u32[]{:S(2)}, u32[]{:S(2)}) %all-to-all-start.2) | async-done | bytes 4194336 | tf_op jit(solution)/shard_map/all_to_all | solution.py:579
  200.5 7.1 %all-to-all-start.3 = ((bf16[16,672,128]{2,1,0:T(8,128)(2,1)}), bf16[16,672,128]{2,1,0:T(8,128)(2,1)S(1)}, u32[]{:S(2)}, u32[]{:S(2)}) async-start(bf16[16,672,128]{2,1,0:T(8,128)(2,1)} %shard_map.128), calls=%async_computation.3 | async-start | bytes 5505024 | tf_op jit(solution)/shard_map/all_to_all | solution.py:579
  207.6 2.8 collective-permute-start.13
  210.5 1.3 collective-permute-start.11
  211.8 4.7 %collective-permute-start.12 = (bf16[2,64,256]{2,1,0:T(8,128)(2,1)S(1)}, bf16[2,64,256]{2,1,0:T(8,128)(2,1)S(1)}, u32[]{:S(2)}, u32[]{:S(2)}) collective-permute-start(bf16[2,64,256]{2,1,0:T(8,128)(2,1)S(1)} %copy-done.25), channel_id=1, source_target_pairs={{0,4},{4,8},{8,12},{12,16},{16,20},{20,24},{24,28},{28,32},{32,36}... | collective-permute-start | bytes 196616 | tf_op jit(solution)/shard_map/ppermute | solution.py:557
  216.5 25.6 %all-to-all-done.3.back_ref = bf16[16,672,128]{2,1,0:T(8,128)(2,1)S(1)} async-done(((bf16[16,672,128]{2,1,0:T(8,128)(2,1)}), bf16[16,672,128]{2,1,0:T(8,128)(2,1)S(1)}, u32[]{:S(2)}, u32[]{:S(2)}) %all-to-all-start.3) | async-done | bytes 2752544 | tf_op jit(solution)/shard_map/all_to_all | solution.py:579
  242.2 1.2 broadcast_dynamic-update-slice_fusion
  244.0 5.0 %all-to-all-start.4 = ((bf16[16,672,128]{2,1,0:T(8,128)(2,1)}), bf16[16,672,128]{2,1,0:T(8,128)(2,1)}, u32[]{:S(2)}, u32[]{:S(2)}) async-start(bf16[16,672,128]{2,1,0:T(8,128)(2,1)} %broadcast_dynamic-update-slice_fusion), calls=%async_computation.4 | async-start | bytes 5505024 | tf_op jit(solution)/shard_map/all_to_all | solution.py:579
  249.0 1.1 slice.18
  250.1 2.8 collective-permute-start.15
  252.9 1.1 slice.19
  254.9 3.1 %collective-permute-start.17 = (bf16[256,256]{1,0:T(8,128)(2,1)S(1)}, bf16[256,256]{1,0:T(8,128)(2,1)S(1)}, u32[]{:S(2)}, u32[]{:S(2)}) collective-permute-start(bf16[256,256]{1,0:T(8,128)(2,1)S(1)} %get-tuple-element.125), channel_id=1, source_target_pairs={{1,0},{2,1},{3,2},{0,3},{5,4},{6,5},{7,6},{4,7},{9,8},{10,9},{11,1... | collective-permute-start | bytes 393224 | tf_op jit(solution)/shard_map/ppermute | solution.py:541
  258.0 0.9 collective-permute-start.19
  258.9 5.0 %shard_map.131 = (bf16[2048,128]{1,0:T(8,128)(2,1)}, bf16[2048,128]{1,0:T(8,128)(2,1)}, f32[2,2,64,128]{3,2,1,0:T(8,128)}) custom-call(s32[128]{0:T(128)} %reshape.110.idx_ref, s32[16]{0:T(128)} %reduce_sum.59.used_ref, s32[2]{0:T(128)} %bitcast.48, f32[2,2048,128]{2,1,0:T(8,128)} %get-tuple-element.105.win_ref, ...), custom_call_target="tpu_custom_call" | custom-call | flops 4194304 | bytes 16777216 | tf_op jit(solution)/shard_map/pallas_call | solution.py:405
  263.9 4.4 %shard_map.130.win_ref = f32[2,2048,128]{2,1,0:T(8,128)} custom-call(s32[128]{0:T(128)} %reshape.110.idx_ref, s32[16]{0:T(128)} %reduce_sum.59.used_ref, f32[2,2048,128]{2,1,0:T(8,128)} %get-tuple-element.102.win_ref, bf16[16,672,128]{2,1,0:T(8,128)(2,1)} %copy-done.2, bf16[2,64,256]{2,1,0:T(8,128)(2,1)} %copy-done.12, bf16[2,64,256]{2,1,0:T(8,128)(2,1)} %copy-done.13), custom_call_target="tpu_custom_call" | custom-call | flops 4194304 | bytes 14680064 | tf_op jit(solution)/shard_map/pallas_call | solution.py:418
  268.3 1.1 collective-permute-done.18.refs_7_
  269.4 2.2 collective-permute-done.19.refs_8_
  272.7 5.1 %shard_map.129 = bf16[2048,256]{1,0:T(8,128)(2,1)} custom-call(bf16[2048,256]{1,0:T(8,128)(2,1)} %get-tuple-element.89.c_ref.refs_0_, bf16[2048,256]{1,0:T(8,128)(2,1)} %collective-permute-done.13.refs_1_, bf16[2048,256]{1,0:T(8,128)(2,1)} %collective-permute-done.14.refs_2_, bf16[1024,256]{1,0:T(8,128)(2,1)} %copy-done.10, bf16[1024,256]{1,0:T(8,128)(2,1)} %copy-done.11, ...), custom_call_target="tpu_custom_call" | custom-call | flops 1073741824 | bytes 18874368 | tf_op jit(solution)/shard_map/pallas_call | solution.py:528
  277.8 5.9 %all-to-all-done.4.back_ref = bf16[16,672,128]{2,1,0:T(8,128)(2,1)} async-done(((bf16[16,672,128]{2,1,0:T(8,128)(2,1)}), bf16[16,672,128]{2,1,0:T(8,128)(2,1)}, u32[]{:S(2)}, u32[]{:S(2)}) %all-to-all-start.4) | async-done | bytes 2752544 | tf_op jit(solution)/shard_map/all_to_all | solution.py:579
  283.7 5.4 %shard_map.132 = (bf16[2048,256]{1,0:T(8,128)(2,1)}, bf16[2048,256]{1,0:T(8,128)(2,1)}, f32[256,1024]{1,0:T(8,128)}) custom-call(s32[128]{0:T(128)} %reshape.110.idx_ref, s32[16]{0:T(128)} %reduce_sum.59.used_ref, s32[2]{0:T(128)} %bitcast.49, s32[1]{0:T(128)} %bitcast.me_ref, f32[2,2048,128]{2,1,0:T(8,128)} %shard_map.130.win_ref, ...), custom_call_target="tpu_custom_call" | custom-call | flops 4194304 | bytes 12582912 | tf_op jit(solution)/shard_map/pallas_call | solution.py:435
  (92 shorter events, 10.5 us)
Async XLA Ops:
  0.6 32.6 %copy-start = (s32[1,512,3]{1,0,2:T(1,128)S(1)}, s32[1,512,3]{1,0,2:T(1,128)}, u32[]{:S(2)}) copy-start(s32[1,512,3]{1,0,2:T(1,128)} %param.14) | copy-start | bytes 18436
  0.7 14.2 %copy-start.23 = (s32[1,512,3]{1,0,2:T(1,128)S(1)}, s32[1,512,3]{1,0,2:T(1,128)}, u32[]{:S(2)}) copy-start(s32[1,512,3]{1,0,2:T(1,128)} %param.13) | copy-start | bytes 18436
  3.0 18.1 %collective-permute-start = (bf16[256,256]{1,0:T(8,128)(2,1)}, bf16[256,256]{1,0:T(8,128)(2,1)S(1)}, u32[]{:S(2)}, u32[]{:S(2)}) collective-permute-start(bf16[256,256]{1,0:T(8,128)(2,1)} %get-tuple-element.68.a), channel_id=1, source_target_pairs={{8,0},{12,4},{16,8},{20,12},{24,16},{28,20},{32,24},{36,28},{40,32... | collective-permute-start | bytes 393224 | tf_op jit(solution)/shard_map/ppermute | solution.py:541
  9.4 11.7 %collective-permute-start.1 = (bf16[384,256]{1,0:T(8,128)(2,1)}, bf16[384,256]{1,0:T(8,128)(2,1)S(1)}, u32[]{:S(2)}, u32[]{:S(2)}) collective-permute-start(bf16[384,256]{1,0:T(8,128)(2,1)} %get-tuple-element.64), channel_id=1, source_target_pairs={{60,0},{0,4},{4,8},{8,12},{12,16},{16,20},{20,24},{24,28},{28,32},... | collective-permute-start | bytes 589832 | tf_op jit(solution)/shard_map/ppermute | solution.py:541
  10.5 10.7 %collective-permute-start.2 = (bf16[384,256]{1,0:T(8,128)(2,1)}, bf16[384,256]{1,0:T(8,128)(2,1)S(1)}, u32[]{:S(2)}, u32[]{:S(2)}) collective-permute-start(bf16[384,256]{1,0:T(8,128)(2,1)} %get-tuple-element.65), channel_id=1, source_target_pairs={{4,0},{8,4},{12,8},{16,12},{20,16},{24,20},{28,24},{32,28},{36,32}... | collective-permute-start | bytes 589832 | tf_op jit(solution)/shard_map/ppermute | solution.py:541
  21.1 0.7 copy-start.22
  21.2 0.7 copy-start.14
  21.2 0.7 copy-start.15
  21.2 5.3 %copy-start.6 = (bf16[1,2048,256]{2,1,0:T(8,128)(2,1)S(1)}, bf16[1,2048,256]{2,1,0:T(8,128)(2,1)}, u32[]{:S(2)}) copy-start(bf16[1,2048,256]{2,1,0:T(8,128)(2,1)} %param.11) | copy-start | bytes 3145732
  21.9 63.3 %all-to-all-start = ((bf16[16,1024,128]{2,1,0:T(8,128)(2,1)}), bf16[16,1024,128]{2,1,0:T(8,128)(2,1)}, u32[]{:S(2)}, u32[]{:S(2)}) async-start(bf16[16,1024,128]{2,1,0:T(8,128)(2,1)} %bitcast.38), calls=%async_computation | async-start | bytes 8388608 | tf_op jit(solution)/shard_map/all_to_all | solution.py:579
  26.5 58.7 %collective-permute-start.3 = (bf16[2048,256]{1,0:T(8,128)(2,1)S(1)}, bf16[2048,256]{1,0:T(8,128)(2,1)S(1)}, u32[]{:S(2)}, u32[]{:S(2)}) collective-permute-start(bf16[2048,256]{1,0:T(8,128)(2,1)S(1)} %bitcast.42), channel_id=1, source_target_pairs={{1,0},{2,1},{3,2},{0,3},{5,4},{6,5},{7,6},{4,7},{9,8},{10,9},{11,1... | collective-permute-start | bytes 3145736 | tf_op jit(solution)/shard_map/ppermute | solution.py:541
  29.4 55.9 %collective-permute-start.4 = (bf16[2048,256]{1,0:T(8,128)(2,1)S(1)}, bf16[2048,256]{1,0:T(8,128)(2,1)S(1)}, u32[]{:S(2)}, u32[]{:S(2)}) collective-permute-start(bf16[2048,256]{1,0:T(8,128)(2,1)S(1)} %bitcast.43), channel_id=1, source_target_pairs={{3,0},{0,1},{1,2},{2,3},{7,4},{4,5},{5,6},{6,7},{11,8},{8,9},{9,10... | collective-permute-start | bytes 3145736 | tf_op jit(solution)/shard_map/ppermute | solution.py:541
  37.6 42.0 %collective-permute-start.5 = (bf16[256,256]{1,0:T(8,128)(2,1)}, bf16[256,256]{1,0:T(8,128)(2,1)S(1)}, u32[]{:S(2)}, u32[]{:S(2)}) collective-permute-start(bf16[256,256]{1,0:T(8,128)(2,1)} %shard_map.122.a), channel_id=1, source_target_pairs={{16,0},{20,4},{24,8},{28,12},{32,16},{36,20},{40,24},{44,28},{48,3... | collective-permute-start | bytes 393224 | tf_op jit(solution)/shard_map/ppermute | solution.py:541
  40.7 42.4 %collective-permute-start.6 = (bf16[256,256]{1,0:T(8,128)(2,1)}, bf16[256,256]{1,0:T(8,128)(2,1)S(1)}, u32[]{:S(2)}, u32[]{:S(2)}) collective-permute-start(bf16[256,256]{1,0:T(8,128)(2,1)} %shard_map.122.a), channel_id=1, source_target_pairs={{48,0},{52,4},{56,8},{60,12},{0,16},{4,20},{8,24},{12,28},{16,32},... | collective-permute-start | bytes 393224 | tf_op jit(solution)/shard_map/ppermute | solution.py:541
  40.7 44.6 %collective-permute-start.7 = (bf16[256,256]{1,0:T(8,128)(2,1)}, bf16[256,256]{1,0:T(8,128)(2,1)S(1)}, u32[]{:S(2)}, u32[]{:S(2)}) collective-permute-start(bf16[256,256]{1,0:T(8,128)(2,1)} %shard_map.122.a), channel_id=1, source_target_pairs={{32,0},{36,4},{40,8},{44,12},{48,16},{52,20},{56,24},{60,28},{0,32... | collective-permute-start | bytes 393224 | tf_op jit(solution)/shard_map/ppermute | solution.py:541
  79.6 5.6 %copy-start.16 = (bf16[256,256]{1,0:T(8,128)(2,1)}, bf16[256,256]{1,0:T(8,128)(2,1)S(1)}, u32[]{:S(2)}) copy-start(bf16[256,256]{1,0:T(8,128)(2,1)S(1)} %collective-permute-done.5.b) | copy-start | bytes 393220
  83.1 2.2 copy-start.17
  85.2 0.7 copy-start.18
  85.2 6.8 %copy-start.4 = (bf16[2048,256]{1,0:T(8,128)(2,1)}, bf16[2048,256]{1,0:T(8,128)(2,1)S(1)}, u32[]{:S(2)}) copy-start(bf16[2048,256]{1,0:T(8,128)(2,1)S(1)} %collective-permute-done.3.refs_1_) | copy-start | bytes 3145732
  85.2 9.7 %copy-start.5 = (bf16[2048,256]{1,0:T(8,128)(2,1)}, bf16[2048,256]{1,0:T(8,128)(2,1)S(1)}, u32[]{:S(2)}) copy-start(bf16[2048,256]{1,0:T(8,128)(2,1)S(1)} %collective-permute-done.4.refs_2_) | copy-start | bytes 3145732
  85.9 59.1 %all-to-all-start.1 = ((bf16[16,1024,128]{2,1,0:T(8,128)(2,1)}), bf16[16,1024,128]{2,1,0:T(8,128)(2,1)}, u32[]{:S(2)}, u32[]{:S(2)}) async-start(bf16[16,1024,128]{2,1,0:T(8,128)(2,1)} %bitcast.37), calls=%async_computation.1 | async-start | bytes 8388608 | tf_op jit(solution)/shard_map/all_to_all | solution.py:579
  92.1 11.6 %collective-permute-start.8 = (bf16[1024,256]{1,0:T(8,128)(2,1)S(1)}, bf16[1024,256]{1,0:T(8,128)(2,1)S(1)}, u32[]{:S(2)}, u32[]{:S(2)}) collective-permute-start(bf16[1024,256]{1,0:T(8,128)(2,1)S(1)} %slice.15), channel_id=1, source_target_pairs={{1,0},{2,1},{3,2},{0,3},{5,4},{6,5},{7,6},{4,7},{9,8},{10,9},{11,1... | collective-permute-start | bytes 1572872 | tf_op jit(solution)/shard_map/ppermute | solution.py:541
  94.9 12.3 %collective-permute-start.9 = (bf16[1024,256]{1,0:T(8,128)(2,1)S(1)}, bf16[1024,256]{1,0:T(8,128)(2,1)S(1)}, u32[]{:S(2)}, u32[]{:S(2)}) collective-permute-start(bf16[1024,256]{1,0:T(8,128)(2,1)S(1)} %slice.16), channel_id=1, source_target_pairs={{3,0},{0,1},{1,2},{2,3},{7,4},{4,5},{5,6},{6,7},{11,8},{8,9},{9,10... | collective-permute-start | bytes 1572872 | tf_op jit(solution)/shard_map/ppermute | solution.py:541
  103.7 3.5 %copy-start.7 = (bf16[1024,256]{1,0:T(8,128)(2,1)}, bf16[1024,256]{1,0:T(8,128)(2,1)S(1)}, u32[]{:S(2)}) copy-start(bf16[1024,256]{1,0:T(8,128)(2,1)S(1)} %collective-permute-done.8.refs_3_) | copy-start | bytes 1572868
  107.2 0.8 copy-start.8
  145.0 55.5 %all-to-all-start.2 = ((bf16[16,1024,128]{2,1,0:T(8,128)(2,1)}), bf16[16,1024,128]{2,1,0:T(8,128)(2,1)}, u32[]{:S(2)}, u32[]{:S(2)}) async-start(bf16[16,1024,128]{2,1,0:T(8,128)(2,1)} %bitcast.39), calls=%async_computation.2 | async-start | bytes 8388608 | tf_op jit(solution)/shard_map/all_to_all | solution.py:579
  183.3 2.1 collective-permute-start.10
  185.5 0.8 copy-start.9
  188.4 22.0 %copy-start.24 = (bf16[2,64,256]{2,1,0:T(8,128)(2,1)S(1)}, bf16[2,64,256]{2,1,0:T(8,128)(2,1)}, u32[]{:S(2)}) copy-start(bf16[2,64,256]{2,1,0:T(8,128)(2,1)} %get-tuple-element.96) | copy-start | bytes 196612
  188.4 23.3 %copy-start.25 = (bf16[2,64,256]{2,1,0:T(8,128)(2,1)S(1)}, bf16[2,64,256]{2,1,0:T(8,128)(2,1)}, u32[]{:S(2)}) copy-start(bf16[2,64,256]{2,1,0:T(8,128)(2,1)} %get-tuple-element.97) | copy-start | bytes 196612
  200.5 41.6 %all-to-all-start.3 = ((bf16[16,672,128]{2,1,0:T(8,128)(2,1)}), bf16[16,672,128]{2,1,0:T(8,128)(2,1)S(1)}, u32[]{:S(2)}, u32[]{:S(2)}) async-start(bf16[16,672,128]{2,1,0:T(8,128)(2,1)} %shard_map.128), calls=%async_computation.3 | async-start | bytes 5505024 | tf_op jit(solution)/shard_map/all_to_all | solution.py:579
  207.6 35.8 %collective-permute-start.13 = (bf16[2048,256]{1,0:T(8,128)(2,1)}, bf16[2048,256]{1,0:T(8,128)(2,1)}, u32[]{:S(2)}, u32[]{:S(2)}) collective-permute-start(bf16[2048,256]{1,0:T(8,128)(2,1)} %get-tuple-element.89.c_ref.refs_0_), channel_id=1, source_target_pairs={{1,0},{2,1},{3,2},{0,3},{5,4},{6,5},{7,6},{4,7},{9,8},{10,9},{11,1... | collective-permute-start | bytes 3145736 | tf_op jit(solution)/shard_map/ppermute | solution.py:541
  210.5 33.0 %collective-permute-start.14 = (bf16[2048,256]{1,0:T(8,128)(2,1)}, bf16[2048,256]{1,0:T(8,128)(2,1)}, u32[]{:S(2)}, u32[]{:S(2)}) collective-permute-start(bf16[2048,256]{1,0:T(8,128)(2,1)} %get-tuple-element.89.c_ref.refs_0_), channel_id=1, source_target_pairs={{3,0},{0,1},{1,2},{2,3},{7,4},{4,5},{5,6},{6,7},{11,8},{8,9},{9,10... | collective-permute-start | bytes 3145736 | tf_op jit(solution)/shard_map/ppermute | solution.py:541
  210.5 32.9 %collective-permute-start.11 = (bf16[2,64,256]{2,1,0:T(8,128)(2,1)S(1)}, bf16[2,64,256]{2,1,0:T(8,128)(2,1)S(1)}, u32[]{:S(2)}, u32[]{:S(2)}) collective-permute-start(bf16[2,64,256]{2,1,0:T(8,128)(2,1)S(1)} %copy-done.24), channel_id=1, source_target_pairs={{4,0},{8,4},{12,8},{16,12},{20,16},{24,20},{28,24},{32,28},{36,32}... | collective-permute-start | bytes 196616 | tf_op jit(solution)/shard_map/ppermute | solution.py:557
  211.8 31.6 %collective-permute-start.12 = (bf16[2,64,256]{2,1,0:T(8,128)(2,1)S(1)}, bf16[2,64,256]{2,1,0:T(8,128)(2,1)S(1)}, u32[]{:S(2)}, u32[]{:S(2)}) collective-permute-start(bf16[2,64,256]{2,1,0:T(8,128)(2,1)S(1)} %copy-done.25), channel_id=1, source_target_pairs={{0,4},{4,8},{8,12},{12,16},{16,20},{20,24},{24,28},{28,32},{32,36}... | collective-permute-start | bytes 196616 | tf_op jit(solution)/shard_map/ppermute | solution.py:557
  242.1 1.8 copy-start.2
  243.4 10.8 %copy-start.3 = (bf16[256,1024]{1,0:T(8,128)(2,1)S(1)}, bf16[256,1024]{1,0:T(8,128)(2,1)}, u32[]{:S(2)}) copy-start(bf16[256,1024]{1,0:T(8,128)(2,1)} %refs_8_.1) | copy-start | bytes 1572868
  244.0 39.7 %all-to-all-start.4 = ((bf16[16,672,128]{2,1,0:T(8,128)(2,1)}), bf16[16,672,128]{2,1,0:T(8,128)(2,1)}, u32[]{:S(2)}, u32[]{:S(2)}) async-start(bf16[16,672,128]{2,1,0:T(8,128)(2,1)} %broadcast_dynamic-update-slice_fusion), calls=%async_computation.4 | async-start | bytes 5505024 | tf_op jit(solution)/shard_map/all_to_all | solution.py:579
  250.1 21.5 %collective-permute-start.15 = (bf16[1024,256]{1,0:T(8,128)(2,1)S(1)}, bf16[1024,256]{1,0:T(8,128)(2,1)S(1)}, u32[]{:S(2)}, u32[]{:S(2)}) collective-permute-start(bf16[1024,256]{1,0:T(8,128)(2,1)S(1)} %slice.18), channel_id=1, source_target_pairs={{1,0},{2,1},{3,2},{0,3},{5,4},{6,5},{7,6},{4,7},{9,8},{10,9},{11,1... | collective-permute-start | bytes 1572872 | tf_op jit(solution)/shard_map/ppermute | solution.py:541
  254.0 17.6 %collective-permute-start.16 = (bf16[1024,256]{1,0:T(8,128)(2,1)S(1)}, bf16[1024,256]{1,0:T(8,128)(2,1)S(1)}, u32[]{:S(2)}, u32[]{:S(2)}) collective-permute-start(bf16[1024,256]{1,0:T(8,128)(2,1)S(1)} %slice.19), channel_id=1, source_target_pairs={{3,0},{0,1},{1,2},{2,3},{7,4},{4,5},{5,6},{6,7},{11,8},{8,9},{9,10... | collective-permute-start | bytes 1572872 | tf_op jit(solution)/shard_map/ppermute | solution.py:541
  254.9 13.4 %collective-permute-start.17 = (bf16[256,256]{1,0:T(8,128)(2,1)S(1)}, bf16[256,256]{1,0:T(8,128)(2,1)S(1)}, u32[]{:S(2)}, u32[]{:S(2)}) collective-permute-start(bf16[256,256]{1,0:T(8,128)(2,1)S(1)} %get-tuple-element.125), channel_id=1, source_target_pairs={{1,0},{2,1},{3,2},{0,3},{5,4},{6,5},{7,6},{4,7},{9,8},{10,9},{11,1... | collective-permute-start | bytes 393224 | tf_op jit(solution)/shard_map/ppermute | solution.py:541
  258.0 11.4 %collective-permute-start.18 = (bf16[256,256]{1,0:T(8,128)(2,1)S(1)}, bf16[256,256]{1,0:T(8,128)(2,1)S(1)}, u32[]{:S(2)}, u32[]{:S(2)}) collective-permute-start(bf16[256,256]{1,0:T(8,128)(2,1)S(1)} %get-tuple-element.124), channel_id=1, source_target_pairs={{2,0},{3,1},{0,2},{1,3},{6,4},{7,5},{4,6},{5,7},{10,8},{11,9},{8,1... | collective-permute-start | bytes 393224 | tf_op jit(solution)/shard_map/ppermute | solution.py:541
  258.0 13.6 %collective-permute-start.19 = (bf16[256,256]{1,0:T(8,128)(2,1)S(1)}, bf16[256,256]{1,0:T(8,128)(2,1)S(1)}, u32[]{:S(2)}, u32[]{:S(2)}) collective-permute-start(bf16[256,256]{1,0:T(8,128)(2,1)S(1)} %get-tuple-element.123), channel_id=1, source_target_pairs={{3,0},{0,1},{1,2},{2,3},{7,4},{4,5},{5,6},{6,7},{11,8},{8,9},{9,10... | collective-permute-start | bytes 393224 | tf_op jit(solution)/shard_map/ppermute | solution.py:541
  268.3 3.4 %copy-start.19 = (bf16[256,256]{1,0:T(8,128)(2,1)}, bf16[256,256]{1,0:T(8,128)(2,1)S(1)}, u32[]{:S(2)}) copy-start(bf16[256,256]{1,0:T(8,128)(2,1)S(1)} %collective-permute-done.17.refs_6_) | copy-start | bytes 393220
  269.4 2.3 copy-start.20
  271.7 0.8 copy-start.10
  271.7 1.0 copy-start.11
  283.7 5.4 %copy-start.1 = (s32[1,512,3]{1,0,2:T(1,128)S(1)}, s32[1,512,3]{1,0,2:T(1,128)}, u32[]{:S(2)}) copy-start(s32[1,512,3]{1,0,2:T(1,128)} %param.14) | copy-start | bytes 18436
  (3 other events, 1.9 us)

commit v10 on v9

--- a/solution.py
+++ b/solution.py
@@ -14,7 +14,7 @@
 LANES = 128
 NEG_FILL = -1e30
 VMEM_LIMIT = 60 * 1024 * 1024
-CARRIED = 160
+CARRIED = 96
 
 NT = (((1,), (1,)), ((), ()))
 NN = (((1,), (0,)), ((), ()))
@@ -353,7 +353,7 @@
 
 def last_kernel(
     capacity, idx_ref, used_ref, glob_ref, me_ref, win_ref, back_ref, kept_ref, dk_in_ref, dv_in_ref,
-    dk_ref, dv_ref, gw_ref, acc,
+    dk_ref, dv_ref, acc,
 ):
     acc[...] = win_ref[...]
     land((capacity // 2, capacity, capacity, CARRIED), idx_ref, used_ref, back_ref, acc)
@@ -392,11 +392,6 @@
             dk_ref[pl.ds(at, BLK), :LANES] = both[0]
             dv_ref[pl.ds(at, BLK), :LANES] = both[1]
 
-    for d in range(back_ref.shape[0]):
-        for j in range(gw_ref.shape[1] // LANES):
-            rows = back_ref[d, 16 * j : 16 * (j + 1), :]
-            gw_ref[16 * d : 16 * (d + 1), j * LANES : (j + 1) * LANES] = rows.astype(jnp.float32)
-
 
 def collect_first(idx, used, glob, win, back, up, down, capacity):
     rows = win.shape[1]
@@ -429,15 +424,14 @@
 def collect_last(idx, used, glob, me, win, back, before, capacity):
     rows = win.shape[1]
     out = jax.ShapeDtypeStruct((rows, 2 * LANES), jnp.bfloat16)
-    weight = jax.ShapeDtypeStruct((2 * LANES, 1024), jnp.float32)
     dk, dv, kept = before
     arrays = (win, back, kept, dk, dv)
     return pl.pallas_call(
         functools.partial(last_kernel, capacity),
         grid=(1,),
         in_specs=[smem()] * 4 + [whole(x.shape) for x in arrays],
-        out_specs=(whole(out.shape), whole(out.shape), whole(weight.shape)),
-        out_shape=(out, out, weight),
+        out_specs=(whole(out.shape), whole(out.shape)),
+        out_shape=(out, out),
         scratch_shapes=[pltpu.VMEM((2, rows, LANES), jnp.float32)],
         compiler_params=params(),
         cost_estimate=pl.CostEstimate(flops=4 << 20, bytes_accessed=12 << 20, transcendentals=0),
@@ -445,7 +439,7 @@
 
 
 def weight_kernel(at_ref, c_ref, *refs):
-    pieces, out_ref, acc = refs[:5], refs[5], refs[6]
+    pieces, (keep_ref, give_ref, acc) = refs[:5], refs[5:]
 
     @pl.when(pl.program_id(0) == 0)
     def _():
@@ -454,28 +448,30 @@
     width = pieces[0].shape[1]
     values = ring_values(pieces)
     for i, g in enumerate(values):
-        acc[:, i * width : (i + 1) * width] += dot(c_ref[...], g, TN)
+        acc[:, :, i * width : (i + 1) * width] += dot(c_ref[...], g, TN).reshape(2, LANES, width)
 
     @pl.when(pl.program_id(0) == pl.num_programs(0) - 1)
     def _():
         for i in range(4):
             to = pl.multiple_of(((at_ref[0] + i) % 4) * width, width)
-            out_ref[:, pl.ds(to, width)] = acc[:, i * width : (i + 1) * width].astype(jnp.bfloat16)
+            part = acc.at[:, :, i * width : (i + 1) * width]
+            keep_ref[:, pl.ds(to, width)] = part[at_ref[1]].astype(jnp.bfloat16)
+            give_ref[:, pl.ds(to, width)] = part[1 - at_ref[1]].astype(jnp.bfloat16)
 
 
 def weight_terms(at, context, pieces):
     rows, width = pieces[0].shape
-    shape = (2 * LANES, 4 * width)
+    shape = (LANES, 4 * width)
     return pl.pallas_call(
         weight_kernel,
         grid_spec=pltpu.PrefetchScalarGridSpec(
             num_scalar_prefetch=1,
             grid=(rows // TILE,),
             in_specs=[pl.BlockSpec((TILE, width), lambda i, at: (i, 0))] + ring_specs(rows, width),
-            out_specs=pl.BlockSpec(shape, lambda i, at: (0, 0)),
-            scratch_shapes=[pltpu.VMEM(shape, jnp.float32)],
+            out_specs=(pl.BlockSpec(shape, lambda i, at: (0, 0)),) * 2,
+            scratch_shapes=[pltpu.VMEM((2, *shape), jnp.float32)],
         ),
-        out_shape=jax.ShapeDtypeStruct(shape, jnp.bfloat16),
+        out_shape=(jax.ShapeDtypeStruct(shape, jnp.bfloat16),) * 2,
         compiler_params=params(),
         cost_estimate=pl.CostEstimate(flops=2 * rows * 1024 * 256, bytes_accessed=16 << 20, transcendentals=0),
     )(at, context, *pieces)
@@ -490,8 +486,9 @@
     terms = (own_ref[...].astype(jnp.float32) + other_ref[...].astype(jnp.float32)).astype(jnp.bfloat16)
     for d in range(out_ref.shape[0]):
         rows = slice(16 * d, 16 * (d + 1))
-        for j in range(terms.shape[1] // LANES):
-            out_ref[d, 16 * j : 16 * (j + 1), :] = terms[rows, j * LANES : (j + 1) * LANES]
+        for j in range(4):
+            column = (d % 2 * 4 + j) * LANES
+            out_ref[d, 16 * j : 16 * (j + 1), :] = terms[d // 2 * 16 : d // 2 * 16 + 16, column : column + LANES]
         out_ref[d, CARRIED - 32 : CARRIED - 16, :] = s0[rows, :]
         out_ref[d, CARRIED - 16 :, :] = s1[rows, :]
 
@@ -513,6 +510,29 @@
     total = jnp.sum(back[:, :CARRIED].astype(jnp.float32), axis=0).astype(jnp.bfloat16)
     spread = jnp.broadcast_to(total[None], (part.shape[0], CARRIED, LANES))
     return lax.dynamic_update_slice_in_dim(part, spread, 0, 1)
+
+
+def weight_kernel_last(at_ref, own_ref, other_ref, out_ref):
+    for half_ref, half in ((own_ref, at_ref[1]), (other_ref, 1 - at_ref[1])):
+        for d in range(half_ref.shape[0]):
+            row = pl.multiple_of(half * LANES + d // 2 * 16, 16)
+            for j in range(4):
+                column = (d % 2 * 4 + j) * LANES
+                tile = half_ref[d, 16 * j : 16 * (j + 1), :].astype(jnp.float32)
+                out_ref[pl.ds(row, 16), column : column + LANES] = tile
+
+
+def weight_last(at, own, other):
+    shape = (2 * LANES, 1024)
+    return pl.pallas_call(
+        weight_kernel_last,
+        grid=(1,),
+        in_specs=[smem(), whole(own.shape), whole(other.shape)],
+        out_specs=whole(shape),
+        out_shape=jax.ShapeDtypeStruct(shape, jnp.float32),
+        compiler_params=params(),
+        cost_estimate=pl.CostEstimate(flops=1 << 18, bytes_accessed=2 << 20, transcendentals=0),
+    )(at, own, other)
 
 
 def project_kernel(*refs):
@@ -572,7 +592,7 @@
     slots = ctx_count * capacity
     barrier = lax.optimization_barrier
     at = me.reshape(1)
-    tp_at = tp_me.reshape(1)
+    tp_at = jnp.stack([tp_me, lax.axis_index("dp")])
     glob_at = global_ids[0]
 
     def exchange(parts):
@@ -627,8 +647,8 @@
 
     back_a = exchange(ret_a.reshape(ctx_count, -1, LANES))
     context, grad_q, win_b, up, down, gsum_b, ret_b, ret_c = half(my_place, fetched_b, (context, grad_q, up, down), 1)
-    terms = weight_terms(tp_at, context, pieces)
-    ret_b = load_terms(terms, shifted(terms, "dp", 1), (gsum_a, gsum_b), ret_b)
+    keep, give = weight_terms(tp_at, context, pieces)
+    ret_b = load_terms(keep, shifted(give, "dp", 1), (gsum_a, gsum_b), ret_b)
     ret_b, back_a = barrier((ret_b, back_a))
 
     back_b = exchange(ret_b)
@@ -646,7 +666,9 @@
         wcols[-by % tp_count] = shifted(part, "tp", -by) if by else part
     projected = project((context, *near, *ring_far(near, "tp")), wcols)
     projected, win_b, first, back_c = barrier((projected, win_b, first, back_c))
-    grad_k, grad_v, grad_weight = collect_last(send_idx, used, glob_at, at, win_b, back_c, first, capacity)
+    weight_own = back_c[:, : CARRIED - 32]
+    grad_weight = weight_last(tp_at, weight_own, shifted(weight_own, "dp", 1))
+    grad_k, grad_v = collect_last(send_idx, used, glob_at, at, win_b, back_c, first, capacity)
     return projected[None], grad_q[None], grad_k[None], grad_v[None], grad_weight
 
 

time: 290 us -> 287 us (0.990)
  waiting for transfers between devices: 105 us -> 99.3 us
    all_to_all x5, waiting for transfers between devices: 48.4 us -> 44.2 us  [exchange(): return lax.all_to_all(parts, 'ctx', split_axis=0, concat_axis=0, tiled=True)]
    ppermute x18 -> x19, waiting for transfers between devices: 56.9 us -> 55.1 us  [shifted(): lax.ppermute(array, axis, [((i + by) % size, i) for i in range(size)])]
    ppermute x18 -> x19, starting transfers between devices: 32.6 us -> 32.7 us  [shifted(): lax.ppermute(array, axis, [((i + by) % size, i) for i in range(size)])]
  transfers between devices with their start and end apart: 25 -> 26, of which waited for: 12 -> 12; matrix products, arithmetic and copies ran while one was open for 4% -> 4% of each run, Pallas kernels for 32% -> 35%
where the time goes in v10:
time: 287 us; the launch traced here: 284 us
  Pallas kernels  103 us (36%)
  waiting for transfers between devices  99.3 us (35%)
  starting transfers between devices  64.6 us (23%)
  local copies, waits for them, and re-layouts  12.6 us (4%)
  other arithmetic  4.04 us (1%)
    ppermute x19, waiting for transfers between devices, shifted(): lax.ppermute(array, axis, [((i + by) % size, i) for i in range(size)])  55.1 us
    pallas_call x2, Pallas kernels, attend(): pl.pallas_call(functools.partial(attend_kernel, blocks, last_block, len(h...  54.2 us
    all_to_all x5, waiting for transfers between devices, exchange(): return lax.all_to_all(parts, 'ctx', split_axis=0, concat_axis=0, tiled=True)  44.2 us
    ppermute x19, starting transfers between devices, shifted(): lax.ppermute(array, axis, [((i + by) % size, i) for i in range(size)])  32.7 us
    all_to_all x5, starting transfers between devices, exchange(): return lax.all_to_all(parts, 'ctx', split_axis=0, concat_axis=0, tiled=True)  26 us
    pallas_call x2, Pallas kernels, pick_blocks(): pl.pallas_call(functools.partial(pick_kernel, slots // 4), grid=(4,), in_...  7.86 us
    pallas_call x1, Pallas kernels, grad_context_of(): pl.pallas_call(grad_context_kernel, grid_spec=pltpu.PrefetchScalarGridSpe...  5.89 us
    ppermute x2, starting transfers between devices, passed_along(): return lax.ppermute(array, axis, pairs)  5.83 us
  transfers between devices with their start and end apart: 26, of which 12 were waited for; matrix products, arithmetic and copies ran while one was open for 4% of the time, Pallas kernels for 35%

profile of v10, /device:TPU:0, one launch (start us, length us, event | category | flops | bytes accessed | tf_op | source)
XLA Modules:
  0.0 284.3 jit_solution(1957623559131940774)
XLA Ops:
  0.7 2.4 shard_map.121
  3.1 6.4 %collective-permute-start = (bf16[256,256]{1,0:T(8,128)(2,1)}, bf16[256,256]{1,0:T(8,128)(2,1)S(1)}, u32[]{:S(2)}, u32[]{:S(2)}) collective-permute-start(bf16[256,256]{1,0:T(8,128)(2,1)} %get-tuple-element.69.a), channel_id=1, source_target_pairs={{8,0},{12,4},{16,8},{20,12},{24,16},{28,20},{32,24},{36,28},{40,32... | collective-permute-start | bytes 393224 | tf_op jit(solution)/shard_map/ppermute | solution.py:561
  9.5 1.0 collective-permute-start.1
  10.5 4.3 %collective-permute-start.2 = (bf16[384,256]{1,0:T(8,128)(2,1)}, bf16[384,256]{1,0:T(8,128)(2,1)S(1)}, u32[]{:S(2)}, u32[]{:S(2)}) collective-permute-start(bf16[384,256]{1,0:T(8,128)(2,1)} %get-tuple-element.66), channel_id=1, source_target_pairs={{4,0},{8,4},{12,8},{16,12},{20,16},{24,20},{28,24},{32,28},{36,32}... | collective-permute-start | bytes 589832 | tf_op jit(solution)/shard_map/ppermute | solution.py:561
  17.1 4.0 %shard_map.120 = bf16[16384,128]{1,0:T(8,128)(2,1)} custom-call(s32[128]{0:T(128)} %reshape.107.idx_ref, bf16[2048,256]{1,0:T(8,128)(2,1)} %bitcast.26, bf16[2048,256]{1,0:T(8,128)(2,1)} %bitcast.34), custom_call_target="tpu_custom_call" | custom-call | bytes 10485760 | tf_op jit(solution)/shard_map/pallas_call | solution.py:57
  21.8 4.7 %all-to-all-start = ((bf16[16,1024,128]{2,1,0:T(8,128)(2,1)}), bf16[16,1024,128]{2,1,0:T(8,128)(2,1)}, u32[]{:S(2)}, u32[]{:S(2)}) async-start(bf16[16,1024,128]{2,1,0:T(8,128)(2,1)} %bitcast.39), calls=%async_computation | async-start | bytes 8388608 | tf_op jit(solution)/shard_map/all_to_all | solution.py:599
  26.5 2.8 collective-permute-start.3
  29.4 3.9 %shard_map.119 = bf16[16384,128]{1,0:T(8,128)(2,1)} custom-call(s32[128]{0:T(128)} %reshape.107.idx_ref, bf16[2048,256]{1,0:T(8,128)(2,1)} %bitcast.27, bf16[2048,256]{1,0:T(8,128)(2,1)} %bitcast.35), custom_call_target="tpu_custom_call" | custom-call | bytes 10485760 | tf_op jit(solution)/shard_map/pallas_call | solution.py:57
  35.8 1.8 shard_map.122.a
  37.5 3.1 %collective-permute-start.5 = (bf16[256,256]{1,0:T(8,128)(2,1)}, bf16[256,256]{1,0:T(8,128)(2,1)S(1)}, u32[]{:S(2)}, u32[]{:S(2)}) collective-permute-start(bf16[256,256]{1,0:T(8,128)(2,1)} %shard_map.122.a), channel_id=1, source_target_pairs={{16,0},{20,4},{24,8},{28,12},{32,16},{36,20},{40,24},{44,28},{48,3... | collective-permute-start | bytes 393224 | tf_op jit(solution)/shard_map/ppermute | solution.py:561
  40.6 2.3 collective-permute-start.7
  42.9 1.2 fusion.4
  44.2 35.0 %collective-permute-done.5.b = bf16[256,256]{1,0:T(8,128)(2,1)S(1)} collective-permute-done((bf16[256,256]{1,0:T(8,128)(2,1)}, bf16[256,256]{1,0:T(8,128)(2,1)S(1)}, u32[]{:S(2)}, u32[]{:S(2)}) %collective-permute-start.5) | collective-permute-done | bytes 131104 | tf_op jit(solution)/shard_map/ppermute | solution.py:561
  79.1 2.5 collective-permute-done.6.c
  81.7 2.7 collective-permute-done.7.d
  85.0 5.8 %all-to-all-start.1 = ((bf16[16,1024,128]{2,1,0:T(8,128)(2,1)}), bf16[16,1024,128]{2,1,0:T(8,128)(2,1)}, u32[]{:S(2)}, u32[]{:S(2)}) async-start(bf16[16,1024,128]{2,1,0:T(8,128)(2,1)} %bitcast.38), calls=%async_computation.1 | async-start | bytes 8388608 | tf_op jit(solution)/shard_map/all_to_all | solution.py:599
  90.8 2.8 collective-permute-start.8
  94.4 1.8 shard_map.124
  96.1 6.2 %collective-permute-done.8.refs_3_ = bf16[1024,256]{1,0:T(8,128)(2,1)S(1)} collective-permute-done((bf16[1024,256]{1,0:T(8,128)(2,1)S(1)}, bf16[1024,256]{1,0:T(8,128)(2,1)S(1)}, u32[]{:S(2)}, u32[]{:S(2)}) %collective-permute-start.8) | collective-permute-done | bytes 524320 | tf_op jit(solution)/shard_map/ppermute | solution.py:561
  102.4 3.5 %collective-permute-done.9.refs_4_ = bf16[1024,256]{1,0:T(8,128)(2,1)S(1)} collective-permute-done((bf16[1024,256]{1,0:T(8,128)(2,1)S(1)}, bf16[1024,256]{1,0:T(8,128)(2,1)S(1)}, u32[]{:S(2)}, u32[]{:S(2)}) %collective-permute-start.9) | collective-permute-done | bytes 524320 | tf_op jit(solution)/shard_map/ppermute | solution.py:561
  106.7 5.9 %shard_map.123.g_ref = bf16[2048,256]{1,0:T(8,128)(2,1)} custom-call(s32[2]{0:T(128)} %pad_add_fusion.at_ref, bf16[2048,256]{1,0:T(8,128)(2,1)} %bitcast.41, bf16[2048,256]{1,0:T(8,128)(2,1)} %copy-done.4, bf16[2048,256]{1,0:T(8,128)(2,1)} %copy-done.5, bf16[1024,256]{1,0:T(8,128)(2,1)} %copy-done.7, bf16[1024,256]{1,0:T(8,128)(2,1)} %copy-done.8, ...), custom_call_target="tpu_custom_call" | custom-call | flops 1073741824 | bytes 16777216 | tf_op jit(solution)/shard_map/pallas_call | solution.py:157
  112.6 27.1 %shard_map.125 = (bf16[2048,256]{1,0:T(8,128)(2,1)}, bf16[2048,256]{1,0:T(8,128)(2,1)}, f32[2,2048,128]{2,1,0:T(8,128)}, bf16[2,64,256]{2,1,0:T(8,128)(2,1)}, bf...) custom-call(s32[1]{0:T(128)} %bitcast.me_ref, ...), custom_call_target="tpu_custom_call" | custom-call | flops 6442450944 | bytes 83886080 | tf_op jit(solution)/shard_map/pallas_call | solution.py:289
  139.6 3.9 %all-to-all-done.1 = bf16[16,1024,128]{2,1,0:T(8,128)(2,1)} async-done(((bf16[16,1024,128]{2,1,0:T(8,128)(2,1)}), bf16[16,1024,128]{2,1,0:T(8,128)(2,1)}, u32[]{:S(2)}, u32[]{:S(2)}) %all-to-all-start.1) | async-done | bytes 4194336 | tf_op jit(solution)/shard_map/all_to_all | solution.py:599
  143.5 5.0 %all-to-all-start.2 = ((bf16[16,1024,128]{2,1,0:T(8,128)(2,1)}), bf16[16,1024,128]{2,1,0:T(8,128)(2,1)}, u32[]{:S(2)}, u32[]{:S(2)}) async-start(bf16[16,1024,128]{2,1,0:T(8,128)(2,1)} %bitcast.40), calls=%async_computation.2 | async-start | bytes 8388608 | tf_op jit(solution)/shard_map/all_to_all | solution.py:599
  148.6 27.2 %shard_map.126 = (bf16[2048,256]{1,0:T(8,128)(2,1)}, bf16[2048,256]{1,0:T(8,128)(2,1)}, f32[2,2048,128]{2,1,0:T(8,128)}, bf16[2,64,256]{2,1,0:T(8,128)(2,1)}, bf...) custom-call(s32[1]{0:T(128)} %bitcast.me_ref, ...), custom_call_target="tpu_custom_call", output_to_operand_aliasing={{0}: (12, {}), {1}: (13, {}), {3}: (14, {}), {4}: (15, {})} | custom-call | flops 6442450944 | bytes 83886080 | tf_op jit(solution)/shard_map/pallas_call | solution.py:289
  175.7 5.8 %shard_map.127 = (bf16[128,1024]{1,0:T(8,128)(2,1)}, bf16[128,1024]{1,0:T(8,128)(2,1)}) custom-call(s32[2]{0:T(128)} %pad_add_fusion.at_ref, bf16[2048,256]{1,0:T(8,128)(2,1)} %get-tuple-element.90.c_ref.refs_0_, bf16[2048,256]{1,0:T(8,128)(2,1)} %bitcast.42, bf16[2048,256]{1,0:T(8,128)(2,1)} %copy-done.4, bf16[2048,256]{1,0:T(8,128)(2,1)} %copy-done.5, ...), custom_call_target="tpu_custom_call" | custom-call | flops 1073741824 | bytes 16777216 | tf_op jit(solution)/shard_map/pallas_call | solution.py:465
  181.6 1.7 collective-permute-done.10.other_ref
  184.0 1.9 shard_map.128
  185.9 13.7 %all-to-all-done.2.back_ref = bf16[16,1024,128]{2,1,0:T(8,128)(2,1)} async-done(((bf16[16,1024,128]{2,1,0:T(8,128)(2,1)}), bf16[16,1024,128]{2,1,0:T(8,128)(2,1)}, u32[]{:S(2)}, u32[]{:S(2)}) %all-to-all-start.2) | async-done | bytes 4194336 | tf_op jit(solution)/shard_map/all_to_all | solution.py:599
  199.6 5.4 %all-to-all-start.3 = ((bf16[16,608,128]{2,1,0:T(8,128)(2,1)}), bf16[16,608,128]{2,1,0:T(8,128)(2,1)S(1)}, u32[]{:S(2)}, u32[]{:S(2)}) async-start(bf16[16,608,128]{2,1,0:T(8,128)(2,1)} %shard_map.128), calls=%async_computation.3 | async-start | bytes 4980736 | tf_op jit(solution)/shard_map/all_to_all | solution.py:599
  205.0 2.8 collective-permute-start.13
  207.8 1.3 collective-permute-start.11
  209.1 4.5 %collective-permute-start.12 = (bf16[2,64,256]{2,1,0:T(8,128)(2,1)S(1)}, bf16[2,64,256]{2,1,0:T(8,128)(2,1)S(1)}, u32[]{:S(2)}, u32[]{:S(2)}) collective-permute-start(bf16[2,64,256]{2,1,0:T(8,128)(2,1)S(1)} %copy-done.27), channel_id=1, source_target_pairs={{0,4},{4,8},{8,12},{12,16},{16,20},{20,24},{24,28},{28,32},{32,36}... | collective-permute-start | bytes 196616 | tf_op jit(solution)/shard_map/ppermute | solution.py:577
  213.7 23.1 %all-to-all-done.3.back_ref = bf16[16,608,128]{2,1,0:T(8,128)(2,1)S(1)} async-done(((bf16[16,608,128]{2,1,0:T(8,128)(2,1)}), bf16[16,608,128]{2,1,0:T(8,128)(2,1)S(1)}, u32[]{:S(2)}, u32[]{:S(2)}) %all-to-all-start.3) | async-done | bytes 2490400 | tf_op jit(solution)/shard_map/all_to_all | solution.py:599
  238.4 5.2 %all-to-all-start.4 = ((bf16[16,608,128]{2,1,0:T(8,128)(2,1)}), bf16[16,608,128]{2,1,0:T(8,128)(2,1)}, u32[]{:S(2)}, u32[]{:S(2)}) async-start(bf16[16,608,128]{2,1,0:T(8,128)(2,1)} %broadcast_dynamic-update-slice_fusion), calls=%async_computation.4 | async-start | bytes 4980736 | tf_op jit(solution)/shard_map/all_to_all | solution.py:599
  243.6 1.1 slice.21
  244.7 2.8 collective-permute-start.15
  247.6 1.1 slice.22
  249.5 3.1 %collective-permute-start.17 = (bf16[256,256]{1,0:T(8,128)(2,1)S(1)}, bf16[256,256]{1,0:T(8,128)(2,1)S(1)}, u32[]{:S(2)}, u32[]{:S(2)}) collective-permute-start(bf16[256,256]{1,0:T(8,128)(2,1)S(1)} %get-tuple-element.127), channel_id=1, source_target_pairs={{1,0},{2,1},{3,2},{0,3},{5,4},{6,5},{7,6},{4,7},{9,8},{10,9},{11,1... | collective-permute-start | bytes 393224 | tf_op jit(solution)/shard_map/ppermute | solution.py:561
  253.5 4.8 %shard_map.131 = (bf16[2048,128]{1,0:T(8,128)(2,1)}, bf16[2048,128]{1,0:T(8,128)(2,1)}, f32[2,2,64,128]{3,2,1,0:T(8,128)}) custom-call(s32[128]{0:T(128)} %reshape.107.idx_ref, s32[16]{0:T(128)} %reduce_sum.59.used_ref, s32[2]{0:T(128)} %bitcast.49, f32[2,2048,128]{2,1,0:T(8,128)} %get-tuple-element.108.win_ref, ...), custom_call_target="tpu_custom_call" | custom-call | flops 4194304 | bytes 16777216 | tf_op jit(solution)/shard_map/pallas_call | solution.py:400
  258.3 4.2 %shard_map.130.win_ref = f32[2,2048,128]{2,1,0:T(8,128)} custom-call(s32[128]{0:T(128)} %reshape.107.idx_ref, s32[16]{0:T(128)} %reduce_sum.59.used_ref, f32[2,2048,128]{2,1,0:T(8,128)} %get-tuple-element.105.win_ref, bf16[16,608,128]{2,1,0:T(8,128)(2,1)} %copy-done.3, bf16[2,64,256]{2,1,0:T(8,128)(2,1)} %copy-done.12, bf16[2,64,256]{2,1,0:T(8,128)(2,1)} %copy-done.13), custom_call_target="tpu_custom_call" | custom-call | flops 4194304 | bytes 14680064 | tf_op jit(solution)/shard_map/pallas_call | solution.py:413
  262.6 1.2 collective-permute-done.18.refs_7_
  263.7 2.2 collective-permute-done.19.refs_8_
  266.9 5.1 %shard_map.129 = bf16[2048,256]{1,0:T(8,128)(2,1)} custom-call(bf16[2048,256]{1,0:T(8,128)(2,1)} %get-tuple-element.90.c_ref.refs_0_, bf16[2048,256]{1,0:T(8,128)(2,1)} %collective-permute-done.13.refs_1_, bf16[2048,256]{1,0:T(8,128)(2,1)} %collective-permute-done.14.refs_2_, bf16[1024,256]{1,0:T(8,128)(2,1)} %copy-done.10, bf16[1024,256]{1,0:T(8,128)(2,1)} %copy-done.11, ...), custom_call_target="tpu_custom_call" | custom-call | flops 1073741824 | bytes 18874368 | tf_op jit(solution)/shard_map/pallas_call | solution.py:548
  272.1 3.5 %all-to-all-done.4.back_ref = bf16[16,608,128]{2,1,0:T(8,128)(2,1)} async-done(((bf16[16,608,128]{2,1,0:T(8,128)(2,1)}), bf16[16,608,128]{2,1,0:T(8,128)(2,1)}, u32[]{:S(2)}, u32[]{:S(2)}) %all-to-all-start.4) | async-done | bytes 2490400 | tf_op jit(solution)/shard_map/all_to_all | solution.py:599
  275.5 1.0 slice.23.own_ref
  276.6 4.9 %shard_map.132 = (bf16[2048,256]{1,0:T(8,128)(2,1)}, bf16[2048,256]{1,0:T(8,128)(2,1)}) custom-call(s32[128]{0:T(128)} %reshape.107.idx_ref, s32[16]{0:T(128)} %reduce_sum.59.used_ref, s32[2]{0:T(128)} %bitcast.50, s32[1]{0:T(128)} %bitcast.me_ref, f32[2,2048,128]{2,1,0:T(8,128)} %shard_map.130.win_ref, bf16[16,608,128]{2,1,0:T(8,128)(2,1)} %all-to-all-done.4.back_ref, ...), custom_call_target="tpu_custom_call" | custom-call | flops 4194304 | bytes 12582912 | tf_op jit(solution)/shard_map/pallas_call | solution.py:429
  282.2 2.1 shard_map.133
  (101 shorter events, 13.4 us)
Async XLA Ops:
  0.6 32.6 %copy-start = (s32[1,512,3]{1,0,2:T(1,128)S(1)}, s32[1,512,3]{1,0,2:T(1,128)}, u32[]{:S(2)}) copy-start(s32[1,512,3]{1,0,2:T(1,128)} %param.14) | copy-start | bytes 18436
  0.7 14.2 %copy-start.25 = (s32[1,512,3]{1,0,2:T(1,128)S(1)}, s32[1,512,3]{1,0,2:T(1,128)}, u32[]{:S(2)}) copy-start(s32[1,512,3]{1,0,2:T(1,128)} %param.13) | copy-start | bytes 18436
  3.1 18.0 %collective-permute-start = (bf16[256,256]{1,0:T(8,128)(2,1)}, bf16[256,256]{1,0:T(8,128)(2,1)S(1)}, u32[]{:S(2)}, u32[]{:S(2)}) collective-permute-start(bf16[256,256]{1,0:T(8,128)(2,1)} %get-tuple-element.69.a), channel_id=1, source_target_pairs={{8,0},{12,4},{16,8},{20,12},{24,16},{28,20},{32,24},{36,28},{40,32... | collective-permute-start | bytes 393224 | tf_op jit(solution)/shard_map/ppermute | solution.py:561
  9.5 11.6 %collective-permute-start.1 = (bf16[384,256]{1,0:T(8,128)(2,1)}, bf16[384,256]{1,0:T(8,128)(2,1)S(1)}, u32[]{:S(2)}, u32[]{:S(2)}) collective-permute-start(bf16[384,256]{1,0:T(8,128)(2,1)} %get-tuple-element.65), channel_id=1, source_target_pairs={{60,0},{0,4},{4,8},{8,12},{12,16},{16,20},{20,24},{24,28},{28,32},... | collective-permute-start | bytes 589832 | tf_op jit(solution)/shard_map/ppermute | solution.py:561
  10.5 10.6 %collective-permute-start.2 = (bf16[384,256]{1,0:T(8,128)(2,1)}, bf16[384,256]{1,0:T(8,128)(2,1)S(1)}, u32[]{:S(2)}, u32[]{:S(2)}) collective-permute-start(bf16[384,256]{1,0:T(8,128)(2,1)} %get-tuple-element.66), channel_id=1, source_target_pairs={{4,0},{8,4},{12,8},{16,12},{20,16},{24,20},{28,24},{32,28},{36,32}... | collective-permute-start | bytes 589832 | tf_op jit(solution)/shard_map/ppermute | solution.py:561
  21.1 0.7 copy-start.16
  21.1 0.8 copy-start.17
  21.1 5.4 %copy-start.6 = (bf16[1,2048,256]{2,1,0:T(8,128)(2,1)S(1)}, bf16[1,2048,256]{2,1,0:T(8,128)(2,1)}, u32[]{:S(2)}) copy-start(bf16[1,2048,256]{2,1,0:T(8,128)(2,1)} %param.11) | copy-start | bytes 3145732
  21.8 62.6 %all-to-all-start = ((bf16[16,1024,128]{2,1,0:T(8,128)(2,1)}), bf16[16,1024,128]{2,1,0:T(8,128)(2,1)}, u32[]{:S(2)}, u32[]{:S(2)}) async-start(bf16[16,1024,128]{2,1,0:T(8,128)(2,1)} %bitcast.39), calls=%async_computation | async-start | bytes 8388608 | tf_op jit(solution)/shard_map/all_to_all | solution.py:599
  26.5 57.8 %collective-permute-start.3 = (bf16[2048,256]{1,0:T(8,128)(2,1)S(1)}, bf16[2048,256]{1,0:T(8,128)(2,1)S(1)}, u32[]{:S(2)}, u32[]{:S(2)}) collective-permute-start(bf16[2048,256]{1,0:T(8,128)(2,1)S(1)} %bitcast.43), channel_id=1, source_target_pairs={{1,0},{2,1},{3,2},{0,3},{5,4},{6,5},{7,6},{4,7},{9,8},{10,9},{11,1... | collective-permute-start | bytes 3145736 | tf_op jit(solution)/shard_map/ppermute | solution.py:561
  29.4 55.0 %collective-permute-start.4 = (bf16[2048,256]{1,0:T(8,128)(2,1)S(1)}, bf16[2048,256]{1,0:T(8,128)(2,1)S(1)}, u32[]{:S(2)}, u32[]{:S(2)}) collective-permute-start(bf16[2048,256]{1,0:T(8,128)(2,1)S(1)} %bitcast.44), channel_id=1, source_target_pairs={{3,0},{0,1},{1,2},{2,3},{7,4},{4,5},{5,6},{6,7},{11,8},{8,9},{9,10... | collective-permute-start | bytes 3145736 | tf_op jit(solution)/shard_map/ppermute | solution.py:561
  37.5 41.6 %collective-permute-start.5 = (bf16[256,256]{1,0:T(8,128)(2,1)}, bf16[256,256]{1,0:T(8,128)(2,1)S(1)}, u32[]{:S(2)}, u32[]{:S(2)}) collective-permute-start(bf16[256,256]{1,0:T(8,128)(2,1)} %shard_map.122.a), channel_id=1, source_target_pairs={{16,0},{20,4},{24,8},{28,12},{32,16},{36,20},{40,24},{44,28},{48,3... | collective-permute-start | bytes 393224 | tf_op jit(solution)/shard_map/ppermute | solution.py:561
  40.6 41.0 %collective-permute-start.6 = (bf16[256,256]{1,0:T(8,128)(2,1)}, bf16[256,256]{1,0:T(8,128)(2,1)S(1)}, u32[]{:S(2)}, u32[]{:S(2)}) collective-permute-start(bf16[256,256]{1,0:T(8,128)(2,1)} %shard_map.122.a), channel_id=1, source_target_pairs={{48,0},{52,4},{56,8},{60,12},{0,16},{4,20},{8,24},{12,28},{16,32},... | collective-permute-start | bytes 393224 | tf_op jit(solution)/shard_map/ppermute | solution.py:561
  40.6 43.7 %collective-permute-start.7 = (bf16[256,256]{1,0:T(8,128)(2,1)}, bf16[256,256]{1,0:T(8,128)(2,1)S(1)}, u32[]{:S(2)}, u32[]{:S(2)}) collective-permute-start(bf16[256,256]{1,0:T(8,128)(2,1)} %shard_map.122.a), channel_id=1, source_target_pairs={{32,0},{36,4},{40,8},{44,12},{48,16},{52,20},{56,24},{60,28},{0,32... | collective-permute-start | bytes 393224 | tf_op jit(solution)/shard_map/ppermute | solution.py:561
  79.1 5.3 %copy-start.18 = (bf16[256,256]{1,0:T(8,128)(2,1)}, bf16[256,256]{1,0:T(8,128)(2,1)S(1)}, u32[]{:S(2)}) copy-start(bf16[256,256]{1,0:T(8,128)(2,1)S(1)} %collective-permute-done.5.b) | copy-start | bytes 393220
  81.7 2.7 copy-start.19
  84.4 6.4 %copy-start.4 = (bf16[2048,256]{1,0:T(8,128)(2,1)}, bf16[2048,256]{1,0:T(8,128)(2,1)S(1)}, u32[]{:S(2)}) copy-start(bf16[2048,256]{1,0:T(8,128)(2,1)S(1)} %collective-permute-done.3.refs_1_) | copy-start | bytes 3145732
  84.4 9.3 %copy-start.5 = (bf16[2048,256]{1,0:T(8,128)(2,1)}, bf16[2048,256]{1,0:T(8,128)(2,1)S(1)}, u32[]{:S(2)}) copy-start(bf16[2048,256]{1,0:T(8,128)(2,1)S(1)} %collective-permute-done.4.refs_2_) | copy-start | bytes 3145732
  85.0 58.5 %all-to-all-start.1 = ((bf16[16,1024,128]{2,1,0:T(8,128)(2,1)}), bf16[16,1024,128]{2,1,0:T(8,128)(2,1)}, u32[]{:S(2)}, u32[]{:S(2)}) async-start(bf16[16,1024,128]{2,1,0:T(8,128)(2,1)} %bitcast.38), calls=%async_computation.1 | async-start | bytes 8388608 | tf_op jit(solution)/shard_map/all_to_all | solution.py:599
  90.8 11.5 %collective-permute-start.8 = (bf16[1024,256]{1,0:T(8,128)(2,1)S(1)}, bf16[1024,256]{1,0:T(8,128)(2,1)S(1)}, u32[]{:S(2)}, u32[]{:S(2)}) collective-permute-start(bf16[1024,256]{1,0:T(8,128)(2,1)S(1)} %slice.18), channel_id=1, source_target_pairs={{1,0},{2,1},{3,2},{0,3},{5,4},{6,5},{7,6},{4,7},{9,8},{10,9},{11,1... | collective-permute-start | bytes 1572872 | tf_op jit(solution)/shard_map/ppermute | solution.py:561
  93.7 12.2 %collective-permute-start.9 = (bf16[1024,256]{1,0:T(8,128)(2,1)S(1)}, bf16[1024,256]{1,0:T(8,128)(2,1)S(1)}, u32[]{:S(2)}, u32[]{:S(2)}) collective-permute-start(bf16[1024,256]{1,0:T(8,128)(2,1)S(1)} %slice.19), channel_id=1, source_target_pairs={{3,0},{0,1},{1,2},{2,3},{7,4},{4,5},{5,6},{6,7},{11,8},{8,9},{9,10... | collective-permute-start | bytes 1572872 | tf_op jit(solution)/shard_map/ppermute | solution.py:561
  102.4 3.5 %copy-start.7 = (bf16[1024,256]{1,0:T(8,128)(2,1)}, bf16[1024,256]{1,0:T(8,128)(2,1)S(1)}, u32[]{:S(2)}) copy-start(bf16[1024,256]{1,0:T(8,128)(2,1)S(1)} %collective-permute-done.8.refs_3_) | copy-start | bytes 1572868
  105.9 0.8 copy-start.8
  143.5 56.1 %all-to-all-start.2 = ((bf16[16,1024,128]{2,1,0:T(8,128)(2,1)}), bf16[16,1024,128]{2,1,0:T(8,128)(2,1)}, u32[]{:S(2)}, u32[]{:S(2)}) async-start(bf16[16,1024,128]{2,1,0:T(8,128)(2,1)} %bitcast.40), calls=%async_computation.2 | async-start | bytes 8388608 | tf_op jit(solution)/shard_map/all_to_all | solution.py:599
  181.6 1.7 collective-permute-start.10
  183.3 0.7 copy-start.14
  185.9 22.0 %copy-start.26 = (bf16[2,64,256]{2,1,0:T(8,128)(2,1)S(1)}, bf16[2,64,256]{2,1,0:T(8,128)(2,1)}, u32[]{:S(2)}) copy-start(bf16[2,64,256]{2,1,0:T(8,128)(2,1)} %get-tuple-element.99) | copy-start | bytes 196612
  185.9 23.2 %copy-start.27 = (bf16[2,64,256]{2,1,0:T(8,128)(2,1)S(1)}, bf16[2,64,256]{2,1,0:T(8,128)(2,1)}, u32[]{:S(2)}) copy-start(bf16[2,64,256]{2,1,0:T(8,128)(2,1)} %get-tuple-element.100) | copy-start | bytes 196612
  199.6 37.1 %all-to-all-start.3 = ((bf16[16,608,128]{2,1,0:T(8,128)(2,1)}), bf16[16,608,128]{2,1,0:T(8,128)(2,1)S(1)}, u32[]{:S(2)}, u32[]{:S(2)}) async-start(bf16[16,608,128]{2,1,0:T(8,128)(2,1)} %shard_map.128), calls=%async_computation.3 | async-start | bytes 4980736 | tf_op jit(solution)/shard_map/all_to_all | solution.py:599
  205.0 32.8 %collective-permute-start.13 = (bf16[2048,256]{1,0:T(8,128)(2,1)}, bf16[2048,256]{1,0:T(8,128)(2,1)}, u32[]{:S(2)}, u32[]{:S(2)}) collective-permute-start(bf16[2048,256]{1,0:T(8,128)(2,1)} %get-tuple-element.90.c_ref.refs_0_), channel_id=1, source_target_pairs={{1,0},{2,1},{3,2},{0,3},{5,4},{6,5},{7,6},{4,7},{9,8},{10,9},{11,1... | collective-permute-start | bytes 3145736 | tf_op jit(solution)/shard_map/ppermute | solution.py:561
  207.8 30.0 %collective-permute-start.14 = (bf16[2048,256]{1,0:T(8,128)(2,1)}, bf16[2048,256]{1,0:T(8,128)(2,1)}, u32[]{:S(2)}, u32[]{:S(2)}) collective-permute-start(bf16[2048,256]{1,0:T(8,128)(2,1)} %get-tuple-element.90.c_ref.refs_0_), channel_id=1, source_target_pairs={{3,0},{0,1},{1,2},{2,3},{7,4},{4,5},{5,6},{6,7},{11,8},{8,9},{9,10... | collective-permute-start | bytes 3145736 | tf_op jit(solution)/shard_map/ppermute | solution.py:561
  207.8 29.9 %collective-permute-start.11 = (bf16[2,64,256]{2,1,0:T(8,128)(2,1)S(1)}, bf16[2,64,256]{2,1,0:T(8,128)(2,1)S(1)}, u32[]{:S(2)}, u32[]{:S(2)}) collective-permute-start(bf16[2,64,256]{2,1,0:T(8,128)(2,1)S(1)} %copy-done.26), channel_id=1, source_target_pairs={{4,0},{8,4},{12,8},{16,12},{20,16},{24,20},{28,24},{32,28},{36,32}... | collective-permute-start | bytes 196616 | tf_op jit(solution)/shard_map/ppermute | solution.py:577
  209.1 28.7 %collective-permute-start.12 = (bf16[2,64,256]{2,1,0:T(8,128)(2,1)S(1)}, bf16[2,64,256]{2,1,0:T(8,128)(2,1)S(1)}, u32[]{:S(2)}, u32[]{:S(2)}) collective-permute-start(bf16[2,64,256]{2,1,0:T(8,128)(2,1)S(1)} %copy-done.27), channel_id=1, source_target_pairs={{0,4},{4,8},{8,12},{12,16},{16,20},{20,24},{24,28},{28,32},{32,36}... | collective-permute-start | bytes 196616 | tf_op jit(solution)/shard_map/ppermute | solution.py:577
  236.8 1.6 copy-start.3
  237.8 11.0 %copy-start.2 = (bf16[256,1024]{1,0:T(8,128)(2,1)S(1)}, bf16[256,1024]{1,0:T(8,128)(2,1)}, u32[]{:S(2)}) copy-start(bf16[256,1024]{1,0:T(8,128)(2,1)} %refs_8_.1) | copy-start | bytes 1572868
  238.4 37.1 %all-to-all-start.4 = ((bf16[16,608,128]{2,1,0:T(8,128)(2,1)}), bf16[16,608,128]{2,1,0:T(8,128)(2,1)}, u32[]{:S(2)}, u32[]{:S(2)}) async-start(bf16[16,608,128]{2,1,0:T(8,128)(2,1)} %broadcast_dynamic-update-slice_fusion), calls=%async_computation.4 | async-start | bytes 4980736 | tf_op jit(solution)/shard_map/all_to_all | solution.py:599
  244.7 21.2 %collective-permute-start.15 = (bf16[1024,256]{1,0:T(8,128)(2,1)S(1)}, bf16[1024,256]{1,0:T(8,128)(2,1)S(1)}, u32[]{:S(2)}, u32[]{:S(2)}) collective-permute-start(bf16[1024,256]{1,0:T(8,128)(2,1)S(1)} %slice.21), channel_id=1, source_target_pairs={{1,0},{2,1},{3,2},{0,3},{5,4},{6,5},{7,6},{4,7},{9,8},{10,9},{11,1... | collective-permute-start | bytes 1572872 | tf_op jit(solution)/shard_map/ppermute | solution.py:561
  248.6 17.3 %collective-permute-start.16 = (bf16[1024,256]{1,0:T(8,128)(2,1)S(1)}, bf16[1024,256]{1,0:T(8,128)(2,1)S(1)}, u32[]{:S(2)}, u32[]{:S(2)}) collective-permute-start(bf16[1024,256]{1,0:T(8,128)(2,1)S(1)} %slice.22), channel_id=1, source_target_pairs={{3,0},{0,1},{1,2},{2,3},{7,4},{4,5},{5,6},{6,7},{11,8},{8,9},{9,10... | collective-permute-start | bytes 1572872 | tf_op jit(solution)/shard_map/ppermute | solution.py:561
  249.5 13.1 %collective-permute-start.17 = (bf16[256,256]{1,0:T(8,128)(2,1)S(1)}, bf16[256,256]{1,0:T(8,128)(2,1)S(1)}, u32[]{:S(2)}, u32[]{:S(2)}) collective-permute-start(bf16[256,256]{1,0:T(8,128)(2,1)S(1)} %get-tuple-element.127), channel_id=1, source_target_pairs={{1,0},{2,1},{3,2},{0,3},{5,4},{6,5},{7,6},{4,7},{9,8},{10,9},{11,1... | collective-permute-start | bytes 393224 | tf_op jit(solution)/shard_map/ppermute | solution.py:561
  252.7 11.1 %collective-permute-start.18 = (bf16[256,256]{1,0:T(8,128)(2,1)S(1)}, bf16[256,256]{1,0:T(8,128)(2,1)S(1)}, u32[]{:S(2)}, u32[]{:S(2)}) collective-permute-start(bf16[256,256]{1,0:T(8,128)(2,1)S(1)} %get-tuple-element.126), channel_id=1, source_target_pairs={{2,0},{3,1},{0,2},{1,3},{6,4},{7,5},{4,6},{5,7},{10,8},{11,9},{8,1... | collective-permute-start | bytes 393224 | tf_op jit(solution)/shard_map/ppermute | solution.py:561
  252.7 13.3 %collective-permute-start.19 = (bf16[256,256]{1,0:T(8,128)(2,1)S(1)}, bf16[256,256]{1,0:T(8,128)(2,1)S(1)}, u32[]{:S(2)}, u32[]{:S(2)}) collective-permute-start(bf16[256,256]{1,0:T(8,128)(2,1)S(1)} %get-tuple-element.125), channel_id=1, source_target_pairs={{3,0},{0,1},{1,2},{2,3},{7,4},{4,5},{5,6},{6,7},{11,8},{8,9},{9,10... | collective-permute-start | bytes 393224 | tf_op jit(solution)/shard_map/ppermute | solution.py:561
  262.6 3.4 %copy-start.21 = (bf16[256,256]{1,0:T(8,128)(2,1)}, bf16[256,256]{1,0:T(8,128)(2,1)S(1)}, u32[]{:S(2)}) copy-start(bf16[256,256]{1,0:T(8,128)(2,1)S(1)} %collective-permute-done.17.refs_6_) | copy-start | bytes 393220
  263.7 2.2 copy-start.22
  265.9 0.8 copy-start.10
  265.9 1.0 copy-start.11
  275.5 8.8 %copy-start.1 = (s32[1,512,3]{1,0,2:T(1,128)S(1)}, s32[1,512,3]{1,0,2:T(1,128)}, u32[]{:S(2)}) copy-start(s32[1,512,3]{1,0,2:T(1,128)} %param.14) | copy-start | bytes 18436
  276.5 5.0 %copy-start.9 = (bf16[16,64,128]{2,1,0:T(8,128)(2,1)}, bf16[16,64,128]{2,1,0:T(8,128)(2,1)S(1)}, u32[]{:S(2)}) copy-start(bf16[16,64,128]{2,1,0:T(8,128)(2,1)S(1)} %slice.23.own_ref) | copy-start | bytes 786436
  276.5 5.0 %collective-permute-start.20 = (bf16[16,64,128]{2,1,0:T(8,128)(2,1)S(1)}, bf16[16,64,128]{2,1,0:T(8,128)(2,1)S(1)}, u32[]{:S(2)}, u32[]{:S(2)}) collective-permute-start(bf16[16,64,128]{2,1,0:T(8,128)(2,1)S(1)} %slice.23.own_ref), channel_id=1, source_target_pairs={{64,0},{0,64},{65,1},{1,65},{66,2},{2,66},{67,3},{3,67},{68,4},{4,... | collective-permute-start | bytes 786440 | tf_op jit(solution)/shard_map/ppermute | solution.py:561
  (6 other events, 3.9 us)

commit v11 on v10

--- a/solution.py
+++ b/solution.py
@@ -13,7 +13,6 @@
 G = 2
 LANES = 128
 NEG_FILL = -1e30
-VMEM_LIMIT = 60 * 1024 * 1024
 CARRIED = 96
 
 NT = (((1,), (1,)), ((), ()))
@@ -35,8 +34,8 @@
     return pl.BlockSpec(shape, lambda i: (0,) * (len(shape) - 1) + (column,))
 
 
-def params(**more):
-    return pltpu.CompilerParams(vmem_limit_bytes=VMEM_LIMIT, **more)
+def params(mebibytes):
+    return pltpu.CompilerParams(vmem_limit_bytes=mebibytes << 20)
 
 
 def pick_kernel(slots, idx_ref, k_ref, v_ref, out_ref):
@@ -60,7 +59,7 @@
         in_specs=[smem(), whole((rows, LANES), column), whole((rows, LANES), column)],
         out_specs=pl.BlockSpec((slots // 4 * 2 * BLK, LANES), lambda i: (i, 0)),
         out_shape=jax.ShapeDtypeStruct((slots * 2 * BLK, LANES), jnp.bfloat16),
-        compiler_params=params(),
+        compiler_params=params(12),
         cost_estimate=pl.CostEstimate(flops=0, bytes_accessed=10 << 20, transcendentals=0),
     )(idx, keys, values)
 
@@ -99,7 +98,7 @@
             out_specs=tuple(pl.BlockSpec((n, width), lambda i, glob, me: (0, 0)) for n in sizes),
         ),
         out_shape=tuple(jax.ShapeDtypeStruct((n, width), jnp.bfloat16) for n in sizes),
-        compiler_params=params(),
+        compiler_params=params(4),
         cost_estimate=pl.CostEstimate(flops=0, bytes_accessed=1 << 19, transcendentals=0),
     )(glob, me, *[keys, values] * 4)
 
@@ -116,7 +115,7 @@
         in_specs=[whole(shape)] * 4,
         out_specs=whole(shape),
         out_shape=jax.ShapeDtypeStruct(shape, jnp.bfloat16),
-        compiler_params=params(),
+        compiler_params=params(4),
         cost_estimate=pl.CostEstimate(flops=0, bytes_accessed=60 << 20, transcendentals=0),
     )(*arrays)
 
@@ -163,7 +162,7 @@
             out_specs=pl.BlockSpec((TILE, heads), lambda i, at: (i, 0)),
         ),
         out_shape=jax.ShapeDtypeStruct((rows, heads), jnp.bfloat16),
-        compiler_params=params(),
+        compiler_params=params(12),
         cost_estimate=pl.CostEstimate(flops=2 * rows * 1024 * heads, bytes_accessed=16 << 20, transcendentals=0),
     )(at, *pieces, weight, weight, weight, weight)
 
@@ -301,7 +300,7 @@
         out_shape=tuple(jax.ShapeDtypeStruct(*shape) for shape in shapes),
         scratch_shapes=scratch,
         input_output_aliases={12: 0, 13: 1, 14: 3, 15: 4} if handed else {},
-        compiler_params=params(),
+        compiler_params=params(44),
         cost_estimate=pl.CostEstimate(
             flops=12 * blocks * 512 * 128 * 128 * 2, bytes_accessed=80 << 20, transcendentals=blocks * 512 * 128
         ),
@@ -404,7 +403,7 @@
         out_specs=(whole(out.shape), whole(out.shape), whole(kept.shape)),
         out_shape=(out, out, kept),
         scratch_shapes=[pltpu.VMEM((2, rows, LANES), jnp.float32)],
-        compiler_params=params(),
+        compiler_params=params(28),
         cost_estimate=pl.CostEstimate(flops=4 << 20, bytes_accessed=16 << 20, transcendentals=0),
     )(idx, used, glob, win, back, up, down)
 
@@ -416,7 +415,7 @@
         in_specs=[smem()] * 2 + [whole(x.shape) for x in (win, back)] + [whole((2, BLK, LANES), 1)] * 2,
         out_specs=whole(win.shape),
         out_shape=jax.ShapeDtypeStruct(win.shape, jnp.float32),
-        compiler_params=params(),
+        compiler_params=params(24),
         cost_estimate=pl.CostEstimate(flops=4 << 20, bytes_accessed=14 << 20, transcendentals=0),
     )(idx, used, win, back, up, down)
 
@@ -433,7 +432,7 @@
         out_specs=(whole(out.shape), whole(out.shape)),
         out_shape=(out, out),
         scratch_shapes=[pltpu.VMEM((2, rows, LANES), jnp.float32)],
-        compiler_params=params(),
+        compiler_params=params(28),
         cost_estimate=pl.CostEstimate(flops=4 << 20, bytes_accessed=12 << 20, transcendentals=0),
     )(idx, used, glob, me, *arrays)
 
@@ -472,7 +471,7 @@
             scratch_shapes=[pltpu.VMEM((2, *shape), jnp.float32)],
         ),
         out_shape=(jax.ShapeDtypeStruct(shape, jnp.bfloat16),) * 2,
-        compiler_params=params(),
+        compiler_params=params(12),
         cost_estimate=pl.CostEstimate(flops=2 * rows * 1024 * 256, bytes_accessed=16 << 20, transcendentals=0),
     )(at, context, *pieces)
 
@@ -501,7 +500,7 @@
         out_specs=carried(part),
         out_shape=jax.ShapeDtypeStruct(part.shape, part.dtype),
         input_output_aliases={4: 0},
-        compiler_params=params(),
+        compiler_params=params(8),
         cost_estimate=pl.CostEstimate(flops=1 << 18, bytes_accessed=4 << 20, transcendentals=0),
     )(own, other, *sums, part)
 
@@ -530,7 +529,7 @@
         in_specs=[smem(), whole(own.shape), whole(other.shape)],
         out_specs=whole(shape),
         out_shape=jax.ShapeDtypeStruct(shape, jnp.float32),
-        compiler_params=params(),
+        compiler_params=params(8),
         cost_estimate=pl.CostEstimate(flops=1 << 18, bytes_accessed=2 << 20, transcendentals=0),
     )(at, own, other)
 
@@ -551,7 +550,7 @@
         in_specs=ring_specs(rows, width) + [pl.BlockSpec(w.shape, lambda i: (0, 0)) for w in weights],
         out_specs=pl.BlockSpec((TILE, width), lambda i: (i, 0)),
         out_shape=jax.ShapeDtypeStruct((rows, width), jnp.bfloat16),
-        compiler_params=params(),
+        compiler_params=params(12),
         cost_estimate=pl.CostEstimate(flops=2 * rows * 1024 * width, bytes_accessed=18 << 20, transcendentals=0),
     )(*pieces, *weights)
 

time: 287 us -> 295 us (1.028)
  local copies, waits for them, and re-layouts: 12.6 us -> 37.6 us
  Pallas kernels: 103 us -> 81.5 us
    unnamed x57 -> x111, local copies, waits for them, and re-layouts: 5.33 us -> 27.5 us
    ppermute x19, waiting for transfers between devices: 55.1 us -> 63.7 us  [shifted(): lax.ppermute(array, axis, [((i + by) % size, i) for i in range(size)])]
    all_to_all x5, waiting for transfers between devices: 44.2 us -> 38.8 us  [exchange(): return lax.all_to_all(parts, 'ctx', split_axis=0, concat_axis=0, tiled=True)]
    pallas_call x2, Pallas kernels: 7.86 us -> 2.77 us  [pick_blocks(): pl.pallas_call(functools.partial(pick_kernel, slots // 4), grid=(4,), in_...]
    all_to_all x5, starting transfers between devices: 26 us -> 31 us  [exchange(): return lax.all_to_all(parts, 'ctx', split_axis=0, concat_axis=0, tiled=True)]
    pallas_call x2, Pallas kernels: 3.56 us -> 0.06 us  [sum_four(): pl.pallas_call(sum_four_kernel, grid=(1,), in_specs=[whole(shape)] * 4, o...]
    ppermute x19, starting transfers between devices: 32.7 us -> 29.5 us  [shifted(): lax.ppermute(array, axis, [((i + by) % size, i) for i in range(size)])]
  transfers between devices with their start and end apart: 26 -> 26, of which waited for: 12 -> 12; matrix products, arithmetic and copies ran while one was open for 4% -> 4% of each run, Pallas kernels for 35% -> 27%
where the time goes in v11:
time: 295 us; the launch traced here: 292 us
  waiting for transfers between devices  102 us (35%)
  Pallas kernels  81.5 us (28%)
  starting transfers between devices  66.3 us (22%)
  local copies, waits for them, and re-layouts  37.6 us (13%)
    ppermute x19, waiting for transfers between devices, shifted(): lax.ppermute(array, axis, [((i + by) % size, i) for i in range(size)])  63.7 us
    pallas_call x2, Pallas kernels, attend(): pl.pallas_call(functools.partial(attend_kernel, blocks, last_block, len(h...  51.6 us
    all_to_all x5, waiting for transfers between devices, exchange(): return lax.all_to_all(parts, 'ctx', split_axis=0, concat_axis=0, tiled=True)  38.8 us
    all_to_all x5, starting transfers between devices, exchange(): return lax.all_to_all(parts, 'ctx', split_axis=0, concat_axis=0, tiled=True)  31 us
    ppermute x19, starting transfers between devices, shifted(): lax.ppermute(array, axis, [((i + by) % size, i) for i in range(size)])  29.5 us
    unnamed x111, local copies, waits for them, and re-layouts  27.5 us
  transfers between devices with their start and end apart: 26, of which 12 were waited for; matrix products, arithmetic and copies ran while one was open for 4% of the time, Pallas kernels for 27%

profile of v11, /device:TPU:0, one launch (start us, length us, event | category | flops | bytes accessed | tf_op | source)
XLA Modules:
  0.0 291.9 jit_solution(3381194059438648587)
XLA Ops:
  1.9 1.2 copy-done.4
  4.4 6.5 %collective-permute-start = (bf16[256,256]{1,0:T(8,128)(2,1)S(1)}, bf16[256,256]{1,0:T(8,128)(2,1)S(1)}, u32[]{:S(2)}, u32[]{:S(2)}) collective-permute-start(bf16[256,256]{1,0:T(8,128)(2,1)S(1)} %get-tuple-element.69.a), channel_id=1, source_target_pairs={{8,0},{12,4},{16,8},{20,12},{24,16},{28,20},{32,24},{36,28},{40,32... | collective-permute-start | bytes 393224 | tf_op jit(solution)/shard_map/ppermute | solution.py:560
  11.9 4.3 %collective-permute-start.2 = (bf16[384,256]{1,0:T(8,128)(2,1)S(1)}, bf16[384,256]{1,0:T(8,128)(2,1)S(1)}, u32[]{:S(2)}, u32[]{:S(2)}) collective-permute-start(bf16[384,256]{1,0:T(8,128)(2,1)S(1)} %get-tuple-element.66), channel_id=1, source_target_pairs={{4,0},{8,4},{12,8},{16,12},{20,16},{24,20},{28,24},{32,28},{36,32}... | collective-permute-start | bytes 589832 | tf_op jit(solution)/shard_map/ppermute | solution.py:560
  19.0 1.4 shard_map.120
  20.4 2.0 copy-done.7
  22.5 4.5 %all-to-all-start = ((bf16[16,1024,128]{2,1,0:T(8,128)(2,1)}), bf16[16,1024,128]{2,1,0:T(8,128)(2,1)}, u32[]{:S(2)}, u32[]{:S(2)}) async-start(bf16[16,1024,128]{2,1,0:T(8,128)(2,1)} %bitcast.39), calls=%async_computation | async-start | bytes 8388608 | tf_op jit(solution)/shard_map/all_to_all | solution.py:598
  27.1 2.8 collective-permute-start.3
  29.9 1.4 shard_map.119
  31.3 2.0 copy-done.6
  34.0 3.1 %collective-permute-start.5 = (bf16[256,256]{1,0:T(8,128)(2,1)S(1)}, bf16[256,256]{1,0:T(8,128)(2,1)S(1)}, u32[]{:S(2)}, u32[]{:S(2)}) collective-permute-start(bf16[256,256]{1,0:T(8,128)(2,1)S(1)} %shard_map.122.a), channel_id=1, source_target_pairs={{16,0},{20,4},{24,8},{28,12},{32,16},{36,20},{40,24},{44,28},{48,3... | collective-permute-start | bytes 393224 | tf_op jit(solution)/shard_map/ppermute | solution.py:560
  37.1 2.3 collective-permute-start.7
  40.0 40.2 %collective-permute-done.5.b = bf16[256,256]{1,0:T(8,128)(2,1)S(1)} collective-permute-done((bf16[256,256]{1,0:T(8,128)(2,1)S(1)}, bf16[256,256]{1,0:T(8,128)(2,1)S(1)}, u32[]{:S(2)}, u32[]{:S(2)}) %collective-permute-start.5) | collective-permute-done | bytes 131104 | tf_op jit(solution)/shard_map/ppermute | solution.py:560
  80.2 3.7 %collective-permute-done.6.c = bf16[256,256]{1,0:T(8,128)(2,1)S(1)} collective-permute-done((bf16[256,256]{1,0:T(8,128)(2,1)S(1)}, bf16[256,256]{1,0:T(8,128)(2,1)S(1)}, u32[]{:S(2)}, u32[]{:S(2)}) %collective-permute-start.6) | collective-permute-done | bytes 131104 | tf_op jit(solution)/shard_map/ppermute | solution.py:560
  83.9 2.3 collective-permute-done.7.d
  86.8 6.9 %all-to-all-start.1 = ((bf16[16,1024,128]{2,1,0:T(8,128)(2,1)}), bf16[16,1024,128]{2,1,0:T(8,128)(2,1)}, u32[]{:S(2)}, u32[]{:S(2)}) async-start(bf16[16,1024,128]{2,1,0:T(8,128)(2,1)} %bitcast.38), calls=%async_computation.1 | async-start | bytes 8388608 | tf_op jit(solution)/shard_map/all_to_all | solution.py:598
  93.7 1.9 slice.18
  95.6 2.8 collective-permute-start.8
  98.4 1.9 slice.19
  103.1 4.5 %collective-permute-done.8.refs_3_ = bf16[1024,256]{1,0:T(8,128)(2,1)S(1)} collective-permute-done((bf16[1024,256]{1,0:T(8,128)(2,1)}, bf16[1024,256]{1,0:T(8,128)(2,1)S(1)}, u32[]{:S(2)}, u32[]{:S(2)}) %collective-permute-start.8) | collective-permute-done | bytes 524320 | tf_op jit(solution)/shard_map/ppermute | solution.py:560
  107.6 5.3 %collective-permute-done.9.refs_4_ = bf16[1024,256]{1,0:T(8,128)(2,1)} collective-permute-done((bf16[1024,256]{1,0:T(8,128)(2,1)}, bf16[1024,256]{1,0:T(8,128)(2,1)}, u32[]{:S(2)}, u32[]{:S(2)}) %collective-permute-start.9) | collective-permute-done | bytes 524320 | tf_op jit(solution)/shard_map/ppermute | solution.py:560
  112.9 1.2 copy-done.14
  114.1 4.4 %shard_map.123.g_ref = bf16[2048,256]{1,0:T(8,128)(2,1)S(1)} custom-call(s32[2]{0:T(128)S(1)} %pad_add_fusion.at_ref, bf16[2048,256]{1,0:T(8,128)(2,1)S(1)} %bitcast.42, bf16[2048,256]{1,0:T(8,128)(2,1)} %collective-permute-done.3.refs_1_, bf16[2048,256]{1,0:T(8,128)(2,1)} %collective-permute-done.4.refs_2_, ...), custom_call_target="tpu_custom_call" | custom-call | flops 1073741824 | bytes 16777216 | tf_op jit(solution)/shard_map/pallas_call | solution.py:156
  118.5 25.6 %shard_map.125 = (bf16[2048,256]{1,0:T(8,128)(2,1)S(1)}, bf16[2048,256]{1,0:T(8,128)(2,1)}, f32[2,2048,128]{2,1,0:T(8,128)S(1)}, bf16[2,64,256]{2,1,0:T(8,128)(2...) custom-call(s32[1]{0:T(128)} %bitcast.me_ref, ...), custom_call_target="tpu_custom_call" | custom-call | flops 6442450944 | bytes 83886080 | tf_op jit(solution)/shard_map/pallas_call | solution.py:288
  145.1 1.3 copy-done.18
  148.6 7.1 %all-to-all-start.2 = ((bf16[16,1024,128]{2,1,0:T(8,128)(2,1)}), bf16[16,1024,128]{2,1,0:T(8,128)(2,1)}, u32[]{:S(2)}, u32[]{:S(2)}) async-start(bf16[16,1024,128]{2,1,0:T(8,128)(2,1)} %bitcast.51), calls=%async_computation.2 | async-start | bytes 8388608 | tf_op jit(solution)/shard_map/all_to_all | solution.py:598
  160.3 1.2 copy-done.45
  163.2 26.0 %shard_map.126 = (bf16[2048,256]{1,0:T(8,128)(2,1)S(1)}, bf16[2048,256]{1,0:T(8,128)(2,1)}, f32[2,2048,128]{2,1,0:T(8,128)S(1)}, bf16[2,64,256]{2,1,0:T(8,128)(2...) custom-call(s32[1]{0:T(128)} %bitcast.me_ref, ...), custom_call_target="tpu_custom_call", output_to_operand_aliasing={{0}: (12, {}), {1}: (13, {}), {3}: (14, {}), {4}: (15, {})} | custom-call | flops 6442450944 | bytes 83886080 | tf_op jit(solution)/shard_map/pallas_call | solution.py:288
  189.2 5.0 %shard_map.127 = (bf16[128,1024]{1,0:T(8,128)(2,1)S(1)}, bf16[128,1024]{1,0:T(8,128)(2,1)S(1)}) custom-call(s32[2]{0:T(128)S(1)} %pad_add_fusion.at_ref, bf16[2048,256]{1,0:T(8,128)(2,1)S(1)} %get-tuple-element.90.c_ref.refs_0_, bf16[2048,256]{1,0:T(8,128)(2,1)S(1)} %bitcast.43, bf16[2048,256]{1,0:T(8,128)(2,1)} %collective-permute-done.3.refs_1_, ...), custom_call_target="tpu_custom_call" | custom-call | flops 1073741824 | bytes 16777216 | tf_op jit(solution)/shard_map/pallas_call | solution.py:464
  194.6 1.5 collective-permute-done.10.other_ref
  196.9 8.0 %all-to-all-done.2.back_ref = bf16[16,1024,128]{2,1,0:T(8,128)(2,1)} async-done(((bf16[16,1024,128]{2,1,0:T(8,128)(2,1)}), bf16[16,1024,128]{2,1,0:T(8,128)(2,1)}, u32[]{:S(2)}, u32[]{:S(2)}) %all-to-all-start.2) | async-done | bytes 4194336 | tf_op jit(solution)/shard_map/all_to_all | solution.py:598
  204.9 7.4 %all-to-all-start.3 = ((bf16[16,608,128]{2,1,0:T(8,128)(2,1)}), bf16[16,608,128]{2,1,0:T(8,128)(2,1)}, u32[]{:S(2)}, u32[]{:S(2)}) async-start(bf16[16,608,128]{2,1,0:T(8,128)(2,1)} %shard_map.128), calls=%async_computation.3 | async-start | bytes 4980736 | tf_op jit(solution)/shard_map/all_to_all | solution.py:598
  212.5 2.0 collective-permute-start.14
  214.5 1.3 collective-permute-start.11
  215.8 4.5 %collective-permute-start.12 = (bf16[2,64,256]{2,1,0:T(8,128)(2,1)S(1)}, bf16[2,64,256]{2,1,0:T(8,128)(2,1)S(1)}, u32[]{:S(2)}, u32[]{:S(2)}) collective-permute-start(bf16[2,64,256]{2,1,0:T(8,128)(2,1)S(1)} %copy-done.53), channel_id=1, source_target_pairs={{0,4},{4,8},{8,12},{12,16},{16,20},{20,24},{24,28},{28,32},{32,36}... | collective-permute-start | bytes 196616 | tf_op jit(solution)/shard_map/ppermute | solution.py:576
  220.4 23.8 %all-to-all-done.3.back_ref = bf16[16,608,128]{2,1,0:T(8,128)(2,1)} async-done(((bf16[16,608,128]{2,1,0:T(8,128)(2,1)}), bf16[16,608,128]{2,1,0:T(8,128)(2,1)}, u32[]{:S(2)}, u32[]{:S(2)}) %all-to-all-start.3) | async-done | bytes 2490400 | tf_op jit(solution)/shard_map/all_to_all | solution.py:598
  246.1 5.1 %all-to-all-start.4 = ((bf16[16,608,128]{2,1,0:T(8,128)(2,1)}), bf16[16,608,128]{2,1,0:T(8,128)(2,1)}, u32[]{:S(2)}, u32[]{:S(2)}) async-start(bf16[16,608,128]{2,1,0:T(8,128)(2,1)} %broadcast_dynamic-update-slice_fusion), calls=%async_computation.4 | async-start | bytes 4980736 | tf_op jit(solution)/shard_map/all_to_all | solution.py:598
  252.0 2.0 slice.22
  254.0 1.9 collective-permute-start.16
  256.0 1.4 collective-permute-start.17
  258.4 3.6 %shard_map.131 = (bf16[2048,128]{1,0:T(8,128)(2,1)S(1)}, bf16[2048,128]{1,0:T(8,128)(2,1)S(1)}, f32[2,2,64,128]{3,2,1,0:T(8,128)S(1)}) custom-call(s32[128]{0:T(128)S(1)} %reshape.107.idx_ref, s32[16]{0:T(128)S(1)} %reduce_sum.59.used_ref, s32[2]{0:T(128)S(1)} %bitcast.47, f32[2,2048,128]{2,1,0:T(8,128)S(1)} %copy-done.19, ...), custom_call_target="tpu_custom_call" | custom-call | flops 4194304 | bytes 16777216 | tf_op jit(solution)/shard_map/pallas_call | solution.py:399
  262.8 2.7 shard_map.130.win_ref
  265.5 1.6 collective-permute-done.17.refs_6_
  267.1 2.0 collective-permute-done.18.refs_7_
  269.1 2.6 collective-permute-done.19.refs_8_
  271.7 4.4 %shard_map.129 = bf16[2048,256]{1,0:T(8,128)(2,1)} custom-call(bf16[2048,256]{1,0:T(8,128)(2,1)S(1)} %copy-done.13, bf16[2048,256]{1,0:T(8,128)(2,1)S(1)} %copy-done.17, bf16[2048,256]{1,0:T(8,128)(2,1)} %collective-permute-done.14.refs_2_, bf16[1024,256]{1,0:T(8,128)(2,1)S(1)} %collective-permute-done.15.refs_3_, ...), custom_call_target="tpu_custom_call" | custom-call | flops 1073741824 | bytes 18874368 | tf_op jit(solution)/shard_map/pallas_call | solution.py:547
  276.1 6.9 %all-to-all-done.4.back_ref = bf16[16,608,128]{2,1,0:T(8,128)(2,1)} async-done(((bf16[16,608,128]{2,1,0:T(8,128)(2,1)}), bf16[16,608,128]{2,1,0:T(8,128)(2,1)}, u32[]{:S(2)}, u32[]{:S(2)}) %all-to-all-start.4) | async-done | bytes 2490400 | tf_op jit(solution)/shard_map/all_to_all | solution.py:598
  286.2 4.1 %shard_map.132 = (bf16[2048,256]{1,0:T(8,128)(2,1)}, bf16[2048,256]{1,0:T(8,128)(2,1)}) custom-call(s32[128]{0:T(128)S(1)} %reshape.107.idx_ref, s32[16]{0:T(128)S(1)} %reduce_sum.59.used_ref, s32[2]{0:T(128)S(1)} %bitcast.48, s32[1]{0:T(128)} %bitcast.me_ref, f32[2,2048,128]{2,1,0:T(8,128)S(1)} %shard_map.130.win_ref, ...), custom_call_target="tpu_custom_call" | custom-call | flops 4194304 | bytes 12582912 | tf_op jit(solution)/shard_map/pallas_call | solution.py:428
  290.3 1.6 shard_map.133
  (155 shorter events, 29.5 us)
Async XLA Ops:
  0.6 32.6 %copy-start = (s32[1,512,3]{1,0,2:T(1,128)S(1)}, s32[1,512,3]{1,0,2:T(1,128)}, u32[]{:S(2)}) copy-start(s32[1,512,3]{1,0,2:T(1,128)} %param.14) | copy-start | bytes 18436
  3.8 12.4 %copy-start.54 = (s32[1,512,3]{1,0,2:T(1,128)S(1)}, s32[1,512,3]{1,0,2:T(1,128)}, u32[]{:S(2)}) copy-start(s32[1,512,3]{1,0,2:T(1,128)} %param.13) | copy-start | bytes 18436
  3.8 15.2 %copy-start.3 = (bf16[1,2048,256]{2,1,0:T(8,128)(2,1)S(1)}, bf16[1,2048,256]{2,1,0:T(8,128)(2,1)}, u32[]{:S(2)}) copy-start(bf16[1,2048,256]{2,1,0:T(8,128)(2,1)} %param.9) | copy-start | bytes 3145732
  3.8 15.3 %copy-start.5 = (bf16[1,2048,256]{2,1,0:T(8,128)(2,1)S(1)}, bf16[1,2048,256]{2,1,0:T(8,128)(2,1)}, u32[]{:S(2)}) copy-start(bf16[1,2048,256]{2,1,0:T(8,128)(2,1)} %param.10) | copy-start | bytes 3145732
  4.4 18.1 %collective-permute-start = (bf16[256,256]{1,0:T(8,128)(2,1)S(1)}, bf16[256,256]{1,0:T(8,128)(2,1)S(1)}, u32[]{:S(2)}, u32[]{:S(2)}) collective-permute-start(bf16[256,256]{1,0:T(8,128)(2,1)S(1)} %get-tuple-element.69.a), channel_id=1, source_target_pairs={{8,0},{12,4},{16,8},{20,12},{24,16},{28,20},{32,24},{36,28},{40,32... | collective-permute-start | bytes 393224 | tf_op jit(solution)/shard_map/ppermute | solution.py:560
  10.8 11.6 %collective-permute-start.1 = (bf16[384,256]{1,0:T(8,128)(2,1)S(1)}, bf16[384,256]{1,0:T(8,128)(2,1)S(1)}, u32[]{:S(2)}, u32[]{:S(2)}) collective-permute-start(bf16[384,256]{1,0:T(8,128)(2,1)S(1)} %get-tuple-element.65), channel_id=1, source_target_pairs={{60,0},{0,4},{4,8},{8,12},{12,16},{16,20},{20,24},{24,28},{28,32},... | collective-permute-start | bytes 589832 | tf_op jit(solution)/shard_map/ppermute | solution.py:560
  11.9 10.6 %collective-permute-start.2 = (bf16[384,256]{1,0:T(8,128)(2,1)S(1)}, bf16[384,256]{1,0:T(8,128)(2,1)S(1)}, u32[]{:S(2)}, u32[]{:S(2)}) collective-permute-start(bf16[384,256]{1,0:T(8,128)(2,1)S(1)} %get-tuple-element.66), channel_id=1, source_target_pairs={{4,0},{8,4},{12,8},{16,12},{20,16},{24,20},{28,24},{32,28},{36,32}... | collective-permute-start | bytes 589832 | tf_op jit(solution)/shard_map/ppermute | solution.py:560
  22.5 11.5 %copy-start.28 = (bf16[384,256]{1,0:T(8,128)(2,1)}, bf16[384,256]{1,0:T(8,128)(2,1)S(1)}, u32[]{:S(2)}) copy-start(bf16[384,256]{1,0:T(8,128)(2,1)S(1)} %collective-permute-done.2.c.after_ref) | copy-start | bytes 589828
  22.5 63.7 %all-to-all-start = ((bf16[16,1024,128]{2,1,0:T(8,128)(2,1)}), bf16[16,1024,128]{2,1,0:T(8,128)(2,1)}, u32[]{:S(2)}, u32[]{:S(2)}) async-start(bf16[16,1024,128]{2,1,0:T(8,128)(2,1)} %bitcast.39), calls=%async_computation | async-start | bytes 8388608 | tf_op jit(solution)/shard_map/all_to_all | solution.py:598
  27.1 59.1 %collective-permute-start.3 = (bf16[2048,256]{1,0:T(8,128)(2,1)}, bf16[2048,256]{1,0:T(8,128)(2,1)}, u32[]{:S(2)}, u32[]{:S(2)}) collective-permute-start(bf16[2048,256]{1,0:T(8,128)(2,1)} %bitcast.40), channel_id=1, source_target_pairs={{1,0},{2,1},{3,2},{0,3},{5,4},{6,5},{7,6},{4,7},{9,8},{10,9},{11,1... | collective-permute-start | bytes 3145736 | tf_op jit(solution)/shard_map/ppermute | solution.py:560
  29.9 56.3 %collective-permute-start.4 = (bf16[2048,256]{1,0:T(8,128)(2,1)}, bf16[2048,256]{1,0:T(8,128)(2,1)}, u32[]{:S(2)}, u32[]{:S(2)}) collective-permute-start(bf16[2048,256]{1,0:T(8,128)(2,1)} %bitcast.41), channel_id=1, source_target_pairs={{3,0},{0,1},{1,2},{2,3},{7,4},{4,5},{5,6},{6,7},{11,8},{8,9},{9,10... | collective-permute-start | bytes 3145736 | tf_op jit(solution)/shard_map/ppermute | solution.py:560
  34.0 46.2 %collective-permute-start.5 = (bf16[256,256]{1,0:T(8,128)(2,1)S(1)}, bf16[256,256]{1,0:T(8,128)(2,1)S(1)}, u32[]{:S(2)}, u32[]{:S(2)}) collective-permute-start(bf16[256,256]{1,0:T(8,128)(2,1)S(1)} %shard_map.122.a), channel_id=1, source_target_pairs={{16,0},{20,4},{24,8},{28,12},{32,16},{36,20},{40,24},{44,28},{48,3... | collective-permute-start | bytes 393224 | tf_op jit(solution)/shard_map/ppermute | solution.py:560
  37.1 46.8 %collective-permute-start.6 = (bf16[256,256]{1,0:T(8,128)(2,1)S(1)}, bf16[256,256]{1,0:T(8,128)(2,1)S(1)}, u32[]{:S(2)}, u32[]{:S(2)}) collective-permute-start(bf16[256,256]{1,0:T(8,128)(2,1)S(1)} %shard_map.122.a), channel_id=1, source_target_pairs={{48,0},{52,4},{56,8},{60,12},{0,16},{4,20},{8,24},{12,28},{16,32},... | collective-permute-start | bytes 393224 | tf_op jit(solution)/shard_map/ppermute | solution.py:560
  37.1 49.1 %collective-permute-start.7 = (bf16[256,256]{1,0:T(8,128)(2,1)S(1)}, bf16[256,256]{1,0:T(8,128)(2,1)S(1)}, u32[]{:S(2)}, u32[]{:S(2)}) collective-permute-start(bf16[256,256]{1,0:T(8,128)(2,1)S(1)} %shard_map.122.a), channel_id=1, source_target_pairs={{32,0},{36,4},{40,8},{44,12},{48,16},{52,20},{56,24},{60,28},{0,32... | collective-permute-start | bytes 393224 | tf_op jit(solution)/shard_map/ppermute | solution.py:560
  80.2 6.0 %copy-start.31 = (bf16[256,256]{1,0:T(8,128)(2,1)}, bf16[256,256]{1,0:T(8,128)(2,1)S(1)}, u32[]{:S(2)}) copy-start(bf16[256,256]{1,0:T(8,128)(2,1)S(1)} %collective-permute-done.5.b) | copy-start | bytes 393220
  86.8 61.8 %all-to-all-start.1 = ((bf16[16,1024,128]{2,1,0:T(8,128)(2,1)}), bf16[16,1024,128]{2,1,0:T(8,128)(2,1)}, u32[]{:S(2)}, u32[]{:S(2)}) async-start(bf16[16,1024,128]{2,1,0:T(8,128)(2,1)} %bitcast.38), calls=%async_computation.1 | async-start | bytes 8388608 | tf_op jit(solution)/shard_map/all_to_all | solution.py:598
  93.7 19.2 %copy-start.8 = (bf16[256,1024]{1,0:T(8,128)(2,1)S(1)}, bf16[256,1024]{1,0:T(8,128)(2,1)}, u32[]{:S(2)}) copy-start(bf16[256,1024]{1,0:T(8,128)(2,1)} %refs_8_.1) | copy-start | bytes 1572868
  95.6 11.9 %collective-permute-start.8 = (bf16[1024,256]{1,0:T(8,128)(2,1)}, bf16[1024,256]{1,0:T(8,128)(2,1)S(1)}, u32[]{:S(2)}, u32[]{:S(2)}) collective-permute-start(bf16[1024,256]{1,0:T(8,128)(2,1)} %slice.18), channel_id=1, source_target_pairs={{1,0},{2,1},{3,2},{0,3},{5,4},{6,5},{7,6},{4,7},{9,8},{10,9},{11,1... | collective-permute-start | bytes 1572872 | tf_op jit(solution)/shard_map/ppermute | solution.py:560
  100.3 12.6 %collective-permute-start.9 = (bf16[1024,256]{1,0:T(8,128)(2,1)}, bf16[1024,256]{1,0:T(8,128)(2,1)}, u32[]{:S(2)}, u32[]{:S(2)}) collective-permute-start(bf16[1024,256]{1,0:T(8,128)(2,1)} %slice.19), channel_id=1, source_target_pairs={{3,0},{0,1},{1,2},{2,3},{7,4},{4,5},{5,6},{6,7},{11,8},{8,9},{9,10... | collective-permute-start | bytes 1572872 | tf_op jit(solution)/shard_map/ppermute | solution.py:560
  103.1 15.4 %copy-start.29 = (bf16[384,256]{1,0:T(8,128)(2,1)S(1)}, bf16[384,256]{1,0:T(8,128)(2,1)}, u32[]{:S(2)}) copy-start(bf16[384,256]{1,0:T(8,128)(2,1)} %copy-done.28) | copy-start | bytes 589828
  103.1 15.4 %copy-start.42 = (s32[96]{0:T(128)S(1)}, s32[96]{0:T(128)}, u32[]{:S(2)}) copy-start(s32[96]{0:T(128)} %get-tuple-element.73.slot_ref.to_ref) | copy-start | bytes 1156
  103.1 15.4 %copy-start.37 = (bf16[256,256]{1,0:T(8,128)(2,1)}, bf16[256,256]{1,0:T(8,128)(2,1)S(1)}, u32[]{:S(2)}) copy-start(bf16[256,256]{1,0:T(8,128)(2,1)S(1)} %shard_map.124) | copy-start | bytes 393220
  148.6 7.1 %copy-start.38 = (bf16[256,256]{1,0:T(8,128)(2,1)S(1)}, bf16[256,256]{1,0:T(8,128)(2,1)}, u32[]{:S(2)}) copy-start(bf16[256,256]{1,0:T(8,128)(2,1)} %copy-done.37) | copy-start | bytes 393220
  148.6 56.3 %all-to-all-start.2 = ((bf16[16,1024,128]{2,1,0:T(8,128)(2,1)}), bf16[16,1024,128]{2,1,0:T(8,128)(2,1)}, u32[]{:S(2)}, u32[]{:S(2)}) async-start(bf16[16,1024,128]{2,1,0:T(8,128)(2,1)} %bitcast.51), calls=%async_computation.2 | async-start | bytes 8388608 | tf_op jit(solution)/shard_map/all_to_all | solution.py:598
  163.2 26.0 %copy-start.15 = (bf16[1,2048,256]{2,1,0:T(8,128)(2,1)S(1)}, bf16[1,2048,256]{2,1,0:T(8,128)(2,1)}, u32[]{:S(2)}) copy-start(bf16[1,2048,256]{2,1,0:T(8,128)(2,1)} %param.11) | copy-start | bytes 3145732
  189.2 5.1 %copy-start.52 = (bf16[2,64,256]{2,1,0:T(8,128)(2,1)}, bf16[2,64,256]{2,1,0:T(8,128)(2,1)S(1)}, u32[]{:S(2)}) copy-start(bf16[2,64,256]{2,1,0:T(8,128)(2,1)S(1)} %get-tuple-element.100) | copy-start | bytes 196612
  194.3 1.8 collective-permute-start.10
  196.9 15.5 %copy-start.12 = (bf16[2048,256]{1,0:T(8,128)(2,1)S(1)}, bf16[2048,256]{1,0:T(8,128)(2,1)}, u32[]{:S(2)}) copy-start(bf16[2048,256]{1,0:T(8,128)(2,1)} %copy-done.11) | copy-start | bytes 3145732
  196.9 17.6 %copy-start.49 = (bf16[2,64,256]{2,1,0:T(8,128)(2,1)S(1)}, bf16[2,64,256]{2,1,0:T(8,128)(2,1)}, u32[]{:S(2)}) copy-start(bf16[2,64,256]{2,1,0:T(8,128)(2,1)} %copy-done.48) | copy-start | bytes 196612
  196.9 18.9 %copy-start.53 = (bf16[2,64,256]{2,1,0:T(8,128)(2,1)S(1)}, bf16[2,64,256]{2,1,0:T(8,128)(2,1)}, u32[]{:S(2)}) copy-start(bf16[2,64,256]{2,1,0:T(8,128)(2,1)} %copy-done.52) | copy-start | bytes 196612
  204.9 39.2 %all-to-all-start.3 = ((bf16[16,608,128]{2,1,0:T(8,128)(2,1)}), bf16[16,608,128]{2,1,0:T(8,128)(2,1)}, u32[]{:S(2)}, u32[]{:S(2)}) async-start(bf16[16,608,128]{2,1,0:T(8,128)(2,1)} %shard_map.128), calls=%async_computation.3 | async-start | bytes 4980736 | tf_op jit(solution)/shard_map/all_to_all | solution.py:598
  212.4 33.6 %collective-permute-start.13 = (bf16[2048,256]{1,0:T(8,128)(2,1)S(1)}, bf16[2048,256]{1,0:T(8,128)(2,1)S(1)}, u32[]{:S(2)}, u32[]{:S(2)}) collective-permute-start(bf16[2048,256]{1,0:T(8,128)(2,1)S(1)} %copy-done.12), channel_id=1, source_target_pairs={{1,0},{2,1},{3,2},{0,3},{5,4},{6,5},{7,6},{4,7},{9,8},{10,9},{11,1... | collective-permute-start | bytes 3145736 | tf_op jit(solution)/shard_map/ppermute | solution.py:560
  212.5 33.6 %collective-permute-start.14 = (bf16[2048,256]{1,0:T(8,128)(2,1)S(1)}, bf16[2048,256]{1,0:T(8,128)(2,1)}, u32[]{:S(2)}, u32[]{:S(2)}) collective-permute-start(bf16[2048,256]{1,0:T(8,128)(2,1)S(1)} %copy-done.12), channel_id=1, source_target_pairs={{3,0},{0,1},{1,2},{2,3},{7,4},{4,5},{5,6},{6,7},{11,8},{8,9},{9,10... | collective-permute-start | bytes 3145736 | tf_op jit(solution)/shard_map/ppermute | solution.py:560
  214.5 31.5 %collective-permute-start.11 = (bf16[2,64,256]{2,1,0:T(8,128)(2,1)S(1)}, bf16[2,64,256]{2,1,0:T(8,128)(2,1)S(1)}, u32[]{:S(2)}, u32[]{:S(2)}) collective-permute-start(bf16[2,64,256]{2,1,0:T(8,128)(2,1)S(1)} %copy-done.49), channel_id=1, source_target_pairs={{4,0},{8,4},{12,8},{16,12},{20,16},{24,20},{28,24},{32,28},{36,32}... | collective-permute-start | bytes 196616 | tf_op jit(solution)/shard_map/ppermute | solution.py:576
  215.8 30.2 %collective-permute-start.12 = (bf16[2,64,256]{2,1,0:T(8,128)(2,1)S(1)}, bf16[2,64,256]{2,1,0:T(8,128)(2,1)S(1)}, u32[]{:S(2)}, u32[]{:S(2)}) collective-permute-start(bf16[2,64,256]{2,1,0:T(8,128)(2,1)S(1)} %copy-done.53), channel_id=1, source_target_pairs={{0,4},{4,8},{8,12},{12,16},{16,20},{20,24},{24,28},{28,32},{32,36}... | collective-permute-start | bytes 196616 | tf_op jit(solution)/shard_map/ppermute | solution.py:576
  246.1 5.1 %copy-start.16 = (bf16[2048,256]{1,0:T(8,128)(2,1)}, bf16[2048,256]{1,0:T(8,128)(2,1)S(1)}, u32[]{:S(2)}) copy-start(bf16[2048,256]{1,0:T(8,128)(2,1)S(1)} %collective-permute-done.13.refs_1_) | copy-start | bytes 3145732
  246.1 37.0 %all-to-all-start.4 = ((bf16[16,608,128]{2,1,0:T(8,128)(2,1)}), bf16[16,608,128]{2,1,0:T(8,128)(2,1)}, u32[]{:S(2)}, u32[]{:S(2)}) async-start(bf16[16,608,128]{2,1,0:T(8,128)(2,1)} %broadcast_dynamic-update-slice_fusion), calls=%async_computation.4 | async-start | bytes 4980736 | tf_op jit(solution)/shard_map/all_to_all | solution.py:598
  251.2 7.2 %copy-start.40 = (s32[1,2]{1,0:T(1,128)S(1)}, s32[1,2]{1,0:T(1,128)}, u32[]{:S(2)}) copy-start(s32[1,2]{1,0:T(1,128)} %param.15) | copy-start | bytes 28
  252.0 6.4 %copy-start.19 = (f32[2,2048,128]{2,1,0:T(8,128)S(1)}, f32[2,2048,128]{2,1,0:T(8,128)}, u32[]{:S(2)}) copy-start(f32[2,2048,128]{2,1,0:T(8,128)} %copy-done.18) | copy-start | bytes 6291460
  252.0 19.7 %collective-permute-start.15 = (bf16[1024,256]{1,0:T(8,128)(2,1)}, bf16[1024,256]{1,0:T(8,128)(2,1)S(1)}, u32[]{:S(2)}, u32[]{:S(2)}) collective-permute-start(bf16[1024,256]{1,0:T(8,128)(2,1)} %slice.21), channel_id=1, source_target_pairs={{1,0},{2,1},{3,2},{0,3},{5,4},{6,5},{7,6},{4,7},{9,8},{10,9},{11,1... | collective-permute-start | bytes 1572872 | tf_op jit(solution)/shard_map/ppermute | solution.py:560
  254.0 17.7 %collective-permute-start.16 = (bf16[1024,256]{1,0:T(8,128)(2,1)}, bf16[1024,256]{1,0:T(8,128)(2,1)}, u32[]{:S(2)}, u32[]{:S(2)}) collective-permute-start(bf16[1024,256]{1,0:T(8,128)(2,1)} %slice.22), channel_id=1, source_target_pairs={{3,0},{0,1},{1,2},{2,3},{7,4},{4,5},{5,6},{6,7},{11,8},{8,9},{9,10... | collective-permute-start | bytes 1572872 | tf_op jit(solution)/shard_map/ppermute | solution.py:560
  256.0 11.1 %collective-permute-start.17 = (bf16[256,256]{1,0:T(8,128)(2,1)S(1)}, bf16[256,256]{1,0:T(8,128)(2,1)S(1)}, u32[]{:S(2)}, u32[]{:S(2)}) collective-permute-start(bf16[256,256]{1,0:T(8,128)(2,1)S(1)} %get-tuple-element.127), channel_id=1, source_target_pairs={{1,0},{2,1},{3,2},{0,3},{5,4},{6,5},{7,6},{4,7},{9,8},{10,9},{11,1... | collective-permute-start | bytes 393224 | tf_op jit(solution)/shard_map/ppermute | solution.py:560
  257.4 11.7 %collective-permute-start.18 = (bf16[256,256]{1,0:T(8,128)(2,1)S(1)}, bf16[256,256]{1,0:T(8,128)(2,1)S(1)}, u32[]{:S(2)}, u32[]{:S(2)}) collective-permute-start(bf16[256,256]{1,0:T(8,128)(2,1)S(1)} %get-tuple-element.126), channel_id=1, source_target_pairs={{2,0},{3,1},{0,2},{1,3},{6,4},{7,5},{4,6},{5,7},{10,8},{11,9},{8,1... | collective-permute-start | bytes 393224 | tf_op jit(solution)/shard_map/ppermute | solution.py:560
  258.1 13.6 %collective-permute-start.19 = (bf16[256,256]{1,0:T(8,128)(2,1)S(1)}, bf16[256,256]{1,0:T(8,128)(2,1)S(1)}, u32[]{:S(2)}, u32[]{:S(2)}) collective-permute-start(bf16[256,256]{1,0:T(8,128)(2,1)S(1)} %get-tuple-element.125), channel_id=1, source_target_pairs={{3,0},{0,1},{1,2},{2,3},{7,4},{4,5},{5,6},{6,7},{11,8},{8,9},{9,10... | collective-permute-start | bytes 393224 | tf_op jit(solution)/shard_map/ppermute | solution.py:560
  262.8 8.9 %copy-start.13 = (bf16[2048,256]{1,0:T(8,128)(2,1)S(1)}, bf16[2048,256]{1,0:T(8,128)(2,1)}, u32[]{:S(2)}) copy-start(bf16[2048,256]{1,0:T(8,128)(2,1)} %copy-done.11) | copy-start | bytes 3145732
  262.8 9.0 %copy-start.17 = (bf16[2048,256]{1,0:T(8,128)(2,1)S(1)}, bf16[2048,256]{1,0:T(8,128)(2,1)}, u32[]{:S(2)}) copy-start(bf16[2048,256]{1,0:T(8,128)(2,1)} %copy-done.16) | copy-start | bytes 3145732
  283.1 8.9 %copy-start.1 = (s32[1,512,3]{1,0,2:T(1,128)S(1)}, s32[1,512,3]{1,0,2:T(1,128)}, u32[]{:S(2)}) copy-start(s32[1,512,3]{1,0,2:T(1,128)} %param.14) | copy-start | bytes 18436
  284.0 6.3 %collective-permute-start.20 = (bf16[16,64,128]{2,1,0:T(8,128)(2,1)S(1)}, bf16[16,64,128]{2,1,0:T(8,128)(2,1)S(1)}, u32[]{:S(2)}, u32[]{:S(2)}) collective-permute-start(bf16[16,64,128]{2,1,0:T(8,128)(2,1)S(1)} %slice.23.own_ref), channel_id=1, source_target_pairs={{64,0},{0,64},{65,1},{1,65},{66,2},{2,66},{67,3},{3,67},{68,4},{4,... | collective-permute-start | bytes 786440 | tf_op jit(solution)/shard_map/ppermute | solution.py:560
  (33 other events, 55.7 us)
